TPU v7x, 32 devices: a whole 2x2x4 slice. The times are simulated.
32 devices in a mesh: section: 2 (over core), seq: 4 (over z), head: 4 (over y, x).
Axes of the slice: x: 2, y: 2, z: 4, core: 2. Of those that a mesh axis runs over, the one named last changes fastest.
Arguments:
- tokens: bfloat16 [2, 1024, 2048], P(None, 'seq'), may hold values from -6 to 6
- cotangent: bfloat16 [2, 1024, 2048], P(None, 'seq'), may hold values from -6 to 6
- doc_starts: int32 [2, 8], replicated, may hold values from 0 to 1023, as said below
- valid_mask: int32 [2, 1024], P(None, 'seq'), may hold values 0 or 1
- gain_attn: bfloat16 [2, 2048], P('section', 'seq'), may hold values from 0.099609375 to 1.8984375
- w_query: bfloat16 [2, 2048, 2048], P('section', 'seq', 'head'), may hold values from -0.125 to 0.125
- w_key: bfloat16 [2, 2048, 2048], P('section', 'seq', 'head'), may hold values from -0.125 to 0.125
- w_value: bfloat16 [2, 2048, 4096], P('section', 'seq', 'head'), may hold values from -0.125 to 0.125
- w_gate_out: bfloat16 [2, 2048, 4096], P('section', 'seq', 'head'), may hold values from -0.125 to 0.125
- w_decay: bfloat16 [2, 2048, 16], P('section', 'seq', 'head'), may hold values from -0.125 to 0.125
- w_beta: bfloat16 [2, 2048, 16], P('section', 'seq', 'head'), may hold values from -0.125 to 0.125
- conv_query: bfloat16 [2, 4, 2048], P('section', None, 'head'), may hold values from -3 to 3
- conv_key: bfloat16 [2, 4, 2048], P('section', None, 'head'), may hold values from -3 to 3
- conv_value: bfloat16 [2, 4, 4096], P('section', None, 'head'), may hold values from -3 to 3
- decay_log: float32 [2, 16], P('section', 'head'), may hold values from -3 to 1.5
- decay_bias: float32 [2, 16], P('section', 'head'), may hold values from -7 to -3
- out_norm: bfloat16 [2, 256], P('section'), may hold values from 0.099609375 to 1.8984375
- w_output: bfloat16 [2, 4096, 2048], P('section', 'head', 'seq'), may hold values from -0.125 to 0.125
- gain_mlp: bfloat16 [2, 2048], P('section', 'seq'), may hold values from 0.099609375 to 1.8984375
- w_gate: bfloat16 [2, 2048, 5632], P('section', 'seq', 'head'), may hold values from -0.125 to 0.125
- w_up: bfloat16 [2, 2048, 5632], P('section', 'seq', 'head'), may hold values from -0.125 to 0.125
- w_down: bfloat16 [2, 5632, 2048], P('section', 'head', 'seq'), may hold values from -0.109375 to 0.109375
Outputs:
- activations: bfloat16 [2, 2, 1024, 2048], P('section', None, 'seq')
- input_grads: bfloat16 [2, 2, 1024, 2048], P('section', None, 'seq')
- branch_rms: float32 [2, 2, 3], P('section')
- grad_gain_attn: float32 [2, 2048], P('section', 'seq')
- grad_w_query: float32 [2, 2048, 2048], P('section', 'seq', 'head')
- grad_w_key: float32 [2, 2048, 2048], P('section', 'seq', 'head')
- grad_w_value: float32 [2, 2048, 4096], P('section', 'seq', 'head')
- grad_w_gate_out: float32 [2, 2048, 4096], P('section', 'seq', 'head')
- grad_w_decay: float32 [2, 2048, 16], P('section', 'seq', 'head')
- grad_w_beta: float32 [2, 2048, 16], P('section', 'seq', 'head')
- grad_conv_query: float32 [2, 4, 2048], P('section', None, 'head')
- grad_conv_key: float32 [2, 4, 2048], P('section', None, 'head')
- grad_conv_value: float32 [2, 4, 4096], P('section', None, 'head')
- grad_decay_log: float32 [2, 16], P('section', 'head')
- grad_decay_bias: float32 [2, 16], P('section', 'head')
- grad_out_norm: float32 [2, 256], P('section')
- grad_w_output: float32 [2, 4096, 2048], P('section', 'head', 'seq')
- grad_gain_mlp: float32 [2, 2048], P('section', 'seq')
- grad_w_gate: float32 [2, 2048, 5632], P('section', 'seq', 'head')
- grad_w_up: float32 [2, 2048, 5632], P('section', 'seq', 'head')
- grad_w_down: float32 [2, 5632, 2048], P('section', 'head', 'seq')
Inputs may be any that keep to these rules, and one draw needn't show every extreme that they name: doc_starts[m] lists the first positions of the documents of micro-batch m in non-decreasing order; a repeated value adds no document; the first entry is 0; in one micro-batch all entries are 0, so one document spans all 1024 tokens; in each other micro-batch the last entry is 1023.
All inputs are finite; a program needn't handle non-finite values. No bound on the sum of `valid_mask` on one device may be relied on, other than what follows from the above.
Results may differ from a plain program's by a relative error of at most 0.04.
Values may be sent and summed in bfloat16 or wider, within the bound.
No kernel may reach another device: no remote copies, remote signals or barrier semaphores. Data moves between devices by JAX's collectives and lax.ppermute only.
A program may use at most 384 MiB of HBM per device.

v0:
```python
import jax
import jax.numpy as jnp
from jax import lax
from jax.sharding import PartitionSpec as P

HEAD_K = 128
HEAD_V = 256
CONVK = 4
BLOCK = 64


epsilon = 1e-06
highest_precision = lax.Precision.HIGHEST


def swapped(value, axis, stride):
    return lax.ppermute(value, axis, [(i, i ^ 1 << stride) for i in range(lax.axis_size(axis))])


def carried_in(value, axis, combine, identity):
    devices, position = (lax.axis_size(axis), lax.axis_index(axis))
    everything = jax.tree.map(
        lambda part, kind: lax.all_gather(part.astype(kind), axis),
        value,
        (jnp.bfloat16, jnp.bfloat16),
    )
    start = jax.tree.map(
        lambda part, zero: jnp.broadcast_to(jnp.asarray(zero, part.dtype), part.shape),
        value,
        identity,
    )

    def step(k, before):
        reached = k < position
        new = combine(
            before, jax.tree.map(lambda part, own: part[k].astype(own.dtype), everything, value)
        )
        return jax.tree.map(lambda a, b: jnp.where(reached, a, b), new, before)

    return lax.fori_loop(0, devices, step, start)


def entering(value, axis, join, neutral):
    count = lax.axis_size(axis)
    place = lax.axis_index(axis)
    ahead = count - 1 - place
    gathered = jax.tree.map(
        lambda a, kind: lax.all_gather(a.astype(kind), axis),
        value,
        jax.tree.map(lambda a: jnp.bfloat16 if a.dtype == jnp.float32 else a.dtype, value),
    )
    state = jax.tree.map(lambda a, e: jnp.zeros_like(a) + jnp.asarray(e, a.dtype), value, neutral)

    def one(step, state):
        source = count - 1 - step
        return join(
            state,
            jax.tree.map(
                lambda a, own: lax.dynamic_index_in_dim(a, source, 0, False).astype(own.dtype),
                gathered,
                value,
            ),
        )

    return lax.fori_loop(0, ahead, one, state)


def passed_along(value, axis, steps):
    count = lax.axis_size(axis)
    first, last = (max(0, -steps), min(count, count - steps))
    return lax.ppermute(value, axis, [(source, source + steps) for source in range(first, last)])


def rms_norm(values, weight):
    return values * lax.rsqrt(jnp.mean(values * values, axis=-1, keepdims=True) + epsilon) * weight


def doc_index(starts, positions):
    counted = jnp.sum(
        (starts[None, :] <= positions[:, None]).astype(jnp.int32), axis=1, dtype=jnp.int32
    )
    return counted - 1


def unit_rows(values):
    return values * lax.rsqrt(jnp.sum(values * values, axis=-1, keepdims=True) + epsilon)


def conv_front(extended, doc_ext, conv_weight):
    length = extended.shape[0] - (CONVK - 1)
    summed = jnp.zeros((length, extended.shape[1]), extended.dtype)
    for tap_index in range(CONVK):
        same_doc = doc_ext[tap_index : tap_index + length] == doc_ext[CONVK - 1 :]
        summed = (
            summed
            + jnp.where(same_doc[:, None], extended[tap_index : tap_index + length], 0.0)
            * conv_weight[tap_index]
        )
    return jax.nn.silu(summed)


def heads_front(extended, doc_ext, mix_pre, conv_weight, decay_scale, decay_shift, head_count):
    activated = conv_front(extended, doc_ext, conv_weight)
    length = activated.shape[0]
    width_k = head_count * HEAD_K
    queries = unit_rows(activated[:, :width_k].reshape(length, head_count, HEAD_K)) * HEAD_K ** (
        -0.5
    )
    key_rows = unit_rows(activated[:, width_k : 2 * width_k].reshape(length, head_count, HEAD_K))
    value_rows = activated[:, 2 * width_k :].reshape(length, head_count, HEAD_V)
    write_rate = jax.nn.sigmoid(mix_pre[:, head_count:])
    log_decay = -jnp.exp(decay_scale) * jax.nn.softplus(mix_pre[:, :head_count] + decay_shift)
    return (queries, key_rows, value_rows, write_rate, log_decay)


def block_terms(queries, key_rows, value_rows, write_rate, log_decay, doc_ids, prev_doc):
    length = queries.shape[1]
    cumulated = jnp.cumsum(log_decay, axis=1)
    row_iota = lax.broadcasted_iota(jnp.int32, (length, length), 0)
    col_iota = lax.broadcasted_iota(jnp.int32, (length, length), 1)
    same_doc = (doc_ids[:, :, None] == doc_ids[:, None, :]) & (col_iota <= row_iota)[None]
    same_mask = same_doc[:, :, :, None]
    exponent = jnp.where(same_mask, cumulated[:, :, None, :] - cumulated[:, None, :, :], 0.0)
    decay_full = jnp.where(same_mask, jnp.exp(exponent), 0.0)
    initial_decay = jnp.where((doc_ids == prev_doc[:, None])[:, :, None], jnp.exp(cumulated), 0.0)
    decay_heads = jnp.transpose(decay_full, (0, 3, 1, 2))
    key_gram = jnp.einsum("nthk,nihk->nhti", key_rows, key_rows, precision=highest_precision)
    strict_mask = (col_iota < row_iota)[None, None]
    lower_part = jnp.where(
        strict_mask,
        jnp.transpose(write_rate, (0, 2, 1))[:, :, :, None] * decay_heads * key_gram,
        0.0,
    )
    system = lower_part + jnp.eye(length, dtype=lower_part.dtype)
    scaled_values = jnp.transpose(write_rate[..., None] * value_rows, (0, 2, 1, 3))
    scaled_keys = jnp.transpose((write_rate * initial_decay)[..., None] * key_rows, (0, 2, 1, 3))
    resolved_values = lax.linalg.triangular_solve(
        system, scaled_values, left_side=True, lower=True, unit_diagonal=True
    )
    resolved_keys = lax.linalg.triangular_solve(
        system, scaled_keys, left_side=True, lower=True, unit_diagonal=True
    )
    query_key = (
        jnp.einsum("nthk,nihk->nhti", queries, key_rows, precision=highest_precision) * decay_heads
    )
    return (resolved_values, resolved_keys, query_key, decay_heads, initial_decay)


def gate_norm(mixed_out, gate_pre, norm_weight, head_count):
    length = mixed_out.shape[0]
    per_head = mixed_out.reshape(length, head_count, HEAD_V)
    gates = gate_pre.reshape(length, head_count, HEAD_V)
    normed = rms_norm(per_head, norm_weight) * jax.nn.silu(gates)
    return normed.reshape(length, head_count * HEAD_V)


def summary(
    extended, mix_pre, conv_weight, decay_scale, decay_shift, doc_ext, prev_docs, head_count
):
    queries, key_rows, value_rows, write_rate, log_decay = heads_front(
        extended, doc_ext, mix_pre, conv_weight, decay_scale, decay_shift, head_count
    )
    length = write_rate.shape[0]
    blocks = length // BLOCK

    def as_blocks(values):
        return values.reshape((blocks, BLOCK) + values.shape[1:])

    block_query_rows = as_blocks(queries)
    block_key_rows = as_blocks(key_rows)
    resolved_values, resolved_keys, query_key, decay_heads, initial_decay = block_terms(
        block_query_rows,
        block_key_rows,
        as_blocks(value_rows),
        as_blocks(write_rate),
        as_blocks(log_decay),
        as_blocks(doc_ext[CONVK - 1 :]),
        prev_docs,
    )
    final_row = decay_heads[:, :, -1, :]
    identity = jnp.eye(HEAD_K, dtype=extended.dtype)
    transfer_blocks = initial_decay[:, -1, :][:, :, None, None] * identity - jnp.einsum(
        "nhi,nihk,nhil->nhkl", final_row, block_key_rows, resolved_keys, precision=highest_precision
    )
    add_blocks = jnp.einsum(
        "nhi,nihk,nhiv->nhkv",
        final_row,
        block_key_rows,
        resolved_values,
        precision=highest_precision,
    )
    local_out = jnp.einsum(
        "nhti,nhiv->nhtv", query_key, resolved_values, precision=highest_precision
    )
    response = jnp.transpose(initial_decay, (0, 2, 1))[..., None] * jnp.transpose(
        block_query_rows, (0, 2, 1, 3)
    ) - jnp.einsum("nhti,nhik->nhtk", query_key, resolved_keys, precision=highest_precision)
    carry_map = jnp.broadcast_to(identity, (head_count, HEAD_K, HEAD_K))
    carried_addend = jnp.zeros((head_count, HEAD_K, HEAD_V), extended.dtype)
    entry_maps = []
    entry_adds = []
    for block_number in range(blocks):
        entry_maps.append(carry_map)
        entry_adds.append(carried_addend)
        carried_addend = (
            jnp.einsum(
                "jme,jed->jmd",
                transfer_blocks[block_number],
                carried_addend,
                precision=highest_precision,
            )
            + add_blocks[block_number]
        )
        carry_map = jnp.einsum(
            "hkl,hlm->hkm", transfer_blocks[block_number], carry_map, precision=highest_precision
        )
    kept = (local_out, response, jnp.stack(entry_maps), jnp.stack(entry_adds))
    return (carry_map, carried_addend, kept)


def finish(kept, running_state):
    local_out, response, entry_maps, entry_adds = kept
    entry_states = (
        jnp.einsum("nhkl,hlv->nhkv", entry_maps, running_state, precision=highest_precision)
        + entry_adds
    )
    result = local_out + jnp.einsum(
        "nhck,nhkv->nhcv", response, entry_states, precision=highest_precision
    )
    blocks, head_count, length, width_v = result.shape
    return jnp.transpose(result, (0, 2, 1, 3)).reshape(blocks * length, head_count * width_v)


def compose(earlier_blocks, later_blocks):
    return (
        jnp.einsum("hkl,hlm->hkm", later_blocks[0], earlier_blocks[0], precision=highest_precision),
        jnp.einsum("jme,jed->jmd", later_blocks[0], earlier_blocks[1], precision=highest_precision)
        + later_blocks[1],
    )


def head_total(values):
    return lax.psum(values.astype(jnp.bfloat16), "head").astype(jnp.float32)


def partner(values):
    return swapped(values, "section", 0)


def proj_t(left, right):
    return lax.dot_general(
        left, right, (((1,), (1,)), ((), ())), preferred_element_type=jnp.float32
    )


def inner_t(left, right):
    return lax.dot_general(
        left, right, (((0,), (0,)), ((), ())), preferred_element_type=jnp.float32
    )


def spread(rows_grads, cols_grads):
    rows_part = (
        lax.psum_scatter(
            rows_grads[0].astype(jnp.bfloat16), "seq", scatter_dimension=0, tiled=True
        ).astype(jnp.float32),
        lax.psum_scatter(
            rows_grads[1].astype(jnp.bfloat16), "seq", scatter_dimension=0, tiled=True
        ).astype(jnp.float32),
        lax.psum_scatter(
            rows_grads[2].astype(jnp.bfloat16), "seq", scatter_dimension=0, tiled=True
        ).astype(jnp.float32),
        lax.psum_scatter(
            rows_grads[3].astype(jnp.bfloat16), "seq", scatter_dimension=0, tiled=True
        ).astype(jnp.float32),
        lax.psum_scatter(
            rows_grads[4].astype(jnp.bfloat16), "seq", scatter_dimension=0, tiled=True
        ).astype(jnp.float32),
    )
    cols_part = (
        lax.psum_scatter(
            cols_grads[0].astype(jnp.bfloat16), "seq", scatter_dimension=1, tiled=True
        ).astype(jnp.float32),
        lax.psum_scatter(
            cols_grads[1].astype(jnp.bfloat16), "seq", scatter_dimension=1, tiled=True
        ).astype(jnp.float32),
    )
    return (rows_part, cols_part)


def shards(
    tokens,
    cotangent,
    doc_starts,
    valid_mask,
    gain_attn,
    w_query,
    w_key,
    w_value,
    w_gate_out,
    w_decay,
    w_beta,
    conv_query,
    conv_key,
    conv_value,
    decay_log,
    decay_bias,
    out_norm,
    w_output,
    gain_mlp,
    w_gate,
    w_up,
    w_down,
):
    micro_count = tokens.shape[0]
    row_count = tokens.shape[1]
    model_width = tokens.shape[2]
    head_count = w_decay.shape[2]
    width_qk = w_query.shape[2]
    width_qkv = 2 * width_qk + w_value.shape[2]
    hidden_width = w_gate.shape[2]
    block_count = row_count // BLOCK
    section_index = lax.axis_index("section")
    shard_index = lax.axis_index("seq")
    full_rows = (
        lax.all_gather(gain_attn[0], "seq", axis=0, tiled=True),
        lax.all_gather(gain_mlp[0], "seq", axis=0, tiled=True),
        lax.all_gather(w_query[0], "seq", axis=0, tiled=True),
        lax.all_gather(w_key[0], "seq", axis=0, tiled=True),
        lax.all_gather(w_value[0], "seq", axis=0, tiled=True),
        lax.all_gather(w_gate_out[0], "seq", axis=0, tiled=True),
        lax.all_gather(w_decay[0], "seq", axis=0, tiled=True),
        lax.all_gather(w_beta[0], "seq", axis=0, tiled=True),
        lax.all_gather(w_gate[0], "seq", axis=0, tiled=True),
        lax.all_gather(w_up[0], "seq", axis=0, tiled=True),
    )
    full_cols = (
        lax.all_gather(w_output[0], "seq", axis=1, tiled=True),
        lax.all_gather(w_down[0], "seq", axis=1, tiled=True),
    )
    attn_gain = full_rows[0].astype(jnp.float32)
    mlp_gain = full_rows[1].astype(jnp.float32)
    proj_weight = jnp.concatenate([full_rows[2], full_rows[3], full_rows[4], full_rows[5]], axis=1)
    mix_weight = jnp.concatenate([full_rows[6], full_rows[7]], axis=1).astype(jnp.float32)
    gate_up_weight = jnp.concatenate([full_rows[8], full_rows[9]], axis=1)
    out_weight = full_cols[0]
    down_weight = full_cols[1]
    conv_weight = jnp.concatenate([conv_query[0], conv_key[0], conv_value[0]], axis=1).astype(
        jnp.float32
    )
    decay_scale = decay_log[0]
    decay_shift = decay_bias[0]
    norm_weight = out_norm[0].astype(jnp.float32)
    ext_pos = (
        shard_index * row_count - (CONVK - 1) + jnp.arange(row_count + CONVK - 1, dtype=jnp.int32)
    )
    block_pos = shard_index * row_count + jnp.arange(block_count, dtype=jnp.int32) * BLOCK - 1

    def carry_backward(shard_map_t, shard_adj):
        identity = jnp.broadcast_to(
            jnp.eye(shard_map_t.shape[1], dtype=jnp.float32), shard_map_t.shape
        )
        suffix = entering(
            (shard_map_t, shard_adj), "seq", compose, (identity, jnp.zeros_like(shard_adj))
        )
        result = suffix[1]
        return result

    def layer_backward(saved, upstream, starts):
        (
            resid_in,
            normed,
            mix_pre,
            extended,
            gate_pre,
            kept,
            running_state,
            shard_map,
            mixed_out,
            gated,
            resid_mid,
            ffn_in,
            gate_up,
            hidden,
        ) = saved
        doc_ext = doc_index(starts, ext_pos)
        prev_docs = doc_index(starts, block_pos)
        grad_ffn = upstream.astype(jnp.bfloat16)
        grad_hidden = proj_t(grad_ffn, down_weight)
        grad_down = inner_t(hidden, grad_ffn)
        _, act_back = jax.vjp(
            lambda gate_in, up_in: jax.nn.silu(gate_in) * up_in,
            gate_up[:, :hidden_width],
            gate_up[:, hidden_width:],
        )
        grad_gate, grad_up = act_back(grad_hidden)
        grad_gate_up = jnp.concatenate([grad_gate, grad_up], axis=1).astype(jnp.bfloat16)
        grad_gu_weight = inner_t(ffn_in, grad_gate_up)
        grad_ffn_in = head_total(proj_t(grad_gate_up, gate_up_weight))
        _, mlp_norm_back = jax.vjp(rms_norm, resid_mid, mlp_gain)
        grad_mid_norm, grad_mlp_gain = mlp_norm_back(grad_ffn_in)
        grad_mid = upstream + grad_mid_norm
        grad_attn = grad_mid.astype(jnp.bfloat16)
        grad_gated = proj_t(grad_attn, out_weight)
        grad_out_weight = inner_t(gated, grad_attn)
        _, gate_back = jax.vjp(
            lambda mixed_in, gate_in, weight_in: gate_norm(
                mixed_in, gate_in, weight_in, head_count
            ),
            mixed_out,
            gate_pre,
            norm_weight,
        )
        grad_mixed, grad_gate_pre, grad_norm_weight = gate_back(grad_gated)
        _, finish_back = jax.vjp(finish, kept, running_state)
        grad_kept, grad_state = finish_back(grad_mixed)
        later_blocks = carry_backward(jnp.swapaxes(shard_map, 1, 2), grad_state)
        gradient_transfer = jnp.einsum(
            "rgm,ram->rga", later_blocks, running_state, precision=highest_precision
        )

        def local_summary(ext_in, mix_in, conv_in, scale_in, shift_in):
            return summary(
                ext_in, mix_in, conv_in, scale_in, shift_in, doc_ext, prev_docs, head_count
            )

        _, summary_back = jax.vjp(
            local_summary, extended, mix_pre, conv_weight, decay_scale, decay_shift
        )
        grad_ext, grad_mix, grad_conv, grad_scale, grad_shift = summary_back(
            (gradient_transfer, later_blocks, grad_kept)
        )
        returned = passed_along(grad_ext[: CONVK - 1], "seq", -1)
        grad_qkv = grad_ext[CONVK - 1 :] + jnp.pad(returned, ((row_count - (CONVK - 1), 0), (0, 0)))
        grad_pre = jnp.concatenate([grad_qkv, grad_gate_pre], axis=1).astype(jnp.bfloat16)
        grad_proj_weight = inner_t(normed, grad_pre)
        normed_float = normed.astype(jnp.float32)
        grad_mix_weight = lax.dot_general(
            normed_float, grad_mix, (((0,), (0,)), ((), ())), precision=highest_precision
        )
        grad_normed = head_total(
            proj_t(grad_pre, proj_weight)
            + lax.dot_general(
                grad_mix, mix_weight, (((1,), (1,)), ((), ())), precision=highest_precision
            )
        )
        _, attn_norm_back = jax.vjp(rms_norm, resid_in.astype(jnp.float32), attn_gain)
        grad_resid_norm, grad_attn_gain = attn_norm_back(grad_normed)
        grad_resid = grad_mid + grad_resid_norm
        rows_grads = (
            grad_attn_gain,
            grad_mlp_gain,
            grad_proj_weight,
            grad_mix_weight,
            grad_gu_weight,
        )
        cols_grads = (grad_out_weight, grad_down)
        small_grads = (grad_conv, grad_scale, grad_shift, grad_norm_weight)
        return (grad_resid, rows_grads, cols_grads, small_grads)

    zero_in = jnp.zeros((row_count, model_width), jnp.bfloat16)
    incoming = zero_in
    stored = None
    activations_buf = jnp.zeros(tokens.shape, jnp.bfloat16)
    stat_sums = jnp.zeros((micro_count, 3), jnp.float32)
    stat_counts = jnp.zeros((micro_count,), jnp.float32)
    for slot_index in range(micro_count + 1):
        chosen_raw = slot_index - section_index
        active = (chosen_raw >= 0) & (chosen_raw < micro_count)
        chosen = jnp.clip(chosen_raw, 0, micro_count - 1)
        resid_in = jnp.where(section_index == 0, tokens[min(slot_index, micro_count - 1)], incoming)
        layer_starts = doc_starts[chosen]
        layer_doc_ext = doc_index(layer_starts, ext_pos)
        layer_prev_docs = doc_index(layer_starts, block_pos)
        resid = resid_in.astype(jnp.float32)
        layer_normed = rms_norm(resid, attn_gain).astype(jnp.bfloat16)
        projected = jnp.dot(layer_normed, proj_weight, preferred_element_type=jnp.float32)
        layer_mix_pre = jnp.dot(
            layer_normed.astype(jnp.float32), mix_weight, precision=highest_precision
        )
        qkv_pre = projected[:, :width_qkv]
        layer_gate_pre = projected[:, width_qkv:]
        rim_rows = passed_along(qkv_pre[row_count - (CONVK - 1) :], "seq", 1)
        layer_extended = jnp.concatenate([rim_rows, qkv_pre], axis=0)
        layer_shard_map, layer_shard_add, layer_kept = summary(
            layer_extended,
            layer_mix_pre,
            conv_weight,
            decay_scale,
            decay_shift,
            layer_doc_ext,
            layer_prev_docs,
            head_count,
        )
        carry_identity = jnp.broadcast_to(
            jnp.eye(layer_shard_map.shape[1], dtype=jnp.float32), layer_shard_map.shape
        )
        prefix = carried_in(
            (layer_shard_map, layer_shard_add),
            "seq",
            compose,
            (carry_identity, jnp.zeros_like(layer_shard_add)),
        )
        carry_result = prefix[1]
        layer_mixed_out = finish(layer_kept, carry_result)
        layer_gated = gate_norm(layer_mixed_out, layer_gate_pre, norm_weight, head_count).astype(
            jnp.bfloat16
        )
        attn = head_total(jnp.dot(layer_gated, out_weight, preferred_element_type=jnp.float32))
        layer_resid_mid = resid + attn
        layer_ffn_in = rms_norm(layer_resid_mid, mlp_gain).astype(jnp.bfloat16)
        layer_gate_up = jnp.dot(layer_ffn_in, gate_up_weight, preferred_element_type=jnp.float32)
        layer_hidden = (
            jax.nn.silu(layer_gate_up[:, :hidden_width]) * layer_gate_up[:, hidden_width:]
        ).astype(jnp.bfloat16)
        ffn = head_total(jnp.dot(layer_hidden, down_weight, preferred_element_type=jnp.float32))
        layer_out = layer_resid_mid + ffn
        layer_saved = (
            resid_in,
            layer_normed,
            layer_mix_pre,
            layer_extended,
            layer_gate_pre,
            layer_kept,
            carry_result,
            layer_shard_map,
            layer_mixed_out,
            layer_gated,
            layer_resid_mid,
            layer_ffn_in,
            layer_gate_up,
            layer_hidden,
        )
        saved, layer_out, attn_out, ffn_out = (layer_saved, layer_out, attn, ffn)
        if stored is None:
            stored = jax.tree.map(
                lambda part_new: jnp.zeros((micro_count,) + part_new.shape, part_new.dtype), saved
            )
        stored = jax.tree.map(
            lambda buffer, part_new: buffer.at[chosen].set(
                jnp.where(active, part_new, buffer[chosen])
            ),
            stored,
            saved,
        )
        outgoing = layer_out.astype(jnp.bfloat16)
        activations_buf = activations_buf.at[chosen].set(
            jnp.where(active, outgoing, activations_buf[chosen])
        )
        weights_valid = valid_mask[chosen].astype(jnp.float32)
        sums_now = jnp.stack(
            [
                jnp.sum(weights_valid * jnp.mean(branch_val * branch_val, axis=-1))
                for branch_val in (layer_out, attn_out, ffn_out)
            ]
        )
        stat_sums = stat_sums.at[chosen].set(jnp.where(active, sums_now, stat_sums[chosen]))
        stat_counts = stat_counts.at[chosen].set(
            jnp.where(active, jnp.sum(weights_valid), stat_counts[chosen])
        )
        if slot_index < micro_count:
            incoming = partner(outgoing)
    rows_acc = None
    cols_acc = None
    small_acc = None
    back_in = zero_in
    grad_inputs = jnp.zeros(tokens.shape, jnp.bfloat16)
    for slot_index in range(micro_count + 1):
        chosen_raw = slot_index - (1 - section_index)
        active = (chosen_raw >= 0) & (chosen_raw < micro_count)
        chosen = jnp.clip(chosen_raw, 0, micro_count - 1)
        saved = jax.tree.map(lambda buffer: buffer[chosen], stored)
        from_loss = (
            cotangent[chosen].astype(jnp.float32) * valid_mask[chosen].astype(jnp.float32)[:, None]
        )
        upstream = jnp.where(section_index == 1, from_loss, back_in.astype(jnp.float32))
        grad_resid, rows_grads, cols_grads, small_grads = layer_backward(
            saved, upstream, doc_starts[chosen]
        )
        rows_grads = jax.tree.map(lambda grad_part: jnp.where(active, grad_part, 0.0), rows_grads)
        cols_grads = jax.tree.map(lambda grad_part: jnp.where(active, grad_part, 0.0), cols_grads)
        small_grads = jax.tree.map(lambda grad_part: jnp.where(active, grad_part, 0.0), small_grads)
        if rows_acc is None:
            rows_acc, cols_acc, small_acc = (rows_grads, cols_grads, small_grads)
        else:
            rows_acc = jax.tree.map(jnp.add, rows_acc, rows_grads)
            cols_acc = jax.tree.map(jnp.add, cols_acc, cols_grads)
            small_acc = jax.tree.map(jnp.add, small_acc, small_grads)
        outgoing = grad_resid.astype(jnp.bfloat16)
        grad_inputs = grad_inputs.at[chosen].set(jnp.where(active, outgoing, grad_inputs[chosen]))
        if slot_index < micro_count:
            back_in = partner(outgoing)
    rows_part, cols_part = spread(rows_acc, cols_acc)
    norm_heads = lax.psum(small_acc[3], "head")
    conv_sum, scale_sum, shift_sum, norm_sum, sums_all, counts_all = (
        lax.psum(small_acc[0].astype(jnp.bfloat16), "seq").astype(jnp.float32),
        lax.psum(small_acc[1].astype(jnp.bfloat16), "seq").astype(jnp.float32),
        lax.psum(small_acc[2].astype(jnp.bfloat16), "seq").astype(jnp.float32),
        lax.psum(norm_heads.astype(jnp.bfloat16), "seq").astype(jnp.float32),
        lax.psum(stat_sums.astype(jnp.bfloat16), "seq").astype(jnp.float32),
        lax.psum(stat_counts.astype(jnp.bfloat16), "seq").astype(jnp.float32),
    )
    branch_rms = jnp.sqrt(sums_all / jnp.maximum(counts_all, 1.0)[:, None])
    proj_part = rows_part[2]
    mix_part = rows_part[3]
    gu_part = rows_part[4]
    return (
        activations_buf[None],
        grad_inputs[None],
        branch_rms[None],
        rows_part[0][None],
        proj_part[:, :width_qk][None],
        proj_part[:, width_qk : 2 * width_qk][None],
        proj_part[:, 2 * width_qk : width_qkv][None],
        proj_part[:, width_qkv:][None],
        mix_part[:, :head_count][None],
        mix_part[:, head_count:][None],
        conv_sum[:, :width_qk][None],
        conv_sum[:, width_qk : 2 * width_qk][None],
        conv_sum[:, 2 * width_qk :][None],
        scale_sum[None],
        shift_sum[None],
        norm_sum[None],
        cols_part[0][None],
        rows_part[1][None],
        gu_part[:, :hidden_width][None],
        gu_part[:, hidden_width:][None],
        cols_part[1][None],
    )


def solution(mesh):
    placed = (
        P(None, "seq", None),
        P(None, "seq", None),
        P(),
        P(None, "seq"),
        P("section", "seq"),
        P("section", "seq", "head"),
        P("section", "seq", "head"),
        P("section", "seq", "head"),
        P("section", "seq", "head"),
        P("section", "seq", "head"),
        P("section", "seq", "head"),
        P("section", None, "head"),
        P("section", None, "head"),
        P("section", None, "head"),
        P("section", "head"),
        P("section", "head"),
        P("section", None),
        P("section", "head", "seq"),
        P("section", "seq"),
        P("section", "seq", "head"),
        P("section", "seq", "head"),
        P("section", "head", "seq"),
    )
    return jax.shard_map(
        shards,
        mesh=mesh,
        in_specs=placed,
        out_specs=(
            P("section", None, "seq", None),
            P("section", None, "seq", None),
            P("section", None, None),
            P("section", "seq"),
            P("section", "seq", "head"),
            P("section", "seq", "head"),
            P("section", "seq", "head"),
            P("section", "seq", "head"),
            P("section", "seq", "head"),
            P("section", "seq", "head"),
            P("section", None, "head"),
            P("section", None, "head"),
            P("section", None, "head"),
            P("section", "head"),
            P("section", "head"),
            P("section", None),
            P("section", "head", "seq"),
            P("section", "seq"),
            P("section", "seq", "head"),
            P("section", "seq", "head"),
            P("section", "head", "seq"),
        ),
        check_vma=False,
    )
```

profile of v0, /device:TPU:1, one launch (start us, length us, event | category | flops | bytes accessed | tf_op | source)
XLA Modules:
  0.0 3403.6 jit_solution(12311602983671506681)
XLA Ops:
  10.1 10.3 all-gather
  20.5 10.4 all-gather.6
  30.9 10.5 all-gather.5
  58.1 46.4 %all-gather.39.cloned.1.call-done = bf16[1,2048,512]{2,1,0:T(8,128)(2,1)} async-done(((bf16[1,512,512]{2,1,0:T(8,128)(2,1)}), bf16[1,2048,512]{2,1,0:T(8,128)(2,1)}) %all-gather.39.cloned.1.call-update) | async-done | bytes 2097168 | tf_op jit(solution)/shard_map/all_gather | solution.py:328
  104.5 81.1 %all-gather.45.cloned.1.call-done = bf16[1,2048,1024]{2,1,0:T(8,128)(2,1)} async-done(((bf16[1,512,1024]{2,1,0:T(8,128)(2,1)}), bf16[1,2048,1024]{2,1,0:T(8,128)(2,1)}) %all-gather.45.cloned.1.call-update) | async-done | bytes 4194320 | tf_op jit(solution)/shard_map/all_gather | solution.py:331
  185.6 80.7 %all-gather.43.cloned.1.call-done = bf16[1,2048,1024]{2,1,0:T(8,128)(2,1)} async-done(((bf16[1,512,1024]{2,1,0:T(8,128)(2,1)}), bf16[1,2048,1024]{2,1,0:T(8,128)(2,1)}) %all-gather.43.cloned.1.call-update) | async-done | bytes 4194320 | tf_op jit(solution)/shard_map/all_gather | solution.py:330
  289.2 79.1 %custom-call.37 = f32[4,4,1,64,64]{3,4,2,1,0:T(8,128)S(1)} custom-call(f32[4,4,1,64,64]{4,3,2,1,0:T(8,128)S(1)} %fusion.286), custom_call_target="InvertDiagBlocksLowerTriangular" | custom-call | tf_op jit(solution)/shard_map/triangular_solve/custom-call.1 | solution.py:137
  397.8 20.8 all-gather.7
  443.9 56.4 %all-gather.49.cloned.1.call-done = bf16[1,1024,2048]{2,1,0:T(8,128)(2,1)} async-done(((bf16[1,1024,512]{2,1,0:T(8,128)(2,1)}), bf16[1,1024,2048]{2,1,0:T(8,128)(2,1)}) %all-gather.49.cloned.1.call-update) | async-done | bytes 4194320 | tf_op jit(solution)/shard_map/all_gather | solution.py:338
  507.0 9.9 all-gather.10
  557.9 106.5 %all-gather.53.cloned.1.call-done = bf16[1,2048,1408]{2,1,0:T(8,128)(2,1)} async-done(((bf16[1,512,1408]{2,1,0:T(8,128)(2,1)}), bf16[1,2048,1408]{2,1,0:T(8,128)(2,1)}) %all-gather.53.cloned.1.call-update) | async-done | bytes 5767184 | tf_op jit(solution)/shard_map/all_gather | solution.py:335
  664.4 106.6 %all-gather.51.cloned.1.call-done = bf16[1,2048,1408]{2,1,0:T(8,128)(2,1)} async-done(((bf16[1,512,1408]{2,1,0:T(8,128)(2,1)}), bf16[1,2048,1408]{2,1,0:T(8,128)(2,1)}) %all-gather.51.cloned.1.call-update) | async-done | bytes 5767184 | tf_op jit(solution)/shard_map/all_gather | solution.py:334
  774.3 10.4 bitcast_dynamic-update-slice_fusion
  788.2 89.3 %all-gather.55.cloned.1.call-done = bf16[1,1408,2048]{2,1,0:T(8,128)(2,1)} async-done(((bf16[1,1408,512]{2,1,0:T(8,128)(2,1)}), bf16[1,1408,2048]{2,1,0:T(8,128)(2,1)}) %all-gather.55.cloned.1.call-update) | async-done | bytes 5767184 | tf_op jit(solution)/shard_map/all_gather | solution.py:339
  895.5 38.4 %all-reduce.102.cloned.1.call-done = bf16[256,2048]{1,0:T(8,128)(2,1)} async-done(((bf16[256,2048]{1,0:T(8,128)(2,1)}), bf16[256,2048]{1,0:T(8,128)(2,1)}) %all-reduce.102.cloned.1.call-update) | async-done | bytes 1048592 | tf_op jit(solution)/shard_map/psum | solution.py:243
  1022.7 80.2 %custom-call.39 = f32[4,4,1,64,64]{3,4,2,1,0:T(8,128)} custom-call(f32[4,4,1,64,64]{4,3,2,1,0:T(8,128)} %fusion.281), custom_call_target="InvertDiagBlocksLowerTriangular" | custom-call | tf_op jit(solution)/shard_map/triangular_solve/custom-call.1 | solution.py:137
  1129.1 20.9 all-gather.14
  1153.0 10.4 while.148
  1196.1 37.1 %all-reduce.104.cloned.1.call-done = bf16[256,2048]{1,0:T(8,128)(2,1)} async-done(((bf16[256,2048]{1,0:T(8,128)(2,1)}), bf16[256,2048]{1,0:T(8,128)(2,1)}) %all-reduce.104.cloned.1.call-update) | async-done | bytes 1048592 | tf_op jit(solution)/shard_map/psum | solution.py:243
  1234.9 10.8 fusion.58
  1266.6 39.6 %all-reduce.106.cloned.1.call-done = bf16[256,2048]{1,0:T(8,128)(2,1)} async-done(((bf16[256,2048]{1,0:T(8,128)(2,1)}), bf16[256,2048]{1,0:T(8,128)(2,1)}) %all-reduce.106.cloned.1.call-update) | async-done | bytes 1048592 | tf_op jit(solution)/shard_map/psum | solution.py:243
  1401.1 11.9 fusion.237
  1450.6 79.1 %custom-call.41 = f32[4,4,1,64,64]{3,4,2,1,0:T(8,128)S(1)} custom-call(f32[4,4,1,64,64]{4,3,2,1,0:T(8,128)S(1)} %fusion.276), custom_call_target="InvertDiagBlocksLowerTriangular" | custom-call | tf_op jit(solution)/shard_map/triangular_solve/custom-call.1 | solution.py:137
  1542.8 13.7 all-gather.16
  1572.5 79.4 %custom-call.44 = f32[4,4,1,64,64]{3,4,2,1,0:T(8,128)S(1)} custom-call(f32[4,4,1,64,64]{4,3,2,1,0:T(8,128)} %get-tuple-element.1707), custom_call_target="InvertDiagBlocksLowerTriangular" | custom-call | tf_op jit(solution)/shard_map/transpose(jvp())/triangular_solve/custom-call.2 | solution.py:137
  1667.0 79.6 %custom-call.50 = f32[4,4,1,64,64]{3,4,2,1,0:T(8,128)S(1)} custom-call(f32[4,4,1,64,64]{4,3,2,1,0:T(8,128)} %get-tuple-element.1708), custom_call_target="InvertDiagBlocksLowerTriangular" | custom-call | tf_op jit(solution)/shard_map/transpose(jvp())/triangular_solve/custom-call.2 | solution.py:137
  1754.3 79.4 %custom-call.56 = f32[4,4,1,64,64]{3,4,2,1,0:T(8,128)S(1)} custom-call(f32[4,4,1,64,64]{4,3,2,1,0:T(8,128)} %get-tuple-element.1706), custom_call_target="InvertDiagBlocksLowerTriangular" | custom-call | tf_op jit(solution)/shard_map/transpose(jvp())/triangular_solve/custom-call.2 | solution.py:137
  1911.5 14.2 all-gather.18
  1939.6 11.7 fusion.57
  1987.7 36.2 %all-reduce.110.cloned.1.call-done = bf16[256,2048]{1,0:T(8,128)(2,1)} async-done(((bf16[256,2048]{1,0:T(8,128)(2,1)}), bf16[256,2048]{1,0:T(8,128)(2,1)}) %all-reduce.110.cloned.1.call-update) | async-done | bytes 1048592 | tf_op jit(solution)/shard_map/psum | solution.py:243
  2165.6 42.6 %all-reduce.112.cloned.1.call-done = bf16[256,2048]{1,0:T(8,128)(2,1)} async-done(((bf16[256,2048]{1,0:T(8,128)(2,1)}), bf16[256,2048]{1,0:T(8,128)(2,1)}) %all-reduce.112.cloned.1.call-update) | async-done | bytes 1048592 | tf_op jit(solution)/shard_map/psum | solution.py:243
  2239.1 15.1 all-gather.20
  2269.3 22.0 all-reduce.114.cloned.1.call-done
  2437.0 13.2 all-gather.22
  2463.9 25.2 all-reduce.116.cloned.1.call-done
  2522.7 42.5 %all-reduce.118.cloned.1.call-done = bf16[256,2048]{1,0:T(8,128)(2,1)} async-done(((bf16[256,2048]{1,0:T(8,128)(2,1)}), bf16[256,2048]{1,0:T(8,128)(2,1)}) %all-reduce.118.cloned.1.call-update) | async-done | bytes 1048592 | tf_op jit(solution)/shard_map/psum | solution.py:243
  2674.5 15.9 multiply_reduce_fusion.11
  2735.0 12.0 add_convert_fusion.2
  2748.7 10.9 fusion.399
  2759.7 9.7 fusion.397
  2769.4 21.5 add_convert_fusion.1
  2792.2 14.0 fusion.415
  2806.2 11.6 fusion.412
  2817.8 23.0 add_convert_fusion
  2897.0 16.4 all-reduce.87
  2928.7 47.9 %reduce-scatter.14.cloned.1.call-done = bf16[1408,512]{1,0:T(8,128)(2,1)} async-done(((bf16[1408,2048]{1,0:T(8,128)(2,1)}), bf16[1408,512]{1,0:T(8,128)(2,1)}) %reduce-scatter.14.cloned.1.call-update) | async-done | bytes 1441808 | tf_op jit(solution)/shard_map/reduce_scatter | solution.py:284
  2979.9 194.6 %reduce-scatter.12.cloned.1.call-done = bf16[512,2816]{1,0:T(8,128)(2,1)} async-done(((bf16[2048,2816]{1,0:T(8,128)(2,1)}), bf16[512,2816]{1,0:T(8,128)(2,1)}) %reduce-scatter.12.cloned.1.call-update) | async-done | bytes 2883600 | tf_op jit(solution)/shard_map/reduce_scatter | solution.py:276
  3179.6 210.1 %reduce-scatter.6.cloned.1.call-done = bf16[512,3072]{1,0:T(8,128)(2,1)} async-done(((bf16[2048,3072]{1,0:T(8,128)(2,1)}), bf16[512,3072]{1,0:T(8,128)(2,1)}) %reduce-scatter.6.cloned.1.call-update) | async-done | bytes 3145744 | tf_op jit(solution)/shard_map/reduce_scatter | solution.py:270
  (2397 shorter events, 1304.8 us)
Async XLA Ops:
  7.3 50.9 %all-gather.41.cloned.1.call-start = ((), (), s32[]{:S(2)}) async-start(), calls=%async_computation.21 | async-start | bytes 2621440 | tf_op jit(solution)/shard_map/all_gather | solution.py:329
  8.0 96.5 %all-gather.39.cloned.1.call-start = ((), (), s32[]{:S(2)}) async-start(), calls=%async_computation.20 | async-start | bytes 2621440 | tf_op jit(solution)/shard_map/all_gather | solution.py:328
  8.7 176.9 %all-gather.45.cloned.1.call-start = ((), (), s32[]{:S(2)}) async-start(), calls=%async_computation.23 | async-start | bytes 5242880 | tf_op jit(solution)/shard_map/all_gather | solution.py:331
  9.5 256.9 %all-gather.43.cloned.1.call-start = ((), (), s32[]{:S(2)}) async-start(), calls=%async_computation.22 | async-start | bytes 5242880 | tf_op jit(solution)/shard_map/all_gather | solution.py:330
  10.1 415.5 %all-gather.47.cloned.1.call-start = ((), (), s32[]{:S(2)}) async-start(), calls=%async_computation.24 | async-start | bytes 1310720 | tf_op jit(solution)/shard_map/all_gather | solution.py:23
  20.5 1319.7 %copy-start.403 = (f32[1,2048]{1,0:T(1,128)}, f32[1,2048]{1,0:T(1,128)S(1)}, u32[]{:S(2)}) copy-start(f32[1,2048]{1,0:T(1,128)S(1)} %convert_element_type.763) | copy-start | bytes 24580
  30.9 1309.3 %copy-start.427 = (bf16[1,2048,4]{1,2,0:T(4,128)(2,1)}, bf16[1,2048,4]{1,2,0:T(4,128)(2,1)S(1)}, u32[]{:S(2)}) copy-start(bf16[1,2048,4]{1,2,0:T(4,128)(2,1)S(1)} %all-gather.6) | copy-start | bytes 49156
  41.4 1298.8 %copy-start.429 = (bf16[1,2048,4]{1,2,0:T(4,128)(2,1)}, bf16[1,2048,4]{1,2,0:T(4,128)(2,1)S(1)}, u32[]{:S(2)}) copy-start(bf16[1,2048,4]{1,2,0:T(4,128)(2,1)S(1)} %all-gather.5) | copy-start | bytes 49156
  42.7 229.8 %copy-start.644 = (f32[256]{0:T(256)}, f32[256]{0:T(256)S(1)}, u32[]{:S(2)}) copy-start(f32[256]{0:T(256)S(1)} %add_rsqrt_fusion.20) | copy-start | bytes 3076
  277.0 2.9 collective-permute-start
  381.1 119.1 %all-gather.49.cloned.1.call-start = ((), (), s32[]{:S(2)}) async-start(), calls=%async_computation.25 | async-start | bytes 5242880 | tf_op jit(solution)/shard_map/all_gather | solution.py:338
  381.7 174.2 %all-reduce.100.cloned.1.call-start = ((), (), s32[]{:S(2)}) async-start(), calls=%async_computation.5 | async-start | bytes 2097152 | tf_op jit(solution)/shard_map/psum | solution.py:243
  383.6 791.3 %copy-start.443 = (f32[1,2,4,128]{3,1,2,0:T(2,128)}, f32[1,2,4,128]{3,1,2,0:T(2,128)S(1)}, u32[]{:S(2)}) copy-start(f32[1,2,4,128]{3,1,2,0:T(2,128)S(1)} %copy.2794) | copy-start | bytes 12292
  504.9 159.6 %all-gather.53.cloned.1.call-start = ((), (), s32[]{:S(2)}) async-start(), calls=%async_computation.27 | async-start | bytes 7208960 | tf_op jit(solution)/shard_map/all_gather | solution.py:335
  505.6 265.4 %all-gather.51.cloned.1.call-start = ((), (), s32[]{:S(2)}) async-start(), calls=%async_computation.26 | async-start | bytes 7208960 | tf_op jit(solution)/shard_map/all_gather | solution.py:334
  506.4 371.1 %all-gather.55.cloned.1.call-start = ((), (), s32[]{:S(2)}) async-start(), calls=%async_computation.28 | async-start | bytes 7208960 | tf_op jit(solution)/shard_map/all_gather | solution.py:339
  507.0 427.0 %all-reduce.102.cloned.1.call-start = ((), (), s32[]{:S(2)}) async-start(), calls=%async_computation.6 | async-start | bytes 2097152 | tf_op jit(solution)/shard_map/psum | solution.py:243
  517.0 789.2 %copy-start.391 = (f32[1,2048]{1,0:T(1,128)}, f32[1,2048]{1,0:T(1,128)S(1)}, u32[]{:S(2)}) copy-start(f32[1,2048]{1,0:T(1,128)S(1)} %convert_element_type.764) | copy-start | bytes 24580
  883.2 269.8 %all-gather.57.cloned.1.call-start = ((), (), s32[]{:S(2)}) async-start(), calls=%async_computation.29 | async-start | bytes 1310720 | tf_op jit(solution)/shard_map/all_gather | solution.py:23
  938.3 10.7 collective-permute-start.1
  953.2 353.0 %copy-start.16 = (bf16[256,2048]{1,0:T(8,128)(2,1)}, bf16[256,2048]{1,0:T(8,128)(2,1)S(1)}, u32[]{:S(2)}) copy-start(bf16[256,2048]{1,0:T(8,128)(2,1)S(1)} %get-tuple-element.1599) | copy-start | bytes 3145732
  960.9 29.4 collective-permute-start.2
  1118.0 115.2 %all-reduce.104.cloned.1.call-start = ((), (), s32[]{:S(2)}) async-start(), calls=%async_computation.7 | async-start | bytes 2097152 | tf_op jit(solution)/shard_map/psum | solution.py:243
  1180.8 125.4 %all-reduce.106.cloned.1.call-start = ((), (), s32[]{:S(2)}) async-start(), calls=%async_computation.8 | async-start | bytes 2097152 | tf_op jit(solution)/shard_map/psum | solution.py:243
  1253.4 606.7 %all-gather.59.cloned.1.call-start = ((), (), s32[]{:S(2)}) async-start(), calls=%async_computation.30 | async-start | bytes 1310720 | tf_op jit(solution)/shard_map/all_gather | solution.py:23
  1312.1 10.9 collective-permute-start.3
  1336.4 54.3 %collective-permute-start.4 = (f32[3,2048]{1,0:T(4,128)}, f32[3,2048]{1,0:T(4,128)}, u32[]{:S(2)}, u32[]{:S(2)}) collective-permute-start(f32[3,2048]{1,0:T(4,128)} %slice.2107), channel_id=1, source_target_pairs={{0,4},{4,8},{8,12},{1,5},{5,9},{9,13},{2,6},{6,10},{10,14},{3,7},{... | collective-permute-start | bytes 73736 | tf_op jit(solution)/shard_map/ppermute | solution.py:71
  1557.8 380.0 %all-reduce.108.cloned.1.call-start = ((), (), s32[]{:S(2)}) async-start(), calls=%async_computation.9 | async-start | bytes 2097152 | tf_op jit(solution)/shard_map/psum | solution.py:243
  1834.6 385.0 %copy-start.433 = (f32[4,4,1,64]{3,2,1,0:T(1,128)}, f32[4,4,1,64]{3,2,1,0:T(1,128)S(1)}, u32[]{:S(2)}) copy-start(f32[4,4,1,64]{3,2,1,0:T(1,128)S(1)} %slice.2171) | copy-start | bytes 12292
  1881.6 142.3 %all-reduce.110.cloned.1.call-start = ((), (), s32[]{:S(2)}) async-start(), calls=%async_computation.10 | async-start | bytes 2097152 | tf_op jit(solution)/shard_map/psum | solution.py:243
  1969.3 114.2 %all-gather.61.cloned.1.call-start = ((), (), s32[]{:S(2)}) async-start(), calls=%async_computation.31 | async-start | bytes 1310720 | tf_op jit(solution)/shard_map/all_gather | solution.py:48
  2055.5 152.7 %all-reduce.112.cloned.1.call-start = ((), (), s32[]{:S(2)}) async-start(), calls=%async_computation.11 | async-start | bytes 2097152 | tf_op jit(solution)/shard_map/psum | solution.py:243
  2139.9 4.8 collective-permute-start.5
  2155.6 135.7 %all-reduce.114.cloned.1.call-start = ((), (), s32[]{:S(2)}) async-start(), calls=%async_computation.12 | async-start | bytes 2097152 | tf_op jit(solution)/shard_map/psum | solution.py:243
  2217.9 8.2 collective-permute-start.6
  2239.0 119.6 %all-gather.63.cloned.1.call-start = ((), (), s32[]{:S(2)}) async-start(), calls=%async_computation.32 | async-start | bytes 1310720 | tf_op jit(solution)/shard_map/all_gather | solution.py:48
  2330.6 158.5 %all-reduce.116.cloned.1.call-start = ((), (), s32[]{:S(2)}) async-start(), calls=%async_computation.13 | async-start | bytes 2097152 | tf_op jit(solution)/shard_map/psum | solution.py:243
  2420.9 5.1 collective-permute-start.7
  2436.9 128.3 %all-reduce.118.cloned.1.call-start = ((), (), s32[]{:S(2)}) async-start(), calls=%async_computation.14 | async-start | bytes 2097152 | tf_op jit(solution)/shard_map/psum | solution.py:243
  2496.5 8.6 collective-permute-start.8
  2513.1 110.4 %all-gather.65.cloned.1.call-start = ((), (), s32[]{:S(2)}) async-start(), calls=%async_computation.33 | async-start | bytes 1310720 | tf_op jit(solution)/shard_map/all_gather | solution.py:48
  2595.5 292.2 %reduce-scatter.8.cloned.1.call-start = ((), (), s32[]{:S(2)}) async-start(), calls=%async_computation.16 | async-start | bytes 40960 | tf_op jit(solution)/shard_map/reduce_scatter | solution.py:273
  2694.3 5.8 collective-permute-start.9
  2700.0 188.4 %all-reduce.120.cloned.1.call-start = ((), (), s32[]{:S(2)}) async-start(), calls=%async_computation.34 | async-start | bytes 4194304 | tf_op jit(solution)/shard_map/psum | solution.py:243
  2709.0 216.8 %reduce-scatter.10.cloned.1.call-start = ((), (), s32[]{:S(2)}) async-start(), calls=%async_computation.17 | async-start | bytes 5242880 | tf_op jit(solution)/shard_map/reduce_scatter | solution.py:281
  2718.7 257.8 %reduce-scatter.14.cloned.1.call-start = ((), (), s32[]{:S(2)}) async-start(), calls=%async_computation.19 | async-start | bytes 7208960 | tf_op jit(solution)/shard_map/reduce_scatter | solution.py:284
  2747.1 427.4 %reduce-scatter.12.cloned.1.call-start = ((), (), s32[]{:S(2)}) async-start(), calls=%async_computation.18 | async-start | bytes 14417920 | tf_op jit(solution)/shard_map/reduce_scatter | solution.py:276
  2791.0 598.7 %reduce-scatter.6.cloned.1.call-start = ((), (), s32[]{:S(2)}) async-start(), calls=%async_computation.15 | async-start | bytes 15728640 | tf_op jit(solution)/shard_map/reduce_scatter | solution.py:270
  (689 other events, 5578.9 us)
Sparse Core Ops, SparseCore 0:
  9.7 48.4 all-gather.40
  59.7 44.8 all-gather.38
  106.1 79.4 all-gather.44
  187.1 79.2 all-gather.42
  381.3 36.6 all-gather.46
  419.3 80.8 all-gather.48
  504.8 51.0 all-reduce.99
  557.5 106.9 all-gather.52
  666.0 104.9 all-gather.50
  772.5 104.9 all-gather.54
  883.3 50.5 all-reduce.101
  1118.1 34.8 all-gather.56
  1180.9 52.2 all-reduce.103
  1253.5 52.6 all-reduce.105
  1558.0 28.0 all-gather.58
  1881.8 52.6 all-reduce.107
  1969.4 54.5 all-reduce.109
  2055.7 27.7 all-gather.60
  2155.7 52.5 all-reduce.111
  2239.1 52.1 all-reduce.113
  2330.8 27.7 all-gather.62
  2437.0 52.0 all-reduce.115
  2513.2 52.0 all-reduce.117
  2595.6 27.7 all-gather.64
  2700.1 17.0 reduce-scatter.7
  2721.0 70.2 all-reduce.119
  2793.4 76.7 reduce-scatter.9
  2872.7 103.8 reduce-scatter.13
  2979.0 195.4 reduce-scatter.11
  3176.8 212.8 reduce-scatter.5
where the time goes:
time: 3420 us; the launch traced here: 3400 us
  waiting for transfers between devices  1330 us (39%)
  other arithmetic  833 us (24%)
  matrix products  642 us (19%)
  local copies, waits for them, and re-layouts  388 us (11%)
  blocking collectives  164 us (5%)
    another operation x9, other arithmetic, block_terms(): lax.linalg.triangular_solve(system, scaled_values, left_side=True, lower=...  481 us
    psum x11, waiting for transfers between devices, head_total(): return lax.psum(values.astype(jnp.bfloat16), 'head').astype(jnp.float32)  286 us
    reduce_scatter x1, waiting for transfers between devices, spread(): lax.psum_scatter(rows_grads[2].astype(jnp.bfloat16), 'seq', scatter_dimen...  210 us
    reduce_scatter x1, waiting for transfers between devices, spread(): lax.psum_scatter(rows_grads[4].astype(jnp.bfloat16), 'seq', scatter_dimen...  195 us
    dot_general x12, matrix products, inner_t(): lax.dot_general(left, right, (((0,), (0,)), ((), ())), preferred_element_...  127 us
    all_gather x1, waiting for transfers between devices, shards(): lax.all_gather(w_gate[0], 'seq', axis=0, tiled=True)  107 us
    all_gather x1, waiting for transfers between devices, shards(): lax.all_gather(w_up[0], 'seq', axis=0, tiled=True)  106 us
    all_gather x1, waiting for transfers between devices, shards(): lax.all_gather(w_down[0], 'seq', axis=1, tiled=True)  89.3 us
  transfers between devices with their start and end apart: 40, of which 26 were waited for; matrix products, arithmetic and copies ran while one was open for 28% of the time, Pallas kernels for 0%

commit v1 on v0

--- a/solution.py
+++ b/solution.py
@@ -1,12 +1,19 @@
+import functools
+
 import jax
 import jax.numpy as jnp
 from jax import lax
+from jax.experimental import pallas as pl
+from jax.experimental.pallas import tpu as pltpu
 from jax.sharding import PartitionSpec as P
 
 HEAD_K = 128
 HEAD_V = 256
 CONVK = 4
 BLOCK = 64
+HALO = 8
+EXTRA = 128
+GROUP = 4
 
 
 epsilon = 1e-06
@@ -629,6 +636,798 @@
     )
 
 
+exact = lax.Precision.HIGHEST
+
+
+def dot_nn(a, b):
+    return lax.dot_general(
+        a, b, (((1,), (0,)), ((), ())), precision=exact, preferred_element_type=jnp.float32
+    )
+
+
+def dot_nt(a, b):
+    return lax.dot_general(
+        a, b, (((1,), (1,)), ((), ())), precision=exact, preferred_element_type=jnp.float32
+    )
+
+
+def dot_tn(a, b):
+    return lax.dot_general(
+        a, b, (((0,), (0,)), ((), ())), precision=exact, preferred_element_type=jnp.float32
+    )
+
+
+@functools.partial(jax.custom_vjp, nondiff_argnums=(1,))
+def shifted(window, steps):
+    if steps == 0:
+        return window[HALO:]
+    return pltpu.roll(window, steps, 0)[HALO:]
+
+
+def shifted_fwd(window, steps):
+    return shifted(window, steps), None
+
+
+def shifted_bwd(steps, _, grad):
+    padded = jnp.concatenate([jnp.zeros((HALO, grad.shape[1]), grad.dtype), grad], axis=0)
+    if steps == 0:
+        return (padded,)
+    return (pltpu.roll(padded, padded.shape[0] - steps, 0),)
+
+
+shifted.defvjp(shifted_fwd, shifted_bwd)
+
+
+def iotas(length):
+    rows = lax.broadcasted_iota(jnp.int32, (length, length), 0)
+    cols = lax.broadcasted_iota(jnp.int32, (length, length), 1)
+    return rows, cols
+
+
+def as_row(column):
+    rows, cols = iotas(column.shape[0])
+    return jnp.sum(jnp.where(rows == cols, column, 0.0), axis=0, keepdims=True)
+
+
+def unit_inverse(lower):
+    length = lower.shape[0]
+    rows, cols = iotas(length)
+    near = jnp.where((rows >> 3) == (cols >> 3), lower, 0.0)
+    result = jnp.where(rows == cols, 1.0, 0.0) - near
+    square = dot_nn(near, near)
+    result = result + dot_nn(result, square)
+    result = result + dot_nn(result, dot_nn(square, square))
+    shift = 3
+    while (1 << shift) < length:
+        off = ((rows >> (shift + 1)) == (cols >> (shift + 1))) & ((rows >> shift) != (cols >> shift))
+        result = result - dot_nn(result, dot_nn(jnp.where(off, lower, 0.0), result))
+        shift += 1
+    return result
+
+
+@jax.custom_vjp
+def inverse_known(lower, inverse):
+    return inverse
+
+
+def inverse_known_fwd(lower, inverse):
+    return inverse, inverse
+
+
+def inverse_known_bwd(inverse, grad):
+    return -dot_nt(dot_tn(inverse, grad), inverse), jnp.zeros_like(grad)
+
+
+inverse_known.defvjp(inverse_known_fwd, inverse_known_bwd)
+
+
+def silu(values):
+    return values / (1.0 + jnp.exp(-values))
+
+
+def sigmoid(values):
+    return 1.0 / (1.0 + jnp.exp(-values))
+
+
+@jax.custom_vjp
+def softplus(values):
+    return jnp.maximum(values, 0.0) + jnp.log1p(jnp.exp(-jnp.abs(values)))
+
+
+def softplus_fwd(values):
+    return softplus(values), values
+
+
+def softplus_bwd(values, grad):
+    return (grad * sigmoid(values),)
+
+
+softplus.defvjp(softplus_fwd, softplus_bwd)
+
+
+def block_front(window, mix_decay, mix_write, taps, decay_log, decay_bias, aux):
+    summed = shifted(window, 0) * taps[3]
+    for steps in range(1, CONVK):
+        summed = summed + jnp.where(aux[:, steps : steps + 1] > 0.0, shifted(window, steps), 0.0) * taps[3 - steps]
+    active = silu(summed)
+    queries = unit_rows(active[:, :HEAD_K]) * HEAD_K ** (-0.5)
+    keys = unit_rows(active[:, HEAD_K : 2 * HEAD_K])
+    values = active[:, 2 * HEAD_K :]
+    write = sigmoid(mix_write)
+    log_decay = -jnp.exp(decay_log) * softplus(mix_decay + decay_bias)
+    rows, cols = iotas(BLOCK)
+    cum = jnp.sum(jnp.where(cols <= rows, as_row(log_decay), 0.0), axis=1, keepdims=True)
+    total = jnp.sum(log_decay, axis=0, keepdims=True)
+    doc = aux[:, 0:1]
+    same = (doc == as_row(doc)) & (cols <= rows)
+    decay = jnp.where(same, jnp.exp(jnp.where(same, cum - as_row(cum), 0.0)), 0.0)
+    entry = jnp.where(aux[:, 4:5] > 0.0, jnp.exp(cum), 0.0)
+    leave = jnp.where(aux[:, 5:6] > 0.0, jnp.exp(total - cum), 0.0)
+    through = jnp.where(aux[BLOCK - 1 : BLOCK, 4:5] > 0.0, jnp.exp(total), 0.0)
+    grams = dot_nt(jnp.concatenate([keys, queries], axis=0), keys)
+    lower = jnp.where(cols < rows, write * decay * grams[:BLOCK], 0.0)
+    mixing = grams[BLOCK:] * decay
+    scaled = jnp.concatenate([write * values, (write * entry) * keys], axis=1)
+    return lower, mixing, scaled, entry * queries, leave * keys, through
+
+
+def block_step(window, mix_decay, mix_write, taps, decay_log, decay_bias, state, aux, inverse):
+    lower, mixing, scaled, queries, keys, through = block_front(
+        window, mix_decay, mix_write, taps, decay_log, decay_bias, aux
+    )
+    if inverse is None:
+        inverse = unit_inverse(lower)
+    else:
+        inverse = inverse_known(lower, inverse)
+    resolved = dot_nn(inverse, scaled)
+    read = dot_nn(jnp.concatenate([resolved[:, HEAD_V:], queries], axis=0), state)
+    written = resolved[:, :HEAD_V] - read[:BLOCK]
+    mixed = read[BLOCK:] + dot_nn(mixing, written)
+    return mixed, through * state + dot_tn(keys, written), inverse
+
+
+def stored_at(number, blocks, parts):
+    shards, slices = parts
+    each = blocks // (shards * slices)
+    shard = number // (slices * each)
+    rest = number - shard * slices * each
+    place = (rest // each * shards + shard) * each + rest % each
+    return pl.multiple_of(place * BLOCK, BLOCK)
+
+
+def fill_window(xh_ref, xbuf, parts):
+    width = xbuf.shape[1]
+    length = xh_ref.shape[0]
+    blocks = length // BLOCK
+    xbuf[0:HALO, :] = jnp.zeros((HALO, width), jnp.float32)
+
+    def copy(index, carry):
+        base = pl.multiple_of(index * BLOCK, BLOCK)
+        stored = stored_at(index, blocks, parts)
+        xbuf[pl.ds(base + HALO, BLOCK), :] = xh_ref[pl.ds(stored, BLOCK), :width].astype(jnp.float32)
+        return carry
+
+    lax.fori_loop(0, length // BLOCK, copy, 0)
+
+
+def load_block(xh_ref, aux_ref, xbuf, base, stored):
+    window = xbuf[pl.ds(base, BLOCK + HALO), :]
+    mix = xh_ref[pl.ds(stored, BLOCK), xbuf.shape[1] :].astype(jnp.float32)
+    aux = aux_ref[pl.ds(base, BLOCK), :]
+    return window, mix[:, 0:1] + mix[:, 2:3], mix[:, 1:2] + mix[:, 3:4], aux
+
+
+def load_taps(taps_ref):
+    return [taps_ref[j : j + 1, :] for j in range(CONVK)]
+
+
+def forward_kernel(parts, xh_ref, aux_ref, taps_ref, scal_ref, mixed_ref, states_ref, inverse_ref, xbuf, state_ref):
+    fill_window(xh_ref, xbuf, parts)
+    state_ref[...] = jnp.zeros_like(state_ref)
+    blocks = xh_ref.shape[0] // BLOCK
+    taps = load_taps(taps_ref)
+    decay_log = scal_ref[0:1, 0:1]
+    decay_bias = scal_ref[0:1, 1:2]
+
+    def group(index, carry):
+        state = state_ref[...]
+        for inner in range(GROUP):
+            number = index * GROUP + inner
+            base = pl.multiple_of(number * BLOCK, BLOCK)
+            stored = stored_at(number, blocks, parts)
+            window, mix_decay, mix_write, aux = load_block(xh_ref, aux_ref, xbuf, base, stored)
+            states_ref[number] = state
+            mixed, state, inverse = block_step(
+                window, mix_decay, mix_write, taps, decay_log, decay_bias, state, aux, None
+            )
+            mixed_ref[pl.ds(stored, BLOCK), :] = mixed.astype(mixed_ref.dtype)
+            inverse_ref[pl.ds(base, BLOCK), :] = inverse
+        state_ref[...] = state
+        return carry
+
+    lax.fori_loop(0, blocks // GROUP, group, 0)
+
+
+def backward_kernel(
+    parts, xh_ref, aux_ref, taps_ref, scal_ref, states_ref, inverse_ref, grad_ref,
+    dxh_ref, dtaps_ref, dscal_ref, xbuf, adjoint_ref, halo_ref,
+):
+    fill_window(xh_ref, xbuf, parts)
+    adjoint_ref[...] = jnp.zeros_like(adjoint_ref)
+    halo_ref[...] = jnp.zeros_like(halo_ref)
+    dtaps_ref[...] = jnp.zeros_like(dtaps_ref)
+    dscal_ref[...] = jnp.zeros_like(dscal_ref)
+    blocks = xh_ref.shape[0] // BLOCK
+    width = xbuf.shape[1]
+    taps = load_taps(taps_ref)
+    decay_log = scal_ref[0:1, 0:1]
+    decay_bias = scal_ref[0:1, 1:2]
+    lanes = lax.broadcasted_iota(jnp.int32, (BLOCK, EXTRA), 1)
+
+    def group(index, carry):
+        adjoint = adjoint_ref[...]
+        halo = halo_ref[...]
+        dtaps = [dtaps_ref[j : j + 1, :] for j in range(CONVK)]
+        dlog = dscal_ref[0:1, 0:1]
+        dbias = dscal_ref[0:1, 1:2]
+        for inner in range(GROUP):
+            number = blocks - 1 - (index * GROUP + inner)
+            base = pl.multiple_of(number * BLOCK, BLOCK)
+            stored = stored_at(number, blocks, parts)
+            window, mix_decay, mix_write, aux = load_block(xh_ref, aux_ref, xbuf, base, stored)
+            inverse = inverse_ref[pl.ds(base, BLOCK), :]
+            grad = grad_ref[pl.ds(stored, BLOCK), :].astype(jnp.float32)
+
+            def run(*inputs):
+                return block_step(*inputs, aux, inverse)[:2]
+
+            _, pull = jax.vjp(
+                run, window, mix_decay, mix_write, taps, decay_log, decay_bias, states_ref[number]
+            )
+            dwindow, ddecay, dwrite, dtaps_now, dlog_now, dbias_now, adjoint = pull((grad, adjoint))
+            own = dwindow[HALO:]
+            own = jnp.concatenate([own[: BLOCK - HALO], own[BLOCK - HALO :] + halo], axis=0)
+            halo = dwindow[:HALO]
+            dtaps = [a + b for a, b in zip(dtaps, dtaps_now)]
+            dlog = dlog + dlog_now
+            dbias = dbias + dbias_now
+            dxh_ref[pl.ds(stored, BLOCK), :width] = own.astype(dxh_ref.dtype)
+            high_decay = ddecay.astype(jnp.bfloat16).astype(jnp.float32)
+            high_write = dwrite.astype(jnp.bfloat16).astype(jnp.float32)
+            mix = jnp.where(lanes == 0, high_decay, jnp.where(lanes == 1, high_write, 0.0))
+            mix = jnp.where(lanes == 2, ddecay - high_decay, jnp.where(lanes == 3, dwrite - high_write, mix))
+            dxh_ref[pl.ds(stored, BLOCK), width:] = mix.astype(dxh_ref.dtype)
+        adjoint_ref[...] = adjoint
+        halo_ref[...] = halo
+        for j in range(CONVK):
+            dtaps_ref[j : j + 1, :] = dtaps[j]
+        dscal_ref[0:1, 0:1] = dlog
+        dscal_ref[0:1, 1:2] = dbias
+        return carry
+
+    lax.fori_loop(0, blocks // GROUP, group, 0)
+
+
+WIDTH = 2 * HEAD_K + HEAD_V
+
+
+def whole():
+    return pl.BlockSpec(memory_space=pltpu.VMEM)
+
+
+def recur_forward(xh, aux, taps, scal, parts):
+    length = xh.shape[0]
+    blocks = length // BLOCK
+    return pl.pallas_call(
+        functools.partial(forward_kernel, parts),
+        out_shape=(
+            jax.ShapeDtypeStruct((length, HEAD_V), jnp.bfloat16),
+            jax.ShapeDtypeStruct((blocks, HEAD_K, HEAD_V), jnp.float32),
+            jax.ShapeDtypeStruct((length, BLOCK), jnp.float32),
+        ),
+        in_specs=[whole()] * 4,
+        out_specs=(whole(),) * 3,
+        scratch_shapes=[
+            pltpu.VMEM((length + HALO, WIDTH), jnp.float32),
+            pltpu.VMEM((HEAD_K, HEAD_V), jnp.float32),
+        ],
+        compiler_params=pltpu.CompilerParams(vmem_limit_bytes=48 * 1024 * 1024),
+        name="recur_forward",
+    )(xh, aux, taps, scal)
+
+
+def recur_backward(xh, aux, taps, scal, states, inverse, grad, parts):
+    length = xh.shape[0]
+    return pl.pallas_call(
+        functools.partial(backward_kernel, parts),
+        out_shape=(
+            jax.ShapeDtypeStruct((length, WIDTH + EXTRA), jnp.bfloat16),
+            jax.ShapeDtypeStruct((8, WIDTH), jnp.float32),
+            jax.ShapeDtypeStruct((8, 128), jnp.float32),
+        ),
+        in_specs=[whole()] * 7,
+        out_specs=(whole(),) * 3,
+        scratch_shapes=[
+            pltpu.VMEM((length + HALO, WIDTH), jnp.float32),
+            pltpu.VMEM((HEAD_K, HEAD_V), jnp.float32),
+            pltpu.VMEM((HALO, WIDTH), jnp.float32),
+        ],
+        compiler_params=pltpu.CompilerParams(vmem_limit_bytes=48 * 1024 * 1024),
+        name="recur_backward",
+    )(xh, aux, taps, scal, states, inverse, grad)
+
+
+def make_aux(starts, length):
+    positions = jnp.arange(length, dtype=jnp.int32)
+    doc = jnp.sum((starts[None, :] <= positions[:, None]).astype(jnp.int32), axis=1)
+    def back(steps):
+        earlier = jnp.concatenate([jnp.full((steps,), -1, jnp.int32), doc[:-steps]])
+        return (earlier == doc).astype(jnp.float32)
+    blocks = doc.reshape(-1, BLOCK)
+    before = jnp.concatenate([jnp.full((1,), -1, jnp.int32), blocks[:-1, -1]])
+    entering = (blocks == before[:, None]).reshape(-1).astype(jnp.float32)
+    leaving = (blocks == blocks[:, -1:]).reshape(-1).astype(jnp.float32)
+    zero = jnp.zeros((length,), jnp.float32)
+    return jnp.stack([doc.astype(jnp.float32), back(1), back(2), back(3), entering, leaving, zero, zero], axis=1)
+
+
+def halves(value, axis):
+    step = 1
+    while step < lax.axis_size(axis):
+        value = value + swapped(value, axis, step.bit_length() - 1)
+        step *= 2
+    return value
+
+
+def by_partner(value, axis):
+    size = lax.axis_size(axis)
+    return [value] + [
+        lax.ppermute(value, axis, [(i, i ^ k) for i in range(size)]) for k in range(1, size)
+    ]
+
+
+def in_order(parts, axis):
+    position = lax.axis_index(axis)
+    parts = list(parts)
+    step = 1
+    while step < len(parts):
+        odd = (position & step) != 0
+        parts = [jnp.where(odd, parts[i ^ step], parts[i]) for i in range(len(parts))]
+        step *= 2
+    return parts
+
+
+def gathered(value, axis):
+    return jnp.concatenate(in_order(by_partner(value, axis), axis), axis=0)
+
+
+def shard_total(partial):
+    size = lax.axis_size("seq")
+    rows, width = partial.shape
+    pieces = partial.astype(jnp.bfloat16).reshape(size, rows // size, width)
+    pieces = lax.all_to_all(pieces, "seq", 0, 0)
+    total = jnp.sum(pieces.astype(jnp.float32), axis=0).astype(jnp.bfloat16)
+    return gathered(total, "seq").astype(jnp.float32)
+
+
+def pick(flag, when, otherwise):
+    return jnp.where(flag, when, otherwise)
+
+
+def both_layers(local, axis):
+    core = lax.axis_index("section")
+    half = local.shape[axis] // 2
+    own = lax.dynamic_slice_in_dim(local, core * half, half, axis)
+    received = partner(lax.dynamic_slice_in_dim(local, (1 - core) * half, half, axis))
+    first = core == 0
+    return pick(first, own, received), pick(first, received, own)
+
+
+def spread_rows(part):
+    part = lax.all_to_all(part, "seq", 0, 0)
+    part = part.reshape(-1, part.shape[2])
+    full = lax.all_gather(part, ("head", "section"), axis=0, tiled=True)
+    return full.reshape(lax.axis_size("head"), -1, part.shape[1])
+
+
+def spread_cols(part):
+    part = lax.all_to_all(part, "seq", 0, 0)
+    part = jnp.swapaxes(part, 0, 1).reshape(part.shape[1], -1)
+    full = lax.all_gather(part, ("section", "head"), axis=0, tiled=True)
+    return full.reshape(2, -1, part.shape[1])
+
+
+def collect_rows(grad):
+    part = lax.psum_scatter(
+        grad.reshape(-1, grad.shape[2]), ("head", "section"), scatter_dimension=0, tiled=True
+    )
+    shards = lax.axis_size("seq")
+    part = lax.all_to_all(part.reshape(shards, -1, part.shape[1]), "seq", 0, 0)
+    return jnp.swapaxes(part, 0, 1)
+
+
+def collect_cols(grad):
+    part = lax.psum_scatter(
+        grad.reshape(-1, grad.shape[2]), ("section", "head"), scatter_dimension=0, tiled=True
+    )
+    shards = lax.axis_size("seq")
+    part = jnp.swapaxes(part.reshape(part.shape[0], shards, -1), 0, 1)
+    return lax.all_to_all(part, "seq", 0, 0)
+
+
+def dot(left, right):
+    return jnp.dot(left, right, preferred_element_type=jnp.float32)
+
+
+def over_halves(value, weight):
+    return jnp.concatenate([dot(value, weight[half]) for half in range(2)], axis=1)
+
+
+def from_halves(value, weight):
+    width = weight.shape[2]
+    return sum(proj_t(value[:, half * width : (half + 1) * width], weight[half]) for half in range(2))
+
+
+def grad_halves(value, grad):
+    width = grad.shape[1] // 2
+    return jnp.stack(
+        [inner_t(value, grad[:, half * width : (half + 1) * width]).astype(jnp.bfloat16) for half in range(2)]
+    )
+
+
+def head_norm(mixed, gate_pre, norm_weight):
+    return rms_norm(mixed, norm_weight) * jax.nn.silu(gate_pre)
+
+
+def layer_forward(resid, gains, weights, small, aux, parts):
+    attn_gain, mlp_gain = gains
+    w_proj, w_mix, w_out, w_gu, w_down = weights
+    taps, scal, norm_weight = small
+    rows = resid.shape[0]
+    slices = w_proj.shape[0]
+    normed = rms_norm(resid, attn_gain).astype(jnp.bfloat16)
+    projected = jnp.stack([dot(normed, w_proj[j]) for j in range(slices)])
+    gate_pre = projected[:, :, WIDTH:]
+    mix = proj_t(normed, w_mix).T.reshape(slices, 2, rows)
+    mix = jnp.swapaxes(mix, 1, 2)
+    mix_high = mix.astype(jnp.bfloat16)
+    mix_low = (mix - mix_high.astype(jnp.float32)).astype(jnp.bfloat16)
+    packed = jnp.concatenate(
+        [
+            projected[:, :, :WIDTH].astype(jnp.bfloat16),
+            mix_high,
+            mix_low,
+            jnp.zeros((slices, rows, EXTRA - 4), jnp.bfloat16),
+        ],
+        axis=2,
+    )
+    xh = lax.all_to_all(packed, "head", 0, 0).reshape(slices * rows, WIDTH + EXTRA)
+    mixed_head, states, inverse = recur_forward(xh, aux, taps, scal, parts)
+    mixed = lax.all_to_all(mixed_head.reshape(slices, rows, HEAD_V), "head", 0, 0)
+    gated = head_norm(mixed.astype(jnp.float32), gate_pre, norm_weight).astype(jnp.bfloat16)
+    gated = jnp.swapaxes(gated, 0, 1).reshape(rows, slices * HEAD_V)
+    attn = shard_total(over_halves(gated, w_out))
+    resid_mid = resid + attn
+    ffn_in = rms_norm(resid_mid, mlp_gain).astype(jnp.bfloat16)
+    gate_up = jnp.stack([dot(ffn_in, w_gu[j]) for j in range(slices)])
+    hidden_width = w_gu.shape[2] // 2
+    hidden = (jax.nn.silu(gate_up[:, :, :hidden_width]) * gate_up[:, :, hidden_width:]).astype(
+        jnp.bfloat16
+    )
+    hidden = jnp.swapaxes(hidden, 0, 1).reshape(rows, slices * hidden_width)
+    ffn = shard_total(over_halves(hidden, w_down))
+    out = resid_mid + ffn
+    saved = (resid, normed, gate_pre, xh, states, inverse, mixed, gated, resid_mid, ffn_in, gate_up, hidden)
+    return out, attn, ffn, saved
+
+
+def layer_backward_fast(upstream, saved, gains, weights, small, aux, parts):
+    attn_gain, mlp_gain = gains
+    w_proj, w_mix, w_out, w_gu, w_down = weights
+    taps, scal, norm_weight = small
+    resid, normed, gate_pre, xh, states, inverse, mixed, gated, resid_mid, ffn_in, gate_up, hidden = saved
+    rows = resid.shape[0]
+    slices = w_proj.shape[0]
+    hidden_width = w_gu.shape[2] // 2
+
+    def by_slice(value):
+        return jnp.swapaxes(value.reshape(rows, slices, -1), 0, 1)
+
+    grad_ffn = upstream.astype(jnp.bfloat16)
+    grad_hidden = by_slice(from_halves(grad_ffn, w_down))
+    grad_down = grad_halves(hidden, grad_ffn)
+    _, act_back = jax.vjp(
+        lambda gate_in, up_in: jax.nn.silu(gate_in) * up_in,
+        gate_up[:, :, :hidden_width],
+        gate_up[:, :, hidden_width:],
+    )
+    grad_gate, grad_up = act_back(grad_hidden)
+    grad_gate_up = jnp.concatenate([grad_gate, grad_up], axis=2).astype(jnp.bfloat16)
+    grad_ffn_in = shard_total(sum(proj_t(grad_gate_up[j], w_gu[j]) for j in range(slices)))
+    grad_gu = jnp.stack([inner_t(ffn_in, grad_gate_up[j]).astype(jnp.bfloat16) for j in range(slices)])
+    _, mlp_norm_back = jax.vjp(rms_norm, resid_mid, mlp_gain)
+    grad_mid_norm, grad_mlp_gain = mlp_norm_back(grad_ffn_in)
+    grad_mid = upstream + grad_mid_norm
+    grad_attn = grad_mid.astype(jnp.bfloat16)
+    grad_gated = by_slice(from_halves(grad_attn, w_out))
+    grad_out = grad_halves(gated, grad_attn)
+    _, gate_back = jax.vjp(head_norm, mixed.astype(jnp.float32), gate_pre, norm_weight)
+    grad_mixed, grad_gate_pre, grad_norm_weight = gate_back(grad_gated)
+    grad_head = lax.all_to_all(grad_mixed.astype(jnp.bfloat16), "head", 0, 0)
+    dxh, dtaps, dscal = recur_backward(
+        xh, aux, taps, scal, states, inverse, grad_head.reshape(slices * rows, HEAD_V), parts
+    )
+    grad_packed = lax.all_to_all(dxh.reshape(slices, rows, WIDTH + EXTRA), "head", 0, 0)
+    grad_mix = grad_packed[:, :, WIDTH : WIDTH + 4].reshape(slices, rows, 2, 2)
+    grad_mix = jnp.transpose(grad_mix, (1, 2, 0, 3)).reshape(rows, 4 * slices)
+    grad_pre = jnp.concatenate(
+        [grad_packed[:, :, :WIDTH], grad_gate_pre.astype(jnp.bfloat16)], axis=2
+    )
+    grad_proj = jnp.stack([inner_t(normed, grad_pre[j]).astype(jnp.bfloat16) for j in range(slices)])
+    grad_w_mix = inner_t(grad_mix, normed)
+    grad_w_mix = grad_w_mix[: 2 * slices] + grad_w_mix[2 * slices :]
+    grad_normed = shard_total(
+        sum(proj_t(grad_pre[j], w_proj[j]) for j in range(slices))
+        + dot(grad_mix, jnp.concatenate([w_mix, w_mix], axis=0))
+    )
+    _, attn_norm_back = jax.vjp(rms_norm, resid, attn_gain)
+    grad_resid_norm, grad_attn_gain = attn_norm_back(grad_normed)
+    grad_resid = grad_mid + grad_resid_norm
+    small_grads = (dtaps[:CONVK], dscal[0, :2], grad_norm_weight, grad_attn_gain, grad_mlp_gain, grad_w_mix)
+    return grad_resid, (grad_proj, grad_out, grad_gu, grad_down), small_grads
+
+
+def fast_shards(
+    tokens,
+    cotangent,
+    doc_starts,
+    valid_mask,
+    gain_attn,
+    w_query,
+    w_key,
+    w_value,
+    w_gate_out,
+    w_decay,
+    w_beta,
+    conv_query,
+    conv_key,
+    conv_value,
+    decay_log,
+    decay_bias,
+    out_norm,
+    w_output,
+    gain_mlp,
+    w_gate,
+    w_up,
+    w_down,
+):
+    core = lax.axis_index("section")
+    first = core == 0
+    shard = lax.axis_index("seq")
+    piece = lax.axis_index("head")
+    shards, slices = lax.axis_size("seq"), lax.axis_size("head")
+    parts = (shards, slices)
+    shard_rows = w_query.shape[1]
+    model_width = tokens.shape[2]
+    sub = tokens.shape[1] // slices
+    length = tokens.shape[1] * shards
+    hidden_width = w_gate.shape[2] // shards
+    hidden_padded = -(-hidden_width // 128) * 128
+
+    def columns(value, width):
+        return jnp.stack([value[:, s * width : (s + 1) * width] for s in range(shards)])
+
+    def halved(value):
+        shape = value.shape[:-1]
+        value = value.reshape(shape + (shards, 2, model_width // (2 * shards)))
+        return jnp.swapaxes(value, -3, -2).reshape(shape + (model_width,))
+
+    proj_local = jnp.concatenate(
+        [
+            columns(w_query[0], HEAD_K),
+            columns(w_key[0], HEAD_K),
+            columns(w_value[0], HEAD_V),
+            columns(w_gate_out[0], HEAD_V),
+        ],
+        axis=2,
+    )
+    fill = ((0, 0), (0, 0), (0, hidden_padded - hidden_width))
+    gu_local = jnp.concatenate(
+        [jnp.pad(columns(w_gate[0], hidden_width), fill), jnp.pad(columns(w_up[0], hidden_width), fill)],
+        axis=2,
+    )
+    out_local = w_output[0].reshape(shards, HEAD_V, shard_rows)
+    down_local = jnp.pad(
+        w_down[0].reshape(shards, hidden_width, shard_rows),
+        ((0, 0), (0, hidden_padded - hidden_width), (0, 0)),
+    )
+    proj_parts = both_layers(proj_local, 1)
+    out_parts = both_layers(out_local, 2)
+    gu_parts = both_layers(gu_local, 1)
+    down_parts = both_layers(down_local, 2)
+
+    conv = jnp.concatenate(
+        [
+            columns(conv_query[0], HEAD_K),
+            columns(conv_key[0], HEAD_K),
+            columns(conv_value[0], HEAD_V),
+        ],
+        axis=2,
+    )
+    taps_own = lax.dynamic_index_in_dim(conv, shard, 0, False).astype(jnp.float32)
+    small_own = jnp.concatenate(
+        [
+            taps_own.reshape(-1),
+            jnp.stack([decay_log[0, shard], decay_bias[0, shard]]),
+            out_norm[0].astype(jnp.float32),
+            gain_attn[0].astype(jnp.float32),
+            gain_mlp[0].astype(jnp.float32),
+            w_decay[0].astype(jnp.float32).T.reshape(-1),
+            w_beta[0].astype(jnp.float32).T.reshape(-1),
+        ]
+    )
+    small_other = partner(small_own)
+    small_layers = (pick(first, small_own, small_other), pick(first, small_other, small_own))
+    taps_size = CONVK * WIDTH
+    norm_at = taps_size + 2
+    gain_at = norm_at + HEAD_V
+    wide = jnp.stack([vector[gain_at:] for vector in small_layers])
+    wide = jnp.concatenate([wide.reshape(-1), valid_mask[core].astype(jnp.float32)])
+    wide = gathered(wide[None], "seq")
+    valid_all = wide[:, wide.shape[1] - tokens.shape[1] :].reshape(shards, slices, sub)
+    valid = lax.dynamic_index_in_dim(valid_all, piece, 1, False).reshape(-1)
+    wide = wide[:, : wide.shape[1] - tokens.shape[1]].reshape(shards, 2, 2 + 2 * shards, 2, shard_rows // 2)
+    gains_all = jnp.transpose(wide[:, :, :2], (1, 2, 3, 0, 4)).reshape(2, 2, model_width)
+    mix_all = wide[:, :, 2:].reshape(shards, 2, 2, shards, 2, shard_rows // 2)
+    mix_all = lax.dynamic_index_in_dim(mix_all, shard, 3, False)
+    mix_all = jnp.transpose(mix_all, (1, 2, 3, 0, 4)).reshape(2, 2, model_width).astype(jnp.bfloat16)
+    mix_all = gathered(mix_all[None], "head")
+    small = []
+    gains = []
+    weights = []
+    for layer in range(2):
+        vector = small_layers[layer]
+        taps = jnp.pad(vector[:taps_size].reshape(CONVK, WIDTH), ((0, 8 - CONVK), (0, 0)))
+        scal = jnp.pad(vector[taps_size:norm_at][None], ((0, 7), (0, 126)))
+        small.append((taps, scal, vector[norm_at:gain_at]))
+        gains.append((gains_all[layer, 0], gains_all[layer, 1]))
+        weights.append(
+            (
+                spread_rows(proj_parts[layer]),
+                mix_all[:, layer].reshape(2 * slices, model_width),
+                spread_cols(out_parts[layer]),
+                spread_rows(gu_parts[layer]),
+                spread_cols(down_parts[layer]),
+            )
+        )
+
+    def my_tokens(value):
+        mine = lax.dynamic_slice_in_dim(value, piece * sub, sub, 0)
+        return halved(gathered(mine, "seq"))
+
+    aux = make_aux(doc_starts[core], length)
+    resid = my_tokens(tokens[core]).astype(jnp.float32)
+    masked = cotangent[core] * valid_mask[core].astype(jnp.bfloat16)[:, None]
+    upstream = my_tokens(masked).astype(jnp.float32)
+
+    def stats(values):
+        return jnp.stack([jnp.sum(valid * jnp.mean(v * v, axis=-1)) for v in values])
+
+    out0, attn0, ffn0, saved0 = layer_forward(resid, gains[0], weights[0], small[0], aux, parts)
+    stats0 = stats((out0, attn0, ffn0))
+    h1 = out0.astype(jnp.bfloat16)
+    out1, attn1, ffn1, saved1 = layer_forward(
+        h1.astype(jnp.float32), gains[1], weights[1], small[1], aux, parts
+    )
+    stats1 = stats((out1, attn1, ffn1))
+    act1 = out1.astype(jnp.bfloat16)
+
+    grad_h1, big1, small1 = layer_backward_fast(
+        upstream, saved1, gains[1], weights[1], small[1], aux, parts
+    )
+    grad_h1 = grad_h1.astype(jnp.bfloat16)
+    grad_tokens, big0, small0 = layer_backward_fast(
+        grad_h1.astype(jnp.float32), saved0, gains[0], weights[0], small[0], aux, parts
+    )
+    grad_tokens = grad_tokens.astype(jnp.bfloat16)
+
+    def placed_tokens(layer0, layer1):
+        layer0, layer1 = (
+            lax.dynamic_slice_in_dim(value, shard * sub, sub, 0) for value in (layer0, layer1)
+        )
+        keep = pick(first, layer0, layer1)
+        received = partner(pick(first, layer1, layer0))
+        both = jnp.stack([pick(first, keep, received), pick(first, received, keep)])
+        pieces = jnp.stack(in_order(by_partner(both, "head"), "head"), axis=1)
+        pieces = pieces.reshape(2, slices * sub, 2, shards, model_width // (2 * shards))
+        return jnp.swapaxes(pieces, 2, 3).reshape(2, slices * sub, model_width)
+
+    activations = placed_tokens(h1, act1)
+    input_grads = placed_tokens(grad_tokens, grad_h1)
+
+    def joined(layer0, layer1, axis):
+        keep = pick(first, layer0, layer1)
+        received = partner(pick(first, layer1, layer0))
+        return jnp.concatenate(
+            [pick(first, keep, received), pick(first, received, keep)], axis=axis
+        ).astype(jnp.float32)
+
+    grad_down = joined(collect_cols(big0[3]), collect_cols(big1[3]), 2)
+    grad_gu = joined(collect_rows(big0[2]), collect_rows(big1[2]), 0)
+    grad_out = joined(collect_cols(big0[1]), collect_cols(big1[1]), 2)
+    grad_proj = joined(collect_rows(big0[0]), collect_rows(big1[0]), 0)
+
+    def pack(grads, sums):
+        dtaps, dscal, dnorm, dattn, dmlp, dmix = grads
+        place = (jnp.arange(2) == core)[:, None]
+        marked = jnp.where(place, jnp.concatenate([sums, jnp.sum(valid)[None]])[None], 0.0)
+        return jnp.concatenate(
+            [dtaps.reshape(-1), dscal, dnorm, marked.reshape(-1), dattn, dmlp, dmix.reshape(-1)]
+        )
+
+    packs = (pack(small0, stats0), pack(small1, stats1))
+    vector = pick(first, packs[0], packs[1]) + partner(pick(first, packs[1], packs[0]))
+    gain_end = norm_at + HEAD_V + 8 + 2 * model_width
+    per_head = gathered(vector[None, :norm_at], "seq")
+    sums_all = halves(vector[norm_at:gain_end], "head")
+    norm_sum = halves(sums_all[:HEAD_V], "seq")
+    stat_sums = sums_all[HEAD_V : HEAD_V + 8].reshape(2, 4)
+    gain_sums = sums_all[HEAD_V + 8 :].reshape(2, 2, shards, shard_rows // 2)
+    gain_sums = lax.dynamic_index_in_dim(gain_sums, shard, 2, False).reshape(2, shard_rows)
+    branch_rms = jnp.sqrt(stat_sums[:, :3] / jnp.maximum(stat_sums[:, 3:], 1.0))
+    mix_grad = vector[gain_end:].reshape(slices, 2, 2, shards, shard_rows // 2)
+    mix_grad = jnp.sum(lax.all_to_all(mix_grad, "head", 0, 0), axis=0)
+    mix_grad = lax.all_to_all(jnp.transpose(mix_grad, (2, 0, 1, 3)), "seq", 0, 0)
+    mix_grad = jnp.transpose(mix_grad, (1, 2, 3, 0)).reshape(2, shard_rows, shards)
+    conv_grad = jnp.swapaxes(per_head[:, :taps_size].reshape(shards, CONVK, WIDTH), 0, 1)
+
+    def conv_part(start, width):
+        return conv_grad[:, :, start : start + width].reshape(1, CONVK, shards * width)
+
+    def proj_part(start, width):
+        return grad_proj[:, :, start : start + width].reshape(1, shard_rows, shards * width)
+
+    def gu_part(start):
+        return grad_gu[:, :, start : start + hidden_width].reshape(1, shard_rows, shards * hidden_width)
+
+    return (
+        activations[None],
+        input_grads[None],
+        branch_rms[None],
+        gain_sums[0][None],
+        proj_part(0, HEAD_K),
+        proj_part(HEAD_K, HEAD_K),
+        proj_part(2 * HEAD_K, HEAD_V),
+        proj_part(2 * HEAD_K + HEAD_V, HEAD_V),
+        mix_grad[0][None],
+        mix_grad[1][None],
+        conv_part(0, HEAD_K),
+        conv_part(HEAD_K, HEAD_K),
+        conv_part(2 * HEAD_K, HEAD_V),
+        per_head[:, taps_size][None],
+        per_head[:, taps_size + 1][None],
+        norm_sum[None],
+        grad_out.reshape(1, shards * HEAD_V, shard_rows),
+        gain_sums[1][None],
+        gu_part(0),
+        gu_part(hidden_padded),
+        grad_down[:, :hidden_width].reshape(1, shards * hidden_width, shard_rows),
+    )
+
+
+def per_device(*args):
+    tokens, w_decay = args[0], args[9]
+    rows = tokens.shape[1]
+    seq, head, section = (lax.axis_size(axis) for axis in ("seq", "head", "section"))
+    one_head_each = w_decay.shape[2] == seq
+    micro_each = tokens.shape[0] == section == 2
+    powers = seq & (seq - 1) == 0 and head & (head - 1) == 0
+    even = rows % (head * BLOCK) == 0 and rows * seq % (BLOCK * GROUP) == 0
+    if one_head_each and micro_each and powers and even:
+        return fast_shards(*args)
+    return shards(*args)
+
+
 def solution(mesh):
     placed = (
         P(None, "seq", None),
@@ -655,7 +1454,7 @@
         P("section", "head", "seq"),
     )
     return jax.shard_map(
-        shards,
+        per_device,
         mesh=mesh,
         in_specs=placed,
         out_specs=(

time: 3420 us -> 1880 us (0.55)
  waiting for transfers between devices: 1330 us -> 514 us
  other arithmetic: 833 us -> 233 us
  matrix products: 642 us -> 161 us
  Pallas kernels: 0 us -> 181 us
  blocking collectives: 164 us -> 321 us
  starting transfers between devices: 20.7 us -> 164 us
  local copies, waits for them, and re-layouts: 388 us -> 271 us
    all_gather x14 -> x8, waiting for transfers between devices: 580 us -> 0.07 us  [the longest x4 0.04 us: spread_cols(): full = lax.all_gather(part, ('section', 'head'), axis=0, tiled=True)]
    another operation x33 -> x24, other arithmetic: 511 us -> 51 us  [the longest x4 14 us: grad_halves(): jnp.stack([inner_t(value, grad[:, half * width:(half + 1) * width]).astyp...]
    reduce_scatter x5 -> x6, waiting for transfers between devices: 453 us -> 64.4 us  [the longest x4 64.4 us: collect_rows(): lax.psum_scatter(grad.reshape(-1, grad.shape[2]), ('head', 'section'), sc...]
    dot_general x222 -> x26, matrix products: 415 us -> 57 us  [dot(): return jnp.dot(left, right, preferred_element_type=jnp.float32)]
    all_to_all x0 -> x12, blocking collectives: none -> 321 us  [the longest x3 123 us: spread_rows(): part = lax.all_to_all(part, 'seq', 0, 0)]
    psum x11 -> x0, waiting for transfers between devices: 286 us -> none  [head_total(): return lax.psum(values.astype(jnp.bfloat16), 'head').astype(jnp.float32)]
    all_to_all x0 -> x22, waiting for transfers between devices: none -> 239 us  [the longest x3 42 us: collect_cols(): return lax.all_to_all(part, 'seq', 0, 0)]
    pallas_call x0 -> x4, Pallas kernels: none -> 181 us  [the longest x2 93.7 us: recur_backward(): pl.pallas_call(functools.partial(backward_kernel, parts), out_shape=(jax....]
  transfers between devices with their start and end apart: 40 -> 99, of which waited for: 26 -> 51; matrix products, arithmetic and copies ran while one was open for 28% -> 30% of each run, Pallas kernels for 0% -> 10%
where the time goes in v1:
time: 1880 us; the launch traced here: 1860 us
  waiting for transfers between devices  514 us (27%)
  blocking collectives  321 us (17%)
  local copies, waits for them, and re-layouts  271 us (14%)
  other arithmetic  233 us (12%)
  Pallas kernels  181 us (10%)
  starting transfers between devices  164 us (9%)
  matrix products  161 us (9%)
    ppermute x45, waiting for transfers between devices, by_partner(): lax.ppermute(value, axis, [(i, i ^ k) for i in range(size)])  180 us
    all_to_all x3, blocking collectives, spread_rows(): part = lax.all_to_all(part, 'seq', 0, 0)  123 us
    all_to_all x4, blocking collectives, shard_total(): pieces = lax.all_to_all(pieces, 'seq', 0, 0)  110 us
    pallas_call x2, Pallas kernels, recur_backward(): pl.pallas_call(functools.partial(backward_kernel, parts), out_shape=(jax....  93.7 us
    pallas_call x2, Pallas kernels, recur_forward(): pl.pallas_call(functools.partial(forward_kernel, parts), out_shape=(jax.S...  87.1 us
    dot_general x26, matrix products, proj_t(): lax.dot_general(left, right, (((1,), (1,)), ((), ())), preferred_element_...  68.4 us
    reduce_scatter x4, waiting for transfers between devices, collect_rows(): lax.psum_scatter(grad.reshape(-1, grad.shape[2]), ('head', 'section'), sc...  64.4 us
    dot_general x26, matrix products, dot(): return jnp.dot(left, right, preferred_element_type=jnp.float32)  57 us
  transfers between devices with their start and end apart: 99, of which 51 were waited for; matrix products, arithmetic and copies ran while one was open for 30% of the time, Pallas kernels for 10%

profile of v1, /device:TPU:1, one launch (start us, length us, event | category | flops | bytes accessed | tf_op | source)
XLA Modules:
  0.0 1863.8 jit_solution(11420455126868457940)
XLA Ops:
  23.5 42.3 %all_to_all.170 = bf16[4,256,768]{2,1,0:T(8,128)(2,1)} all-to-all(bf16[4,256,768]{2,1,0:T(8,128)(2,1)S(1)} %get-tuple-element.273), channel_id=1, replica_groups=mesh['section'=2,'seq'=4,'head'=4] {'seq'}, dimensions={0} | all-to-all | bytes 3145728 | tf_op jit(solution)/shard_map/all_to_all | solution.py:1027
  70.9 16.5 all_to_all.171
  97.2 40.1 %all_to_all.172 = bf16[4,256,768]{2,1,0:T(8,128)(2,1)} all-to-all(bf16[4,256,768]{2,1,0:T(8,128)(2,1)S(1)} %get-tuple-element.271), channel_id=1, replica_groups=mesh['section'=2,'seq'=4,'head'=4] {'seq'}, dimensions={0} | all-to-all | bytes 3145728 | tf_op jit(solution)/shard_map/all_to_all | solution.py:1027
  141.8 22.7 %all_to_all.173 = bf16[4,384,256]{2,1,0:T(8,128)(2,1)S(1)} all-to-all(bf16[4,384,256]{2,1,0:T(8,128)(2,1)S(1)} %get-tuple-element.284), channel_id=1, replica_groups=mesh['section'=2,'seq'=4,'head'=4] {'seq'}, dimensions={0} | all-to-all | bytes 1572864 | tf_op jit(solution)/shard_map/all_to_all | solution.py:1034
  165.6 40.6 %all_to_all.174 = bf16[4,256,768]{2,1,0:T(8,128)(2,1)} all-to-all(bf16[4,256,768]{2,1,0:T(8,128)(2,1)} %get-tuple-element.272), channel_id=1, replica_groups=mesh['section'=2,'seq'=4,'head'=4] {'seq'}, dimensions={0} | all-to-all | bytes 3145728 | tf_op jit(solution)/shard_map/all_to_all | solution.py:1027
  206.3 16.5 all_to_all.175
  232.7 25.6 %all-to-all-done.14 = bf16[4,384,256]{2,1,0:T(8,128)(2,1)S(1)} async-done(((bf16[4,384,256]{2,1,0:T(8,128)(2,1)}), bf16[4,384,256]{2,1,0:T(8,128)(2,1)S(1)}, u32[]{:S(2)}, u32[]{:S(2)}) %all-to-all-start.14) | async-done | bytes 786464 | tf_op jit(solution)/shard_map/all_to_all | solution.py:1034
  325.0 22.0 %all-to-all-done.13 = bf16[4,256,768]{2,1,0:T(8,128)(2,1)} async-done(((bf16[4,256,768]{2,1,0:T(8,128)(2,1)}), bf16[4,256,768]{2,1,0:T(8,128)(2,1)}, u32[]{:S(2)}, u32[]{:S(2)}) %all-to-all-start.13) | async-done | bytes 1572896 | tf_op jit(solution)/shard_map/all_to_all | solution.py:1027
  354.8 27.2 %all-to-all-done.1 = bf16[4,256,640]{2,1,0:T(8,128)(2,1)} async-done(((bf16[4,256,640]{2,1,0:T(8,128)(2,1)}), bf16[4,256,640]{2,1,0:T(8,128)(2,1)}, u32[]{:S(2)}, u32[]{:S(2)}) %all-to-all-start.1) | async-done | bytes 1310752 | tf_op jit(solution)/shard_map/all_to_all | solution.py:1104
  382.0 43.5 %recur_forward.2 = (bf16[1024,256]{1,0:T(8,128)(2,1)}, f32[16,128,256]{2,1,0:T(8,128)S(1)}, f32[1024,64]{1,0:T(8,128)S(1)}) custom-call(bf16[1024,640]{1,0:T(8,128)(2,1)} %bitcast.61.xh_ref, f32[1024,8]{1,0:T(8,128)S(1)} %copy.557.aux_ref, f32[8,512]{1,0:T(8,128)S(1)} %pad.27.taps_ref, f32[8,128]{1,0:T(8,128)S(1)} %pad.28.scal_ref), custom_call_target="tpu_custom_call" | custom-call | tf_op jit(solution)/shard_map/recur_forward/pallas_call | solution.py:921
  449.8 26.2 %all_to_all.176 = bf16[4,64,2048]{2,1,0:T(8,128)(2,1)} all-to-all(bf16[4,64,2048]{2,1,0:T(8,128)(2,1)S(1)} %pad_maximum_fusion.18), channel_id=1, replica_groups=mesh['section'=2,'seq'=4,'head'=4] {'seq'}, dimensions={0} | all-to-all | bytes 2097152 | tf_op jit(solution)/shard_map/all_to_all | solution.py:1008
  484.8 14.6 collective-permute-done.13
  537.6 27.5 %all_to_all.177 = bf16[4,64,2048]{2,1,0:T(8,128)(2,1)} all-to-all(bf16[4,64,2048]{2,1,0:T(8,128)(2,1)S(1)} %pad_maximum_fusion.20), channel_id=1, replica_groups=mesh['section'=2,'seq'=4,'head'=4] {'seq'}, dimensions={0} | all-to-all | bytes 2097152 | tf_op jit(solution)/shard_map/all_to_all | solution.py:1008
  574.8 14.6 collective-permute-done.18
  634.3 14.6 all-to-all-done.9
  648.9 43.5 %recur_forward.3 = (bf16[1024,256]{1,0:T(8,128)(2,1)}, f32[16,128,256]{2,1,0:T(8,128)S(1)}, f32[1024,64]{1,0:T(8,128)S(1)}) custom-call(bf16[1024,640]{1,0:T(8,128)(2,1)} %bitcast.103.xh_ref, f32[1024,8]{1,0:T(8,128)S(1)} %copy.557.aux_ref, f32[8,512]{1,0:T(8,128)S(1)} %pad.32.taps_ref, f32[8,128]{1,0:T(8,128)S(1)} %pad.33.scal_ref), custom_call_target="tpu_custom_call" | custom-call | tf_op jit(solution)/shard_map/recur_forward/pallas_call | solution.py:921
  722.3 20.0 %collective-permute-done.30 = bf16[64,2048]{1,0:T(8,128)(2,1)S(1)} collective-permute-done((bf16[64,2048]{1,0:T(8,128)(2,1)S(1)}, bf16[64,2048]{1,0:T(8,128)(2,1)S(1)}, u32[]{:S(2)}, u32[]{:S(2)}) %collective-permute-start.30) | collective-permute-done | bytes 262176 | tf_op jit(solution)/shard_map/ppermute | solution.py:985
  742.3 23.6 %collective-permute-done.31 = bf16[64,2048]{1,0:T(8,128)(2,1)S(1)} collective-permute-done((bf16[64,2048]{1,0:T(8,128)(2,1)S(1)}, bf16[64,2048]{1,0:T(8,128)(2,1)S(1)}, u32[]{:S(2)}, u32[]{:S(2)}) %collective-permute-start.31) | collective-permute-done | bytes 262176 | tf_op jit(solution)/shard_map/ppermute | solution.py:985
  785.9 9.5 collective-permute-done.21
  826.1 28.9 %all_to_all.178 = bf16[4,64,2048]{2,1,0:T(8,128)(2,1)} all-to-all(bf16[4,64,2048]{2,1,0:T(8,128)(2,1)S(1)} %bitcast.660), channel_id=1, replica_groups=mesh['section'=2,'seq'=4,'head'=4] {'seq'}, dimensions={0} | all-to-all | bytes 2097152 | tf_op jit(solution)/shard_map/all_to_all | solution.py:1008
  865.1 14.2 collective-permute-done.34
  888.9 8.8 fusion.172
  905.2 6.5 copy.604
  936.7 46.9 %recur_backward.2 = (bf16[1024,640]{1,0:T(8,128)(2,1)}, f32[8,512]{1,0:T(8,128)S(1)}, f32[8,128]{1,0:T(8,128)S(1)}) custom-call(bf16[1024,640]{1,0:T(8,128)(2,1)} %bitcast.103.xh_ref, f32[1024,8]{1,0:T(8,128)S(1)} %copy.557.aux_ref, f32[8,512]{1,0:T(8,128)S(1)} %pad.32.taps_ref, f32[8,128]{1,0:T(8,128)S(1)} %pad.33.scal_ref, f32[16,128,256]{2,1,0:T(8,128)} %copy-done.3, ...), custom_call_target="tpu_custom_call" | custom-call | tf_op jit(solution)/shard_map/recur_backward/pallas_call | solution.py:941
  997.9 6.8 all-to-all-start.15
  1047.2 6.1 pad_maximum_fusion.5
  1053.4 14.8 all-to-all-done.19
  1074.1 16.6 collective-permute-done.24
  1111.7 11.3 fusion.173
  1155.1 27.6 %all_to_all.179 = bf16[4,64,2048]{2,1,0:T(8,128)(2,1)} all-to-all(bf16[4,64,2048]{2,1,0:T(8,128)(2,1)S(1)} %bitcast.661), channel_id=1, replica_groups=mesh['section'=2,'seq'=4,'head'=4] {'seq'}, dimensions={0} | all-to-all | bytes 2097152 | tf_op jit(solution)/shard_map/all_to_all | solution.py:1008
  1192.3 14.6 collective-permute-done.40
  1216.6 10.0 fusion.176
  1234.3 6.5 copy.601
  1309.1 8.6 all_to_all.180
  1317.7 46.9 %recur_backward.3 = (bf16[1024,640]{1,0:T(8,128)(2,1)}, f32[8,512]{1,0:T(8,128)S(1)}, f32[8,128]{1,0:T(8,128)S(1)}) custom-call(bf16[1024,640]{1,0:T(8,128)(2,1)} %bitcast.61.xh_ref, f32[1024,8]{1,0:T(8,128)S(1)} %copy.557.aux_ref, f32[8,512]{1,0:T(8,128)S(1)} %pad.27.taps_ref, f32[8,128]{1,0:T(8,128)S(1)} %copy-done.7, f32[16,128,256]{2,1,0:T(8,128)} %copy-done.2, ...), custom_call_target="tpu_custom_call" | custom-call | tf_op jit(solution)/shard_map/recur_backward/pallas_call | solution.py:941
  1371.3 13.3 all-to-all-done.22
  1425.3 18.6 all-to-all-done.23
  1453.3 12.6 collective-permute-done.43
  1492.8 13.3 all-to-all-done.29
  1519.4 17.5 all-to-all-done.33
  1543.1 11.2 all-to-all-done.28
  1554.3 23.4 %all_to_all.181 = bf16[4,384,256]{2,1,0:T(8,128)(2,1)} all-to-all(bf16[4,384,256]{2,1,0:T(8,128)(2,1)} %copy.610), channel_id=1, replica_groups=mesh['section'=2,'seq'=4,'head'=4] {'seq'}, dimensions={0} | all-to-all | bytes 1572864 | tf_op jit(solution)/shard_map/all_to_all | solution.py:1055
  1591.3 27.3 %all-to-all-done.31 = bf16[4,256,768]{2,1,0:T(8,128)(2,1)} async-done(((bf16[4,256,768]{2,1,0:T(8,128)(2,1)}), bf16[4,256,768]{2,1,0:T(8,128)(2,1)}, u32[]{:S(2)}, u32[]{:S(2)}) %all-to-all-start.31) | async-done | bytes 1572896 | tf_op jit(solution)/shard_map/all_to_all | solution.py:1045
  1626.0 10.7 collective-permute-done.29
  1687.5 10.1 collective-permute-done.56
  1702.2 7.0 collective-permute-done.57
  1711.0 60.1 %reduce-scatter.13.cloned.1.call-done = bf16[1024,768]{1,0:T(8,128)(2,1)} async-done(((bf16[8192,768]{1,0:T(8,128)(2,1)}), bf16[1024,768]{1,0:T(8,128)(2,1)}) %reduce-scatter.13.cloned.1.call-update) | async-done | bytes 1572880 | tf_op jit(solution)/shard_map/reduce_scatter | solution.py:1041
  1801.1 11.0 all-to-all-done.24
  (1098 shorter events, 843.4 us)
Async XLA Ops:
  7.2 305.6 %all-gather.9.cloned.1.call-start = ((), (), s32[]{:S(2)}) async-start(), calls=%async_computation.42 | async-start | bytes 14155776 | tf_op jit(solution)/shard_map/all_gather | solution.py:1029
  65.8 379.2 %all-gather.11.cloned.1.call-start = ((), (), s32[]{:S(2)}) async-start(), calls=%async_computation.43 | async-start | bytes 4718592 | tf_op jit(solution)/shard_map/all_gather | solution.py:1036
  88.3 425.3 %all-gather.13.cloned.1.call-start = ((), (), s32[]{:S(2)}) async-start(), calls=%async_computation.44 | async-start | bytes 14155776 | tf_op jit(solution)/shard_map/all_gather | solution.py:1029
  137.3 394.0 %all-gather.15.cloned.1.call-start = ((), (), s32[]{:S(2)}) async-start(), calls=%async_computation.45 | async-start | bytes 7077888 | tf_op jit(solution)/shard_map/all_gather | solution.py:1036
  165.6 440.3 %all-gather.17.cloned.1.call-start = ((), (), s32[]{:S(2)}) async-start(), calls=%async_computation.46 | async-start | bytes 14155776 | tf_op jit(solution)/shard_map/all_gather | solution.py:1029
  206.2 503.8 %all-gather.19.cloned.1.call-start = ((), (), s32[]{:S(2)}) async-start(), calls=%async_computation.47 | async-start | bytes 4718592 | tf_op jit(solution)/shard_map/all_gather | solution.py:1036
  223.9 34.4 %all-to-all-start.14 = ((bf16[4,384,256]{2,1,0:T(8,128)(2,1)}), bf16[4,384,256]{2,1,0:T(8,128)(2,1)S(1)}, u32[]{:S(2)}, u32[]{:S(2)}) async-start(bf16[4,384,256]{2,1,0:T(8,128)(2,1)} %get-tuple-element.283), calls=%async_computation.14 | async-start | bytes 1572864 | tf_op jit(solution)/shard_map/all_to_all | solution.py:1034
  227.5 541.4 %all-gather.23.cloned.1.call-start = ((), (), s32[]{:S(2)}) async-start(), calls=%async_computation.49 | async-start | bytes 7077888 | tf_op jit(solution)/shard_map/all_gather | solution.py:1036
  229.5 50.2 %collective-permute-start = (bf16[64,2048]{1,0:T(8,128)(2,1)}, bf16[64,2048]{1,0:T(8,128)(2,1)S(1)}, u32[]{:S(2)}, u32[]{:S(2)}) collective-permute-start(bf16[64,2048]{1,0:T(8,128)(2,1)} %dynamic-slice_bitcast_fusion.1), channel_id=1, source_target_pairs={{0,12},{4,8},{8,4},{12,0},{1,13},{5,9},{9,5},{13,1},{2,14},{6,10},... | collective-permute-start | bytes 786440 | tf_op jit(solution)/shard_map/ppermute | solution.py:985
  232.7 47.0 %collective-permute-start.1 = (bf16[64,2048]{1,0:T(8,128)(2,1)}, bf16[64,2048]{1,0:T(8,128)(2,1)S(1)}, u32[]{:S(2)}, u32[]{:S(2)}) collective-permute-start(bf16[64,2048]{1,0:T(8,128)(2,1)} %dynamic-slice_bitcast_fusion.1), channel_id=1, source_target_pairs={{0,8},{4,12},{8,0},{12,4},{1,9},{5,13},{9,1},{13,5},{2,10},{6,14},... | collective-permute-start | bytes 786440 | tf_op jit(solution)/shard_map/ppermute | solution.py:985
  306.1 40.9 %all-to-all-start.13 = ((bf16[4,256,768]{2,1,0:T(8,128)(2,1)}), bf16[4,256,768]{2,1,0:T(8,128)(2,1)}, u32[]{:S(2)}, u32[]{:S(2)}) async-start(bf16[4,256,768]{2,1,0:T(8,128)(2,1)} %get-tuple-element.270), calls=%async_computation.13 | async-start | bytes 3145728 | tf_op jit(solution)/shard_map/all_to_all | solution.py:1027
  347.0 34.9 %all-to-all-start.1 = ((bf16[4,256,640]{2,1,0:T(8,128)(2,1)}), bf16[4,256,640]{2,1,0:T(8,128)(2,1)}, u32[]{:S(2)}, u32[]{:S(2)}) async-start(bf16[4,256,640]{2,1,0:T(8,128)(2,1)} %maximum_maximum_fusion.1), calls=%async_computation.1 | async-start | bytes 2621440 | tf_op jit(solution)/shard_map/all_to_all | solution.py:1104
  351.6 458.5 %all-gather.21.cloned.1.call-start = ((), (), s32[]{:S(2)}) async-start(), calls=%async_computation.48 | async-start | bytes 14155776 | tf_op jit(solution)/shard_map/all_gather | solution.py:1029
  714.7 58.7 %all-to-all-start.12 = ((bf16[4,64,2048]{2,1,0:T(8,128)(2,1)}), bf16[4,64,2048]{2,1,0:T(8,128)(2,1)S(1)}, u32[]{:S(2)}, u32[]{:S(2)}) async-start(bf16[4,64,2048]{2,1,0:T(8,128)(2,1)} %pad_maximum_fusion.23), calls=%async_computation.12 | async-start | bytes 2097152 | tf_op jit(solution)/shard_map/all_to_all | solution.py:1008
  718.3 766.6 %reduce-scatter.19.cloned.1.call-start = ((), (), s32[]{:S(2)}) async-start(), calls=%async_computation.53 | async-start | bytes 4718592 | tf_op jit(solution)/shard_map/reduce_scatter | solution.py:1050
  718.7 23.6 %collective-permute-start.30 = (bf16[64,2048]{1,0:T(8,128)(2,1)S(1)}, bf16[64,2048]{1,0:T(8,128)(2,1)S(1)}, u32[]{:S(2)}, u32[]{:S(2)}) collective-permute-start(bf16[64,2048]{1,0:T(8,128)(2,1)S(1)} %dynamic-slice_multiply_fusion.2), channel_id=1, source_target_pairs={{0,12},{4,8},{8,4},{12,0},{1,13},{5,9},{9,5},{13,1},{2,14},{6,10},... | collective-permute-start | bytes 786440 | tf_op jit(solution)/shard_map/ppermute | solution.py:985
  722.0 44.0 %collective-permute-start.31 = (bf16[64,2048]{1,0:T(8,128)(2,1)S(1)}, bf16[64,2048]{1,0:T(8,128)(2,1)S(1)}, u32[]{:S(2)}, u32[]{:S(2)}) collective-permute-start(bf16[64,2048]{1,0:T(8,128)(2,1)S(1)} %dynamic-slice_multiply_fusion.2), channel_id=1, source_target_pairs={{0,8},{4,12},{8,0},{12,4},{1,9},{5,13},{9,1},{13,5},{2,10},{6,14},... | collective-permute-start | bytes 786440 | tf_op jit(solution)/shard_map/ppermute | solution.py:985
  722.0 44.0 %collective-permute-start.32 = (bf16[64,2048]{1,0:T(8,128)(2,1)S(1)}, bf16[64,2048]{1,0:T(8,128)(2,1)S(1)}, u32[]{:S(2)}, u32[]{:S(2)}) collective-permute-start(bf16[64,2048]{1,0:T(8,128)(2,1)S(1)} %dynamic-slice_multiply_fusion.2), channel_id=1, source_target_pairs={{0,4},{4,0},{8,12},{12,8},{1,5},{5,1},{9,13},{13,9},{2,6},{6,2},{1... | collective-permute-start | bytes 786440 | tf_op jit(solution)/shard_map/ppermute | solution.py:985
  997.9 30.2 %all-to-all-start.15 = ((bf16[4,64,2048]{2,1,0:T(8,128)(2,1)}), bf16[4,64,2048]{2,1,0:T(8,128)(2,1)}, u32[]{:S(2)}, u32[]{:S(2)}) async-start(bf16[4,64,2048]{2,1,0:T(8,128)(2,1)} %pad_maximum_fusion.26), calls=%async_computation.15 | async-start | bytes 2097152 | tf_op jit(solution)/shard_map/all_to_all | solution.py:1008
  1028.1 40.1 %all-to-all-start.19 = ((bf16[4,64,2048]{2,1,0:T(8,128)(2,1)}), bf16[4,64,2048]{2,1,0:T(8,128)(2,1)}, u32[]{:S(2)}, u32[]{:S(2)}) async-start(bf16[4,64,2048]{2,1,0:T(8,128)(2,1)} %bitcast.659), calls=%async_computation.19 | async-start | bytes 2097152 | tf_op jit(solution)/shard_map/all_to_all | solution.py:1008
  1032.3 477.1 %reduce-scatter.27.cloned.1.call-start = ((), (), s32[]{:S(2)}) async-start(), calls=%async_computation.57 | async-start | bytes 7077888
  1043.7 26.8 %collective-permute-start.23 = (bf16[64,2048]{1,0:T(8,128)(2,1)}, bf16[64,2048]{1,0:T(8,128)(2,1)}, u32[]{:S(2)}, u32[]{:S(2)}) collective-permute-start(bf16[64,2048]{1,0:T(8,128)(2,1)} %reduce_sum.490), channel_id=1, source_target_pairs={{0,12},{4,8},{8,4},{12,0},{1,13},{5,9},{9,5},{13,1},{2,14},{6,10},... | collective-permute-start | bytes 786440 | tf_op jit(solution)/shard_map/ppermute | solution.py:985
  1046.8 43.8 %collective-permute-start.24 = (bf16[64,2048]{1,0:T(8,128)(2,1)}, bf16[64,2048]{1,0:T(8,128)(2,1)}, u32[]{:S(2)}, u32[]{:S(2)}) collective-permute-start(bf16[64,2048]{1,0:T(8,128)(2,1)} %reduce_sum.490), channel_id=1, source_target_pairs={{0,8},{4,12},{8,0},{12,4},{1,9},{5,13},{9,1},{13,5},{2,10},{6,14},... | collective-permute-start | bytes 786440 | tf_op jit(solution)/shard_map/ppermute | solution.py:985
  1046.8 43.8 %collective-permute-start.25 = (bf16[64,2048]{1,0:T(8,128)(2,1)}, bf16[64,2048]{1,0:T(8,128)(2,1)}, u32[]{:S(2)}, u32[]{:S(2)}) collective-permute-start(bf16[64,2048]{1,0:T(8,128)(2,1)} %reduce_sum.490), channel_id=1, source_target_pairs={{0,4},{4,0},{8,12},{12,8},{1,5},{5,1},{9,13},{13,9},{2,6},{6,2},{1... | collective-permute-start | bytes 786440 | tf_op jit(solution)/shard_map/ppermute | solution.py:985
  1053.4 464.0 %reduce-scatter.17.cloned.1.call-start = ((), (), s32[]{:S(2)}) async-start(), calls=%async_computation.52 | async-start | bytes 4718592 | tf_op jit(solution)/shard_map/reduce_scatter | solution.py:1050
  1070.5 29.8 %collective-permute-start.36 = (bf16[64,2048]{1,0:T(8,128)(2,1)}, bf16[64,2048]{1,0:T(8,128)(2,1)}, u32[]{:S(2)}, u32[]{:S(2)}) collective-permute-start(bf16[64,2048]{1,0:T(8,128)(2,1)} %reduce_sum.494), channel_id=1, source_target_pairs={{0,12},{4,8},{8,4},{12,0},{1,13},{5,9},{9,5},{13,1},{2,14},{6,10},... | collective-permute-start | bytes 786440 | tf_op jit(solution)/shard_map/ppermute | solution.py:985
  1070.5 31.4 %collective-permute-start.37 = (bf16[64,2048]{1,0:T(8,128)(2,1)}, bf16[64,2048]{1,0:T(8,128)(2,1)}, u32[]{:S(2)}, u32[]{:S(2)}) collective-permute-start(bf16[64,2048]{1,0:T(8,128)(2,1)} %reduce_sum.494), channel_id=1, source_target_pairs={{0,8},{4,12},{8,0},{12,4},{1,9},{5,13},{9,1},{13,5},{2,10},{6,14},... | collective-permute-start | bytes 786440 | tf_op jit(solution)/shard_map/ppermute | solution.py:985
  1070.5 31.4 %collective-permute-start.38 = (bf16[64,2048]{1,0:T(8,128)(2,1)}, bf16[64,2048]{1,0:T(8,128)(2,1)}, u32[]{:S(2)}, u32[]{:S(2)}) collective-permute-start(bf16[64,2048]{1,0:T(8,128)(2,1)} %reduce_sum.494), channel_id=1, source_target_pairs={{0,4},{4,0},{8,12},{12,8},{1,5},{5,1},{9,13},{13,9},{2,6},{6,2},{1... | collective-permute-start | bytes 786440 | tf_op jit(solution)/shard_map/ppermute | solution.py:985
  1240.9 299.5 %reduce-scatter.25.cloned.1.call-start = ((), (), s32[]{:S(2)}) async-start(), calls=%async_computation.56 | async-start | bytes 7077888
  1249.8 327.9 %reduce-scatter.23.cloned.1.call-start = ((), (), s32[]{:S(2)}) async-start(), calls=%async_computation.55 | async-start | bytes 14155776 | tf_op jit(solution)/shard_map/reduce_scatter | solution.py:1041
  1264.6 326.7 %reduce-scatter.15.cloned.1.call-start = ((), (), s32[]{:S(2)}) async-start(), calls=%async_computation.51 | async-start | bytes 14155776 | tf_op jit(solution)/shard_map/reduce_scatter | solution.py:1041
  1278.8 389.4 %reduce-scatter.21.cloned.1.call-start = ((), (), s32[]{:S(2)}) async-start(), calls=%async_computation.54 | async-start | bytes 14155776 | tf_op jit(solution)/shard_map/reduce_scatter | solution.py:1041
  1369.2 401.9 %reduce-scatter.13.cloned.1.call-start = ((), (), s32[]{:S(2)}) async-start(), calls=%async_computation.50 | async-start | bytes 14155776 | tf_op jit(solution)/shard_map/reduce_scatter | solution.py:1041
  1414.8 29.0 %all-to-all-start.23 = ((bf16[4,64,2048]{2,1,0:T(8,128)(2,1)}), bf16[4,64,2048]{2,1,0:T(8,128)(2,1)S(1)}, u32[]{:S(2)}, u32[]{:S(2)}) async-start(bf16[4,64,2048]{2,1,0:T(8,128)(2,1)} %bitcast.167), calls=%async_computation.23 | async-start | bytes 2097152 | tf_op jit(solution)/shard_map/all_to_all | solution.py:1008
  1444.8 21.1 %collective-permute-start.43 = (bf16[64,2048]{1,0:T(8,128)(2,1)}, bf16[64,2048]{1,0:T(8,128)(2,1)S(1)}, u32[]{:S(2)}, u32[]{:S(2)}) collective-permute-start(bf16[64,2048]{1,0:T(8,128)(2,1)} %reduce_sum.499), channel_id=1, source_target_pairs={{0,8},{4,12},{8,0},{12,4},{1,9},{5,13},{9,1},{13,5},{2,10},{6,14},... | collective-permute-start | bytes 786440 | tf_op jit(solution)/shard_map/ppermute | solution.py:985
  1513.8 23.1 %all-to-all-start.33 = ((bf16[4,384,256]{2,1,0:T(8,128)(2,1)}), bf16[4,384,256]{2,1,0:T(8,128)(2,1)S(1)}, u32[]{:S(2)}, u32[]{:S(2)}) async-start(bf16[4,384,256]{2,1,0:T(8,128)(2,1)} %copy.613), calls=%async_computation.39 | async-start | bytes 1572864 | tf_op jit(solution)/shard_map/all_to_all | solution.py:1055
  1577.7 40.9 %all-to-all-start.31 = ((bf16[4,256,768]{2,1,0:T(8,128)(2,1)}), bf16[4,256,768]{2,1,0:T(8,128)(2,1)}, u32[]{:S(2)}, u32[]{:S(2)}) async-start(bf16[4,256,768]{2,1,0:T(8,128)(2,1)} %bitcast.684), calls=%async_computation.37 | async-start | bytes 3145728 | tf_op jit(solution)/shard_map/all_to_all | solution.py:1045
  1588.6 33.6 %collective-permute-start.27 = (bf16[2,64,2048]{2,1,0:T(8,128)(2,1)}, bf16[2,64,2048]{2,1,0:T(8,128)(2,1)S(1)}, u32[]{:S(2)}, u32[]{:S(2)}) collective-permute-start(bf16[2,64,2048]{2,1,0:T(8,128)(2,1)} %pad_maximum_fusion.32), channel_id=1, source_target_pairs={{0,3},{1,2},{2,1},{3,0},{4,7},{5,6},{6,5},{7,4},{8,11},{9,10},{10,... | collective-permute-start | bytes 1572872 | tf_op jit(solution)/shard_map/ppermute | solution.py:985
  1589.5 36.5 %collective-permute-start.28 = (bf16[2,64,2048]{2,1,0:T(8,128)(2,1)}, bf16[2,64,2048]{2,1,0:T(8,128)(2,1)}, u32[]{:S(2)}, u32[]{:S(2)}) collective-permute-start(bf16[2,64,2048]{2,1,0:T(8,128)(2,1)} %pad_maximum_fusion.32), channel_id=1, source_target_pairs={{0,2},{1,3},{2,0},{3,1},{4,6},{5,7},{6,4},{7,5},{8,10},{9,11},{10,... | collective-permute-start | bytes 1572872 | tf_op jit(solution)/shard_map/ppermute | solution.py:985
  1590.3 46.3 %collective-permute-start.29 = (bf16[2,64,2048]{2,1,0:T(8,128)(2,1)}, bf16[2,64,2048]{2,1,0:T(8,128)(2,1)}, u32[]{:S(2)}, u32[]{:S(2)}) collective-permute-start(bf16[2,64,2048]{2,1,0:T(8,128)(2,1)} %pad_maximum_fusion.32), channel_id=1, source_target_pairs={{0,1},{1,0},{2,3},{3,2},{4,5},{5,4},{6,7},{7,6},{8,9},{9,8},{10,11... | collective-permute-start | bytes 1572872 | tf_op jit(solution)/shard_map/ppermute | solution.py:985
  1618.6 45.4 %all-to-all-start.25 = ((bf16[4,256,768]{2,1,0:T(8,128)(2,1)}), bf16[4,256,768]{2,1,0:T(8,128)(2,1)S(1)}, u32[]{:S(2)}, u32[]{:S(2)}) async-start(bf16[4,256,768]{2,1,0:T(8,128)(2,1)} %bitcast.683), calls=%async_computation.27 | async-start | bytes 3145728 | tf_op jit(solution)/shard_map/all_to_all | solution.py:1045
  1660.2 21.9 %collective-permute-start.45 = (bf16[64,2048]{1,0:T(8,128)(2,1)}, bf16[64,2048]{1,0:T(8,128)(2,1)}, u32[]{:S(2)}, u32[]{:S(2)}) collective-permute-start(bf16[64,2048]{1,0:T(8,128)(2,1)} %get-tuple-element.240), channel_id=1, source_target_pairs={{0,16},{16,0},{1,17},{17,1},{2,18},{18,2},{3,19},{19,3},{4,20},{20... | collective-permute-start | bytes 786440 | tf_op jit(solution)/shard_map/ppermute | solution.py:24
  1668.3 102.8 %all-to-all-start.30 = ((bf16[4,256,768]{2,1,0:T(8,128)(2,1)}), bf16[4,256,768]{2,1,0:T(8,128)(2,1)}, u32[]{:S(2)}, u32[]{:S(2)}) async-start(bf16[4,256,768]{2,1,0:T(8,128)(2,1)} %bitcast.681), calls=%async_computation.35 | async-start | bytes 3145728 | tf_op jit(solution)/shard_map/all_to_all | solution.py:1045
  1684.8 90.8 %collective-permute-start.46 = (bf16[2,64,2048]{2,1,0:T(8,128)(2,1)}, bf16[2,64,2048]{2,1,0:T(8,128)(2,1)}, u32[]{:S(2)}, u32[]{:S(2)}) collective-permute-start(bf16[2,64,2048]{2,1,0:T(8,128)(2,1)} %pad_maximum_fusion.33), channel_id=1, source_target_pairs={{0,3},{1,2},{2,1},{3,0},{4,7},{5,6},{6,5},{7,4},{8,11},{9,10},{10,... | collective-permute-start | bytes 1572872 | tf_op jit(solution)/shard_map/ppermute | solution.py:985
  1685.7 90.0 %collective-permute-start.47 = (bf16[2,64,2048]{2,1,0:T(8,128)(2,1)}, bf16[2,64,2048]{2,1,0:T(8,128)(2,1)}, u32[]{:S(2)}, u32[]{:S(2)}) collective-permute-start(bf16[2,64,2048]{2,1,0:T(8,128)(2,1)} %pad_maximum_fusion.33), channel_id=1, source_target_pairs={{0,2},{1,3},{2,0},{3,1},{4,6},{5,7},{6,4},{7,5},{8,10},{9,11},{10,... | collective-permute-start | bytes 1572872 | tf_op jit(solution)/shard_map/ppermute | solution.py:985
  1686.4 89.3 %collective-permute-start.48 = (bf16[2,64,2048]{2,1,0:T(8,128)(2,1)}, bf16[2,64,2048]{2,1,0:T(8,128)(2,1)}, u32[]{:S(2)}, u32[]{:S(2)}) collective-permute-start(bf16[2,64,2048]{2,1,0:T(8,128)(2,1)} %pad_maximum_fusion.33), channel_id=1, source_target_pairs={{0,1},{1,0},{2,3},{3,2},{4,5},{5,4},{6,7},{7,6},{8,9},{9,8},{10,11... | collective-permute-start | bytes 1572872 | tf_op jit(solution)/shard_map/ppermute | solution.py:985
  1771.0 41.1 %all-to-all-start.24 = ((bf16[4,256,768]{2,1,0:T(8,128)(2,1)}), bf16[4,256,768]{2,1,0:T(8,128)(2,1)}, u32[]{:S(2)}, u32[]{:S(2)}) async-start(bf16[4,256,768]{2,1,0:T(8,128)(2,1)} %bitcast.682), calls=%async_computation.25 | async-start | bytes 3145728 | tf_op jit(solution)/shard_map/all_to_all | solution.py:1045
  1814.9 21.5 %collective-permute-start.52 = (bf16[256,4,768]{2,0,1:T(8,128)(2,1)}, bf16[256,4,768]{2,0,1:T(8,128)(2,1)}, u32[]{:S(2)}, u32[]{:S(2)}) collective-permute-start(bf16[256,4,768]{2,0,1:T(8,128)(2,1)} %select_bitcast_fusion.1), channel_id=1, source_target_pairs={{0,16},{16,0},{1,17},{17,1},{2,18},{18,2},{3,19},{19,3},{4,20},{20... | collective-permute-start | bytes 4718600 | tf_op jit(solution)/shard_map/ppermute | solution.py:24
  (277 other events, 3781.5 us)
Sparse Core Ops, SparseCore 0:
  65.9 72.3 all-gather.8
  140.2 37.4 all-gather.10
  179.6 72.1 all-gather.12
  253.5 46.2 all-gather.14
  301.5 85.6 all-gather.16
  388.9 37.0 all-gather.18
  427.9 45.3 all-gather.22
  475.2 72.1 all-gather.20
  911.8 53.8 reduce-scatter.18
  1053.5 66.8 reduce-scatter.26
  1241.0 51.5 reduce-scatter.16
  1296.2 61.8 reduce-scatter.24
  1361.6 92.3 reduce-scatter.22
  1457.4 92.3 reduce-scatter.14
  1553.2 115.0 reduce-scatter.20
  1671.6 99.3 reduce-scatter.12

commit v2 on v1

--- a/solution.py
+++ b/solution.py
@@ -11,6 +11,8 @@
 HEAD_V = 256
 CONVK = 4
 BLOCK = 64
+RECUR_FLOPS = 40_000_000
+VMEM_LIMIT = 48 * 1024 * 1024
 HALO = 8
 EXTRA = 128
 GROUP = 4
@@ -931,7 +933,10 @@
             pltpu.VMEM((length + HALO, WIDTH), jnp.float32),
             pltpu.VMEM((HEAD_K, HEAD_V), jnp.float32),
         ],
-        compiler_params=pltpu.CompilerParams(vmem_limit_bytes=48 * 1024 * 1024),
+        compiler_params=pltpu.CompilerParams(vmem_limit_bytes=VMEM_LIMIT),
+        cost_estimate=pl.CostEstimate(
+            flops=length * RECUR_FLOPS, bytes_accessed=length * 8192, transcendentals=0
+        ),
         name="recur_forward",
     )(xh, aux, taps, scal)
 
@@ -952,7 +957,10 @@
             pltpu.VMEM((HEAD_K, HEAD_V), jnp.float32),
             pltpu.VMEM((HALO, WIDTH), jnp.float32),
         ],
-        compiler_params=pltpu.CompilerParams(vmem_limit_bytes=48 * 1024 * 1024),
+        compiler_params=pltpu.CompilerParams(vmem_limit_bytes=VMEM_LIMIT),
+        cost_estimate=pl.CostEstimate(
+            flops=length * RECUR_FLOPS, bytes_accessed=length * 8192, transcendentals=0
+        ),
         name="recur_backward",
     )(xh, aux, taps, scal, states, inverse, grad)
 
@@ -971,6 +979,671 @@
     return jnp.stack([doc.astype(jnp.float32), back(1), back(2), back(3), entering, leaving, zero, zero], axis=1)
 
 
+def dot(left, right):
+    return lax.dot_general(
+        left, right, (((1,), (0,)), ((), ())), preferred_element_type=jnp.float32
+    )
+
+
+def in_vmem():
+    return pl.BlockSpec(memory_space=pltpu.VMEM)
+
+
+def in_smem():
+    return pl.BlockSpec(memory_space=pltpu.SMEM)
+
+
+def held(shape):
+    return pl.BlockSpec(shape, lambda step: (0,) * len(shape))
+
+
+def slab(shape, axis):
+    return pl.BlockSpec(shape, lambda step: tuple(step if d == axis else 0 for d in range(len(shape))))
+
+
+def like(shape, dtype):
+    return jax.ShapeDtypeStruct(shape, dtype)
+
+
+def run(kernel, grid, in_specs, out_specs, out_shape, scratch, name, flops, moved, args):
+    return pl.pallas_call(
+        kernel,
+        grid=grid,
+        in_specs=in_specs,
+        out_specs=out_specs,
+        out_shape=out_shape,
+        scratch_shapes=scratch,
+        compiler_params=pltpu.CompilerParams(vmem_limit_bytes=VMEM_LIMIT),
+        cost_estimate=pl.CostEstimate(flops=flops, bytes_accessed=moved, transcendentals=0),
+        name=name,
+    )(*args)
+
+
+def row_scale(value):
+    return lax.rsqrt(jnp.mean(value * value, axis=-1, keepdims=True) + epsilon)
+
+
+def mean_square(value, valid):
+    return jnp.sum(valid * jnp.mean(value * value, axis=-1, keepdims=True), axis=0, keepdims=True)
+
+
+def norm_adjoint(value, gain, grad):
+    scale = row_scale(value)
+    unit = value * scale
+    scaled = grad * gain
+    dvalue = scale * (scaled - unit * jnp.mean(scaled * unit, axis=-1, keepdims=True))
+    return dvalue, jnp.sum(grad * unit, axis=0, keepdims=True)
+
+
+def each_piece(me_ref, part_refs):
+    rows = part_refs[0].shape[0]
+    for number, part in enumerate(part_refs):
+        start = (me_ref[0] ^ number) * rows
+        yield pl.ds(pl.multiple_of(start, rows), rows), part
+
+
+def put_stat(stat_ref, column, value):
+    stat_ref[0:1, column : column + 1] += value
+
+
+def mix_rows(mix_ref):
+    mix = mix_ref[0]
+    return jnp.concatenate([mix, jnp.zeros((EXTRA - mix.shape[0], mix.shape[1]), mix.dtype)], axis=0)
+
+
+def project_kernel(kind, pieces, *refs):
+    me_ref, valid_ref, gain_ref = refs[:3]
+    part_refs = refs[3 : 3 + pieces]
+    refs = refs[3 + pieces :]
+    if kind == "next":
+        base_ref, refs = refs[0], refs[1:]
+    w_ref, mix_ref, resid_ref, normed_ref, packed_ref, gate_ref, stat_ref = refs
+
+    @pl.when(pl.program_id(0) == 0)
+    def _():
+        stat_ref[...] = jnp.zeros_like(stat_ref)
+        for where, part in each_piece(me_ref, part_refs):
+            value = part[...].astype(jnp.float32)
+            if kind == "next":
+                valid = valid_ref[where, :]
+                put_stat(stat_ref, 1, mean_square(value, valid))
+                value = value + base_ref[where, :]
+                put_stat(stat_ref, 0, mean_square(value, valid))
+            rounded = value.astype(jnp.bfloat16)
+            resid_ref[where, :] = rounded
+            value = rounded.astype(jnp.float32)
+            normed_ref[where, :] = (value * row_scale(value) * gain_ref[...]).astype(jnp.bfloat16)
+
+    normed = normed_ref[...]
+    result = dot(normed, w_ref[0])
+    packed_ref[0, :, :WIDTH] = result[:, :WIDTH].astype(jnp.bfloat16)
+    gate_ref[0] = result[:, WIDTH:]
+    mix = proj_t(normed, mix_rows(mix_ref))
+    lanes = lax.broadcasted_iota(jnp.int32, mix.shape, 1)
+    low = mix - mix.astype(jnp.bfloat16).astype(jnp.float32)
+    mix = jnp.where(lanes < 2, mix, jnp.where(lanes < 4, low, 0.0))
+    packed_ref[0, :, WIDTH:] = mix.astype(jnp.bfloat16)
+
+
+def project(me, valid, gain, parts, base, w_proj, w_mix):
+    slices, width, columns = w_proj.shape
+    sub = parts[0].shape[0]
+    rows = sub * len(parts)
+    kind = "first" if base is None else "next"
+    return run(
+        functools.partial(project_kernel, kind, len(parts)),
+        (slices,),
+        [in_smem(), held((rows, 1)), held((1, width))]
+        + [held((sub, width))] * len(parts)
+        + ([] if base is None else [held((rows, width))])
+        + [slab((1, width, columns), 0), slab((1, 16, width), 0)],
+        (
+            held((rows, width)),
+            held((rows, width)),
+            slab((1, rows, WIDTH + EXTRA), 0),
+            slab((1, rows, HEAD_V), 0),
+            held((8, 128)),
+        ),
+        (
+            like((rows, width), jnp.bfloat16),
+            like((rows, width), jnp.bfloat16),
+            like((slices, rows, WIDTH + EXTRA), jnp.bfloat16),
+            like((slices, rows, HEAD_V), jnp.float32),
+            like((8, 128), jnp.float32),
+        ),
+        [],
+        "project_" + kind,
+        2 * rows * width * columns * slices,
+        w_proj.size * 2 + rows * width * 12,
+        [me, valid, gain] + list(parts) + ([] if base is None else [base]) + [w_proj, w_mix],
+    )
+
+
+def output_kernel(mixed_ref, gate_ref, norm_ref, w_ref, gated_ref, pieces_ref):
+    slices = mixed_ref.shape[0]
+
+    @pl.when(pl.program_id(0) == 0)
+    def _():
+        for j in range(slices):
+            value = mixed_ref[j].astype(jnp.float32)
+            normed = value * row_scale(value) * norm_ref[...] * silu(gate_ref[j])
+            gated_ref[:, j * HEAD_V : (j + 1) * HEAD_V] = normed.astype(jnp.bfloat16)
+
+    result = dot(gated_ref[...], w_ref[0]).astype(jnp.bfloat16)
+    pieces_ref[...] = result.reshape(pieces_ref.shape)
+
+
+def output(mixed, gate_pre, norm_weight, w_out, shards):
+    slices, rows, _ = mixed.shape
+    _, inner, half = w_out.shape
+    return run(
+        output_kernel,
+        (2,),
+        [held(mixed.shape), held(gate_pre.shape), held((1, HEAD_V)), slab((1, inner, half), 0)],
+        (held((rows, inner)), slab((shards, rows // shards, half), 2)),
+        (like((rows, inner), jnp.bfloat16), like((shards, rows // shards, 2 * half), jnp.bfloat16)),
+        [],
+        "output",
+        4 * rows * inner * half,
+        w_out.size * 2 + rows * inner * 12,
+        [mixed, gate_pre, norm_weight, w_out],
+    )
+
+
+def feed_kernel(pieces, *refs):
+    me_ref, valid_ref, gain_ref = refs[:3]
+    part_refs = refs[3 : 3 + pieces]
+    base_ref, w_gu_ref, w_down_ref, mid_ref, normed_ref, gate_up_ref, hidden_ref, pieces_ref, stat_ref, total = refs[
+        3 + pieces :
+    ]
+    step = pl.program_id(0)
+    half = w_down_ref.shape[2]
+
+    @pl.when(step == 0)
+    def _():
+        stat_ref[...] = jnp.zeros_like(stat_ref)
+        total[...] = jnp.zeros_like(total)
+        for where, part in each_piece(me_ref, part_refs):
+            value = part[...].astype(jnp.float32)
+            put_stat(stat_ref, 0, mean_square(value, valid_ref[where, :]))
+            value = value + base_ref[where, :].astype(jnp.float32)
+            mid_ref[where, :] = value
+            normed_ref[where, :] = (value * row_scale(value) * gain_ref[...]).astype(jnp.bfloat16)
+
+    result = dot(normed_ref[...], w_gu_ref[0])
+    gate_up_ref[0] = result
+    width = result.shape[1] // 2
+    hidden = (silu(result[:, :width]) * result[:, width:]).astype(jnp.bfloat16)
+    hidden_ref[...] = hidden
+    for c in range(2):
+        total[:, c * half : (c + 1) * half] += dot(hidden, w_down_ref[c])
+
+    @pl.when(step == pl.num_programs(0) - 1)
+    def _():
+        pieces_ref[...] = total[...].astype(jnp.bfloat16).reshape(pieces_ref.shape)
+
+
+def feed(me, valid, gain, parts, base, w_gu, w_down, shards):
+    slices, width, columns = w_gu.shape
+    sub = parts[0].shape[0]
+    rows = sub * len(parts)
+    hidden = columns // 2
+    half = width // 2
+    return run(
+        functools.partial(feed_kernel, len(parts)),
+        (slices,),
+        [in_smem(), held((rows, 1)), held((1, width))]
+        + [held((sub, width))] * len(parts)
+        + [held((rows, width)), slab((1, width, columns), 0), slab((2, hidden, half), 1)],
+        (
+            held((rows, width)),
+            held((rows, width)),
+            slab((1, rows, columns), 0),
+            slab((rows, hidden), 1),
+            held((shards, rows // shards, width)),
+            held((8, 128)),
+        ),
+        (
+            like((rows, width), jnp.float32),
+            like((rows, width), jnp.bfloat16),
+            like((slices, rows, columns), jnp.float32),
+            like((rows, slices * hidden), jnp.bfloat16),
+            like((shards, rows // shards, width), jnp.bfloat16),
+            like((8, 128), jnp.float32),
+        ),
+        [pltpu.VMEM((rows, width), jnp.float32)],
+        "feed",
+        2 * rows * width * (columns + hidden) * slices,
+        (w_gu.size + w_down.size) * 2 + rows * width * 16,
+        [me, valid, gain] + list(parts) + [base, w_gu, w_down],
+    )
+
+
+def close_kernel(pieces, *refs):
+    me_ref, valid_ref = refs[:2]
+    part_refs = refs[2 : 2 + pieces]
+    base_ref, out_ref, stat_ref = refs[2 + pieces :]
+    stat_ref[...] = jnp.zeros_like(stat_ref)
+    for where, part in each_piece(me_ref, part_refs):
+        value = part[...].astype(jnp.float32)
+        valid = valid_ref[where, :]
+        put_stat(stat_ref, 1, mean_square(value, valid))
+        value = value + base_ref[where, :]
+        put_stat(stat_ref, 0, mean_square(value, valid))
+        out_ref[where, :] = value.astype(jnp.bfloat16)
+
+
+def close(me, valid, parts, base):
+    return run(
+        functools.partial(close_kernel, len(parts)),
+        (),
+        [in_smem()] + [in_vmem()] * (2 + len(parts)),
+        (in_vmem(), in_vmem()),
+        (like(base.shape, jnp.bfloat16), like((8, 128), jnp.float32)),
+        [],
+        "close",
+        base.size * 6,
+        base.size * 8,
+        [me, valid] + list(parts) + [base],
+    )
+
+
+def sum_kernel(pieces_ref, total_ref):
+    total = pieces_ref[0].astype(jnp.float32)
+    for k in range(1, pieces_ref.shape[0]):
+        total = total + pieces_ref[k].astype(jnp.float32)
+    total_ref[...] = total.astype(total_ref.dtype)
+
+
+def sum_pieces(pieces):
+    return run(
+        sum_kernel,
+        (),
+        [in_vmem()],
+        in_vmem(),
+        like(pieces.shape[1:], pieces.dtype),
+        [],
+        "sum_pieces",
+        pieces.size,
+        pieces.size * 3,
+        [pieces],
+    )
+
+
+def feed_back_kernel(up_ref, gate_up_ref, w_gu_ref, w_down_ref, grad_ref, pieces_ref, total):
+    step = pl.program_id(0)
+    half = w_down_ref.shape[2]
+    width = gate_up_ref.shape[2] // 2
+    upstream = up_ref[...]
+    grad_hidden = proj_t(upstream[:, :half], w_down_ref[0]) + proj_t(upstream[:, half:], w_down_ref[1])
+    gate = gate_up_ref[0, :, :width]
+    up = gate_up_ref[0, :, width:]
+    sig = sigmoid(gate)
+    grad_ref[0, :, :width] = (grad_hidden * up * (sig * (1.0 + gate * (1.0 - sig)))).astype(jnp.bfloat16)
+    grad_ref[0, :, width:] = (grad_hidden * (gate * sig)).astype(jnp.bfloat16)
+    part = proj_t(grad_ref[0], w_gu_ref[0])
+
+    @pl.when(step == 0)
+    def _():
+        total[...] = part
+
+    @pl.when(step > 0)
+    def _():
+        total[...] += part
+
+    @pl.when(step == pl.num_programs(0) - 1)
+    def _():
+        pieces_ref[...] = total[...].astype(jnp.bfloat16).reshape(pieces_ref.shape)
+
+
+def feed_back(upstream, gate_up, w_gu, w_down, shards):
+    slices, width, columns = w_gu.shape
+    rows = upstream.shape[0]
+    hidden = columns // 2
+    half = width // 2
+    return run(
+        feed_back_kernel,
+        (slices,),
+        [
+            held((rows, width)),
+            slab((1, rows, columns), 0),
+            slab((1, width, columns), 0),
+            slab((2, hidden, half), 1),
+        ],
+        (slab((1, rows, columns), 0), held((shards, rows // shards, width))),
+        (
+            like((slices, rows, columns), jnp.bfloat16),
+            like((shards, rows // shards, width), jnp.bfloat16),
+        ),
+        [pltpu.VMEM((rows, width), jnp.float32)],
+        "feed_back",
+        2 * rows * width * (columns + hidden) * slices,
+        (w_gu.size + w_down.size) * 2 + gate_up.size * 6 + rows * width * 4,
+        [upstream, gate_up, w_gu, w_down],
+    )
+
+
+def mid_back_kernel(pieces, *refs):
+    me_ref, gain_ref = refs[:2]
+    part_refs = refs[2 : 2 + pieces]
+    (
+        mid_ref, up_ref, w_ref, mixed_ref, gate_ref, norm_ref,
+        grad_mid_ref, grad_attn_ref, dgain_ref, dmixed_ref, dgate_ref, dnorm_ref,
+    ) = refs[2 + pieces :]
+    half = w_ref.shape[2]
+
+    @pl.when(pl.program_id(0) == 0)
+    def _():
+        dgain_ref[...] = jnp.zeros_like(dgain_ref)
+        dnorm_ref[...] = jnp.zeros_like(dnorm_ref)
+        for where, part in each_piece(me_ref, part_refs):
+            dvalue, dgain = norm_adjoint(mid_ref[where, :], gain_ref[...], part[...].astype(jnp.float32))
+            dvalue = dvalue + up_ref[where, :].astype(jnp.float32)
+            grad_mid_ref[where, :] = dvalue
+            grad_attn_ref[where, :] = dvalue.astype(jnp.bfloat16)
+            dgain_ref[...] += dgain
+
+    grad = grad_attn_ref[...]
+    grad_gated = proj_t(grad[:, :half], w_ref[0]) + proj_t(grad[:, half:], w_ref[1])
+    value = mixed_ref[0].astype(jnp.float32)
+    scale = row_scale(value)
+    unit = value * scale
+    weight = norm_ref[...]
+    gate = gate_ref[0]
+    sig = sigmoid(gate)
+    dgate_ref[0] = (grad_gated * unit * weight * (sig * (1.0 + gate * (1.0 - sig)))).astype(jnp.bfloat16)
+    dscaled = grad_gated * (gate * sig)
+    dnorm_ref[...] += jnp.sum(dscaled * unit, axis=0, keepdims=True)
+    dunit = dscaled * weight
+    dmixed = scale * (dunit - unit * jnp.mean(dunit * unit, axis=-1, keepdims=True))
+    dmixed_ref[0] = dmixed.astype(jnp.bfloat16)
+
+
+def mid_back(me, gain, parts, mid, upstream, w_out, mixed, gate_pre, norm_weight):
+    slices, rows, _ = mixed.shape
+    width = mid.shape[1]
+    half = width // 2
+    sub = parts[0].shape[0]
+    return run(
+        functools.partial(mid_back_kernel, len(parts)),
+        (slices,),
+        [in_smem(), held((1, width))]
+        + [held((sub, width))] * len(parts)
+        + [
+            held((rows, width)),
+            held((rows, width)),
+            slab((2, HEAD_V, half), 1),
+            slab((1, rows, HEAD_V), 0),
+            slab((1, rows, HEAD_V), 0),
+            held((1, HEAD_V)),
+        ],
+        (
+            held((rows, width)),
+            held((rows, width)),
+            held((1, width)),
+            slab((1, rows, HEAD_V), 0),
+            slab((1, rows, HEAD_V), 0),
+            held((1, HEAD_V)),
+        ),
+        (
+            like((rows, width), jnp.float32),
+            like((rows, width), jnp.bfloat16),
+            like((1, width), jnp.float32),
+            like((slices, rows, HEAD_V), jnp.bfloat16),
+            like((slices, rows, HEAD_V), jnp.bfloat16),
+            like((1, HEAD_V), jnp.float32),
+        ),
+        [],
+        "mid_back",
+        2 * rows * width * HEAD_V * slices,
+        w_out.size * 2 + rows * width * 20,
+        [me, gain] + list(parts) + [mid, upstream, w_out, mixed, gate_pre, norm_weight],
+    )
+
+
+def project_back_kernel(packed_ref, dgate_ref, w_ref, mix_ref, normed_ref, grad_ref, pieces_ref, dmix_ref, total):
+    step = pl.program_id(0)
+    grad_ref[0, :, :WIDTH] = packed_ref[0, :, :WIDTH]
+    grad_ref[0, :, WIDTH:] = dgate_ref[0]
+    mix = packed_ref[0, :, WIDTH:]
+    part = proj_t(grad_ref[0], w_ref[0]) + dot(mix, mix_rows(mix_ref))
+    dmix = inner_t(mix, normed_ref[...])
+    dmix_ref[0] = jnp.concatenate([dmix[0:2] + dmix[2:4], dmix[2:8]], axis=0)
+
+    @pl.when(step == 0)
+    def _():
+        total[...] = part
+
+    @pl.when(step > 0)
+    def _():
+        total[...] += part
+
+    @pl.when(step == pl.num_programs(0) - 1)
+    def _():
+        pieces_ref[...] = total[...].astype(jnp.bfloat16).reshape(pieces_ref.shape)
+
+
+def project_back(packed, dgate, w_proj, w_mix, normed, shards):
+    slices, width, columns = w_proj.shape
+    rows = normed.shape[0]
+    return run(
+        project_back_kernel,
+        (slices,),
+        [
+            slab((1, rows, WIDTH + EXTRA), 0),
+            slab((1, rows, HEAD_V), 0),
+            slab((1, width, columns), 0),
+            slab((1, 16, width), 0),
+            held((rows, width)),
+        ],
+        (
+            slab((1, rows, columns), 0),
+            held((shards, rows // shards, width)),
+            slab((1, 8, width), 0),
+        ),
+        (
+            like((slices, rows, columns), jnp.bfloat16),
+            like((shards, rows // shards, width), jnp.bfloat16),
+            like((slices, 8, width), jnp.float32),
+        ),
+        [pltpu.VMEM((rows, width), jnp.float32)],
+        "project_back",
+        2 * rows * width * columns * slices,
+        w_proj.size * 2 + rows * width * 12,
+        [packed, dgate, w_proj, w_mix, normed],
+    )
+
+
+def norm_back_kernel(pieces, *refs):
+    me_ref, gain_ref = refs[:2]
+    part_refs = refs[2 : 2 + pieces]
+    resid_ref, mid_ref, out_ref, dgain_ref = refs[2 + pieces :]
+    dgain_ref[...] = jnp.zeros_like(dgain_ref)
+    for where, part in each_piece(me_ref, part_refs):
+        value = resid_ref[where, :].astype(jnp.float32)
+        dvalue, dgain = norm_adjoint(value, gain_ref[...], part[...].astype(jnp.float32))
+        out_ref[where, :] = (dvalue + mid_ref[where, :]).astype(jnp.bfloat16)
+        dgain_ref[...] += dgain
+
+
+def norm_back(me, gain, parts, resid, grad_mid):
+    return run(
+        functools.partial(norm_back_kernel, len(parts)),
+        (),
+        [in_smem()] + [in_vmem()] * (3 + len(parts)),
+        (in_vmem(), in_vmem()),
+        (like(resid.shape, jnp.bfloat16), like(gain.shape, jnp.float32)),
+        [],
+        "norm_back",
+        resid.size * 10,
+        resid.size * 10,
+        [me, gain] + list(parts) + [resid, grad_mid],
+    )
+
+
+def weight_grad_kernel(left_ref, right_ref, out_ref):
+    right = right_ref[0] if len(right_ref.shape) == 3 else right_ref[...]
+    out_ref[0] = inner_t(left_ref[...], right).astype(jnp.bfloat16)
+
+
+def grad_rows(left, right):
+    rows, width = left.shape
+    slices, _, columns = right.shape
+    return run(
+        weight_grad_kernel,
+        (slices,),
+        [held((rows, width)), slab((1, rows, columns), 0)],
+        slab((1, width, columns), 0),
+        like((slices, width, columns), jnp.bfloat16),
+        [],
+        "grad_rows",
+        2 * rows * width * columns * slices,
+        slices * width * columns * 2 + rows * width * 2 + right.size * 2,
+        [left, right],
+    )
+
+
+def grad_cols_kernel(hidden_ref, up_ref, gated_ref, grad_ref, out_ref):
+    rows = hidden_ref.shape[1]
+    out_ref[0, 0, :rows] = inner_t(hidden_ref[...], up_ref[...]).astype(jnp.bfloat16)
+    out_ref[0, 0, rows:] = inner_t(gated_ref[...], grad_ref[...]).astype(jnp.bfloat16)
+
+
+def grad_cols(hidden, upstream, gated, grad_attn, slices):
+    rows, width = upstream.shape
+    half = width // 2
+    first, second = hidden.shape[1] // slices, gated.shape[1] // slices
+
+    def piece(columns):
+        return pl.BlockSpec((rows, columns), lambda c, j: (0, j))
+
+    def side():
+        return pl.BlockSpec((rows, half), lambda c, j: (0, c))
+
+    result = run(
+        grad_cols_kernel,
+        (2, slices),
+        [piece(first), side(), piece(second), side()],
+        pl.BlockSpec((1, 1, first + second, half), lambda c, j: (c, j, 0, 0)),
+        like((2, slices, first + second, half), jnp.bfloat16),
+        [],
+        "grad_cols",
+        4 * rows * (first + second) * slices * half,
+        2 * slices * (first + second) * half * 2 + rows * width * 4,
+        [hidden, upstream, gated, grad_attn],
+    )
+    return result.reshape(2, slices * (first + second), half)
+
+
+def place_kernel(pieces, *refs):
+    me_ref, out_ref = refs[0], refs[-1]
+    for where, part in each_piece(me_ref, refs[1:-1]):
+        out_ref[where, :] = part[...]
+
+
+def place(me, parts):
+    sub, width = parts[0].shape
+    shape = (sub * len(parts), width)
+    return run(
+        functools.partial(place_kernel, len(parts)),
+        (),
+        [in_smem()] + [in_vmem()] * len(parts),
+        in_vmem(),
+        like(shape, parts[0].dtype),
+        [],
+        "place",
+        0,
+        4 * sub * width * len(parts),
+        [me] + list(parts),
+    )
+
+
+def place_cols_kernel(pieces, *refs):
+    me_ref, out_ref = refs[0], refs[-1]
+    width = refs[1].shape[1]
+    for number, part in enumerate(refs[1:-1]):
+        start = pl.multiple_of((me_ref[0] ^ number) * width, width)
+        out_ref[:, pl.ds(start, width)] = part[...]
+
+
+def place_cols(me, parts):
+    rows, width = parts[0].shape
+    shape = (rows, width * len(parts))
+    return run(
+        functools.partial(place_cols_kernel, len(parts)),
+        (),
+        [in_smem()] + [in_vmem()] * len(parts),
+        in_vmem(),
+        like(shape, parts[0].dtype),
+        [],
+        "place_cols",
+        0,
+        4 * rows * width * len(parts),
+        [me] + list(parts),
+    )
+
+
+def finish_rows_kernel(widths, side_ref, layer0_ref, layer1_ref, received_ref, *out_refs):
+    side = side_ref[0]
+    own = jnp.where(side == 0, layer0_ref[0], layer1_ref[0]).astype(jnp.float32)
+    other = received_ref[0].astype(jnp.float32)
+    rows = own.shape[0]
+    start = 0
+    for width, out_ref in zip(widths, out_refs):
+        out_ref[pl.ds(pl.multiple_of(side * rows, rows), rows), :] = own[:, start : start + width]
+        out_ref[pl.ds(pl.multiple_of((1 - side) * rows, rows), rows), :] = other[:, start : start + width]
+        start += width
+
+
+def finish_rows(side, layer0, layer1, received, widths):
+    shards, rows, columns = layer0.shape
+    return run(
+        functools.partial(finish_rows_kernel, widths),
+        (shards,),
+        [in_smem()] + [slab((1, rows, columns), 0)] * 3,
+        tuple(slab((2 * rows, width), 1) for width in widths),
+        tuple(like((2 * rows, shards * width), jnp.float32) for width in widths),
+        [],
+        "finish_rows",
+        0,
+        layer0.size * 14,
+        [side, layer0, layer1, received],
+    )
+
+
+def finish_cols_kernel(hidden, side_ref, layer0_ref, layer1_ref, received_ref, down_ref, out_ref):
+    side = side_ref[0]
+    own = jnp.where(side == 0, layer0_ref[0], layer1_ref[0]).astype(jnp.float32)
+    other = received_ref[0].astype(jnp.float32)
+    first = own.shape[0] - out_ref.shape[0]
+    columns = own.shape[1]
+    here = pl.ds(pl.multiple_of(side * columns, columns), columns)
+    there = pl.ds(pl.multiple_of((1 - side) * columns, columns), columns)
+    down_ref[:, here] = own[:hidden]
+    down_ref[:, there] = other[:hidden]
+    out_ref[:, here] = own[first:]
+    out_ref[:, there] = other[first:]
+
+
+def finish_cols(side, layer0, layer1, received, hidden):
+    shards, rows, columns = layer0.shape
+    return run(
+        functools.partial(finish_cols_kernel, hidden),
+        (shards,),
+        [in_smem()] + [slab((1, rows, columns), 0)] * 3,
+        (slab((hidden, 2 * columns), 0), slab((HEAD_V, 2 * columns), 0)),
+        (
+            like((shards * hidden, 2 * columns), jnp.float32),
+            like((shards * HEAD_V, 2 * columns), jnp.float32),
+        ),
+        [],
+        "finish_cols",
+        0,
+        layer0.size * 14,
+        [side, layer0, layer1, received],
+    )
+
+
 def halves(value, axis):
     step = 1
     while step < lax.axis_size(axis):
@@ -1001,13 +1674,13 @@
     return jnp.concatenate(in_order(by_partner(value, axis), axis), axis=0)
 
 
-def shard_total(partial):
-    size = lax.axis_size("seq")
-    rows, width = partial.shape
-    pieces = partial.astype(jnp.bfloat16).reshape(size, rows // size, width)
-    pieces = lax.all_to_all(pieces, "seq", 0, 0)
-    total = jnp.sum(pieces.astype(jnp.float32), axis=0).astype(jnp.bfloat16)
-    return gathered(total, "seq").astype(jnp.float32)
+def move_pieces(pieces):
+    return lax.all_to_all(pieces, "seq", 0, 0)
+
+
+def exchange(pieces, beside=()):
+    pieces, beside = lax.optimization_barrier((move_pieces(pieces), beside))
+    return by_partner(sum_pieces(pieces), "seq"), beside
 
 
 def pick(flag, when, otherwise):
@@ -1023,158 +1696,113 @@
     return pick(first, own, received), pick(first, received, own)
 
 
+def move_rows(part):
+    return lax.all_to_all(part, "seq", 0, 0).reshape(-1, part.shape[2])
+
+
+def move_cols(part):
+    part = lax.all_to_all(part, "seq", 0, 0)
+    return jnp.swapaxes(part, 0, 1).reshape(part.shape[1], -1)
+
+
+def sent_pieces(part, me):
+    size = lax.axis_size("seq")
+    own = lax.dynamic_index_in_dim(part, me[0], 0, False)
+    return [own] + [
+        lax.ppermute(
+            lax.dynamic_index_in_dim(part, me[0] ^ k, 0, False),
+            "seq",
+            [(i, i ^ k) for i in range(size)],
+        )
+        for k in range(1, size)
+    ]
+
+
+def move_rows_freely(part, me):
+    return place(me, sent_pieces(part, me))
+
+
+def move_cols_freely(part, me):
+    return place_cols(me, sent_pieces(part, me))
+
+
 def spread_rows(part):
-    part = lax.all_to_all(part, "seq", 0, 0)
-    part = part.reshape(-1, part.shape[2])
     full = lax.all_gather(part, ("head", "section"), axis=0, tiled=True)
     return full.reshape(lax.axis_size("head"), -1, part.shape[1])
 
 
 def spread_cols(part):
-    part = lax.all_to_all(part, "seq", 0, 0)
-    part = jnp.swapaxes(part, 0, 1).reshape(part.shape[1], -1)
     full = lax.all_gather(part, ("section", "head"), axis=0, tiled=True)
     return full.reshape(2, -1, part.shape[1])
 
 
-def collect_rows(grad):
-    part = lax.psum_scatter(
+def reduce_rows(grad):
+    return lax.psum_scatter(
         grad.reshape(-1, grad.shape[2]), ("head", "section"), scatter_dimension=0, tiled=True
     )
+
+
+def reduce_cols(grad):
+    return lax.psum_scatter(
+        grad.reshape(-1, grad.shape[2]), ("section", "head"), scatter_dimension=0, tiled=True
+    )
+
+
+def collect_rows(part):
     shards = lax.axis_size("seq")
-    part = lax.all_to_all(part.reshape(shards, -1, part.shape[1]), "seq", 0, 0)
-    return jnp.swapaxes(part, 0, 1)
-
-
-def collect_cols(grad):
-    part = lax.psum_scatter(
-        grad.reshape(-1, grad.shape[2]), ("section", "head"), scatter_dimension=0, tiled=True
-    )
+    return lax.all_to_all(part.reshape(shards, -1, part.shape[1]), "seq", 0, 0)
+
+
+def collect_cols(part):
     shards = lax.axis_size("seq")
     part = jnp.swapaxes(part.reshape(part.shape[0], shards, -1), 0, 1)
     return lax.all_to_all(part, "seq", 0, 0)
 
 
-def dot(left, right):
-    return jnp.dot(left, right, preferred_element_type=jnp.float32)
-
-
-def over_halves(value, weight):
-    return jnp.concatenate([dot(value, weight[half]) for half in range(2)], axis=1)
-
-
-def from_halves(value, weight):
-    width = weight.shape[2]
-    return sum(proj_t(value[:, half * width : (half + 1) * width], weight[half]) for half in range(2))
-
-
-def grad_halves(value, grad):
-    width = grad.shape[1] // 2
-    return jnp.stack(
-        [inner_t(value, grad[:, half * width : (half + 1) * width]).astype(jnp.bfloat16) for half in range(2)]
-    )
-
-
-def head_norm(mixed, gate_pre, norm_weight):
-    return rms_norm(mixed, norm_weight) * jax.nn.silu(gate_pre)
-
-
-def layer_forward(resid, gains, weights, small, aux, parts):
+def collect_cols_freely(part, me):
+    shards = lax.axis_size("seq")
+    part = jnp.swapaxes(part.reshape(part.shape[0], shards, -1), 0, 1)
+    return place(me, sent_pieces(part, me)).reshape(part.shape)
+
+
+def after(value, other):
+    return lax.optimization_barrier((value, other))[0]
+
+
+def layer_backward_fast(me, upstream, saved, gains, weights, small, aux, parts, plan):
+    before_mid, early_gu, start, then = plan
     attn_gain, mlp_gain = gains
     w_proj, w_mix, w_out, w_gu, w_down = weights
     taps, scal, norm_weight = small
-    rows = resid.shape[0]
-    slices = w_proj.shape[0]
-    normed = rms_norm(resid, attn_gain).astype(jnp.bfloat16)
-    projected = jnp.stack([dot(normed, w_proj[j]) for j in range(slices)])
-    gate_pre = projected[:, :, WIDTH:]
-    mix = proj_t(normed, w_mix).T.reshape(slices, 2, rows)
-    mix = jnp.swapaxes(mix, 1, 2)
-    mix_high = mix.astype(jnp.bfloat16)
-    mix_low = (mix - mix_high.astype(jnp.float32)).astype(jnp.bfloat16)
-    packed = jnp.concatenate(
-        [
-            projected[:, :, :WIDTH].astype(jnp.bfloat16),
-            mix_high,
-            mix_low,
-            jnp.zeros((slices, rows, EXTRA - 4), jnp.bfloat16),
-        ],
-        axis=2,
-    )
-    xh = lax.all_to_all(packed, "head", 0, 0).reshape(slices * rows, WIDTH + EXTRA)
-    mixed_head, states, inverse = recur_forward(xh, aux, taps, scal, parts)
-    mixed = lax.all_to_all(mixed_head.reshape(slices, rows, HEAD_V), "head", 0, 0)
-    gated = head_norm(mixed.astype(jnp.float32), gate_pre, norm_weight).astype(jnp.bfloat16)
-    gated = jnp.swapaxes(gated, 0, 1).reshape(rows, slices * HEAD_V)
-    attn = shard_total(over_halves(gated, w_out))
-    resid_mid = resid + attn
-    ffn_in = rms_norm(resid_mid, mlp_gain).astype(jnp.bfloat16)
-    gate_up = jnp.stack([dot(ffn_in, w_gu[j]) for j in range(slices)])
-    hidden_width = w_gu.shape[2] // 2
-    hidden = (jax.nn.silu(gate_up[:, :, :hidden_width]) * gate_up[:, :, hidden_width:]).astype(
-        jnp.bfloat16
-    )
-    hidden = jnp.swapaxes(hidden, 0, 1).reshape(rows, slices * hidden_width)
-    ffn = shard_total(over_halves(hidden, w_down))
-    out = resid_mid + ffn
-    saved = (resid, normed, gate_pre, xh, states, inverse, mixed, gated, resid_mid, ffn_in, gate_up, hidden)
-    return out, attn, ffn, saved
-
-
-def layer_backward_fast(upstream, saved, gains, weights, small, aux, parts):
-    attn_gain, mlp_gain = gains
-    w_proj, w_mix, w_out, w_gu, w_down = weights
-    taps, scal, norm_weight = small
-    resid, normed, gate_pre, xh, states, inverse, mixed, gated, resid_mid, ffn_in, gate_up, hidden = saved
-    rows = resid.shape[0]
-    slices = w_proj.shape[0]
-    hidden_width = w_gu.shape[2] // 2
-
-    def by_slice(value):
-        return jnp.swapaxes(value.reshape(rows, slices, -1), 0, 1)
-
-    grad_ffn = upstream.astype(jnp.bfloat16)
-    grad_hidden = by_slice(from_halves(grad_ffn, w_down))
-    grad_down = grad_halves(hidden, grad_ffn)
-    _, act_back = jax.vjp(
-        lambda gate_in, up_in: jax.nn.silu(gate_in) * up_in,
-        gate_up[:, :, :hidden_width],
-        gate_up[:, :, hidden_width:],
-    )
-    grad_gate, grad_up = act_back(grad_hidden)
-    grad_gate_up = jnp.concatenate([grad_gate, grad_up], axis=2).astype(jnp.bfloat16)
-    grad_ffn_in = shard_total(sum(proj_t(grad_gate_up[j], w_gu[j]) for j in range(slices)))
-    grad_gu = jnp.stack([inner_t(ffn_in, grad_gate_up[j]).astype(jnp.bfloat16) for j in range(slices)])
-    _, mlp_norm_back = jax.vjp(rms_norm, resid_mid, mlp_gain)
-    grad_mid_norm, grad_mlp_gain = mlp_norm_back(grad_ffn_in)
-    grad_mid = upstream + grad_mid_norm
-    grad_attn = grad_mid.astype(jnp.bfloat16)
-    grad_gated = by_slice(from_halves(grad_attn, w_out))
-    grad_out = grad_halves(gated, grad_attn)
-    _, gate_back = jax.vjp(head_norm, mixed.astype(jnp.float32), gate_pre, norm_weight)
-    grad_mixed, grad_gate_pre, grad_norm_weight = gate_back(grad_gated)
-    grad_head = lax.all_to_all(grad_mixed.astype(jnp.bfloat16), "head", 0, 0)
-    dxh, dtaps, dscal = recur_backward(
-        xh, aux, taps, scal, states, inverse, grad_head.reshape(slices * rows, HEAD_V), parts
-    )
-    grad_packed = lax.all_to_all(dxh.reshape(slices, rows, WIDTH + EXTRA), "head", 0, 0)
-    grad_mix = grad_packed[:, :, WIDTH : WIDTH + 4].reshape(slices, rows, 2, 2)
-    grad_mix = jnp.transpose(grad_mix, (1, 2, 0, 3)).reshape(rows, 4 * slices)
-    grad_pre = jnp.concatenate(
-        [grad_packed[:, :, :WIDTH], grad_gate_pre.astype(jnp.bfloat16)], axis=2
-    )
-    grad_proj = jnp.stack([inner_t(normed, grad_pre[j]).astype(jnp.bfloat16) for j in range(slices)])
-    grad_w_mix = inner_t(grad_mix, normed)
-    grad_w_mix = grad_w_mix[: 2 * slices] + grad_w_mix[2 * slices :]
-    grad_normed = shard_total(
-        sum(proj_t(grad_pre[j], w_proj[j]) for j in range(slices))
-        + dot(grad_mix, jnp.concatenate([w_mix, w_mix], axis=0))
-    )
-    _, attn_norm_back = jax.vjp(rms_norm, resid, attn_gain)
-    grad_resid_norm, grad_attn_gain = attn_norm_back(grad_normed)
-    grad_resid = grad_mid + grad_resid_norm
-    small_grads = (dtaps[:CONVK], dscal[0, :2], grad_norm_weight, grad_attn_gain, grad_mlp_gain, grad_w_mix)
-    return grad_resid, (grad_proj, grad_out, grad_gu, grad_down), small_grads
+    resid, normed, gate_pre, mixer, mid, ffn_in, gate_up, hidden = saved
+    xh, states, inverse, mixed, gated = mixer
+    shards = parts[0]
+    slices, rows, _ = mixed.shape
+    grad_gate_up, pieces = feed_back(upstream, gate_up, w_gu, w_down, shards)
+    grad_gu = grad_rows(ffn_in, grad_gate_up)
+    sums, _ = exchange(pieces, grad_gu)
+    sums, sum_gu = before_mid(sums, grad_gu)
+    grad_mid, grad_attn, dmlp, dmixed, dgate, dnorm = mid_back(
+        me, mlp_gain, sums, mid, upstream, w_out, mixed, gate_pre, norm_weight
+    )
+    grad_both = grad_cols(hidden, upstream, gated, grad_attn, slices)
+    grad_head = lax.all_to_all(dmixed, "head", 0, 0).reshape(slices * rows, HEAD_V)
+    grad_head, grad_both, sum_gu = early_gu(grad_head, grad_both, sum_gu)
+    running = start(grad_head)
+    dxh, dtaps, dscal = recur_backward(xh, aux, taps, scal, states, inverse, grad_head, parts)
+    dxh, running = lax.optimization_barrier((dxh, running))
+    packed = lax.all_to_all(dxh.reshape(slices, rows, WIDTH + EXTRA), "head", 0, 0)
+    packed, sum_gu = lax.optimization_barrier((packed, sum_gu))
+    sum_both = reduce_cols(after(grad_both, sum_gu))
+    running = then(running)
+    grad_pre, pieces, dmix = project_back(packed, dgate, w_proj, w_mix, normed, shards)
+    grad_proj = grad_rows(normed, grad_pre)
+    sums, _ = exchange(pieces, grad_proj)
+    sums, sum_both, running = lax.optimization_barrier((sums, sum_both, running))
+    sum_proj = reduce_rows(after(grad_proj, sum_both))
+    grad_resid, dattn = norm_back(me, attn_gain, sums, resid, grad_mid)
+    small_grads = (dtaps[:CONVK], dscal[0, :2], dnorm[0], dattn[0], dmlp[0], dmix[:, :2])
+    return grad_resid, (sum_proj, sum_gu, sum_both), small_grads, running
 
 
 def fast_shards(
@@ -1282,6 +1910,10 @@
     mix_all = lax.dynamic_index_in_dim(mix_all, shard, 3, False)
     mix_all = jnp.transpose(mix_all, (1, 2, 3, 0, 4)).reshape(2, 2, model_width).astype(jnp.bfloat16)
     mix_all = gathered(mix_all[None], "head")
+    mix_all = jnp.swapaxes(mix_all, 0, 1)
+    mix_all = jnp.concatenate(
+        [mix_all, mix_all, jnp.zeros((2, slices, 12, model_width), jnp.bfloat16)], axis=2
+    )
     small = []
     gains = []
     weights = []
@@ -1289,48 +1921,72 @@
         vector = small_layers[layer]
         taps = jnp.pad(vector[:taps_size].reshape(CONVK, WIDTH), ((0, 8 - CONVK), (0, 0)))
         scal = jnp.pad(vector[taps_size:norm_at][None], ((0, 7), (0, 126)))
-        small.append((taps, scal, vector[norm_at:gain_at]))
-        gains.append((gains_all[layer, 0], gains_all[layer, 1]))
-        weights.append(
-            (
-                spread_rows(proj_parts[layer]),
-                mix_all[:, layer].reshape(2 * slices, model_width),
-                spread_cols(out_parts[layer]),
-                spread_rows(gu_parts[layer]),
-                spread_cols(down_parts[layer]),
-            )
-        )
+        small.append((taps, scal, vector[None, norm_at:gain_at]))
+        gains.append((gains_all[layer, 0][None], gains_all[layer, 1][None]))
 
     def my_tokens(value):
         mine = lax.dynamic_slice_in_dim(value, piece * sub, sub, 0)
-        return halved(gathered(mine, "seq"))
-
+        return by_partner(halved(mine), "seq")
+
+    me = shard[None].astype(jnp.int32)
+    valid = valid[:, None]
     aux = make_aux(doc_starts[core], length)
-    resid = my_tokens(tokens[core]).astype(jnp.float32)
     masked = cotangent[core] * valid_mask[core].astype(jnp.bfloat16)[:, None]
-    upstream = my_tokens(masked).astype(jnp.float32)
-
-    def stats(values):
-        return jnp.stack([jnp.sum(valid * jnp.mean(v * v, axis=-1)) for v in values])
-
-    out0, attn0, ffn0, saved0 = layer_forward(resid, gains[0], weights[0], small[0], aux, parts)
-    stats0 = stats((out0, attn0, ffn0))
-    h1 = out0.astype(jnp.bfloat16)
-    out1, attn1, ffn1, saved1 = layer_forward(
-        h1.astype(jnp.float32), gains[1], weights[1], small[1], aux, parts
-    )
-    stats1 = stats((out1, attn1, ffn1))
-    act1 = out1.astype(jnp.bfloat16)
-
-    grad_h1, big1, small1 = layer_backward_fast(
-        upstream, saved1, gains[1], weights[1], small[1], aux, parts
-    )
-    grad_h1 = grad_h1.astype(jnp.bfloat16)
-    grad_tokens, big0, small0 = layer_backward_fast(
-        grad_h1.astype(jnp.float32), saved0, gains[0], weights[0], small[0], aux, parts
-    )
-    grad_tokens = grad_tokens.astype(jnp.bfloat16)
-
+
+    token_parts, base = my_tokens(tokens[core]), None
+    proj0 = after(move_rows(proj_parts[0]), (token_parts, gains, small, valid))
+    out0 = move_cols(after(out_parts[0], proj0))
+    gu0 = move_rows(after(gu_parts[0], out0))
+    down0 = move_cols_freely(after(down_parts[0], gu0), me)
+    weights = [
+        (spread_rows(proj0), mix_all[0], spread_cols(out0), spread_rows(gu0), None)
+    ]
+
+    saved = []
+    stats = []
+    for layer in range(2):
+        w_proj, w_mix, w_out, w_gu, w_down = weights[layer]
+        attn_gain, mlp_gain = gains[layer]
+        resid, normed, packed, gate_pre, stat = project(
+            me, valid, attn_gain, token_parts, base, w_proj, w_mix
+        )
+        stats.append(stat)
+        xh = lax.all_to_all(packed, "head", 0, 0).reshape(slices * valid.shape[0], WIDTH + EXTRA)
+        if layer == 0:
+            xh, down0 = lax.optimization_barrier((xh, down0))
+            w_down = spread_cols(down0)
+            weights[0] = (w_proj, w_mix, w_out, w_gu, w_down)
+            proj1 = move_rows(after(proj_parts[1], xh))
+            out1 = move_cols_freely(after(out_parts[1], xh), me)
+            down1 = move_cols_freely(after(down_parts[1], xh), me)
+        else:
+            gu1 = move_rows_freely(after(gu_parts[1], xh), me)
+            masked = my_tokens(after(masked, xh))
+        mixed_head, states, inverse = recur_forward(xh, aux, *small[layer][:2], parts)
+        if layer == 0:
+            mixed_head, proj1 = lax.optimization_barrier((mixed_head, proj1))
+        else:
+            mixed_head, gu1, masked = lax.optimization_barrier((mixed_head, gu1, masked))
+            w_gu = spread_rows(gu1)
+            weights[1] = (w_proj, w_mix, w_out, w_gu, w_down)
+        mixed = lax.all_to_all(mixed_head.reshape(gate_pre.shape), "head", 0, 0)
+        gated, pieces = output(mixed, gate_pre, small[layer][2], w_out, shards)
+        mixer = (xh, states, inverse, mixed, gated)
+        mix_parts, _ = exchange(pieces)
+        base, ffn_in, gate_up, hidden, pieces, stat = feed(
+            me, valid, mlp_gain, mix_parts, resid, w_gu, w_down, shards
+        )
+        stats.append(stat)
+        saved.append((resid, normed, gate_pre, mixer, base, ffn_in, gate_up, hidden))
+        if layer == 0:
+            pieces, out1, down1 = lax.optimization_barrier((pieces, out1, down1))
+            weights.append(
+                (spread_rows(proj1), mix_all[1], spread_cols(out1), None, spread_cols(down1))
+            )
+            token_parts, _ = exchange(pieces)
+    h1 = saved[1][0]
+    stats0 = jnp.stack([stats[2][0, 0], stats[1][0, 0], stats[2][0, 1]])
+    upstream = place(me, masked)
     def placed_tokens(layer0, layer1):
         layer0, layer1 = (
             lax.dynamic_slice_in_dim(value, shard * sub, sub, 0) for value in (layer0, layer1)
@@ -1342,7 +1998,62 @@
         pieces = pieces.reshape(2, slices * sub, 2, shards, model_width // (2 * shards))
         return jnp.swapaxes(pieces, 2, 3).reshape(2, slices * sub, model_width)
 
+    def plan_last():
+        def before_mid(sums, grad_gu):
+            return sums, reduce_rows(grad_gu)
+
+        def early_gu(grad_head, grad_both, sum_gu):
+            return lax.optimization_barrier((grad_head, grad_both, sum_gu))
+
+        def start(anchor):
+            return move_pieces(after(pieces, anchor))
+
+        def then(moved):
+            return by_partner(sum_pieces(moved), "seq")
+
+        return before_mid, early_gu, start, then
+
+    grad_h1, big1, small1, last_parts = layer_backward_fast(
+        me, upstream, saved[1], gains[1], weights[1], small[1], aux, parts, plan_last()
+    )
+    sum_proj1, sum_gu1, sum_both1 = big1
+    act1, stat = close(me, valid, last_parts, base)
+    stats1 = jnp.stack([stat[0, 0], stats[3][0, 0], stat[0, 1]])
     activations = placed_tokens(h1, act1)
+    early = {}
+
+    def plan_first():
+        def before_mid(sums, grad_gu):
+            sums, early["proj"], early["activations"] = lax.optimization_barrier(
+                (sums, sum_proj1, activations)
+            )
+            return sums, reduce_rows(after(grad_gu, early["proj"]))
+
+        def early_gu(grad_head, grad_both, sum_gu):
+            grad_head, grad_both = lax.optimization_barrier((grad_head, grad_both))
+            return grad_head, grad_both, sum_gu
+
+        def start(anchor):
+            gu = collect_rows(after(sum_gu1, anchor))
+            both = collect_cols_freely(after(sum_both1, anchor), me)
+            early["both"] = both
+            return gu
+
+        def then(moved):
+            return moved, early["both"]
+
+        return before_mid, early_gu, start, then
+
+    grad_tokens, big0, small0, (moved_gu1, moved_both1) = layer_backward_fast(
+        me, grad_h1, saved[0], gains[0], weights[0], small[0], aux, parts, plan_first()
+    )
+    sum_proj0, sum_gu0, sum_both0 = big0
+    activations = early["activations"]
+    moved_proj1 = collect_rows(after(early["proj"], sum_both0))
+    moved_gu0 = collect_rows(after(sum_gu0, moved_proj1))
+    moved_both0 = collect_cols(after(sum_both0, moved_gu0))
+    moved_proj0 = collect_rows(sum_proj0)
+
     input_grads = placed_tokens(grad_tokens, grad_h1)
 
     def joined(layer0, layer1, axis):
@@ -1352,10 +2063,15 @@
             [pick(first, keep, received), pick(first, received, keep)], axis=axis
         ).astype(jnp.float32)
 
-    grad_down = joined(collect_cols(big0[3]), collect_cols(big1[3]), 2)
-    grad_gu = joined(collect_rows(big0[2]), collect_rows(big1[2]), 0)
-    grad_out = joined(collect_cols(big0[1]), collect_cols(big1[1]), 2)
-    grad_proj = joined(collect_rows(big0[0]), collect_rows(big1[0]), 0)
+    side = core[None].astype(jnp.int32)
+    grad_down, grad_out = finish_cols(
+        side, moved_both0, moved_both1, partner(pick(first, moved_both1, moved_both0)), hidden_width
+    )
+    grad_gu = joined(moved_gu0, moved_gu1, 1)
+    grad_proj = finish_rows(
+        side, moved_proj0, moved_proj1, partner(pick(first, moved_proj1, moved_proj0)),
+        (HEAD_K, HEAD_K, HEAD_V, HEAD_V),
+    )
 
     def pack(grads, sums):
         dtaps, dscal, dnorm, dattn, dmlp, dmix = grads
@@ -1384,21 +2100,19 @@
     def conv_part(start, width):
         return conv_grad[:, :, start : start + width].reshape(1, CONVK, shards * width)
 
-    def proj_part(start, width):
-        return grad_proj[:, :, start : start + width].reshape(1, shard_rows, shards * width)
-
     def gu_part(start):
-        return grad_gu[:, :, start : start + hidden_width].reshape(1, shard_rows, shards * hidden_width)
+        part = jnp.swapaxes(grad_gu[:, :, start : start + hidden_width], 0, 1)
+        return part.reshape(1, shard_rows, shards * hidden_width)
 
     return (
         activations[None],
         input_grads[None],
         branch_rms[None],
         gain_sums[0][None],
-        proj_part(0, HEAD_K),
-        proj_part(HEAD_K, HEAD_K),
-        proj_part(2 * HEAD_K, HEAD_V),
-        proj_part(2 * HEAD_K + HEAD_V, HEAD_V),
+        grad_proj[0][None],
+        grad_proj[1][None],
+        grad_proj[2][None],
+        grad_proj[3][None],
         mix_grad[0][None],
         mix_grad[1][None],
         conv_part(0, HEAD_K),
@@ -1407,11 +2121,11 @@
         per_head[:, taps_size][None],
         per_head[:, taps_size + 1][None],
         norm_sum[None],
-        grad_out.reshape(1, shards * HEAD_V, shard_rows),
+        grad_out[None],
         gain_sums[1][None],
         gu_part(0),
         gu_part(hidden_padded),
-        grad_down[:, :hidden_width].reshape(1, shards * hidden_width, shard_rows),
+        grad_down[None],
     )
 
 

time: 1880 us -> 1500 us (0.80)
  other arithmetic: 233 us -> 44.6 us
  Pallas kernels: 181 us -> 357 us
  matrix products: 161 us -> 0 us
  blocking collectives: 321 us -> 178 us
  local copies, waits for them, and re-layouts: 271 us -> 193 us
  starting transfers between devices: 164 us -> 206 us
    pallas_call x0 -> x37, Pallas kernels: none -> 179 us  [run(): pl.pallas_call(kernel, grid=grid, in_specs=in_specs, out_specs=out_specs,...]
    dot_general x78 -> x0, matrix products: 161 us -> none  [the longest x26 68.4 us: proj_t(): lax.dot_general(left, right, (((1,), (1,)), ((), ())), preferred_element_...]
    all_to_all x12 -> x7, blocking collectives: 321 us -> 178 us  [the longest x3 74.7 us: move_pieces(): return lax.all_to_all(pieces, 'seq', 0, 0)]
    reduce_sum x24 -> x1, other arithmetic: 79.7 us -> 0.61 us  [pack(): jnp.sum(valid)[None]]
    ppermute x0 -> x15, waiting for transfers between devices: none -> 70.2 us  [sent_pieces(): lax.ppermute(lax.dynamic_index_in_dim(part, me[0] ^ k, 0, False), 'seq',...]
    unnamed x476 -> x358, local copies, waits for them, and re-layouts: 50.9 us -> 107 us
    concatenate x34 -> x1, local copies, waits for them, and re-layouts: 55.6 us -> 0.08 us  [fast_shards(): jnp.concatenate([mix_all, mix_all, jnp.zeros((2, slices, 12, model_width)...]
    another operation x14 -> x0, other arithmetic: 43.8 us -> none  [the longest x4 14 us: grad_halves(): jnp.stack([inner_t(value, grad[:, half * width:(half + 1) * width]).astyp...]
  transfers between devices with their start and end apart: 99 -> 109, of which waited for: 51 -> 46; matrix products, arithmetic and copies ran while one was open for 30% -> 10% of each run, Pallas kernels for 10% -> 21%
where the time goes in v2:
time: 1500 us; the launch traced here: 1490 us
  waiting for transfers between devices  496 us (33%)
  Pallas kernels  357 us (24%)
  starting transfers between devices  206 us (14%)
  local copies, waits for them, and re-layouts  193 us (13%)
  blocking collectives  178 us (12%)
  other arithmetic  44.6 us (3%)
  between operations  16.1 us (1%)
    pallas_call x37, Pallas kernels, run(): pl.pallas_call(kernel, grid=grid, in_specs=in_specs, out_specs=out_specs,...  179 us
    ppermute x45, waiting for transfers between devices, by_partner(): lax.ppermute(value, axis, [(i, i ^ k) for i in range(size)])  151 us
    unnamed x358, local copies, waits for them, and re-layouts  107 us
    pallas_call x2, Pallas kernels, recur_backward(): pl.pallas_call(functools.partial(backward_kernel, parts), out_shape=(jax....  91.7 us
    pallas_call x2, Pallas kernels, recur_forward(): pl.pallas_call(functools.partial(forward_kernel, parts), out_shape=(jax.S...  86.4 us
    all_to_all x3, blocking collectives, move_pieces(): return lax.all_to_all(pieces, 'seq', 0, 0)  74.7 us
    ppermute x15, waiting for transfers between devices, sent_pieces(): lax.ppermute(lax.dynamic_index_in_dim(part, me[0] ^ k, 0, False), 'seq',...  70.2 us
    ppermute x45, starting transfers between devices, by_partner(): lax.ppermute(value, axis, [(i, i ^ k) for i in range(size)])  66.8 us
  transfers between devices with their start and end apart: 109, of which 46 were waited for; matrix products, arithmetic and copies ran while one was open for 10% of the time, Pallas kernels for 21%

profile of v2, /device:TPU:1, one launch (start us, length us, event | category | flops | bytes accessed | tf_op | source)
XLA Modules:
  0.0 1491.7 jit_solution(4542109751396690744)
XLA Ops:
  42.4 26.9 %collective-permute-done.4.refs_4_ = bf16[64,2048]{1,0:T(8,128)(2,1)S(1)} collective-permute-done((bf16[64,2048]{1,0:T(8,128)(2,1)S(1)}, bf16[64,2048]{1,0:T(8,128)(2,1)S(1)}, u32[]{:S(2)}, u32[]{:S(2)}) %collective-permute-start.4) | collective-permute-done | bytes 262176 | tf_op jit(solution)/shard_map/ppermute | solution.py:1658
  82.8 16.5 %all_to_all.135 = bf16[4,256,256]{2,1,0:T(8,128)(2,1)S(1)} all-to-all(bf16[4,256,256]{2,1,0:T(8,128)(2,1)S(1)} %get-tuple-element.166), channel_id=1, replica_groups=mesh['section'=2,'seq'=4,'head'=4] {'seq'}, dimensions={0} | all-to-all | bytes 1048576 | tf_op jit(solution)/shard_map/all_to_all | solution.py:1704
  109.8 40.1 %all_to_all.136 = bf16[4,256,768]{2,1,0:T(8,128)(2,1)} all-to-all(bf16[4,256,768]{2,1,0:T(8,128)(2,1)S(1)} %get-tuple-element.167), channel_id=1, replica_groups=mesh['section'=2,'seq'=4,'head'=4] {'seq'}, dimensions={0} | all-to-all | bytes 3145728 | tf_op jit(solution)/shard_map/all_to_all | solution.py:1700
  158.5 8.7 project_first.1
  183.1 11.6 collective-permute-done.15.refs_3_
  205.4 43.5 %recur_forward.2 = (bf16[1024,256]{1,0:T(8,128)(2,1)}, f32[16,128,256]{2,1,0:T(8,128)S(1)}, f32[1024,64]{1,0:T(8,128)S(1)}) custom-call(bf16[1024,640]{1,0:T(8,128)(2,1)} %bitcast.67.xh_ref, f32[1024,8]{1,0:T(8,128)S(1)} %copy.158.aux_ref, f32[8,512]{1,0:T(8,128)S(1)} %copy-done.106, f32[8,128]{1,0:T(8,128)S(1)} %copy-done.118), custom_call_target="tpu_custom_call" | custom-call | flops 40960000000 | bytes 8388608 | tf_op jit(solution)/shard_map/recur_forward/pallas_call | solution.py:923
  254.6 13.5 all-to-all-done.5.mixed_ref.refs_9_
  288.7 24.3 %all-to-all-done.6.pieces_ref = bf16[4,64,2048]{2,1,0:T(8,128)(2,1)S(1)} async-done(((bf16[4,64,2048]{2,1,0:T(8,128)(2,1)}), bf16[4,64,2048]{2,1,0:T(8,128)(2,1)S(1)}, u32[]{:S(2)}, u32[]{:S(2)}) %all-to-all-start.6) | async-done | bytes 1048608 | tf_op jit(solution)/shard_map/all_to_all | solution.py:1678
  313.2 9.0 collective-permute-start.18
  322.2 9.2 collective-permute-done.21.refs_3_
  334.7 19.0 %collective-permute-done.24.refs_3_ = bf16[384,256]{1,0:T(8,128)(2,1)S(1)} collective-permute-done((bf16[384,256]{1,0:T(8,128)(2,1)}, bf16[384,256]{1,0:T(8,128)(2,1)S(1)}, u32[]{:S(2)}, u32[]{:S(2)}) %collective-permute-start.24) | collective-permute-done | bytes 196640 | tf_op jit(solution)/shard_map/ppermute | solution.py:1712
  359.0 15.7 %feed.2 = (f32[256,2048]{1,0:T(8,128)}, bf16[256,2048]{1,0:T(8,128)(2,1)S(1)}, f32[4,256,768]{2,1,0:T(8,128)}, bf16[256,1536]{1,0:T(8,128)(2,1)S(1)}, bf16[4,64,...) custom-call(s32[1]{0:T(128)} %bitcast.2.refs_0_, f32[256,1]{1,0:T(8,128)S(1)} %copy.160.refs_1_, ...), custom_call_target="tpu_custom_call" | custom-call | flops 4831838208 | bytes 27262976 | tf_op jit(solution)/shard_map/feed/pallas_call | solution.py:1009
  377.3 27.4 %all_to_all.137.pieces_ref = bf16[4,64,2048]{2,1,0:T(8,128)(2,1)S(1)} all-to-all(bf16[4,64,2048]{2,1,0:T(8,128)(2,1)S(1)} %get-tuple-element.180), channel_id=1, replica_groups=mesh['section'=2,'seq'=4,'head'=4] {'seq'}, dimensions={0} | all-to-all | bytes 2097152 | tf_op jit(solution)/shard_map/all_to_all | solution.py:1678
  412.7 14.0 collective-permute-done.27.refs_5_
  427.4 9.3 project_next.1
  443.9 18.8 %all-to-all-done.8 = bf16[4,256,640]{2,1,0:T(8,128)(2,1)} async-done(((bf16[4,256,640]{2,1,0:T(8,128)(2,1)}), bf16[4,256,640]{2,1,0:T(8,128)(2,1)}, u32[]{:S(2)}, u32[]{:S(2)}) %all-to-all-start.8) | async-done | bytes 1310752 | tf_op jit(solution)/shard_map/all_to_all | solution.py:1954
  475.9 16.6 %collective-permute-start.29 = (bf16[256,768]{1,0:T(8,128)(2,1)}, bf16[256,768]{1,0:T(8,128)(2,1)S(1)}, u32[]{:S(2)}, u32[]{:S(2)}) collective-permute-start(bf16[256,768]{1,0:T(8,128)(2,1)} %get-tuple-element.419), channel_id=1, source_target_pairs={{0,4},{4,0},{8,12},{12,8},{1,5},{5,1},{9,13},{13,9},{2,6},{6,2},{1... | collective-permute-start | bytes 1179656 | tf_op jit(solution)/shard_map/ppermute | solution.py:1712
  494.9 42.8 %recur_forward.3 = (bf16[1024,256]{1,0:T(8,128)(2,1)S(1)}, f32[16,128,256]{2,1,0:T(8,128)S(1)}, f32[1024,64]{1,0:T(8,128)S(1)}) custom-call(bf16[1024,640]{1,0:T(8,128)(2,1)} %bitcast.106.xh_ref, f32[1024,8]{1,0:T(8,128)S(1)} %copy-done.59, f32[8,512]{1,0:T(8,128)S(1)} %copy-done.108, f32[8,128]{1,0:T(8,128)S(1)} %copy-done.120), custom_call_target="tpu_custom_call" | custom-call | flops 40960000000 | bytes 8388608 | tf_op jit(solution)/shard_map/recur_forward/pallas_call | solution.py:923
  554.5 17.4 %all_to_all.138.pieces_ref = bf16[4,64,2048]{2,1,0:T(8,128)(2,1)S(1)} all-to-all(bf16[4,64,2048]{2,1,0:T(8,128)(2,1)S(1)} %get-tuple-element.196), channel_id=1, replica_groups=mesh['section'=2,'seq'=4,'head'=4] {'seq'}, dimensions={0} | all-to-all | bytes 2097152 | tf_op jit(solution)/shard_map/all_to_all | solution.py:1678
  582.0 14.6 collective-permute-done.36.refs_5_
  596.7 27.4 %all-gather.21.cloned.1.call-done = bf16[8192,768]{1,0:T(8,128)(2,1)} async-done(((bf16[1024,768]{1,0:T(8,128)(2,1)}), bf16[8192,768]{1,0:T(8,128)(2,1)}) %all-gather.21.cloned.1.call-update) | async-done | bytes 12582928 | tf_op jit(solution)/shard_map/all_gather | solution.py:1730
  624.7 14.7 feed.3
  640.3 11.1 feed_back.2
  659.0 29.9 %all_to_all.139.pieces_ref = bf16[4,64,2048]{2,1,0:T(8,128)(2,1)S(1)} all-to-all(bf16[4,64,2048]{2,1,0:T(8,128)(2,1)} %copy-done.45), channel_id=1, replica_groups=mesh['section'=2,'seq'=4,'head'=4] {'seq'}, dimensions={0} | all-to-all | bytes 2097152 | tf_op jit(solution)/shard_map/all_to_all | solution.py:1678
  697.5 13.9 collective-permute-done.39.refs_4_
  711.3 7.8 mid_back.2
  737.4 16.5 %reduce-scatter.11.cloned.1.call-done = bf16[1024,768]{1,0:T(8,128)(2,1)} async-done(((bf16[8192,768]{1,0:T(8,128)(2,1)}), bf16[1024,768]{1,0:T(8,128)(2,1)}) %reduce-scatter.11.cloned.1.call-update) | async-done | bytes 1572880 | tf_op jit(solution)/shard_map/reduce_scatter | solution.py:1740
  758.9 45.9 %recur_backward.2 = (bf16[1024,640]{1,0:T(8,128)(2,1)S(1)}, f32[8,512]{1,0:T(8,128)S(1)}, f32[8,128]{1,0:T(8,128)S(1)}) custom-call(bf16[1024,640]{1,0:T(8,128)(2,1)} %bitcast.106.xh_ref, f32[1024,8]{1,0:T(8,128)S(1)} %copy-done.60, f32[8,512]{1,0:T(8,128)S(1)} %copy-done.109, f32[8,128]{1,0:T(8,128)S(1)} %copy-done.121, f32[16,128,256]{2,1,0:T(8,128)} %copy-done.132, ...), custom_call_target="tpu_custom_call" | custom-call | flops 40960000000 | bytes 8388608 | tf_op jit(solution)/shard_map/recur_backward/pallas_call | solution.py:946
  808.0 19.8 %all_to_all.140.packed_ref = bf16[4,256,640]{2,1,0:T(8,128)(2,1)S(1)} all-to-all(bf16[4,256,640]{2,1,0:T(8,128)(2,1)} %bitcast.325), channel_id=1, replica_groups=mesh['section'=2,'seq'=4,'head'=4] {'head'}, dimensions={0} | all-to-all | bytes 2621440 | tf_op jit(solution)/shard_map/all_to_all | solution.py:1794
  830.0 9.3 project_back.2
  859.9 22.4 %all-to-all-done.15.pieces_ref = bf16[4,64,2048]{2,1,0:T(8,128)(2,1)S(1)} async-done(((bf16[4,64,2048]{2,1,0:T(8,128)(2,1)}), bf16[4,64,2048]{2,1,0:T(8,128)(2,1)S(1)}, u32[]{:S(2)}, u32[]{:S(2)}) %all-to-all-start.15) | async-done | bytes 1048608 | tf_op jit(solution)/shard_map/all_to_all | solution.py:1678
  883.3 11.2 collective-permute-start.41
  894.5 15.5 %reduce-scatter.19.cloned.1.call-done = bf16[640,1024]{1,0:T(8,128)(2,1)} async-done(((bf16[5120,1024]{1,0:T(8,128)(2,1)}), bf16[640,1024]{1,0:T(8,128)(2,1)}) %reduce-scatter.19.cloned.1.call-update) | async-done | bytes 1310736
  927.0 14.3 feed_back.3
  959.0 14.6 collective-permute-done.53
  974.3 22.3 %collective-permute-done.51 = bf16[2,64,2048]{2,1,0:T(8,128)(2,1)S(1)} collective-permute-done((bf16[2,64,2048]{2,1,0:T(8,128)(2,1)S(1)}, bf16[2,64,2048]{2,1,0:T(8,128)(2,1)S(1)}, u32[]{:S(2)}, u32[]{:S(2)}) %collective-permute-start.51) | collective-permute-done | bytes 524320 | tf_op jit(solution)/shard_map/ppermute | solution.py:1658
  1014.5 9.0 collective-permute-done.48.refs_4_
  1036.2 8.0 mid_back.3
  1066.7 45.8 %recur_backward.3 = (bf16[1024,640]{1,0:T(8,128)(2,1)S(1)}, f32[8,512]{1,0:T(8,128)S(1)}, f32[8,128]{1,0:T(8,128)S(1)}) custom-call(bf16[1024,640]{1,0:T(8,128)(2,1)} %bitcast.67.xh_ref, f32[1024,8]{1,0:T(8,128)S(1)} %copy-done.61, f32[8,512]{1,0:T(8,128)S(1)} %copy-done.107, f32[8,128]{1,0:T(8,128)S(1)} %copy-done.119, f32[16,128,256]{2,1,0:T(8,128)} %copy-done.131, ...), custom_call_target="tpu_custom_call" | custom-call | flops 40960000000 | bytes 8388608 | tf_op jit(solution)/shard_map/recur_backward/pallas_call | solution.py:946
  1112.6 27.1 %all_to_all.141.packed_ref = bf16[4,256,640]{2,1,0:T(8,128)(2,1)S(1)} all-to-all(bf16[4,256,640]{2,1,0:T(8,128)(2,1)S(1)} %bitcast.324), channel_id=1, replica_groups=mesh['section'=2,'seq'=4,'head'=4] {'head'}, dimensions={0} | all-to-all | bytes 2621440 | tf_op jit(solution)/shard_map/all_to_all | solution.py:1794
  1141.4 8.6 project_back.3
  1186.1 27.4 %collective-permute-done.58.refs_3_ = bf16[640,256]{1,0:T(8,128)(2,1)S(1)} collective-permute-done((bf16[640,256]{1,0:T(8,128)(2,1)}, bf16[640,256]{1,0:T(8,128)(2,1)S(1)}, u32[]{:S(2)}, u32[]{:S(2)}) %collective-permute-start.58) | collective-permute-done | bytes 327712 | tf_op jit(solution)/shard_map/ppermute | solution.py:1712
  1215.7 9.6 reduce-scatter.21.cloned.1.call-done
  1271.8 36.1 %all-to-all-done.22.layer1_ref = bf16[4,256,768]{2,1,0:T(8,128)(2,1)S(1)} async-done(((bf16[4,256,768]{2,1,0:T(8,128)(2,1)}), bf16[4,256,768]{2,1,0:T(8,128)(2,1)S(1)}, u32[]{:S(2)}, u32[]{:S(2)}) %all-to-all-start.22) | async-done | bytes 1572896 | tf_op jit(solution)/shard_map/all_to_all | solution.py:1753
  1327.4 29.2 %all-to-all-done.25 = bf16[4,256,768]{2,1,0:T(8,128)(2,1)S(1)} async-done(((bf16[4,256,768]{2,1,0:T(8,128)(2,1)}), bf16[4,256,768]{2,1,0:T(8,128)(2,1)S(1)}, u32[]{:S(2)}, u32[]{:S(2)}) %all-to-all-start.25) | async-done | bytes 1572896 | tf_op jit(solution)/shard_map/all_to_all | solution.py:1753
  1376.3 9.1 collective-permute-done.71
  1390.1 7.6 collective-permute-done.72
  1420.9 11.7 collective-permute-done.61
  (764 shorter events, 551.0 us)
Async XLA Ops:
  35.4 40.0 %all-to-all-start = ((bf16[4,256,768]{2,1,0:T(8,128)(2,1)}), bf16[4,256,768]{2,1,0:T(8,128)(2,1)S(1)}, u32[]{:S(2)}, u32[]{:S(2)}) async-start(bf16[4,256,768]{2,1,0:T(8,128)(2,1)} %get-tuple-element.402), calls=%async_computation | async-start | bytes 3145728 | tf_op jit(solution)/shard_map/all_to_all | solution.py:1700
  39.0 118.4 %all-gather.9.cloned.1.call-start = ((), (), s32[]{:S(2)}) async-start(), calls=%async_computation.33 | async-start | bytes 14155776 | tf_op jit(solution)/shard_map/all_gather | solution.py:1730
  76.6 178.0 %all-gather.11.cloned.1.call-start = ((), (), s32[]{:S(2)}) async-start(), calls=%async_computation.34 | async-start | bytes 4718592 | tf_op jit(solution)/shard_map/all_gather | solution.py:1735
  100.2 255.5 %all-gather.13.cloned.1.call-start = ((), (), s32[]{:S(2)}) async-start(), calls=%async_computation.35 | async-start | bytes 14155776 | tf_op jit(solution)/shard_map/all_gather | solution.py:1730
  173.6 183.5 %all-gather.15.cloned.1.call-start = ((), (), s32[]{:S(2)}) async-start(), calls=%async_computation.36 | async-start | bytes 7077888 | tf_op jit(solution)/shard_map/all_gather | solution.py:1735
  200.4 50.6 %all-to-all-start.4 = ((bf16[4,256,768]{2,1,0:T(8,128)(2,1)}), bf16[4,256,768]{2,1,0:T(8,128)(2,1)}, u32[]{:S(2)}, u32[]{:S(2)}) async-start(bf16[4,256,768]{2,1,0:T(8,128)(2,1)} %get-tuple-element.171), calls=%async_computation.4 | async-start | bytes 3145728 | tf_op jit(solution)/shard_map/all_to_all | solution.py:1700
  204.8 221.9 %all-gather.17.cloned.1.call-start = ((), (), s32[]{:S(2)}) async-start(), calls=%async_computation.37 | async-start | bytes 14155776 | tf_op jit(solution)/shard_map/all_gather | solution.py:1730
  273.6 39.4 %all-to-all-start.6 = ((bf16[4,64,2048]{2,1,0:T(8,128)(2,1)}), bf16[4,64,2048]{2,1,0:T(8,128)(2,1)S(1)}, u32[]{:S(2)}, u32[]{:S(2)}) async-start(bf16[4,64,2048]{2,1,0:T(8,128)(2,1)} %copy-done.43), calls=%async_computation.6 | async-start | bytes 2097152 | tf_op jit(solution)/shard_map/all_to_all | solution.py:1678
  277.9 267.6 %all-gather.19.cloned.1.call-start = ((), (), s32[]{:S(2)}) async-start(), calls=%async_computation.38 | async-start | bytes 4718592 | tf_op jit(solution)/shard_map/all_gather | solution.py:1735
  280.0 51.4 %collective-permute-start.25 = (bf16[384,256]{1,0:T(8,128)(2,1)}, bf16[384,256]{1,0:T(8,128)(2,1)}, u32[]{:S(2)}, u32[]{:S(2)}) collective-permute-start(bf16[384,256]{1,0:T(8,128)(2,1)} %get-tuple-element.443), channel_id=1, source_target_pairs={{0,12},{4,8},{8,4},{12,0},{1,13},{5,9},{9,5},{13,1},{2,14},{6,10},... | collective-permute-start | bytes 589832 | tf_op jit(solution)/shard_map/ppermute | solution.py:1712
  285.1 46.2 %collective-permute-start.21 = (bf16[256,256]{1,0:T(8,128)(2,1)}, bf16[256,256]{1,0:T(8,128)(2,1)}, u32[]{:S(2)}, u32[]{:S(2)}) collective-permute-start(bf16[256,256]{1,0:T(8,128)(2,1)} %get-tuple-element.454), channel_id=1, source_target_pairs={{0,8},{4,12},{8,0},{12,4},{1,9},{5,13},{9,1},{13,5},{2,10},{6,14},... | collective-permute-start | bytes 393224 | tf_op jit(solution)/shard_map/ppermute | solution.py:1712
  285.7 45.7 %collective-permute-start.20 = (bf16[256,256]{1,0:T(8,128)(2,1)}, bf16[256,256]{1,0:T(8,128)(2,1)}, u32[]{:S(2)}, u32[]{:S(2)}) collective-permute-start(bf16[256,256]{1,0:T(8,128)(2,1)} %get-tuple-element.455), channel_id=1, source_target_pairs={{0,4},{4,0},{8,12},{12,8},{1,5},{5,1},{9,13},{13,9},{2,6},{6,2},{1... | collective-permute-start | bytes 393224 | tf_op jit(solution)/shard_map/ppermute | solution.py:1712
  313.1 42.6 %collective-permute-start.19 = (bf16[64,2048]{1,0:T(8,128)(2,1)S(1)}, bf16[64,2048]{1,0:T(8,128)(2,1)S(1)}, u32[]{:S(2)}, u32[]{:S(2)}) collective-permute-start(bf16[64,2048]{1,0:T(8,128)(2,1)S(1)} %sum_pieces.8.refs_3_), channel_id=1, source_target_pairs={{0,12},{4,8},{8,4},{12,0},{1,13},{5,9},{9,5},{13,1},{2,14},{6,10},... | collective-permute-start | bytes 786440 | tf_op jit(solution)/shard_map/ppermute | solution.py:1658
  313.2 42.5 %collective-permute-start.18 = (bf16[64,2048]{1,0:T(8,128)(2,1)S(1)}, bf16[64,2048]{1,0:T(8,128)(2,1)S(1)}, u32[]{:S(2)}, u32[]{:S(2)}) collective-permute-start(bf16[64,2048]{1,0:T(8,128)(2,1)S(1)} %sum_pieces.8.refs_3_), channel_id=1, source_target_pairs={{0,8},{4,12},{8,0},{12,4},{1,9},{5,13},{9,1},{13,5},{2,10},{6,14},... | collective-permute-start | bytes 786440 | tf_op jit(solution)/shard_map/ppermute | solution.py:1658
  376.6 200.3 %all-gather.23.cloned.1.call-start = ((), (), s32[]{:S(2)}) async-start(), calls=%async_computation.40 | async-start | bytes 7077888 | tf_op jit(solution)/shard_map/all_gather | solution.py:1735
  443.8 180.2 %all-gather.21.cloned.1.call-start = ((), (), s32[]{:S(2)}) async-start(), calls=%async_computation.39 | async-start | bytes 14155776 | tf_op jit(solution)/shard_map/all_gather | solution.py:1730
  472.3 69.7 %collective-permute-start.34 = (bf16[64,2048]{1,0:T(8,128)(2,1)S(1)}, bf16[64,2048]{1,0:T(8,128)(2,1)}, u32[]{:S(2)}, u32[]{:S(2)}) collective-permute-start(bf16[64,2048]{1,0:T(8,128)(2,1)S(1)} %reshape.423.refs_1_), channel_id=1, source_target_pairs={{0,12},{4,8},{8,4},{12,0},{1,13},{5,9},{9,5},{13,1},{2,14},{6,10},... | collective-permute-start | bytes 786440 | tf_op jit(solution)/shard_map/ppermute | solution.py:1658
  472.6 69.4 %collective-permute-start.33 = (bf16[64,2048]{1,0:T(8,128)(2,1)S(1)}, bf16[64,2048]{1,0:T(8,128)(2,1)}, u32[]{:S(2)}, u32[]{:S(2)}) collective-permute-start(bf16[64,2048]{1,0:T(8,128)(2,1)S(1)} %reshape.423.refs_1_), channel_id=1, source_target_pairs={{0,8},{4,12},{8,0},{12,4},{1,9},{5,13},{9,1},{13,5},{2,10},{6,14},... | collective-permute-start | bytes 786440 | tf_op jit(solution)/shard_map/ppermute | solution.py:1658
  472.6 69.4 %collective-permute-start.32 = (bf16[64,2048]{1,0:T(8,128)(2,1)S(1)}, bf16[64,2048]{1,0:T(8,128)(2,1)}, u32[]{:S(2)}, u32[]{:S(2)}) collective-permute-start(bf16[64,2048]{1,0:T(8,128)(2,1)S(1)} %reshape.423.refs_1_), channel_id=1, source_target_pairs={{0,4},{4,0},{8,12},{12,8},{1,5},{5,1},{9,13},{13,9},{2,6},{6,2},{1... | collective-permute-start | bytes 786440 | tf_op jit(solution)/shard_map/ppermute | solution.py:1658
  475.9 64.8 %collective-permute-start.30 = (bf16[256,768]{1,0:T(8,128)(2,1)}, bf16[256,768]{1,0:T(8,128)(2,1)S(1)}, u32[]{:S(2)}, u32[]{:S(2)}) collective-permute-start(bf16[256,768]{1,0:T(8,128)(2,1)} %get-tuple-element.418), channel_id=1, source_target_pairs={{0,8},{4,12},{8,0},{12,4},{1,9},{5,13},{9,1},{13,5},{2,10},{6,14},... | collective-permute-start | bytes 1179656 | tf_op jit(solution)/shard_map/ppermute | solution.py:1712
  475.9 64.8 %collective-permute-start.29 = (bf16[256,768]{1,0:T(8,128)(2,1)}, bf16[256,768]{1,0:T(8,128)(2,1)S(1)}, u32[]{:S(2)}, u32[]{:S(2)}) collective-permute-start(bf16[256,768]{1,0:T(8,128)(2,1)} %get-tuple-element.419), channel_id=1, source_target_pairs={{0,4},{4,0},{8,12},{12,8},{1,5},{5,1},{9,13},{13,9},{2,6},{6,2},{1... | collective-permute-start | bytes 1179656 | tf_op jit(solution)/shard_map/ppermute | solution.py:1712
  545.5 208.3 %reduce-scatter.11.cloned.1.call-start = ((), (), s32[]{:S(2)}) async-start(), calls=%async_computation.41 | async-start | bytes 14155776 | tf_op jit(solution)/shard_map/reduce_scatter | solution.py:1740
  753.8 53.2 %all-to-all-start.13 = ((bf16[4,64,2048]{2,1,0:T(8,128)(2,1)}), bf16[4,64,2048]{2,1,0:T(8,128)(2,1)S(1)}, u32[]{:S(2)}, u32[]{:S(2)}) async-start(bf16[4,64,2048]{2,1,0:T(8,128)(2,1)} %get-tuple-element.213), calls=%async_computation.14 | async-start | bytes 2097152 | tf_op jit(solution)/shard_map/all_to_all | solution.py:1678
  757.4 152.7 %reduce-scatter.19.cloned.1.call-start = ((), (), s32[]{:S(2)}) async-start(), calls=%async_computation.45 | async-start | bytes 11796480
  842.2 40.1 %all-to-all-start.15 = ((bf16[4,64,2048]{2,1,0:T(8,128)(2,1)}), bf16[4,64,2048]{2,1,0:T(8,128)(2,1)S(1)}, u32[]{:S(2)}, u32[]{:S(2)}) async-start(bf16[4,64,2048]{2,1,0:T(8,128)(2,1)} %copy-done.44), calls=%async_computation.16 | async-start | bytes 2097152 | tf_op jit(solution)/shard_map/all_to_all | solution.py:1678
  845.9 186.1 %reduce-scatter.13.cloned.1.call-start = ((), (), s32[]{:S(2)}) async-start(), calls=%async_computation.42 | async-start | bytes 14155776 | tf_op jit(solution)/shard_map/reduce_scatter | solution.py:1740
  850.1 62.4 %collective-permute-start.45 = (bf16[64,2048]{1,0:T(8,128)(2,1)}, bf16[64,2048]{1,0:T(8,128)(2,1)S(1)}, u32[]{:S(2)}, u32[]{:S(2)}) collective-permute-start(bf16[64,2048]{1,0:T(8,128)(2,1)} %sum_pieces.13.refs_2_), channel_id=1, source_target_pairs={{0,8},{4,12},{8,0},{12,4},{1,9},{5,13},{9,1},{13,5},{2,10},{6,14},... | collective-permute-start | bytes 786440 | tf_op jit(solution)/shard_map/ppermute | solution.py:1658
  850.1 63.1 %collective-permute-start.44 = (bf16[64,2048]{1,0:T(8,128)(2,1)}, bf16[64,2048]{1,0:T(8,128)(2,1)}, u32[]{:S(2)}, u32[]{:S(2)}) collective-permute-start(bf16[64,2048]{1,0:T(8,128)(2,1)} %sum_pieces.13.refs_2_), channel_id=1, source_target_pairs={{0,4},{4,0},{8,12},{12,8},{1,5},{5,1},{9,13},{13,9},{2,6},{6,2},{1... | collective-permute-start | bytes 786440 | tf_op jit(solution)/shard_map/ppermute | solution.py:1658
  943.4 54.7 %all-to-all-start.16 = ((bf16[4,64,2048]{2,1,0:T(8,128)(2,1)}), bf16[4,64,2048]{2,1,0:T(8,128)(2,1)S(1)}, u32[]{:S(2)}, u32[]{:S(2)}) async-start(bf16[4,64,2048]{2,1,0:T(8,128)(2,1)} %copy-done.41), calls=%async_computation.17 | async-start | bytes 2097152 | tf_op jit(solution)/shard_map/all_to_all | solution.py:1678
  947.0 193.2 %reduce-scatter.15.cloned.1.call-start = ((), (), s32[]{:S(2)}) async-start(), calls=%async_computation.43 | async-start | bytes 14155776 | tf_op jit(solution)/shard_map/reduce_scatter | solution.py:1740
  950.4 46.2 %collective-permute-start.51 = (bf16[2,64,2048]{2,1,0:T(8,128)(2,1)S(1)}, bf16[2,64,2048]{2,1,0:T(8,128)(2,1)S(1)}, u32[]{:S(2)}, u32[]{:S(2)}) collective-permute-start(bf16[2,64,2048]{2,1,0:T(8,128)(2,1)S(1)} %pad_maximum_fusion.2), channel_id=1, source_target_pairs={{0,3},{1,2},{2,1},{3,0},{4,7},{5,6},{6,5},{7,4},{8,11},{9,10},{10,... | collective-permute-start | bytes 1572872 | tf_op jit(solution)/shard_map/ppermute | solution.py:1658
  1060.8 51.8 %all-to-all-start.18 = ((bf16[4,256,768]{2,1,0:T(8,128)(2,1)}), bf16[4,256,768]{2,1,0:T(8,128)(2,1)}, u32[]{:S(2)}, u32[]{:S(2)}) async-start(bf16[4,256,768]{2,1,0:T(8,128)(2,1)} %bitcast.379), calls=%async_computation.20 | async-start | bytes 3145728 | tf_op jit(solution)/shard_map/all_to_all | solution.py:1753
  1065.4 159.9 %reduce-scatter.21.cloned.1.call-start = ((), (), s32[]{:S(2)}) async-start(), calls=%async_computation.46 | async-start | bytes 11796480
  1156.0 200.6 %reduce-scatter.17.cloned.1.call-start = ((), (), s32[]{:S(2)}) async-start(), calls=%async_computation.44 | async-start | bytes 14155776 | tf_op jit(solution)/shard_map/reduce_scatter | solution.py:1740
  1165.1 48.4 %collective-permute-start.58 = (bf16[640,256]{1,0:T(8,128)(2,1)}, bf16[640,256]{1,0:T(8,128)(2,1)S(1)}, u32[]{:S(2)}, u32[]{:S(2)}) collective-permute-start(bf16[640,256]{1,0:T(8,128)(2,1)} %bitcast.391), channel_id=1, source_target_pairs={{0,8},{4,12},{8,0},{12,4},{1,9},{5,13},{9,1},{13,5},{2,10},{6,14},... | collective-permute-start | bytes 983048 | tf_op jit(solution)/shard_map/ppermute | solution.py:1712
  1167.2 46.3 %collective-permute-start.59 = (bf16[640,256]{1,0:T(8,128)(2,1)}, bf16[640,256]{1,0:T(8,128)(2,1)}, u32[]{:S(2)}, u32[]{:S(2)}) collective-permute-start(bf16[640,256]{1,0:T(8,128)(2,1)} %bitcast.390), channel_id=1, source_target_pairs={{0,12},{4,8},{8,4},{12,0},{1,13},{5,9},{9,5},{13,1},{2,14},{6,10},... | collective-permute-start | bytes 983048 | tf_op jit(solution)/shard_map/ppermute | solution.py:1712
  1181.4 46.3 %collective-permute-start.56 = (bf16[64,2048]{1,0:T(8,128)(2,1)S(1)}, bf16[64,2048]{1,0:T(8,128)(2,1)S(1)}, u32[]{:S(2)}, u32[]{:S(2)}) collective-permute-start(bf16[64,2048]{1,0:T(8,128)(2,1)S(1)} %sum_pieces.15.refs_2_), channel_id=1, source_target_pairs={{0,12},{4,8},{8,4},{12,0},{1,13},{5,9},{9,5},{13,1},{2,14},{6,10},... | collective-permute-start | bytes 786440 | tf_op jit(solution)/shard_map/ppermute | solution.py:1658
  1181.5 50.3 %collective-permute-start.55 = (bf16[64,2048]{1,0:T(8,128)(2,1)S(1)}, bf16[64,2048]{1,0:T(8,128)(2,1)S(1)}, u32[]{:S(2)}, u32[]{:S(2)}) collective-permute-start(bf16[64,2048]{1,0:T(8,128)(2,1)S(1)} %sum_pieces.15.refs_2_), channel_id=1, source_target_pairs={{0,8},{4,12},{8,0},{12,4},{1,9},{5,13},{9,1},{13,5},{2,10},{6,14},... | collective-permute-start | bytes 786440 | tf_op jit(solution)/shard_map/ppermute | solution.py:1658
  1181.5 51.0 %collective-permute-start.54 = (bf16[64,2048]{1,0:T(8,128)(2,1)S(1)}, bf16[64,2048]{1,0:T(8,128)(2,1)S(1)}, u32[]{:S(2)}, u32[]{:S(2)}) collective-permute-start(bf16[64,2048]{1,0:T(8,128)(2,1)S(1)} %sum_pieces.15.refs_2_), channel_id=1, source_target_pairs={{0,4},{4,0},{8,12},{12,8},{1,5},{5,1},{9,13},{13,9},{2,6},{6,2},{1... | collective-permute-start | bytes 786440 | tf_op jit(solution)/shard_map/ppermute | solution.py:1658
  1267.5 40.4 %all-to-all-start.22 = ((bf16[4,256,768]{2,1,0:T(8,128)(2,1)}), bf16[4,256,768]{2,1,0:T(8,128)(2,1)S(1)}, u32[]{:S(2)}, u32[]{:S(2)}) async-start(bf16[4,256,768]{2,1,0:T(8,128)(2,1)} %bitcast.378), calls=%async_computation.26 | async-start | bytes 3145728 | tf_op jit(solution)/shard_map/all_to_all | solution.py:1753
  1316.2 40.4 %all-to-all-start.25 = ((bf16[4,256,768]{2,1,0:T(8,128)(2,1)}), bf16[4,256,768]{2,1,0:T(8,128)(2,1)S(1)}, u32[]{:S(2)}, u32[]{:S(2)}) async-start(bf16[4,256,768]{2,1,0:T(8,128)(2,1)} %bitcast.380), calls=%async_computation.29 | async-start | bytes 3145728 | tf_op jit(solution)/shard_map/all_to_all | solution.py:1753
  1323.7 41.9 %collective-permute-start.70 = (f32[1,2050]{1,0:T(1,128)S(1)}, f32[1,2050]{1,0:T(1,128)S(1)}, u32[]{:S(2)}, u32[]{:S(2)}) collective-permute-start(f32[1,2050]{1,0:T(1,128)S(1)} %broadcast_in_dim.114), channel_id=1, source_target_pairs={{0,4},{4,0},{8,12},{12,8},{1,5},{5,1},{9,13},{13,9},{2,6},{6,2},{1... | collective-permute-start | bytes 24608 | tf_op jit(solution)/shard_map/ppermute | solution.py:1658
  1325.2 40.4 %collective-permute-start.69 = (f32[1,2050]{1,0:T(1,128)S(1)}, f32[1,2050]{1,0:T(1,128)S(1)}, u32[]{:S(2)}, u32[]{:S(2)}) collective-permute-start(f32[1,2050]{1,0:T(1,128)S(1)} %broadcast_in_dim.114), channel_id=1, source_target_pairs={{0,8},{4,12},{8,0},{12,4},{1,9},{5,13},{9,1},{13,5},{2,10},{6,14},... | collective-permute-start | bytes 24608 | tf_op jit(solution)/shard_map/ppermute | solution.py:1658
  1327.3 39.5 %collective-permute-start.68 = (f32[1,2050]{1,0:T(1,128)S(1)}, f32[1,2050]{1,0:T(1,128)}, u32[]{:S(2)}, u32[]{:S(2)}) collective-permute-start(f32[1,2050]{1,0:T(1,128)S(1)} %broadcast_in_dim.114), channel_id=1, source_target_pairs={{0,12},{4,8},{8,4},{12,0},{1,13},{5,9},{9,5},{13,1},{2,14},{6,10},... | collective-permute-start | bytes 24608 | tf_op jit(solution)/shard_map/ppermute | solution.py:1658
  1357.7 43.0 %all-to-all-start.21 = ((bf16[4,256,768]{2,1,0:T(8,128)(2,1)}), bf16[4,256,768]{2,1,0:T(8,128)(2,1)S(1)}, u32[]{:S(2)}, u32[]{:S(2)}) async-start(bf16[4,256,768]{2,1,0:T(8,128)(2,1)} %bitcast.381), calls=%async_computation.25 | async-start | bytes 3145728 | tf_op jit(solution)/shard_map/all_to_all | solution.py:1753
  1362.4 42.8 %collective-permute-start.60 = (bf16[64,2048]{1,0:T(8,128)(2,1)S(1)}, bf16[64,2048]{1,0:T(8,128)(2,1)}, u32[]{:S(2)}, u32[]{:S(2)}) collective-permute-start(bf16[64,2048]{1,0:T(8,128)(2,1)S(1)} %broadcast_select_fusion.22), channel_id=1, source_target_pairs={{0,16},{16,0},{1,17},{17,1},{2,18},{18,2},{3,19},{19,3},{4,20},{20... | collective-permute-start | bytes 786440 | tf_op jit(solution)/shard_map/ppermute | solution.py:26
  1412.1 41.7 %collective-permute-start.74 = (bf16[4,256,768]{2,1,0:T(8,128)(2,1)}, bf16[4,256,768]{2,1,0:T(8,128)(2,1)}, u32[]{:S(2)}, u32[]{:S(2)}) collective-permute-start(bf16[4,256,768]{2,1,0:T(8,128)(2,1)} %broadcast_select_fusion.2), channel_id=1, source_target_pairs={{0,16},{16,0},{1,17},{17,1},{2,18},{18,2},{3,19},{19,3},{4,20},{20... | collective-permute-start | bytes 4718600 | tf_op jit(solution)/shard_map/ppermute | solution.py:26
  1437.1 43.3 %collective-permute-start.67 = (bf16[4,256,768]{2,1,0:T(8,128)(2,1)}, bf16[4,256,768]{2,1,0:T(8,128)(2,1)}, u32[]{:S(2)}, u32[]{:S(2)}) collective-permute-start(bf16[4,256,768]{2,1,0:T(8,128)(2,1)} %broadcast_select_fusion.4), channel_id=1, source_target_pairs={{0,16},{16,0},{1,17},{17,1},{2,18},{18,2},{3,19},{19,3},{4,20},{20... | collective-permute-start | bytes 4718600 | tf_op jit(solution)/shard_map/ppermute | solution.py:26
  (232 other events, 2567.8 us)
Sparse Core Ops, SparseCore 0:
  76.7 72.4 all-gather.8
  151.1 50.7 all-gather.10
  203.8 77.9 all-gather.12
  284.1 45.4 all-gather.14
  331.3 72.1 all-gather.16
  405.2 36.7 all-gather.18
  444.4 50.9 all-gather.22
  542.1 81.8 all-gather.20
  659.1 94.6 reduce-scatter.10
  827.9 82.0 reduce-scatter.18
  917.6 114.3 reduce-scatter.12
  1035.4 104.7 reduce-scatter.14
  1143.6 81.6 reduce-scatter.20
  1233.4 92.3 reduce-scatter.16

commit v3 on v2

--- a/solution.py
+++ b/solution.py
@@ -11,11 +11,15 @@
 HEAD_V = 256
 CONVK = 4
 BLOCK = 64
+SECTION = "section"
+SEQ = "seq"
+HEAD = "head"
+LANES = 128
 RECUR_FLOPS = 40_000_000
 VMEM_LIMIT = 48 * 1024 * 1024
 HALO = 8
 EXTRA = 128
-GROUP = 4
+GROUP = 8
 
 
 epsilon = 1e-06
@@ -249,11 +253,11 @@
 
 
 def head_total(values):
-    return lax.psum(values.astype(jnp.bfloat16), "head").astype(jnp.float32)
+    return lax.psum(values.astype(jnp.bfloat16), HEAD).astype(jnp.float32)
 
 
 def partner(values):
-    return swapped(values, "section", 0)
+    return swapped(values, SECTION, 0)
 
 
 def proj_t(left, right):
@@ -271,27 +275,27 @@
 def spread(rows_grads, cols_grads):
     rows_part = (
         lax.psum_scatter(
-            rows_grads[0].astype(jnp.bfloat16), "seq", scatter_dimension=0, tiled=True
+            rows_grads[0].astype(jnp.bfloat16), SEQ, scatter_dimension=0, tiled=True
         ).astype(jnp.float32),
         lax.psum_scatter(
-            rows_grads[1].astype(jnp.bfloat16), "seq", scatter_dimension=0, tiled=True
+            rows_grads[1].astype(jnp.bfloat16), SEQ, scatter_dimension=0, tiled=True
         ).astype(jnp.float32),
         lax.psum_scatter(
-            rows_grads[2].astype(jnp.bfloat16), "seq", scatter_dimension=0, tiled=True
+            rows_grads[2].astype(jnp.bfloat16), SEQ, scatter_dimension=0, tiled=True
         ).astype(jnp.float32),
         lax.psum_scatter(
-            rows_grads[3].astype(jnp.bfloat16), "seq", scatter_dimension=0, tiled=True
+            rows_grads[3].astype(jnp.bfloat16), SEQ, scatter_dimension=0, tiled=True
         ).astype(jnp.float32),
         lax.psum_scatter(
-            rows_grads[4].astype(jnp.bfloat16), "seq", scatter_dimension=0, tiled=True
+            rows_grads[4].astype(jnp.bfloat16), SEQ, scatter_dimension=0, tiled=True
         ).astype(jnp.float32),
     )
     cols_part = (
         lax.psum_scatter(
-            cols_grads[0].astype(jnp.bfloat16), "seq", scatter_dimension=1, tiled=True
+            cols_grads[0].astype(jnp.bfloat16), SEQ, scatter_dimension=1, tiled=True
         ).astype(jnp.float32),
         lax.psum_scatter(
-            cols_grads[1].astype(jnp.bfloat16), "seq", scatter_dimension=1, tiled=True
+            cols_grads[1].astype(jnp.bfloat16), SEQ, scatter_dimension=1, tiled=True
         ).astype(jnp.float32),
     )
     return (rows_part, cols_part)
@@ -329,23 +333,23 @@
     width_qkv = 2 * width_qk + w_value.shape[2]
     hidden_width = w_gate.shape[2]
     block_count = row_count // BLOCK
-    section_index = lax.axis_index("section")
-    shard_index = lax.axis_index("seq")
+    section_index = lax.axis_index(SECTION)
+    shard_index = lax.axis_index(SEQ)
     full_rows = (
-        lax.all_gather(gain_attn[0], "seq", axis=0, tiled=True),
-        lax.all_gather(gain_mlp[0], "seq", axis=0, tiled=True),
-        lax.all_gather(w_query[0], "seq", axis=0, tiled=True),
-        lax.all_gather(w_key[0], "seq", axis=0, tiled=True),
-        lax.all_gather(w_value[0], "seq", axis=0, tiled=True),
-        lax.all_gather(w_gate_out[0], "seq", axis=0, tiled=True),
-        lax.all_gather(w_decay[0], "seq", axis=0, tiled=True),
-        lax.all_gather(w_beta[0], "seq", axis=0, tiled=True),
-        lax.all_gather(w_gate[0], "seq", axis=0, tiled=True),
-        lax.all_gather(w_up[0], "seq", axis=0, tiled=True),
+        lax.all_gather(gain_attn[0], SEQ, axis=0, tiled=True),
+        lax.all_gather(gain_mlp[0], SEQ, axis=0, tiled=True),
+        lax.all_gather(w_query[0], SEQ, axis=0, tiled=True),
+        lax.all_gather(w_key[0], SEQ, axis=0, tiled=True),
+        lax.all_gather(w_value[0], SEQ, axis=0, tiled=True),
+        lax.all_gather(w_gate_out[0], SEQ, axis=0, tiled=True),
+        lax.all_gather(w_decay[0], SEQ, axis=0, tiled=True),
+        lax.all_gather(w_beta[0], SEQ, axis=0, tiled=True),
+        lax.all_gather(w_gate[0], SEQ, axis=0, tiled=True),
+        lax.all_gather(w_up[0], SEQ, axis=0, tiled=True),
     )
     full_cols = (
-        lax.all_gather(w_output[0], "seq", axis=1, tiled=True),
-        lax.all_gather(w_down[0], "seq", axis=1, tiled=True),
+        lax.all_gather(w_output[0], SEQ, axis=1, tiled=True),
+        lax.all_gather(w_down[0], SEQ, axis=1, tiled=True),
     )
     attn_gain = full_rows[0].astype(jnp.float32)
     mlp_gain = full_rows[1].astype(jnp.float32)
@@ -370,7 +374,7 @@
             jnp.eye(shard_map_t.shape[1], dtype=jnp.float32), shard_map_t.shape
         )
         suffix = entering(
-            (shard_map_t, shard_adj), "seq", compose, (identity, jnp.zeros_like(shard_adj))
+            (shard_map_t, shard_adj), SEQ, compose, (identity, jnp.zeros_like(shard_adj))
         )
         result = suffix[1]
         return result
@@ -439,7 +443,7 @@
         grad_ext, grad_mix, grad_conv, grad_scale, grad_shift = summary_back(
             (gradient_transfer, later_blocks, grad_kept)
         )
-        returned = passed_along(grad_ext[: CONVK - 1], "seq", -1)
+        returned = passed_along(grad_ext[: CONVK - 1], SEQ, -1)
         grad_qkv = grad_ext[CONVK - 1 :] + jnp.pad(returned, ((row_count - (CONVK - 1), 0), (0, 0)))
         grad_pre = jnp.concatenate([grad_qkv, grad_gate_pre], axis=1).astype(jnp.bfloat16)
         grad_proj_weight = inner_t(normed, grad_pre)
@@ -489,7 +493,7 @@
         )
         qkv_pre = projected[:, :width_qkv]
         layer_gate_pre = projected[:, width_qkv:]
-        rim_rows = passed_along(qkv_pre[row_count - (CONVK - 1) :], "seq", 1)
+        rim_rows = passed_along(qkv_pre[row_count - (CONVK - 1) :], SEQ, 1)
         layer_extended = jnp.concatenate([rim_rows, qkv_pre], axis=0)
         layer_shard_map, layer_shard_add, layer_kept = summary(
             layer_extended,
@@ -506,7 +510,7 @@
         )
         prefix = carried_in(
             (layer_shard_map, layer_shard_add),
-            "seq",
+            SEQ,
             compose,
             (carry_identity, jnp.zeros_like(layer_shard_add)),
         )
@@ -600,14 +604,14 @@
         if slot_index < micro_count:
             back_in = partner(outgoing)
     rows_part, cols_part = spread(rows_acc, cols_acc)
-    norm_heads = lax.psum(small_acc[3], "head")
+    norm_heads = lax.psum(small_acc[3], HEAD)
     conv_sum, scale_sum, shift_sum, norm_sum, sums_all, counts_all = (
-        lax.psum(small_acc[0].astype(jnp.bfloat16), "seq").astype(jnp.float32),
-        lax.psum(small_acc[1].astype(jnp.bfloat16), "seq").astype(jnp.float32),
-        lax.psum(small_acc[2].astype(jnp.bfloat16), "seq").astype(jnp.float32),
-        lax.psum(norm_heads.astype(jnp.bfloat16), "seq").astype(jnp.float32),
-        lax.psum(stat_sums.astype(jnp.bfloat16), "seq").astype(jnp.float32),
-        lax.psum(stat_counts.astype(jnp.bfloat16), "seq").astype(jnp.float32),
+        lax.psum(small_acc[0].astype(jnp.bfloat16), SEQ).astype(jnp.float32),
+        lax.psum(small_acc[1].astype(jnp.bfloat16), SEQ).astype(jnp.float32),
+        lax.psum(small_acc[2].astype(jnp.bfloat16), SEQ).astype(jnp.float32),
+        lax.psum(norm_heads.astype(jnp.bfloat16), SEQ).astype(jnp.float32),
+        lax.psum(stat_sums.astype(jnp.bfloat16), SEQ).astype(jnp.float32),
+        lax.psum(stat_counts.astype(jnp.bfloat16), SEQ).astype(jnp.float32),
     )
     branch_rms = jnp.sqrt(sums_all / jnp.maximum(counts_all, 1.0)[:, None])
     proj_part = rows_part[2]
@@ -638,25 +642,53 @@
     )
 
 
-exact = lax.Precision.HIGHEST
+def high_low(value):
+    high = value.astype(jnp.bfloat16)
+    return high, (value - high.astype(jnp.float32)).astype(jnp.bfloat16)
+
+
+@functools.partial(jax.custom_vjp, nondiff_argnums=(2,))
+def fine_dot(a, b, dims):
+    a_high, a_low = high_low(a)
+    b_high, b_low = high_low(b)
+
+    def part(x, y):
+        return lax.dot_general(x, y, (dims, ((), ())), preferred_element_type=jnp.float32)
+
+    return part(a_high, b_high) + (part(a_high, b_low) + part(a_low, b_high))
+
+
+def fine_dot_fwd(a, b, dims):
+    return fine_dot(a, b, dims), (a, b)
+
+
+def fine_dot_bwd(dims, kept, grad):
+    a, b = kept
+    (a_dim,), (b_dim,) = dims
+    if a_dim == 1:
+        da = fine_dot(grad, b, ((1,), (1 - b_dim,)))
+    else:
+        da = fine_dot(b, grad, ((1 - b_dim,), (1,)))
+    if b_dim == 0:
+        db = fine_dot(a, grad, ((1 - a_dim,), (0,)))
+    else:
+        db = fine_dot(grad, a, ((0,), (1 - a_dim,)))
+    return da, db
+
+
+fine_dot.defvjp(fine_dot_fwd, fine_dot_bwd)
 
 
 def dot_nn(a, b):
-    return lax.dot_general(
-        a, b, (((1,), (0,)), ((), ())), precision=exact, preferred_element_type=jnp.float32
-    )
+    return fine_dot(a, b, ((1,), (0,)))
 
 
 def dot_nt(a, b):
-    return lax.dot_general(
-        a, b, (((1,), (1,)), ((), ())), precision=exact, preferred_element_type=jnp.float32
-    )
+    return fine_dot(a, b, ((1,), (1,)))
 
 
 def dot_tn(a, b):
-    return lax.dot_general(
-        a, b, (((0,), (0,)), ((), ())), precision=exact, preferred_element_type=jnp.float32
-    )
+    return fine_dot(a, b, ((0,), (0,)))
 
 
 @functools.partial(jax.custom_vjp, nondiff_argnums=(1,))
@@ -691,20 +723,28 @@
     return jnp.sum(jnp.where(rows == cols, column, 0.0), axis=0, keepdims=True)
 
 
-def unit_inverse(lower):
-    length = lower.shape[0]
+def unit_inverses(lowers):
+    length = lowers[0].shape[0]
     rows, cols = iotas(length)
-    near = jnp.where((rows >> 3) == (cols >> 3), lower, 0.0)
-    result = jnp.where(rows == cols, 1.0, 0.0) - near
-    square = dot_nn(near, near)
-    result = result + dot_nn(result, square)
-    result = result + dot_nn(result, dot_nn(square, square))
+    eye = jnp.where(rows == cols, 1.0, 0.0)
+    near = [jnp.where((rows >> 3) == (cols >> 3), lower, 0.0) for lower in lowers]
+    results = [eye - part for part in near]
+    squares = [dot_nn(part, part) for part in near]
+    steps = [dot_nn(result, square) for result, square in zip(results, squares)]
+    squares = [dot_nn(square, square) for square in squares]
+    results = [result + step for result, step in zip(results, steps)]
+    steps = [dot_nn(result, square) for result, square in zip(results, squares)]
+    results = [result + step for result, step in zip(results, steps)]
     shift = 3
     while (1 << shift) < length:
         off = ((rows >> (shift + 1)) == (cols >> (shift + 1))) & ((rows >> shift) != (cols >> shift))
-        result = result - dot_nn(result, dot_nn(jnp.where(off, lower, 0.0), result))
+        steps = [
+            dot_nn(jnp.where(off, lower, 0.0), result) for lower, result in zip(lowers, results)
+        ]
+        steps = [dot_nn(result, step) for result, step in zip(results, steps)]
+        results = [result - step for result, step in zip(results, steps)]
         shift += 1
-    return result
+    return results
 
 
 @jax.custom_vjp
@@ -773,48 +813,41 @@
     return lower, mixing, scaled, entry * queries, leave * keys, through
 
 
-def block_step(window, mix_decay, mix_write, taps, decay_log, decay_bias, state, aux, inverse):
+def block_prepare(window, mix_decay, mix_write, taps, decay_log, decay_bias, aux, inverse):
     lower, mixing, scaled, queries, keys, through = block_front(
         window, mix_decay, mix_write, taps, decay_log, decay_bias, aux
     )
-    if inverse is None:
-        inverse = unit_inverse(lower)
-    else:
-        inverse = inverse_known(lower, inverse)
-    resolved = dot_nn(inverse, scaled)
+    return mixing, dot_nn(inverse_known(lower, inverse), scaled), queries, keys, through
+
+
+def block_core(mixing, resolved, queries, keys, through, state):
     read = dot_nn(jnp.concatenate([resolved[:, HEAD_V:], queries], axis=0), state)
     written = resolved[:, :HEAD_V] - read[:BLOCK]
     mixed = read[BLOCK:] + dot_nn(mixing, written)
-    return mixed, through * state + dot_tn(keys, written), inverse
-
-
-def stored_at(number, blocks, parts):
+    return mixed, through * state + dot_tn(keys, written)
+
+
+def each_slice(piece_ref, refs, parts):
     shards, slices = parts
-    each = blocks // (shards * slices)
-    shard = number // (slices * each)
-    rest = number - shard * slices * each
-    place = (rest // each * shards + shard) * each + rest % each
-    return pl.multiple_of(place * BLOCK, BLOCK)
-
-
-def fill_window(xh_ref, xbuf, parts):
+    sub = refs[0].shape[0] // shards
+    for number, ref in enumerate(refs):
+        for shard in range(shards):
+            start = (shard * slices + (piece_ref[0] ^ number)) * sub
+            yield pl.multiple_of(start, sub), pl.ds(shard * sub, sub), sub, ref
+
+
+def fill_inputs(piece_ref, xh_refs, parts, xbuf, mixbuf):
     width = xbuf.shape[1]
-    length = xh_ref.shape[0]
-    blocks = length // BLOCK
     xbuf[0:HALO, :] = jnp.zeros((HALO, width), jnp.float32)
-
-    def copy(index, carry):
-        base = pl.multiple_of(index * BLOCK, BLOCK)
-        stored = stored_at(index, blocks, parts)
-        xbuf[pl.ds(base + HALO, BLOCK), :] = xh_ref[pl.ds(stored, BLOCK), :width].astype(jnp.float32)
-        return carry
-
-    lax.fori_loop(0, length // BLOCK, copy, 0)
-
-
-def load_block(xh_ref, aux_ref, xbuf, base, stored):
+    for start, there, sub, ref in each_slice(piece_ref, xh_refs, parts):
+        here = pl.ds(pl.multiple_of(start + HALO, HALO), sub)
+        xbuf[here, :] = ref[there, :width].astype(jnp.float32)
+        mixbuf[pl.ds(start, sub), :] = ref[there, width:].astype(jnp.float32)
+
+
+def load_block(aux_ref, xbuf, mixbuf, base):
     window = xbuf[pl.ds(base, BLOCK + HALO), :]
-    mix = xh_ref[pl.ds(stored, BLOCK), xbuf.shape[1] :].astype(jnp.float32)
+    mix = mixbuf[pl.ds(base, BLOCK), :]
     aux = aux_ref[pl.ds(base, BLOCK), :]
     return window, mix[:, 0:1] + mix[:, 2:3], mix[:, 1:2] + mix[:, 3:4], aux
 
@@ -823,43 +856,55 @@
     return [taps_ref[j : j + 1, :] for j in range(CONVK)]
 
 
-def forward_kernel(parts, xh_ref, aux_ref, taps_ref, scal_ref, mixed_ref, states_ref, inverse_ref, xbuf, state_ref):
-    fill_window(xh_ref, xbuf, parts)
+def forward_kernel(parts, piece_ref, *refs):
+    slices = parts[1]
+    xh_refs, refs = refs[:slices], refs[slices:]
+    aux_ref, taps_ref, scal_ref, *mixed_refs = refs[: 3 + slices]
+    states_ref, inverse_ref, xbuf, mixbuf, mixed_buf, state_ref = refs[3 + slices :]
+    fill_inputs(piece_ref, xh_refs, parts, xbuf, mixbuf)
     state_ref[...] = jnp.zeros_like(state_ref)
-    blocks = xh_ref.shape[0] // BLOCK
+    blocks = aux_ref.shape[0] // BLOCK
     taps = load_taps(taps_ref)
     decay_log = scal_ref[0:1, 0:1]
     decay_bias = scal_ref[0:1, 1:2]
 
     def group(index, carry):
         state = state_ref[...]
+        places, fronts = [], []
         for inner in range(GROUP):
             number = index * GROUP + inner
             base = pl.multiple_of(number * BLOCK, BLOCK)
-            stored = stored_at(number, blocks, parts)
-            window, mix_decay, mix_write, aux = load_block(xh_ref, aux_ref, xbuf, base, stored)
+            window, mix_decay, mix_write, aux = load_block(aux_ref, xbuf, mixbuf, base)
+            places.append((number, base))
+            fronts.append(block_front(window, mix_decay, mix_write, taps, decay_log, decay_bias, aux))
+        inverses = unit_inverses([front[0] for front in fronts])
+        resolved = [dot_nn(inverse, front[2]) for inverse, front in zip(inverses, fronts)]
+        for (number, base), front, inverse, solved in zip(places, fronts, inverses, resolved):
             states_ref[number] = state
-            mixed, state, inverse = block_step(
-                window, mix_decay, mix_write, taps, decay_log, decay_bias, state, aux, None
-            )
-            mixed_ref[pl.ds(stored, BLOCK), :] = mixed.astype(mixed_ref.dtype)
             inverse_ref[pl.ds(base, BLOCK), :] = inverse
+            mixed, state = block_core(front[1], solved, *front[3:], state)
+            mixed_buf[pl.ds(base, BLOCK), :] = mixed.astype(mixed_buf.dtype)
         state_ref[...] = state
         return carry
 
     lax.fori_loop(0, blocks // GROUP, group, 0)
-
-
-def backward_kernel(
-    parts, xh_ref, aux_ref, taps_ref, scal_ref, states_ref, inverse_ref, grad_ref,
-    dxh_ref, dtaps_ref, dscal_ref, xbuf, adjoint_ref, halo_ref,
-):
-    fill_window(xh_ref, xbuf, parts)
+    for start, there, sub, ref in each_slice(piece_ref, mixed_refs, parts):
+        ref[there, :] = mixed_buf[pl.ds(start, sub), :]
+
+
+def backward_kernel(parts, piece_ref, *refs):
+    slices = parts[1]
+    xh_refs, grad_refs, refs = refs[:slices], refs[slices : 2 * slices], refs[2 * slices :]
+    aux_ref, taps_ref, scal_ref, states_ref, inverse_ref, *dxh_refs = refs[: 5 + slices]
+    dtaps_ref, dscal_ref, xbuf, mixbuf, grad_buf, dxh_buf, adjoint_ref, halo_ref = refs[5 + slices :]
+    fill_inputs(piece_ref, xh_refs, parts, xbuf, mixbuf)
+    for start, there, sub, ref in each_slice(piece_ref, grad_refs, parts):
+        grad_buf[pl.ds(start, sub), :] = ref[there, :]
     adjoint_ref[...] = jnp.zeros_like(adjoint_ref)
     halo_ref[...] = jnp.zeros_like(halo_ref)
     dtaps_ref[...] = jnp.zeros_like(dtaps_ref)
     dscal_ref[...] = jnp.zeros_like(dscal_ref)
-    blocks = xh_ref.shape[0] // BLOCK
+    blocks = aux_ref.shape[0] // BLOCK
     width = xbuf.shape[1]
     taps = load_taps(taps_ref)
     decay_log = scal_ref[0:1, 0:1]
@@ -872,33 +917,38 @@
         dtaps = [dtaps_ref[j : j + 1, :] for j in range(CONVK)]
         dlog = dscal_ref[0:1, 0:1]
         dbias = dscal_ref[0:1, 1:2]
+        places, prepares, cores = [], [], []
         for inner in range(GROUP):
             number = blocks - 1 - (index * GROUP + inner)
             base = pl.multiple_of(number * BLOCK, BLOCK)
-            stored = stored_at(number, blocks, parts)
-            window, mix_decay, mix_write, aux = load_block(xh_ref, aux_ref, xbuf, base, stored)
+            window, mix_decay, mix_write, aux = load_block(aux_ref, xbuf, mixbuf, base)
             inverse = inverse_ref[pl.ds(base, BLOCK), :]
-            grad = grad_ref[pl.ds(stored, BLOCK), :].astype(jnp.float32)
-
-            def run(*inputs):
-                return block_step(*inputs, aux, inverse)[:2]
-
-            _, pull = jax.vjp(
-                run, window, mix_decay, mix_write, taps, decay_log, decay_bias, states_ref[number]
+            prepared, pull = jax.vjp(
+                functools.partial(block_prepare, aux=aux, inverse=inverse),
+                window, mix_decay, mix_write, taps, decay_log, decay_bias,
             )
-            dwindow, ddecay, dwrite, dtaps_now, dlog_now, dbias_now, adjoint = pull((grad, adjoint))
+            places.append(base)
+            prepares.append(pull)
+            cores.append(jax.vjp(block_core, *prepared, states_ref[number])[1])
+        dprepared = []
+        for base, pull in zip(places, cores):
+            grad = grad_buf[pl.ds(base, BLOCK), :].astype(jnp.float32)
+            *dparts, adjoint = pull((grad, adjoint))
+            dprepared.append(tuple(dparts))
+        for base, pull, dparts in zip(places, prepares, dprepared):
+            dwindow, ddecay, dwrite, dtaps_now, dlog_now, dbias_now = pull(dparts)
             own = dwindow[HALO:]
             own = jnp.concatenate([own[: BLOCK - HALO], own[BLOCK - HALO :] + halo], axis=0)
             halo = dwindow[:HALO]
             dtaps = [a + b for a, b in zip(dtaps, dtaps_now)]
             dlog = dlog + dlog_now
             dbias = dbias + dbias_now
-            dxh_ref[pl.ds(stored, BLOCK), :width] = own.astype(dxh_ref.dtype)
+            dxh_buf[pl.ds(base, BLOCK), :width] = own.astype(dxh_buf.dtype)
             high_decay = ddecay.astype(jnp.bfloat16).astype(jnp.float32)
             high_write = dwrite.astype(jnp.bfloat16).astype(jnp.float32)
             mix = jnp.where(lanes == 0, high_decay, jnp.where(lanes == 1, high_write, 0.0))
             mix = jnp.where(lanes == 2, ddecay - high_decay, jnp.where(lanes == 3, dwrite - high_write, mix))
-            dxh_ref[pl.ds(stored, BLOCK), width:] = mix.astype(dxh_ref.dtype)
+            dxh_buf[pl.ds(base, BLOCK), width:] = mix.astype(dxh_buf.dtype)
         adjoint_ref[...] = adjoint
         halo_ref[...] = halo
         for j in range(CONVK):
@@ -908,6 +958,8 @@
         return carry
 
     lax.fori_loop(0, blocks // GROUP, group, 0)
+    for start, there, sub, ref in each_slice(piece_ref, dxh_refs, parts):
+        ref[there, :] = dxh_buf[pl.ds(start, sub), :]
 
 
 WIDTH = 2 * HEAD_K + HEAD_V
@@ -917,52 +969,61 @@
     return pl.BlockSpec(memory_space=pltpu.VMEM)
 
 
-def recur_forward(xh, aux, taps, scal, parts):
-    length = xh.shape[0]
+def recur_cost(length):
+    return pl.CostEstimate(flops=length * RECUR_FLOPS, bytes_accessed=length * 8192, transcendentals=0)
+
+
+def recur_forward(piece, xh, aux, taps, scal, parts):
+    length = aux.shape[0]
     blocks = length // BLOCK
-    return pl.pallas_call(
+    slices = len(xh)
+    *mixed, states, inverse = pl.pallas_call(
         functools.partial(forward_kernel, parts),
-        out_shape=(
-            jax.ShapeDtypeStruct((length, HEAD_V), jnp.bfloat16),
+        out_shape=(jax.ShapeDtypeStruct((length // slices, HEAD_V), jnp.bfloat16),) * slices
+        + (
             jax.ShapeDtypeStruct((blocks, HEAD_K, HEAD_V), jnp.float32),
             jax.ShapeDtypeStruct((length, BLOCK), jnp.float32),
         ),
-        in_specs=[whole()] * 4,
-        out_specs=(whole(),) * 3,
+        in_specs=[pl.BlockSpec(memory_space=pltpu.SMEM)] + [whole()] * (slices + 3),
+        out_specs=(whole(),) * (slices + 2),
         scratch_shapes=[
             pltpu.VMEM((length + HALO, WIDTH), jnp.float32),
+            pltpu.VMEM((length, EXTRA), jnp.float32),
+            pltpu.VMEM((length, HEAD_V), jnp.bfloat16),
             pltpu.VMEM((HEAD_K, HEAD_V), jnp.float32),
         ],
         compiler_params=pltpu.CompilerParams(vmem_limit_bytes=VMEM_LIMIT),
-        cost_estimate=pl.CostEstimate(
-            flops=length * RECUR_FLOPS, bytes_accessed=length * 8192, transcendentals=0
-        ),
+        cost_estimate=recur_cost(length),
         name="recur_forward",
-    )(xh, aux, taps, scal)
-
-
-def recur_backward(xh, aux, taps, scal, states, inverse, grad, parts):
-    length = xh.shape[0]
-    return pl.pallas_call(
+    )(piece, *xh, aux, taps, scal)
+    return mixed, states, inverse
+
+
+def recur_backward(piece, xh, grad, aux, taps, scal, states, inverse, parts):
+    length = aux.shape[0]
+    slices = len(xh)
+    *dxh, dtaps, dscal = pl.pallas_call(
         functools.partial(backward_kernel, parts),
-        out_shape=(
-            jax.ShapeDtypeStruct((length, WIDTH + EXTRA), jnp.bfloat16),
+        out_shape=(jax.ShapeDtypeStruct((length // slices, WIDTH + EXTRA), jnp.bfloat16),) * slices
+        + (
             jax.ShapeDtypeStruct((8, WIDTH), jnp.float32),
             jax.ShapeDtypeStruct((8, 128), jnp.float32),
         ),
-        in_specs=[whole()] * 7,
-        out_specs=(whole(),) * 3,
+        in_specs=[pl.BlockSpec(memory_space=pltpu.SMEM)] + [whole()] * (2 * slices + 5),
+        out_specs=(whole(),) * (slices + 2),
         scratch_shapes=[
             pltpu.VMEM((length + HALO, WIDTH), jnp.float32),
+            pltpu.VMEM((length, EXTRA), jnp.float32),
+            pltpu.VMEM((length, HEAD_V), jnp.bfloat16),
+            pltpu.VMEM((length, WIDTH + EXTRA), jnp.bfloat16),
             pltpu.VMEM((HEAD_K, HEAD_V), jnp.float32),
             pltpu.VMEM((HALO, WIDTH), jnp.float32),
         ],
         compiler_params=pltpu.CompilerParams(vmem_limit_bytes=VMEM_LIMIT),
-        cost_estimate=pl.CostEstimate(
-            flops=length * RECUR_FLOPS, bytes_accessed=length * 8192, transcendentals=0
-        ),
+        cost_estimate=recur_cost(length),
         name="recur_backward",
-    )(xh, aux, taps, scal, states, inverse, grad)
+    )(piece, *xh, *grad, aux, taps, scal, states, inverse)
+    return dxh, dtaps, dscal
 
 
 def make_aux(starts, length):
@@ -1040,6 +1101,11 @@
     for number, part in enumerate(part_refs):
         start = (me_ref[0] ^ number) * rows
         yield pl.ds(pl.multiple_of(start, rows), rows), part
+
+
+def hand_out(me_ref, total_ref, piece_refs):
+    for where, piece in each_piece(me_ref, piece_refs):
+        piece[...] = total_ref[where, :].astype(piece.dtype)
 
 
 def put_stat(stat_ref, column, value):
@@ -1119,45 +1185,55 @@
     )
 
 
-def output_kernel(mixed_ref, gate_ref, norm_ref, w_ref, gated_ref, pieces_ref):
-    slices = mixed_ref.shape[0]
+def output_kernel(slices, me_ref, piece_ref, *refs):
+    mixed_refs, refs = refs[:slices], refs[slices:]
+    gate_ref, norm_ref, w_ref, gated_ref, kept_ref, *piece_refs, total = refs
 
     @pl.when(pl.program_id(0) == 0)
     def _():
-        for j in range(slices):
-            value = mixed_ref[j].astype(jnp.float32)
+        for number, mixed_ref in enumerate(mixed_refs):
+            j = piece_ref[0] ^ number
+            kept_ref[j] = mixed_ref[...]
+            value = mixed_ref[...].astype(jnp.float32)
             normed = value * row_scale(value) * norm_ref[...] * silu(gate_ref[j])
-            gated_ref[:, j * HEAD_V : (j + 1) * HEAD_V] = normed.astype(jnp.bfloat16)
-
-    result = dot(gated_ref[...], w_ref[0]).astype(jnp.bfloat16)
-    pieces_ref[...] = result.reshape(pieces_ref.shape)
-
-
-def output(mixed, gate_pre, norm_weight, w_out, shards):
-    slices, rows, _ = mixed.shape
-    _, inner, half = w_out.shape
-    return run(
-        output_kernel,
+            start = pl.multiple_of(j * HEAD_V, HEAD_V)
+            gated_ref[:, pl.ds(start, HEAD_V)] = normed.astype(jnp.bfloat16)
+
+    weight = w_ref[0].reshape(gated_ref.shape[1], w_ref.shape[3])
+    total[...] = dot(gated_ref[...], weight)
+    hand_out(me_ref, total, piece_refs)
+
+
+def output(me, piece, mixed, gate_pre, norm_weight, w_cols, shards):
+    slices, rows, _ = gate_pre.shape
+    inner, half = slices * HEAD_V, w_cols.shape[3]
+    sub = rows // shards
+    gated, kept, *pieces = run(
+        functools.partial(output_kernel, slices),
         (2,),
-        [held(mixed.shape), held(gate_pre.shape), held((1, HEAD_V)), slab((1, inner, half), 0)],
-        (held((rows, inner)), slab((shards, rows // shards, half), 2)),
-        (like((rows, inner), jnp.bfloat16), like((shards, rows // shards, 2 * half), jnp.bfloat16)),
-        [],
+        [in_smem(), in_smem()]
+        + [held((rows, HEAD_V))] * slices
+        + [held(gate_pre.shape), held((1, HEAD_V)), slab((1, slices, HEAD_V, half), 0)],
+        (held((rows, inner)), held(gate_pre.shape)) + (slab((sub, half), 1),) * shards,
+        (like((rows, inner), jnp.bfloat16), like(gate_pre.shape, jnp.bfloat16))
+        + (like((sub, 2 * half), jnp.bfloat16),) * shards,
+        [pltpu.VMEM((rows, half), jnp.float32)],
         "output",
         4 * rows * inner * half,
-        w_out.size * 2 + rows * inner * 12,
-        [mixed, gate_pre, norm_weight, w_out],
-    )
+        inner * half * 4 + rows * inner * 12,
+        [me, piece] + list(mixed) + [gate_pre, norm_weight, w_cols],
+    )
+    return gated, kept, pieces
 
 
 def feed_kernel(pieces, *refs):
     me_ref, valid_ref, gain_ref = refs[:3]
     part_refs = refs[3 : 3 + pieces]
-    base_ref, w_gu_ref, w_down_ref, mid_ref, normed_ref, gate_up_ref, hidden_ref, pieces_ref, stat_ref, total = refs[
-        3 + pieces :
-    ]
+    base_ref, w_gu_ref = refs[3 + pieces : 5 + pieces]
+    down_refs = refs[5 + pieces : -6 - pieces]
+    mid_ref, normed_ref, gate_up_ref, hidden_ref, *piece_refs, stat_ref, total = refs[-6 - pieces :]
     step = pl.program_id(0)
-    half = w_down_ref.shape[2]
+    half = down_refs[0].shape[3]
 
     @pl.when(step == 0)
     def _():
@@ -1176,106 +1252,124 @@
     hidden = (silu(result[:, :width]) * result[:, width:]).astype(jnp.bfloat16)
     hidden_ref[...] = hidden
     for c in range(2):
-        total[:, c * half : (c + 1) * half] += dot(hidden, w_down_ref[c])
+        part = sum(
+            dot(hidden[:, k * LANES : (k + 1) * LANES], ref[c, 0]) for k, ref in enumerate(down_refs)
+        )
+        total[:, c * half : (c + 1) * half] += part
 
     @pl.when(step == pl.num_programs(0) - 1)
     def _():
-        pieces_ref[...] = total[...].astype(jnp.bfloat16).reshape(pieces_ref.shape)
-
-
-def feed(me, valid, gain, parts, base, w_gu, w_down, shards):
+        hand_out(me_ref, total, piece_refs)
+
+
+def down_slabs(w_cols, hidden):
+    half = w_cols.shape[3]
+
+    def block(number):
+        return pl.BlockSpec((2, 1, LANES, half), lambda step: (0, step, number, 0))
+
+    first = HEAD_V // LANES
+    return [block(first + k) for k in range(hidden // LANES)]
+
+
+def feed(me, valid, gain, parts, base, w_gu, w_cols):
     slices, width, columns = w_gu.shape
     sub = parts[0].shape[0]
     rows = sub * len(parts)
     hidden = columns // 2
-    half = width // 2
-    return run(
+    mid, normed, gate_up, hidden, *pieces, stat = run(
         functools.partial(feed_kernel, len(parts)),
         (slices,),
         [in_smem(), held((rows, 1)), held((1, width))]
         + [held((sub, width))] * len(parts)
-        + [held((rows, width)), slab((1, width, columns), 0), slab((2, hidden, half), 1)],
+        + [held((rows, width)), slab((1, width, columns), 0)]
+        + down_slabs(w_cols, hidden),
         (
             held((rows, width)),
             held((rows, width)),
             slab((1, rows, columns), 0),
             slab((rows, hidden), 1),
-            held((shards, rows // shards, width)),
-            held((8, 128)),
-        ),
+        )
+        + (held((sub, width)),) * len(parts)
+        + (held((8, 128)),),
         (
             like((rows, width), jnp.float32),
             like((rows, width), jnp.bfloat16),
             like((slices, rows, columns), jnp.float32),
             like((rows, slices * hidden), jnp.bfloat16),
-            like((shards, rows // shards, width), jnp.bfloat16),
-            like((8, 128), jnp.float32),
-        ),
+        )
+        + (like((sub, width), jnp.bfloat16),) * len(parts)
+        + (like((8, 128), jnp.float32),),
         [pltpu.VMEM((rows, width), jnp.float32)],
         "feed",
         2 * rows * width * (columns + hidden) * slices,
-        (w_gu.size + w_down.size) * 2 + rows * width * 16,
-        [me, valid, gain] + list(parts) + [base, w_gu, w_down],
-    )
-
-
-def close_kernel(pieces, *refs):
-    me_ref, valid_ref = refs[:2]
-    part_refs = refs[2 : 2 + pieces]
-    base_ref, out_ref, stat_ref = refs[2 + pieces :]
+        (w_gu.size + hidden * slices * width) * 2 + rows * width * 16,
+        [me, valid, gain] + list(parts) + [base, w_gu] + [w_cols] * (hidden // LANES),
+    )
+    return mid, normed, gate_up, hidden, pieces, stat
+
+
+def close_kernel(valid_ref, part_ref, base_ref, out_ref, stat_ref):
     stat_ref[...] = jnp.zeros_like(stat_ref)
-    for where, part in each_piece(me_ref, part_refs):
-        value = part[...].astype(jnp.float32)
-        valid = valid_ref[where, :]
-        put_stat(stat_ref, 1, mean_square(value, valid))
-        value = value + base_ref[where, :]
-        put_stat(stat_ref, 0, mean_square(value, valid))
-        out_ref[where, :] = value.astype(jnp.bfloat16)
-
-
-def close(me, valid, parts, base):
+    value = part_ref[...].astype(jnp.float32)
+    valid = valid_ref[...]
+    put_stat(stat_ref, 1, mean_square(value, valid))
+    value = value + base_ref[...]
+    put_stat(stat_ref, 0, mean_square(value, valid))
+    out_ref[...] = value.astype(jnp.bfloat16)
+
+
+def close(valid, part, base):
     return run(
-        functools.partial(close_kernel, len(parts)),
+        close_kernel,
         (),
-        [in_smem()] + [in_vmem()] * (2 + len(parts)),
+        [in_vmem()] * 3,
         (in_vmem(), in_vmem()),
         (like(base.shape, jnp.bfloat16), like((8, 128), jnp.float32)),
         [],
         "close",
         base.size * 6,
         base.size * 8,
-        [me, valid] + list(parts) + [base],
-    )
-
-
-def sum_kernel(pieces_ref, total_ref):
-    total = pieces_ref[0].astype(jnp.float32)
-    for k in range(1, pieces_ref.shape[0]):
-        total = total + pieces_ref[k].astype(jnp.float32)
-    total_ref[...] = total.astype(total_ref.dtype)
+        [valid, part, base],
+    )
+
+
+def sum_kernel(*refs):
+    total = refs[0][...].astype(jnp.float32)
+    for ref in refs[1:-1]:
+        total = total + ref[...].astype(jnp.float32)
+    refs[-1][...] = total.astype(refs[-1].dtype)
 
 
 def sum_pieces(pieces):
+    size = pieces[0].size
     return run(
         sum_kernel,
         (),
-        [in_vmem()],
+        [in_vmem()] * len(pieces),
         in_vmem(),
-        like(pieces.shape[1:], pieces.dtype),
+        like(pieces[0].shape, pieces[0].dtype),
         [],
         "sum_pieces",
-        pieces.size,
-        pieces.size * 3,
-        [pieces],
-    )
-
-
-def feed_back_kernel(up_ref, gate_up_ref, w_gu_ref, w_down_ref, grad_ref, pieces_ref, total):
+        size * len(pieces),
+        size * 2 * (len(pieces) + 1),
+        list(pieces),
+    )
+
+
+def feed_back_kernel(shards, me_ref, up_ref, gate_up_ref, w_gu_ref, *refs):
+    down_refs, (grad_ref, *piece_refs, total) = refs[: -2 - shards], refs[-2 - shards :]
     step = pl.program_id(0)
-    half = w_down_ref.shape[2]
+    half = down_refs[0].shape[3]
     width = gate_up_ref.shape[2] // 2
     upstream = up_ref[...]
-    grad_hidden = proj_t(upstream[:, :half], w_down_ref[0]) + proj_t(upstream[:, half:], w_down_ref[1])
+    grad_hidden = jnp.concatenate(
+        [
+            proj_t(upstream[:, :half], ref[0, 0]) + proj_t(upstream[:, half:], ref[1, 0])
+            for ref in down_refs
+        ],
+        axis=1,
+    )
     gate = gate_up_ref[0, :, :width]
     up = gate_up_ref[0, :, width:]
     sig = sigmoid(gate)
@@ -1293,34 +1387,33 @@
 
     @pl.when(step == pl.num_programs(0) - 1)
     def _():
-        pieces_ref[...] = total[...].astype(jnp.bfloat16).reshape(pieces_ref.shape)
-
-
-def feed_back(upstream, gate_up, w_gu, w_down, shards):
+        hand_out(me_ref, total, piece_refs)
+
+
+def feed_back(me, upstream, gate_up, w_gu, w_cols, shards):
     slices, width, columns = w_gu.shape
     rows = upstream.shape[0]
     hidden = columns // 2
-    half = width // 2
-    return run(
-        feed_back_kernel,
+    sub = rows // shards
+    grad, *pieces = run(
+        functools.partial(feed_back_kernel, shards),
         (slices,),
         [
+            in_smem(),
             held((rows, width)),
             slab((1, rows, columns), 0),
             slab((1, width, columns), 0),
-            slab((2, hidden, half), 1),
-        ],
-        (slab((1, rows, columns), 0), held((shards, rows // shards, width))),
-        (
-            like((slices, rows, columns), jnp.bfloat16),
-            like((shards, rows // shards, width), jnp.bfloat16),
-        ),
+        ]
+        + down_slabs(w_cols, hidden),
+        (slab((1, rows, columns), 0),) + (held((sub, width)),) * shards,
+        (like((slices, rows, columns), jnp.bfloat16),) + (like((sub, width), jnp.bfloat16),) * shards,
         [pltpu.VMEM((rows, width), jnp.float32)],
         "feed_back",
         2 * rows * width * (columns + hidden) * slices,
-        (w_gu.size + w_down.size) * 2 + gate_up.size * 6 + rows * width * 4,
-        [upstream, gate_up, w_gu, w_down],
-    )
+        (w_gu.size + hidden * slices * width) * 2 + gate_up.size * 6 + rows * width * 4,
+        [me, upstream, gate_up, w_gu] + [w_cols] * (hidden // LANES),
+    )
+    return grad, pieces
 
 
 def mid_back_kernel(pieces, *refs):
@@ -1330,7 +1423,7 @@
         mid_ref, up_ref, w_ref, mixed_ref, gate_ref, norm_ref,
         grad_mid_ref, grad_attn_ref, dgain_ref, dmixed_ref, dgate_ref, dnorm_ref,
     ) = refs[2 + pieces :]
-    half = w_ref.shape[2]
+    half = w_ref.shape[3]
 
     @pl.when(pl.program_id(0) == 0)
     def _():
@@ -1344,7 +1437,7 @@
             dgain_ref[...] += dgain
 
     grad = grad_attn_ref[...]
-    grad_gated = proj_t(grad[:, :half], w_ref[0]) + proj_t(grad[:, half:], w_ref[1])
+    grad_gated = proj_t(grad[:, :half], w_ref[0, 0]) + proj_t(grad[:, half:], w_ref[1, 0])
     value = mixed_ref[0].astype(jnp.float32)
     scale = row_scale(value)
     unit = value * scale
@@ -1359,7 +1452,7 @@
     dmixed_ref[0] = dmixed.astype(jnp.bfloat16)
 
 
-def mid_back(me, gain, parts, mid, upstream, w_out, mixed, gate_pre, norm_weight):
+def mid_back(me, gain, parts, mid, upstream, w_cols, mixed, gate_pre, norm_weight):
     slices, rows, _ = mixed.shape
     width = mid.shape[1]
     half = width // 2
@@ -1372,7 +1465,7 @@
         + [
             held((rows, width)),
             held((rows, width)),
-            slab((2, HEAD_V, half), 1),
+            slab((2, 1, HEAD_V, half), 1),
             slab((1, rows, HEAD_V), 0),
             slab((1, rows, HEAD_V), 0),
             held((1, HEAD_V)),
@@ -1396,62 +1489,62 @@
         [],
         "mid_back",
         2 * rows * width * HEAD_V * slices,
-        w_out.size * 2 + rows * width * 20,
-        [me, gain] + list(parts) + [mid, upstream, w_out, mixed, gate_pre, norm_weight],
-    )
-
-
-def project_back_kernel(packed_ref, dgate_ref, w_ref, mix_ref, normed_ref, grad_ref, pieces_ref, dmix_ref, total):
+        slices * HEAD_V * width * 2 + rows * width * 20,
+        [me, gain] + list(parts) + [mid, upstream, w_cols, mixed, gate_pre, norm_weight],
+    )
+
+
+def project_back_kernel(shards, slices, me_ref, piece_ref, *refs):
+    part_refs, refs = refs[:slices], refs[slices:]
+    dgate_ref, w_ref, mix_ref, normed_ref, grad_ref, dmix_ref, *piece_refs, packed, total = refs
     step = pl.program_id(0)
-    grad_ref[0, :, :WIDTH] = packed_ref[0, :, :WIDTH]
+
+    @pl.when(step == 0)
+    def _():
+        for number, part in enumerate(part_refs):
+            packed[piece_ref[0] ^ number] = part[...]
+        total[...] = jnp.zeros_like(total)
+
+    grad_ref[0, :, :WIDTH] = packed[step, :, :WIDTH]
     grad_ref[0, :, WIDTH:] = dgate_ref[0]
-    mix = packed_ref[0, :, WIDTH:]
-    part = proj_t(grad_ref[0], w_ref[0]) + dot(mix, mix_rows(mix_ref))
+    mix = packed[step, :, WIDTH:]
+    total[...] += proj_t(grad_ref[0], w_ref[0]) + dot(mix, mix_rows(mix_ref))
     dmix = inner_t(mix, normed_ref[...])
     dmix_ref[0] = jnp.concatenate([dmix[0:2] + dmix[2:4], dmix[2:8]], axis=0)
 
-    @pl.when(step == 0)
-    def _():
-        total[...] = part
-
-    @pl.when(step > 0)
-    def _():
-        total[...] += part
-
     @pl.when(step == pl.num_programs(0) - 1)
     def _():
-        pieces_ref[...] = total[...].astype(jnp.bfloat16).reshape(pieces_ref.shape)
-
-
-def project_back(packed, dgate, w_proj, w_mix, normed, shards):
+        hand_out(me_ref, total, piece_refs)
+
+
+def project_back(me, piece, packed, dgate, w_proj, w_mix, normed, shards):
     slices, width, columns = w_proj.shape
     rows = normed.shape[0]
-    return run(
-        project_back_kernel,
+    sub = rows // shards
+    grad, dmix, *pieces = run(
+        functools.partial(project_back_kernel, shards, slices),
         (slices,),
-        [
-            slab((1, rows, WIDTH + EXTRA), 0),
+        [in_smem(), in_smem()]
+        + [held((rows, WIDTH + EXTRA))] * slices
+        + [
             slab((1, rows, HEAD_V), 0),
             slab((1, width, columns), 0),
             slab((1, 16, width), 0),
             held((rows, width)),
         ],
-        (
-            slab((1, rows, columns), 0),
-            held((shards, rows // shards, width)),
-            slab((1, 8, width), 0),
-        ),
-        (
-            like((slices, rows, columns), jnp.bfloat16),
-            like((shards, rows // shards, width), jnp.bfloat16),
-            like((slices, 8, width), jnp.float32),
-        ),
-        [pltpu.VMEM((rows, width), jnp.float32)],
+        (slab((1, rows, columns), 0), slab((1, 8, width), 0)) + (held((sub, width)),) * shards,
+        (like((slices, rows, columns), jnp.bfloat16), like((slices, 8, width), jnp.float32))
+        + (like((sub, width), jnp.bfloat16),) * shards,
+        [
+            pltpu.VMEM((slices, rows, WIDTH + EXTRA), jnp.bfloat16),
+            pltpu.VMEM((rows, width), jnp.float32),
+        ],
         "project_back",
         2 * rows * width * columns * slices,
         w_proj.size * 2 + rows * width * 12,
-        [packed, dgate, w_proj, w_mix, normed],
-    )
+        [me, piece] + list(packed) + [dgate, w_proj, w_mix, normed],
+    )
+    return grad, pieces, dmix
 
 
 def norm_back_kernel(pieces, *refs):
@@ -1505,8 +1598,8 @@
 
 def grad_cols_kernel(hidden_ref, up_ref, gated_ref, grad_ref, out_ref):
     rows = hidden_ref.shape[1]
-    out_ref[0, 0, :rows] = inner_t(hidden_ref[...], up_ref[...]).astype(jnp.bfloat16)
-    out_ref[0, 0, rows:] = inner_t(gated_ref[...], grad_ref[...]).astype(jnp.bfloat16)
+    out_ref[0, 0, :-rows] = inner_t(gated_ref[...], grad_ref[...]).astype(jnp.bfloat16)
+    out_ref[0, 0, -rows:] = inner_t(hidden_ref[...], up_ref[...]).astype(jnp.bfloat16)
 
 
 def grad_cols(hidden, upstream, gated, grad_attn, slices):
@@ -1615,14 +1708,14 @@
     side = side_ref[0]
     own = jnp.where(side == 0, layer0_ref[0], layer1_ref[0]).astype(jnp.float32)
     other = received_ref[0].astype(jnp.float32)
-    first = own.shape[0] - out_ref.shape[0]
+    first = out_ref.shape[0]
     columns = own.shape[1]
     here = pl.ds(pl.multiple_of(side * columns, columns), columns)
     there = pl.ds(pl.multiple_of((1 - side) * columns, columns), columns)
-    down_ref[:, here] = own[:hidden]
-    down_ref[:, there] = other[:hidden]
-    out_ref[:, here] = own[first:]
-    out_ref[:, there] = other[first:]
+    down_ref[:, here] = own[first : first + hidden]
+    down_ref[:, there] = other[first : first + hidden]
+    out_ref[:, here] = own[:first]
+    out_ref[:, there] = other[:first]
 
 
 def finish_cols(side, layer0, layer1, received, hidden):
@@ -1644,6 +1737,107 @@
     )
 
 
+def finish_gu_kernel(hidden, side_ref, layer0_ref, layer1_ref, received_ref, gate_ref, up_ref):
+    side = side_ref[0]
+    shards, rows, columns = layer0_ref.shape
+    here = pl.ds(pl.multiple_of(side * rows, rows), rows)
+    there = pl.ds(pl.multiple_of((1 - side) * rows, rows), rows)
+    for s in range(shards):
+        own = jnp.where(side == 0, layer0_ref[s], layer1_ref[s]).astype(jnp.float32)
+        other = received_ref[s].astype(jnp.float32)
+        for start, out_ref in ((0, gate_ref), (columns // 2, up_ref)):
+            out_ref[here, s * hidden : (s + 1) * hidden] = own[:, start : start + hidden]
+            out_ref[there, s * hidden : (s + 1) * hidden] = other[:, start : start + hidden]
+
+
+def finish_gu(side, layer0, layer1, received, hidden):
+    shards, rows, _ = layer0.shape
+    return run(
+        functools.partial(finish_gu_kernel, hidden),
+        (),
+        [in_smem()] + [in_vmem()] * 3,
+        (in_vmem(), in_vmem()),
+        (like((2 * rows, shards * hidden), jnp.float32),) * 2,
+        [],
+        "finish_gu",
+        0,
+        layer0.size * 14,
+        [side, layer0, layer1, received],
+    )
+
+
+def place_tokens_kernel(shards, me_ref, *refs):
+    part_refs, out_ref = refs[:-1], refs[-1]
+    micros, rows, width = part_refs[0].shape
+    columns = width // (2 * shards)
+    for number, part in enumerate(part_refs):
+        where = pl.ds(pl.multiple_of((me_ref[0] ^ number) * rows, rows), rows)
+        for half in range(2):
+            for s in range(shards):
+                source = (half * shards + s) * columns
+                target = (s * 2 + half) * columns
+                for m in range(micros):
+                    out_ref[m, where, target : target + columns] = part[m, :, source : source + columns]
+
+
+def place_tokens(me, parts, shards):
+    micros, sub, width = parts[0].shape
+    shape = (micros, sub * len(parts), width)
+    return run(
+        functools.partial(place_tokens_kernel, shards),
+        (),
+        [in_smem()] + [in_vmem()] * len(parts),
+        in_vmem(),
+        like(shape, parts[0].dtype),
+        [],
+        "place_tokens",
+        0,
+        4 * micros * sub * width * len(parts),
+        [me] + list(parts),
+    )
+
+
+def join_cols_kernel(part_ref, out_ref):
+    out_ref[...] = part_ref[0]
+
+
+def join_cols(part):
+    shards, rows, columns = part.shape
+    return run(
+        join_cols_kernel,
+        (shards,),
+        [slab((1, rows, columns), 0)],
+        slab((rows, columns), 1),
+        like((rows, shards * columns), part.dtype),
+        [],
+        "join_cols",
+        0,
+        part.size * 4,
+        [part],
+    )
+
+
+def split_cols_kernel(whole_ref, out_ref):
+    out_ref[0] = whole_ref[...]
+
+
+def split_cols(whole, shards):
+    rows, width = whole.shape
+    columns = width // shards
+    return run(
+        split_cols_kernel,
+        (shards,),
+        [slab((rows, columns), 1)],
+        slab((1, rows, columns), 0),
+        like((shards, rows, columns), whole.dtype),
+        [],
+        "split_cols",
+        0,
+        whole.size * 4,
+        [whole],
+    )
+
+
 def halves(value, axis):
     step = 1
     while step < lax.axis_size(axis):
@@ -1674,13 +1868,19 @@
     return jnp.concatenate(in_order(by_partner(value, axis), axis), axis=0)
 
 
-def move_pieces(pieces):
-    return lax.all_to_all(pieces, "seq", 0, 0)
-
-
-def exchange(pieces, beside=()):
-    pieces, beside = lax.optimization_barrier((move_pieces(pieces), beside))
-    return by_partner(sum_pieces(pieces), "seq"), beside
+def swap_pieces(pieces, axis):
+    size = lax.axis_size(axis)
+    return [pieces[0]] + [
+        lax.ppermute(pieces[n], axis, [(i, i ^ n) for i in range(size)]) for n in range(1, size)
+    ]
+
+
+def for_partners(parts, me):
+    return [lax.dynamic_index_in_dim(parts, me[0] ^ n, 0, False) for n in range(parts.shape[0])]
+
+
+def exchange(pieces):
+    return by_partner(sum_pieces(swap_pieces(pieces, SEQ)), SEQ)
 
 
 def pick(flag, when, otherwise):
@@ -1688,7 +1888,7 @@
 
 
 def both_layers(local, axis):
-    core = lax.axis_index("section")
+    core = lax.axis_index(SECTION)
     half = local.shape[axis] // 2
     own = lax.dynamic_slice_in_dim(local, core * half, half, axis)
     received = partner(lax.dynamic_slice_in_dim(local, (1 - core) * half, half, axis))
@@ -1697,110 +1897,83 @@
 
 
 def move_rows(part):
-    return lax.all_to_all(part, "seq", 0, 0).reshape(-1, part.shape[2])
+    return lax.all_to_all(part, SEQ, 0, 0).reshape(-1, part.shape[2])
 
 
 def move_cols(part):
-    part = lax.all_to_all(part, "seq", 0, 0)
-    return jnp.swapaxes(part, 0, 1).reshape(part.shape[1], -1)
-
-
-def sent_pieces(part, me):
-    size = lax.axis_size("seq")
-    own = lax.dynamic_index_in_dim(part, me[0], 0, False)
-    return [own] + [
-        lax.ppermute(
-            lax.dynamic_index_in_dim(part, me[0] ^ k, 0, False),
-            "seq",
-            [(i, i ^ k) for i in range(size)],
-        )
-        for k in range(1, size)
-    ]
-
-
-def move_rows_freely(part, me):
-    return place(me, sent_pieces(part, me))
-
-
-def move_cols_freely(part, me):
-    return place_cols(me, sent_pieces(part, me))
+    return join_cols(lax.all_to_all(part, SEQ, 0, 0))
 
 
 def spread_rows(part):
-    full = lax.all_gather(part, ("head", "section"), axis=0, tiled=True)
-    return full.reshape(lax.axis_size("head"), -1, part.shape[1])
+    full = lax.all_gather(part, (HEAD, SECTION), axis=0, tiled=True)
+    return full.reshape(lax.axis_size(HEAD), -1, part.shape[1])
 
 
 def spread_cols(part):
-    full = lax.all_gather(part, ("section", "head"), axis=0, tiled=True)
-    return full.reshape(2, -1, part.shape[1])
+    full = lax.all_gather(part, (SECTION, HEAD), axis=0, tiled=True)
+    return full.reshape(2, lax.axis_size(HEAD), -1, part.shape[1])
 
 
 def reduce_rows(grad):
     return lax.psum_scatter(
-        grad.reshape(-1, grad.shape[2]), ("head", "section"), scatter_dimension=0, tiled=True
+        grad.reshape(-1, grad.shape[2]), (HEAD, SECTION), scatter_dimension=0, tiled=True
     )
 
 
 def reduce_cols(grad):
     return lax.psum_scatter(
-        grad.reshape(-1, grad.shape[2]), ("section", "head"), scatter_dimension=0, tiled=True
+        grad.reshape(-1, grad.shape[2]), (SECTION, HEAD), scatter_dimension=0, tiled=True
     )
 
 
 def collect_rows(part):
-    shards = lax.axis_size("seq")
-    return lax.all_to_all(part.reshape(shards, -1, part.shape[1]), "seq", 0, 0)
+    shards = lax.axis_size(SEQ)
+    return lax.all_to_all(part.reshape(shards, -1, part.shape[1]), SEQ, 0, 0)
 
 
 def collect_cols(part):
-    shards = lax.axis_size("seq")
-    part = jnp.swapaxes(part.reshape(part.shape[0], shards, -1), 0, 1)
-    return lax.all_to_all(part, "seq", 0, 0)
-
-
-def collect_cols_freely(part, me):
-    shards = lax.axis_size("seq")
-    part = jnp.swapaxes(part.reshape(part.shape[0], shards, -1), 0, 1)
-    return place(me, sent_pieces(part, me)).reshape(part.shape)
+    return lax.all_to_all(split_cols(part, lax.axis_size(SEQ)), SEQ, 0, 0)
 
 
 def after(value, other):
     return lax.optimization_barrier((value, other))[0]
 
 
-def layer_backward_fast(me, upstream, saved, gains, weights, small, aux, parts, plan):
-    before_mid, early_gu, start, then = plan
+def layer_backward_fast(me, piece, upstream, saved, gains, weights, small, aux, parts, plan):
+    at_mid, sum_rows, start, at_end, at_out, sum_cols, before_end, last_due = plan
     attn_gain, mlp_gain = gains
-    w_proj, w_mix, w_out, w_gu, w_down = weights
+    w_proj, w_mix, w_cols, w_gu = weights
     taps, scal, norm_weight = small
     resid, normed, gate_pre, mixer, mid, ffn_in, gate_up, hidden = saved
     xh, states, inverse, mixed, gated = mixer
     shards = parts[0]
     slices, rows, _ = mixed.shape
-    grad_gate_up, pieces = feed_back(upstream, gate_up, w_gu, w_down, shards)
+    grad_gate_up, pieces = feed_back(me, upstream, gate_up, w_gu, w_cols, shards)
     grad_gu = grad_rows(ffn_in, grad_gate_up)
-    sums, _ = exchange(pieces, grad_gu)
-    sums, sum_gu = before_mid(sums, grad_gu)
+    pieces = swap_pieces(pieces, SEQ)
+    pieces, _ = lax.optimization_barrier((pieces, grad_gu))
+    sums = at_mid(by_partner(sum_pieces(pieces), SEQ))
     grad_mid, grad_attn, dmlp, dmixed, dgate, dnorm = mid_back(
-        me, mlp_gain, sums, mid, upstream, w_out, mixed, gate_pre, norm_weight
+        me, mlp_gain, sums, mid, upstream, w_cols, mixed, gate_pre, norm_weight
     )
     grad_both = grad_cols(hidden, upstream, gated, grad_attn, slices)
-    grad_head = lax.all_to_all(dmixed, "head", 0, 0).reshape(slices * rows, HEAD_V)
-    grad_head, grad_both, sum_gu = early_gu(grad_head, grad_both, sum_gu)
-    running = start(grad_head)
-    dxh, dtaps, dscal = recur_backward(xh, aux, taps, scal, states, inverse, grad_head, parts)
-    dxh, running = lax.optimization_barrier((dxh, running))
-    packed = lax.all_to_all(dxh.reshape(slices, rows, WIDTH + EXTRA), "head", 0, 0)
-    packed, sum_gu = lax.optimization_barrier((packed, sum_gu))
-    sum_both = reduce_cols(after(grad_both, sum_gu))
-    running = then(running)
-    grad_pre, pieces, dmix = project_back(packed, dgate, w_proj, w_mix, normed, shards)
+    grad_head = swap_pieces(for_partners(dmixed, piece), HEAD)
+    grad_head, grad_both = lax.optimization_barrier((grad_head, grad_both))
+    sum_gu = sum_rows(grad_gu, dmixed)
+    running = start(grad_head, sum_gu)
+    dxh, dtaps, dscal = recur_backward(piece, xh, grad_head, aux, taps, scal, states, inverse, parts)
+    dxh, running = at_end(dxh, running, sum_gu)
+    packed = swap_pieces(dxh, HEAD)
+    grad_pre, pieces, dmix = project_back(me, piece, packed, dgate, w_proj, w_mix, normed, shards)
+    pieces, running = at_out(pieces, running)
     grad_proj = grad_rows(normed, grad_pre)
-    sums, _ = exchange(pieces, grad_proj)
-    sums, sum_both, running = lax.optimization_barrier((sums, sum_both, running))
-    sum_proj = reduce_rows(after(grad_proj, sum_both))
+    pieces = swap_pieces(pieces, SEQ)
+    pieces, _ = lax.optimization_barrier((pieces, grad_proj))
+    sums, sum_both = sum_cols(grad_both, (sum_gu, dxh), pieces)
+    sums, running = lax.optimization_barrier((sums, running))
+    sums = before_end(sums)
     grad_resid, dattn = norm_back(me, attn_gain, sums, resid, grad_mid)
+    sum_proj = reduce_rows(after(grad_proj, last_due(sum_both, sums, sum_gu, grad_resid)))
     small_grads = (dtaps[:CONVK], dscal[0, :2], dnorm[0], dattn[0], dmlp[0], dmix[:, :2])
     return grad_resid, (sum_proj, sum_gu, sum_both), small_grads, running
 
@@ -1829,11 +2002,11 @@
     w_up,
     w_down,
 ):
-    core = lax.axis_index("section")
+    core = lax.axis_index(SECTION)
     first = core == 0
-    shard = lax.axis_index("seq")
-    piece = lax.axis_index("head")
-    shards, slices = lax.axis_size("seq"), lax.axis_size("head")
+    shard = lax.axis_index(SEQ)
+    piece = lax.axis_index(HEAD)
+    shards, slices = lax.axis_size(SEQ), lax.axis_size(HEAD)
     parts = (shards, slices)
     shard_rows = w_query.shape[1]
     model_width = tokens.shape[2]
@@ -1864,15 +2037,17 @@
         [jnp.pad(columns(w_gate[0], hidden_width), fill), jnp.pad(columns(w_up[0], hidden_width), fill)],
         axis=2,
     )
-    out_local = w_output[0].reshape(shards, HEAD_V, shard_rows)
-    down_local = jnp.pad(
-        w_down[0].reshape(shards, hidden_width, shard_rows),
-        ((0, 0), (0, hidden_padded - hidden_width), (0, 0)),
+    cols_local = jnp.concatenate(
+        [
+            w_output[0].reshape(shards, HEAD_V, shard_rows),
+            w_down[0].reshape(shards, hidden_width, shard_rows),
+            jnp.zeros((shards, hidden_padded - hidden_width, shard_rows), jnp.bfloat16),
+        ],
+        axis=1,
     )
     proj_parts = both_layers(proj_local, 1)
-    out_parts = both_layers(out_local, 2)
+    cols_parts = both_layers(cols_local, 2)
     gu_parts = both_layers(gu_local, 1)
-    down_parts = both_layers(down_local, 2)
 
     conv = jnp.concatenate(
         [
@@ -1894,6 +2069,7 @@
             w_beta[0].astype(jnp.float32).T.reshape(-1),
         ]
     )
+    small_own = after(small_own, proj_parts[0])
     small_other = partner(small_own)
     small_layers = (pick(first, small_own, small_other), pick(first, small_other, small_own))
     taps_size = CONVK * WIDTH
@@ -1901,7 +2077,7 @@
     gain_at = norm_at + HEAD_V
     wide = jnp.stack([vector[gain_at:] for vector in small_layers])
     wide = jnp.concatenate([wide.reshape(-1), valid_mask[core].astype(jnp.float32)])
-    wide = gathered(wide[None], "seq")
+    wide = gathered(wide[None], SEQ)
     valid_all = wide[:, wide.shape[1] - tokens.shape[1] :].reshape(shards, slices, sub)
     valid = lax.dynamic_index_in_dim(valid_all, piece, 1, False).reshape(-1)
     wide = wide[:, : wide.shape[1] - tokens.shape[1]].reshape(shards, 2, 2 + 2 * shards, 2, shard_rows // 2)
@@ -1909,7 +2085,7 @@
     mix_all = wide[:, :, 2:].reshape(shards, 2, 2, shards, 2, shard_rows // 2)
     mix_all = lax.dynamic_index_in_dim(mix_all, shard, 3, False)
     mix_all = jnp.transpose(mix_all, (1, 2, 3, 0, 4)).reshape(2, 2, model_width).astype(jnp.bfloat16)
-    mix_all = gathered(mix_all[None], "head")
+    mix_all = gathered(mix_all[None], HEAD)
     mix_all = jnp.swapaxes(mix_all, 0, 1)
     mix_all = jnp.concatenate(
         [mix_all, mix_all, jnp.zeros((2, slices, 12, model_width), jnp.bfloat16)], axis=2
@@ -1926,157 +2102,170 @@
 
     def my_tokens(value):
         mine = lax.dynamic_slice_in_dim(value, piece * sub, sub, 0)
-        return by_partner(halved(mine), "seq")
+        return by_partner(halved(mine), SEQ)
 
     me = shard[None].astype(jnp.int32)
+    place_at = piece[None].astype(jnp.int32)
     valid = valid[:, None]
     aux = make_aux(doc_starts[core], length)
     masked = cotangent[core] * valid_mask[core].astype(jnp.bfloat16)[:, None]
 
     token_parts, base = my_tokens(tokens[core]), None
-    proj0 = after(move_rows(proj_parts[0]), (token_parts, gains, small, valid))
-    out0 = move_cols(after(out_parts[0], proj0))
-    gu0 = move_rows(after(gu_parts[0], out0))
-    down0 = move_cols_freely(after(down_parts[0], gu0), me)
-    weights = [
-        (spread_rows(proj0), mix_all[0], spread_cols(out0), spread_rows(gu0), None)
-    ]
+    proj0 = after(move_rows(proj_parts[0]), (small_layers, cols_parts, gu_parts))
+    cols0 = lax.all_to_all(after(cols_parts[0], proj0), SEQ, 0, 0)
+    cols0 = join_cols(after(cols0, (token_parts, gains, small, valid, mix_all)))
+    gu0 = move_rows(after(gu_parts[0], cols0))
+    weights = [(spread_rows(proj0), mix_all[0], spread_cols(cols0), None)]
 
     saved = []
     stats = []
     for layer in range(2):
-        w_proj, w_mix, w_out, w_gu, w_down = weights[layer]
+        w_proj, w_mix, w_cols, w_gu = weights[layer]
         attn_gain, mlp_gain = gains[layer]
         resid, normed, packed, gate_pre, stat = project(
             me, valid, attn_gain, token_parts, base, w_proj, w_mix
         )
         stats.append(stat)
-        xh = lax.all_to_all(packed, "head", 0, 0).reshape(slices * valid.shape[0], WIDTH + EXTRA)
+        xh = swap_pieces(for_partners(packed, place_at), HEAD)
         if layer == 0:
-            xh, down0 = lax.optimization_barrier((xh, down0))
-            w_down = spread_cols(down0)
-            weights[0] = (w_proj, w_mix, w_out, w_gu, w_down)
-            proj1 = move_rows(after(proj_parts[1], xh))
-            out1 = move_cols_freely(after(out_parts[1], xh), me)
-            down1 = move_cols_freely(after(down_parts[1], xh), me)
+            xh, gu0 = lax.optimization_barrier((xh, gu0))
+            w_gu = spread_rows(gu0)
+            weights[0] = (w_proj, w_mix, w_cols, w_gu)
+            masked = my_tokens(after(masked, gu0))
+        mixed, states, inverse = recur_forward(place_at, xh, aux, *small[layer][:2], parts)
+        mixed = swap_pieces(mixed, HEAD)
+        if layer == 0:
+            mixed, masked = lax.optimization_barrier((mixed, masked))
+            proj1 = move_rows(after(proj_parts[1], mixed))
         else:
-            gu1 = move_rows_freely(after(gu_parts[1], xh), me)
-            masked = my_tokens(after(masked, xh))
-        mixed_head, states, inverse = recur_forward(xh, aux, *small[layer][:2], parts)
+            mixed, gu1 = lax.optimization_barrier((mixed, gu1))
+            w_gu = spread_rows(gu1)
+            weights[1] = (w_proj, w_mix, w_cols, w_gu)
+        gated, kept, pieces = output(me, place_at, mixed, gate_pre, small[layer][2], w_cols, shards)
+        mixer = (xh, states, inverse, kept, gated)
+        mix_parts = exchange(pieces)
         if layer == 0:
-            mixed_head, proj1 = lax.optimization_barrier((mixed_head, proj1))
-        else:
-            mixed_head, gu1, masked = lax.optimization_barrier((mixed_head, gu1, masked))
-            w_gu = spread_rows(gu1)
-            weights[1] = (w_proj, w_mix, w_out, w_gu, w_down)
-        mixed = lax.all_to_all(mixed_head.reshape(gate_pre.shape), "head", 0, 0)
-        gated, pieces = output(mixed, gate_pre, small[layer][2], w_out, shards)
-        mixer = (xh, states, inverse, mixed, gated)
-        mix_parts, _ = exchange(pieces)
+            mix_parts, proj1 = lax.optimization_barrier((mix_parts, proj1))
         base, ffn_in, gate_up, hidden, pieces, stat = feed(
-            me, valid, mlp_gain, mix_parts, resid, w_gu, w_down, shards
+            me, valid, mlp_gain, mix_parts, resid, w_gu, w_cols
         )
         stats.append(stat)
         saved.append((resid, normed, gate_pre, mixer, base, ffn_in, gate_up, hidden))
         if layer == 0:
-            pieces, out1, down1 = lax.optimization_barrier((pieces, out1, down1))
-            weights.append(
-                (spread_rows(proj1), mix_all[1], spread_cols(out1), None, spread_cols(down1))
-            )
-            token_parts, _ = exchange(pieces)
+            cols1 = move_cols(after(cols_parts[1], pieces))
+            token_parts = exchange(pieces)
+            token_parts, cols1 = lax.optimization_barrier((token_parts, cols1))
+            gu1 = move_rows(after(gu_parts[1], token_parts))
+            weights.append((spread_rows(proj1), mix_all[1], spread_cols(cols1), None))
     h1 = saved[1][0]
-    stats0 = jnp.stack([stats[2][0, 0], stats[1][0, 0], stats[2][0, 1]])
+    stats0 = jnp.stack([stats[2][0, 0], stats[1][0, 0], stats[2][0, 1]]) / shards
     upstream = place(me, masked)
     def placed_tokens(layer0, layer1):
         layer0, layer1 = (
-            lax.dynamic_slice_in_dim(value, shard * sub, sub, 0) for value in (layer0, layer1)
+            value if value.shape[0] == sub else lax.dynamic_slice_in_dim(value, shard * sub, sub, 0)
+            for value in (layer0, layer1)
         )
         keep = pick(first, layer0, layer1)
         received = partner(pick(first, layer1, layer0))
         both = jnp.stack([pick(first, keep, received), pick(first, received, keep)])
-        pieces = jnp.stack(in_order(by_partner(both, "head"), "head"), axis=1)
-        pieces = pieces.reshape(2, slices * sub, 2, shards, model_width // (2 * shards))
-        return jnp.swapaxes(pieces, 2, 3).reshape(2, slices * sub, model_width)
+        return place_tokens(piece[None].astype(jnp.int32), by_partner(both, HEAD), shards)
+
+    early = {}
+
+    def all_sums(pieces):
+        return by_partner(sum_pieces(pieces), SEQ)
 
     def plan_last():
-        def before_mid(sums, grad_gu):
-            return sums, reduce_rows(grad_gu)
-
-        def early_gu(grad_head, grad_both, sum_gu):
-            return lax.optimization_barrier((grad_head, grad_both, sum_gu))
-
-        def start(anchor):
-            return move_pieces(after(pieces, anchor))
-
-        def then(moved):
-            return by_partner(sum_pieces(moved), "seq")
-
-        return before_mid, early_gu, start, then
-
-    grad_h1, big1, small1, last_parts = layer_backward_fast(
-        me, upstream, saved[1], gains[1], weights[1], small[1], aux, parts, plan_last()
+        def at_mid(sums):
+            return sums
+
+        def sum_rows(grad_gu, anchor):
+            return reduce_rows(grad_gu)
+
+        def start(anchor, sum_gu):
+            return swap_pieces(after(pieces, anchor), SEQ)
+
+        def at_end(dxh, running, sum_gu):
+            dxh, running = lax.optimization_barrier((dxh, running))
+            return dxh, (running, collect_rows(after(sum_gu, dxh)))
+
+        def at_out(pieces, running):
+            return lax.optimization_barrier((pieces, running))
+
+        def sum_cols(grad_both, due, pieces):
+            sum_both = reduce_cols(after(grad_both, due))
+            return lax.optimization_barrier((all_sums(pieces), sum_both))
+
+        def before_end(sums):
+            return sums
+
+        def last_due(sum_both, sums, sum_gu, grad_resid):
+            return sum_both, sums
+
+        return at_mid, sum_rows, start, at_end, at_out, sum_cols, before_end, last_due
+
+    grad_h1, big1, small1, (last_sum, moved_gu1) = layer_backward_fast(
+        me, place_at, upstream, saved[1], gains[1], weights[1], small[1], aux, parts, plan_last()
     )
     sum_proj1, sum_gu1, sum_both1 = big1
-    act1, stat = close(me, valid, last_parts, base)
-    stats1 = jnp.stack([stat[0, 0], stats[3][0, 0], stat[0, 1]])
+    last_sum = sum_pieces(last_sum)
+    moved_both1 = collect_cols(after(sum_both1, grad_h1))
+    here = shard * sub
+    valid_here = lax.dynamic_slice_in_dim(valid, here, sub, 0)
+    act1, stat = close(valid_here, last_sum, lax.dynamic_slice_in_dim(base, here, sub, 0))
+    stats1 = jnp.stack([stat[0, 0], stats[3][0, 0] / shards, stat[0, 1]])
     activations = placed_tokens(h1, act1)
-    early = {}
 
     def plan_first():
-        def before_mid(sums, grad_gu):
-            sums, early["proj"], early["activations"] = lax.optimization_barrier(
-                (sums, sum_proj1, activations)
-            )
-            return sums, reduce_rows(after(grad_gu, early["proj"]))
-
-        def early_gu(grad_head, grad_both, sum_gu):
-            grad_head, grad_both = lax.optimization_barrier((grad_head, grad_both))
-            return grad_head, grad_both, sum_gu
-
-        def start(anchor):
-            gu = collect_rows(after(sum_gu1, anchor))
-            both = collect_cols_freely(after(sum_both1, anchor), me)
-            early["both"] = both
-            return gu
-
-        def then(moved):
-            return moved, early["both"]
-
-        return before_mid, early_gu, start, then
-
-    grad_tokens, big0, small0, (moved_gu1, moved_both1) = layer_backward_fast(
-        me, grad_h1, saved[0], gains[0], weights[0], small[0], aux, parts, plan_first()
+        def at_mid(sums):
+            sums, early["both"] = lax.optimization_barrier((sums, moved_both1))
+            return sums
+
+        def sum_rows(grad_gu, anchor):
+            return reduce_rows(after(grad_gu, (sum_proj1, anchor)))
+
+        def start(anchor, sum_gu):
+            return collect_rows(after(sum_proj1, anchor))
+
+        def at_end(dxh, running, sum_gu):
+            return lax.optimization_barrier((dxh, running))
+
+        def at_out(pieces, running):
+            return pieces, running
+
+        def sum_cols(grad_both, due, pieces):
+            sum_both = reduce_cols(after(grad_both, (due, pieces)))
+            return all_sums(pieces), sum_both
+
+        def before_end(sums):
+            return sums
+
+        def last_due(sum_both, sums, sum_gu, grad_resid):
+            early["gu"] = collect_rows(after(sum_gu, grad_resid))
+            return sum_both, early["gu"], placed_tokens(grad_resid, grad_h1)
+
+        return at_mid, sum_rows, start, at_end, at_out, sum_cols, before_end, last_due
+
+    grad_tokens, big0, small0, moved_proj1 = layer_backward_fast(
+        me, place_at, grad_h1, saved[0], gains[0], weights[0], small[0], aux, parts, plan_first()
     )
     sum_proj0, sum_gu0, sum_both0 = big0
-    activations = early["activations"]
-    moved_proj1 = collect_rows(after(early["proj"], sum_both0))
-    moved_gu0 = collect_rows(after(sum_gu0, moved_proj1))
+    moved_both1 = early["both"]
+    moved_gu0 = early["gu"]
     moved_both0 = collect_cols(after(sum_both0, moved_gu0))
-    moved_proj0 = collect_rows(sum_proj0)
-
     input_grads = placed_tokens(grad_tokens, grad_h1)
-
-    def joined(layer0, layer1, axis):
-        keep = pick(first, layer0, layer1)
-        received = partner(pick(first, layer1, layer0))
-        return jnp.concatenate(
-            [pick(first, keep, received), pick(first, received, keep)], axis=axis
-        ).astype(jnp.float32)
-
     side = core[None].astype(jnp.int32)
     grad_down, grad_out = finish_cols(
         side, moved_both0, moved_both1, partner(pick(first, moved_both1, moved_both0)), hidden_width
     )
-    grad_gu = joined(moved_gu0, moved_gu1, 1)
-    grad_proj = finish_rows(
-        side, moved_proj0, moved_proj1, partner(pick(first, moved_proj1, moved_proj0)),
-        (HEAD_K, HEAD_K, HEAD_V, HEAD_V),
+    grad_gate, grad_up = finish_gu(
+        side, moved_gu0, moved_gu1, partner(pick(first, moved_gu1, moved_gu0)), hidden_width
     )
 
     def pack(grads, sums):
         dtaps, dscal, dnorm, dattn, dmlp, dmix = grads
         place = (jnp.arange(2) == core)[:, None]
-        marked = jnp.where(place, jnp.concatenate([sums, jnp.sum(valid)[None]])[None], 0.0)
+        marked = jnp.where(place, jnp.concatenate([sums, (jnp.sum(valid) / shards)[None]])[None], 0.0)
         return jnp.concatenate(
             [dtaps.reshape(-1), dscal, dnorm, marked.reshape(-1), dattn, dmlp, dmix.reshape(-1)]
         )
@@ -2084,25 +2273,30 @@
     packs = (pack(small0, stats0), pack(small1, stats1))
     vector = pick(first, packs[0], packs[1]) + partner(pick(first, packs[1], packs[0]))
     gain_end = norm_at + HEAD_V + 8 + 2 * model_width
-    per_head = gathered(vector[None, :norm_at], "seq")
-    sums_all = halves(vector[norm_at:gain_end], "head")
-    norm_sum = halves(sums_all[:HEAD_V], "seq")
-    stat_sums = sums_all[HEAD_V : HEAD_V + 8].reshape(2, 4)
+    per_head = gathered(vector[None, :norm_at], SEQ)
+    sums_all = halves(vector[norm_at:gain_end], HEAD)
+    norm_sum = halves(sums_all[: HEAD_V + 8], SEQ)
+    stat_sums = norm_sum[HEAD_V:].reshape(2, 4)
+    norm_sum = norm_sum[:HEAD_V]
     gain_sums = sums_all[HEAD_V + 8 :].reshape(2, 2, shards, shard_rows // 2)
     gain_sums = lax.dynamic_index_in_dim(gain_sums, shard, 2, False).reshape(2, shard_rows)
     branch_rms = jnp.sqrt(stat_sums[:, :3] / jnp.maximum(stat_sums[:, 3:], 1.0))
     mix_grad = vector[gain_end:].reshape(slices, 2, 2, shards, shard_rows // 2)
-    mix_grad = jnp.sum(lax.all_to_all(mix_grad, "head", 0, 0), axis=0)
-    mix_grad = lax.all_to_all(jnp.transpose(mix_grad, (2, 0, 1, 3)), "seq", 0, 0)
+    mix_grad = jnp.sum(lax.all_to_all(mix_grad, HEAD, 0, 0), axis=0)
+    mix_grad = lax.all_to_all(jnp.transpose(mix_grad, (2, 0, 1, 3)), SEQ, 0, 0)
     mix_grad = jnp.transpose(mix_grad, (1, 2, 3, 0)).reshape(2, shard_rows, shards)
+    others = (input_grads, grad_down, grad_out, grad_gate, grad_up, mix_grad, norm_sum, gain_sums, per_head)
+    sum_proj0, others = lax.optimization_barrier((sum_proj0, others))
+    input_grads, grad_down, grad_out, grad_gate, grad_up, mix_grad, norm_sum, gain_sums, per_head = others
+    moved_proj0 = collect_rows(sum_proj0)
+    grad_proj = finish_rows(
+        side, moved_proj0, moved_proj1, partner(pick(first, moved_proj1, moved_proj0)),
+        (HEAD_K, HEAD_K, HEAD_V, HEAD_V),
+    )
     conv_grad = jnp.swapaxes(per_head[:, :taps_size].reshape(shards, CONVK, WIDTH), 0, 1)
 
     def conv_part(start, width):
         return conv_grad[:, :, start : start + width].reshape(1, CONVK, shards * width)
-
-    def gu_part(start):
-        part = jnp.swapaxes(grad_gu[:, :, start : start + hidden_width], 0, 1)
-        return part.reshape(1, shard_rows, shards * hidden_width)
 
     return (
         activations[None],
@@ -2123,8 +2317,8 @@
         norm_sum[None],
         grad_out[None],
         gain_sums[1][None],
-        gu_part(0),
-        gu_part(hidden_padded),
+        grad_gate[None],
+        grad_up[None],
         grad_down[None],
     )
 
@@ -2132,7 +2326,7 @@
 def per_device(*args):
     tokens, w_decay = args[0], args[9]
     rows = tokens.shape[1]
-    seq, head, section = (lax.axis_size(axis) for axis in ("seq", "head", "section"))
+    seq, head, section = (lax.axis_size(axis) for axis in (SEQ, HEAD, SECTION))
     one_head_each = w_decay.shape[2] == seq
     micro_each = tokens.shape[0] == section == 2
     powers = seq & (seq - 1) == 0 and head & (head - 1) == 0
@@ -2144,55 +2338,55 @@
 
 def solution(mesh):
     placed = (
-        P(None, "seq", None),
-        P(None, "seq", None),
+        P(None, SEQ, None),
+        P(None, SEQ, None),
         P(),
-        P(None, "seq"),
-        P("section", "seq"),
-        P("section", "seq", "head"),
-        P("section", "seq", "head"),
-        P("section", "seq", "head"),
-        P("section", "seq", "head"),
-        P("section", "seq", "head"),
-        P("section", "seq", "head"),
-        P("section", None, "head"),
-        P("section", None, "head"),
-        P("section", None, "head"),
-        P("section", "head"),
-        P("section", "head"),
-        P("section", None),
-        P("section", "head", "seq"),
-        P("section", "seq"),
-        P("section", "seq", "head"),
-        P("section", "seq", "head"),
-        P("section", "head", "seq"),
+        P(None, SEQ),
+        P(SECTION, SEQ),
+        P(SECTION, SEQ, HEAD),
+        P(SECTION, SEQ, HEAD),
+        P(SECTION, SEQ, HEAD),
+        P(SECTION, SEQ, HEAD),
+        P(SECTION, SEQ, HEAD),
+        P(SECTION, SEQ, HEAD),
+        P(SECTION, None, HEAD),
+        P(SECTION, None, HEAD),
+        P(SECTION, None, HEAD),
+        P(SECTION, HEAD),
+        P(SECTION, HEAD),
+        P(SECTION, None),
+        P(SECTION, HEAD, SEQ),
+        P(SECTION, SEQ),
+        P(SECTION, SEQ, HEAD),
+        P(SECTION, SEQ, HEAD),
+        P(SECTION, HEAD, SEQ),
     )
     return jax.shard_map(
         per_device,
         mesh=mesh,
         in_specs=placed,
         out_specs=(
-            P("section", None, "seq", None),
-            P("section", None, "seq", None),
-            P("section", None, None),
-            P("section", "seq"),
-            P("section", "seq", "head"),
-            P("section", "seq", "head"),
-            P("section", "seq", "head"),
-            P("section", "seq", "head"),
-            P("section", "seq", "head"),
-            P("section", "seq", "head"),
-            P("section", None, "head"),
-            P("section", None, "head"),
-            P("section", None, "head"),
-            P("section", "head"),
-            P("section", "head"),
-            P("section", None),
-            P("section", "head", "seq"),
-            P("section", "seq"),
-            P("section", "seq", "head"),
-            P("section", "seq", "head"),
-            P("section", "head", "seq"),
+            P(SECTION, None, SEQ, None),
+            P(SECTION, None, SEQ, None),
+            P(SECTION, None, None),
+            P(SECTION, SEQ),
+            P(SECTION, SEQ, HEAD),
+            P(SECTION, SEQ, HEAD),
+            P(SECTION, SEQ, HEAD),
+            P(SECTION, SEQ, HEAD),
+            P(SECTION, SEQ, HEAD),
+            P(SECTION, SEQ, HEAD),
+            P(SECTION, None, HEAD),
+            P(SECTION, None, HEAD),
+            P(SECTION, None, HEAD),
+            P(SECTION, HEAD),
+            P(SECTION, HEAD),
+            P(SECTION, None),
+            P(SECTION, HEAD, SEQ),
+            P(SECTION, SEQ),
+            P(SECTION, SEQ, HEAD),
+            P(SECTION, SEQ, HEAD),
+            P(SECTION, HEAD, SEQ),
         ),
         check_vma=False,
     )

time: 1500 us -> 1320 us (0.88)
  blocking collectives: 178 us -> 0 us
  waiting for transfers between devices: 496 us -> 589 us
  Pallas kernels: 357 us -> 285 us
  local copies, waits for them, and re-layouts: 193 us -> 152 us
  starting transfers between devices: 206 us -> 229 us
    all_to_all x7 -> x0, blocking collectives: 178 us -> none  [the longest x3 74.7 us: move_pieces(): return lax.all_to_all(pieces, 'seq', 0, 0)]
    ppermute x15 -> x48, waiting for transfers between devices: 70.2 us -> 223 us  [swap_pieces(): lax.ppermute(pieces[n], axis, [(i, i ^ n) for i in range(size)])]
    all_to_all x20 -> x14, waiting for transfers between devices: 174 us -> 105 us  [the longest x4 39.2 us: move_rows(): return lax.all_to_all(part, SEQ, 0, 0).reshape(-1, part.shape[2])]
    pallas_call x2, Pallas kernels: 86.4 us -> 38.9 us  [recur_forward(): pl.pallas_call(functools.partial(forward_kernel, parts), out_shape=(jax.S...]
    ppermute x45 -> x42, waiting for transfers between devices: 151 us -> 198 us  [by_partner(): lax.ppermute(value, axis, [(i, i ^ k) for i in range(size)])]
    ppermute x45 -> x42, starting transfers between devices: 66.8 us -> 108 us  [by_partner(): lax.ppermute(value, axis, [(i, i ^ k) for i in range(size)])]
    pallas_call x2, Pallas kernels: 91.7 us -> 62.5 us  [recur_backward(): pl.pallas_call(functools.partial(backward_kernel, parts), out_shape=(jax....]
    unnamed x16 -> x12, waiting for transfers between devices: 26 us -> 0.2 us
  transfers between devices with their start and end apart: 109 -> 130, of which waited for: 46 -> 61; matrix products, arithmetic and copies ran while one was open for 10% -> 6% of each run, Pallas kernels for 21% -> 19%
where the time goes in v3:
time: 1320 us; the launch traced here: 1310 us
  waiting for transfers between devices  589 us (45%)
  Pallas kernels  285 us (22%)
  starting transfers between devices  229 us (17%)
  local copies, waits for them, and re-layouts  152 us (12%)
  other arithmetic  39.9 us (3%)
  between operations  17.6 us (1%)
    ppermute x48, waiting for transfers between devices, swap_pieces(): lax.ppermute(pieces[n], axis, [(i, i ^ n) for i in range(size)])  223 us
    ppermute x42, waiting for transfers between devices, by_partner(): lax.ppermute(value, axis, [(i, i ^ k) for i in range(size)])  198 us
    pallas_call x39, Pallas kernels, run(): pl.pallas_call(kernel, grid=grid, in_specs=in_specs, out_specs=out_specs,...  183 us
    unnamed x445, local copies, waits for them, and re-layouts  115 us
    ppermute x42, starting transfers between devices, by_partner(): lax.ppermute(value, axis, [(i, i ^ k) for i in range(size)])  108 us
    pallas_call x2, Pallas kernels, recur_backward(): pl.pallas_call(functools.partial(backward_kernel, parts), out_shape=(jax....  62.5 us
    ppermute x48, starting transfers between devices, swap_pieces(): lax.ppermute(pieces[n], axis, [(i, i ^ n) for i in range(size)])  49.9 us
    all_to_all x4, waiting for transfers between devices, move_rows(): return lax.all_to_all(part, SEQ, 0, 0).reshape(-1, part.shape[2])  39.2 us
  transfers between devices with their start and end apart: 130, of which 61 were waited for; matrix products, arithmetic and copies ran while one was open for 6% of the time, Pallas kernels for 19%

profile of v3, /device:TPU:1, one launch (start us, length us, event | category | flops | bytes accessed | tf_op | source)
XLA Modules:
  0.0 1312.2 jit_solution(9792142607173491552)
XLA Ops:
  44.7 23.7 %all-to-all-done = bf16[4,256,768]{2,1,0:T(8,128)(2,1)} async-done(((bf16[4,256,768]{2,1,0:T(8,128)(2,1)}), bf16[4,256,768]{2,1,0:T(8,128)(2,1)}, u32[]{:S(2)}, u32[]{:S(2)}) %all-to-all-start) | async-done | bytes 1572896 | tf_op jit(solution)/shard_map/all_to_all | solution.py:1900
  81.4 12.0 collective-permute-done.3
  104.0 18.0 %collective-permute-done.5.refs_4_ = bf16[64,2048]{1,0:T(8,128)(2,1)S(1)} collective-permute-done((bf16[64,2048]{1,0:T(8,128)(2,1)S(1)}, bf16[64,2048]{1,0:T(8,128)(2,1)S(1)}, u32[]{:S(2)}, u32[]{:S(2)}) %collective-permute-start.5) | collective-permute-done | bytes 262176 | tf_op jit(solution)/shard_map/ppermute | solution.py:1852
  142.1 8.5 project_first.1
  155.3 15.5 %all-to-all-done.2 = bf16[4,256,768]{2,1,0:T(8,128)(2,1)} async-done(((bf16[4,256,768]{2,1,0:T(8,128)(2,1)}), bf16[4,256,768]{2,1,0:T(8,128)(2,1)}, u32[]{:S(2)}, u32[]{:S(2)}) %all-to-all-start.2) | async-done | bytes 1572896 | tf_op jit(solution)/shard_map/all_to_all | solution.py:1900
  188.8 19.8 %recur_forward.2 = (bf16[256,256]{1,0:T(8,128)(2,1)S(1)}, bf16[256,256]{1,0:T(8,128)(2,1)}, bf16[256,256]{1,0:T(8,128)(2,1)S(1)}, bf16[256,256]{1,0:T(8,128)(2,1...) custom-call(s32[1]{0:T(128)} %bitcast.piece_ref.me_ref, bf16[256,640]{1,0:T(8,128)(2,1)S(1)} %get-tuple-element.271.refs_0_, ...), custom_call_target="tpu_custom_call" | custom-call | flops 40960000000 | bytes 8388608 | tf_op jit(solution)/shard_map/recur_forward/pallas_call | solution.py:980
  226.5 12.0 collective-permute-done.20.refs_3_
  253.9 19.0 %collective-permute-done.22.refs_1_ = bf16[64,2048]{1,0:T(8,128)(2,1)S(1)} collective-permute-done((bf16[64,2048]{1,0:T(8,128)(2,1)S(1)}, bf16[64,2048]{1,0:T(8,128)(2,1)S(1)}, u32[]{:S(2)}, u32[]{:S(2)}) %collective-permute-start.22) | collective-permute-done | bytes 262176 | tf_op jit(solution)/shard_map/ppermute | solution.py:1874
  272.9 23.1 %collective-permute-done.23.refs_2_ = bf16[64,2048]{1,0:T(8,128)(2,1)S(1)} collective-permute-done((bf16[64,2048]{1,0:T(8,128)(2,1)S(1)}, bf16[64,2048]{1,0:T(8,128)(2,1)S(1)}, u32[]{:S(2)}, u32[]{:S(2)}) %collective-permute-start.23) | collective-permute-done | bytes 262176 | tf_op jit(solution)/shard_map/ppermute | solution.py:1874
  296.7 12.3 collective-permute-start.26
  309.0 16.9 %collective-permute-done.26.refs_5_ = bf16[64,2048]{1,0:T(8,128)(2,1)S(1)} collective-permute-done((bf16[64,2048]{1,0:T(8,128)(2,1)S(1)}, bf16[64,2048]{1,0:T(8,128)(2,1)S(1)}, u32[]{:S(2)}, u32[]{:S(2)}) %collective-permute-start.26) | collective-permute-done | bytes 262176 | tf_op jit(solution)/shard_map/ppermute | solution.py:1852
  326.0 14.3 %feed.2 = (f32[256,2048]{1,0:T(8,128)}, bf16[256,2048]{1,0:T(8,128)(2,1)S(1)}, f32[4,256,768]{2,1,0:T(8,128)}, bf16[256,1536]{1,0:T(8,128)(2,1)S(1)}, bf16[64,20...) custom-call(s32[1]{0:T(128)} %bitcast.1.refs_0_.me_ref, ...), custom_call_target="tpu_custom_call" | custom-call | flops 4831838208 | bytes 27262976 | tf_op jit(solution)/shard_map/feed/pallas_call | solution.py:1070
  350.0 21.8 %collective-permute-done.28.refs_1_ = bf16[64,2048]{1,0:T(8,128)(2,1)S(1)} collective-permute-done((bf16[64,2048]{1,0:T(8,128)(2,1)S(1)}, bf16[64,2048]{1,0:T(8,128)(2,1)S(1)}, u32[]{:S(2)}, u32[]{:S(2)}) %collective-permute-start.28) | collective-permute-done | bytes 262176 | tf_op jit(solution)/shard_map/ppermute | solution.py:1874
  371.8 22.1 %collective-permute-done.29.refs_2_ = bf16[64,2048]{1,0:T(8,128)(2,1)S(1)} collective-permute-done((bf16[64,2048]{1,0:T(8,128)(2,1)S(1)}, bf16[64,2048]{1,0:T(8,128)(2,1)S(1)}, u32[]{:S(2)}, u32[]{:S(2)}) %collective-permute-start.29) | collective-permute-done | bytes 262176 | tf_op jit(solution)/shard_map/ppermute | solution.py:1874
  394.2 12.6 collective-permute-start.32
  408.5 15.3 %collective-permute-done.32.refs_5_ = bf16[64,2048]{1,0:T(8,128)(2,1)S(1)} collective-permute-done((bf16[64,2048]{1,0:T(8,128)(2,1)S(1)}, bf16[64,2048]{1,0:T(8,128)(2,1)S(1)}, u32[]{:S(2)}, u32[]{:S(2)}) %collective-permute-start.32) | collective-permute-done | bytes 262176 | tf_op jit(solution)/shard_map/ppermute | solution.py:1852
  429.1 9.9 project_next.1
  463.0 19.1 %recur_forward.3 = (bf16[256,256]{1,0:T(8,128)(2,1)S(1)}, bf16[256,256]{1,0:T(8,128)(2,1)S(1)}, bf16[256,256]{1,0:T(8,128)(2,1)S(1)}, bf16[256,256]{1,0:T(8,128)...) custom-call(s32[1]{0:T(128)} %bitcast.piece_ref.me_ref, bf16[256,640]{1,0:T(8,128)(2,1)S(1)} %get-tuple-element.534.refs_0_, ...), custom_call_target="tpu_custom_call" | custom-call | flops 40960000000 | bytes 8388608 | tf_op jit(solution)/shard_map/recur_forward/pallas_call | solution.py:980
  498.2 8.6 all-gather.15.cloned.1.call-done
  514.2 9.2 collective-permute-done.40.refs_1_
  533.8 10.6 collective-permute-start.44
  545.9 14.7 %collective-permute-done.44.refs_5_ = bf16[64,2048]{1,0:T(8,128)(2,1)S(1)} collective-permute-done((bf16[64,2048]{1,0:T(8,128)(2,1)S(1)}, bf16[64,2048]{1,0:T(8,128)(2,1)S(1)}, u32[]{:S(2)}, u32[]{:S(2)}) %collective-permute-start.44) | collective-permute-done | bytes 262176 | tf_op jit(solution)/shard_map/ppermute | solution.py:1852
  562.0 18.6 %all-gather.17.cloned.1.call-done = bf16[8192,768]{1,0:T(8,128)(2,1)} async-done(((bf16[1024,768]{1,0:T(8,128)(2,1)}), bf16[8192,768]{1,0:T(8,128)(2,1)}) %all-gather.17.cloned.1.call-update) | async-done | bytes 12582928 | tf_op jit(solution)/shard_map/all_gather | solution.py:1908
  585.1 13.3 %feed.3 = (f32[256,2048]{1,0:T(8,128)}, bf16[256,2048]{1,0:T(8,128)(2,1)S(1)}, f32[4,256,768]{2,1,0:T(8,128)}, bf16[256,1536]{1,0:T(8,128)(2,1)S(1)}, bf16[64,20...) custom-call(s32[1]{0:T(128)} %bitcast.1.refs_0_.me_ref, ...), custom_call_target="tpu_custom_call" | custom-call | flops 4831838208 | bytes 27262976 | tf_op jit(solution)/shard_map/feed/pallas_call | solution.py:1070
  600.8 12.7 feed_back.2
  623.8 9.4 collective-permute-done.46.refs_1_
  633.1 8.1 collective-permute-done.48.refs_3_
  643.5 10.7 collective-permute-start.50
  654.2 16.3 %collective-permute-done.50.refs_4_ = bf16[64,2048]{1,0:T(8,128)(2,1)S(1)} collective-permute-done((bf16[64,2048]{1,0:T(8,128)(2,1)S(1)}, bf16[64,2048]{1,0:T(8,128)(2,1)S(1)}, u32[]{:S(2)}, u32[]{:S(2)}) %collective-permute-start.50) | collective-permute-done | bytes 262176 | tf_op jit(solution)/shard_map/ppermute | solution.py:1852
  693.7 31.0 %recur_backward.2 = (bf16[256,640]{1,0:T(8,128)(2,1)S(1)}, bf16[256,640]{1,0:T(8,128)(2,1)S(1)}, bf16[256,640]{1,0:T(8,128)(2,1)S(1)}, bf16[256,640]{1,0:T(8,128...) custom-call(s32[1]{0:T(128)} %bitcast.piece_ref.me_ref, bf16[256,640]{1,0:T(8,128)(2,1)S(1)} %copy-done.63, ...), custom_call_target="tpu_custom_call" | custom-call | flops 40960000000 | bytes 8388608 | tf_op jit(solution)/shard_map/recur_backward/pallas_call | solution.py:1005
  748.9 9.2 project_back.2
  762.8 8.7 all-to-all-done.6.layer1_ref
  791.6 9.0 collective-permute-start.65
  800.6 14.6 %collective-permute-done.65.refs_4_ = bf16[64,2048]{1,0:T(8,128)(2,1)S(1)} collective-permute-done((bf16[64,2048]{1,0:T(8,128)(2,1)S(1)}, bf16[64,2048]{1,0:T(8,128)(2,1)S(1)}, u32[]{:S(2)}, u32[]{:S(2)}) %collective-permute-start.65) | collective-permute-done | bytes 262176 | tf_op jit(solution)/shard_map/ppermute | solution.py:1852
  828.4 15.2 %feed_back.3 = (bf16[4,256,768]{2,1,0:T(8,128)(2,1)S(1)}, bf16[64,2048]{1,0:T(8,128)(2,1)S(1)}, bf16[64,2048]{1,0:T(8,128)(2,1)S(1)}, bf16[64,2048]{1,0:T(8,128)(2,1)S(1)}, bf16[64,2048]{1,0:T(8,128)(2,1)S(1)}) custom-call(s32[1]{0:T(128)} %bitcast.1.refs_0_.me_ref, bf16[256,2048]{1,0:T(8,128)(2,1)S(1)} %get-tuple-element.410.up_ref.refs_7_, ...), custom_call_target="tpu_custom_call" | custom-call | flops 4831838208 | bytes 25690112 | tf_op jit(solution)/shard_map/feed_back/pallas_call | solution.py:1070
  853.8 20.6 %collective-permute-done.72.refs_2_ = bf16[64,2048]{1,0:T(8,128)(2,1)S(1)} collective-permute-done((bf16[64,2048]{1,0:T(8,128)(2,1)S(1)}, bf16[64,2048]{1,0:T(8,128)(2,1)S(1)}, u32[]{:S(2)}, u32[]{:S(2)}) %collective-permute-start.72) | collective-permute-done | bytes 262176 | tf_op jit(solution)/shard_map/ppermute | solution.py:1874
  874.9 9.7 collective-permute-start.75
  884.6 19.8 %collective-permute-done.75.refs_4_ = bf16[64,2048]{1,0:T(8,128)(2,1)S(1)} collective-permute-done((bf16[64,2048]{1,0:T(8,128)(2,1)S(1)}, bf16[64,2048]{1,0:T(8,128)(2,1)S(1)}, u32[]{:S(2)}, u32[]{:S(2)}) %collective-permute-start.75) | collective-permute-done | bytes 262176 | tf_op jit(solution)/shard_map/ppermute | solution.py:1852
  948.9 31.5 %recur_backward.3 = (bf16[256,640]{1,0:T(8,128)(2,1)S(1)}, bf16[256,640]{1,0:T(8,128)(2,1)S(1)}, bf16[256,640]{1,0:T(8,128)(2,1)S(1)}, bf16[256,640]{1,0:T(8,128...) custom-call(s32[1]{0:T(128)} %bitcast.piece_ref.me_ref, bf16[256,640]{1,0:T(8,128)(2,1)S(1)} %copy-done.61, ...), custom_call_target="tpu_custom_call" | custom-call | flops 40960000000 | bytes 8388608 | tf_op jit(solution)/shard_map/recur_backward/pallas_call | solution.py:1005
  993.0 12.9 collective-permute-done.82.refs_3_
  1009.2 8.6 project_back.3
  1037.9 12.1 collective-permute-start.87
  1050.0 18.5 %collective-permute-done.87.refs_4_ = bf16[64,2048]{1,0:T(8,128)(2,1)S(1)} collective-permute-done((bf16[64,2048]{1,0:T(8,128)(2,1)S(1)}, bf16[64,2048]{1,0:T(8,128)(2,1)S(1)}, u32[]{:S(2)}, u32[]{:S(2)}) %collective-permute-start.87) | collective-permute-done | bytes 262176 | tf_op jit(solution)/shard_map/ppermute | solution.py:1852
  1088.6 22.8 %collective-permute-done.92.refs_3_ = bf16[2,64,2048]{2,1,0:T(8,128)(2,1)S(1)} collective-permute-done((bf16[2,64,2048]{2,1,0:T(8,128)(2,1)S(1)}, bf16[2,64,2048]{2,1,0:T(8,128)(2,1)S(1)}, u32[]{:S(2)}, u32[]{:S(2)}) %collective-permute-start.92) | collective-permute-done | bytes 524320 | tf_op jit(solution)/shard_map/ppermute | solution.py:1852
  1111.4 11.8 collective-permute-done.91.refs_2_
  1127.5 23.0 %reduce-scatter.15.cloned.1.call-done.whole_ref = bf16[640,1024]{1,0:T(8,128)(2,1)} async-done(((bf16[5120,1024]{1,0:T(8,128)(2,1)}), bf16[640,1024]{1,0:T(8,128)(2,1)}) %reduce-scatter.15.cloned.1.call-update) | async-done | bytes 1310736 | tf_op jit(solution)/shard_map/reduce_scatter | solution.py:1924
  1189.0 21.0 %all-to-all-done.10.layer0_ref = bf16[4,640,256]{2,1,0:T(8,128)(2,1)} async-done(((bf16[4,640,256]{2,1,0:T(8,128)(2,1)}), bf16[4,640,256]{2,1,0:T(8,128)(2,1)}, u32[]{:S(2)}, u32[]{:S(2)}) %all-to-all-start.10) | async-done | bytes 1310752 | tf_op jit(solution)/shard_map/all_to_all | solution.py:1935
  1260.6 26.9 %all-to-all-done.13.layer0_ref = bf16[4,256,768]{2,1,0:T(8,128)(2,1)S(1)} async-done(((bf16[4,256,768]{2,1,0:T(8,128)(2,1)}), bf16[4,256,768]{2,1,0:T(8,128)(2,1)S(1)}, u32[]{:S(2)}, u32[]{:S(2)}) %all-to-all-start.13) | async-done | bytes 1572896 | tf_op jit(solution)/shard_map/all_to_all | solution.py:1931
  (867 shorter events, 539.6 us)
Async XLA Ops:
  25.7 42.8 %all-to-all-start = ((bf16[4,256,768]{2,1,0:T(8,128)(2,1)}), bf16[4,256,768]{2,1,0:T(8,128)(2,1)}, u32[]{:S(2)}, u32[]{:S(2)}) async-start(bf16[4,256,768]{2,1,0:T(8,128)(2,1)} %get-tuple-element.514), calls=%async_computation | async-start | bytes 3145728 | tf_op jit(solution)/shard_map/all_to_all | solution.py:1900
  31.6 109.5 %all-gather.7.cloned.1.call-start = ((), (), s32[]{:S(2)}) async-start(), calls=%async_computation.20 | async-start | bytes 14155776 | tf_op jit(solution)/shard_map/all_gather | solution.py:1908
  69.1 34.9 %collective-permute-start.7 = (bf16[64,2048]{1,0:T(8,128)(2,1)S(1)}, bf16[64,2048]{1,0:T(8,128)(2,1)S(1)}, u32[]{:S(2)}, u32[]{:S(2)}) collective-permute-start(bf16[64,2048]{1,0:T(8,128)(2,1)S(1)} %reshape.346.refs_3_), channel_id=1, source_target_pairs={{0,12},{4,8},{8,4},{12,0},{1,13},{5,9},{9,5},{13,1},{2,14},{6,10},... | collective-permute-start | bytes 786440 | tf_op jit(solution)/shard_map/ppermute | solution.py:1852
  70.3 33.7 %collective-permute-start.6 = (bf16[64,2048]{1,0:T(8,128)(2,1)S(1)}, bf16[64,2048]{1,0:T(8,128)(2,1)S(1)}, u32[]{:S(2)}, u32[]{:S(2)}) collective-permute-start(bf16[64,2048]{1,0:T(8,128)(2,1)S(1)} %reshape.346.refs_3_), channel_id=1, source_target_pairs={{0,8},{4,12},{8,0},{12,4},{1,9},{5,13},{9,1},{13,5},{2,10},{6,14},... | collective-permute-start | bytes 786440 | tf_op jit(solution)/shard_map/ppermute | solution.py:1852
  93.9 34.4 %all-to-all-start.1 = ((bf16[4,640,256]{2,1,0:T(8,128)(2,1)}), bf16[4,640,256]{2,1,0:T(8,128)(2,1)S(1)}, u32[]{:S(2)}, u32[]{:S(2)}) async-start(bf16[4,640,256]{2,1,0:T(8,128)(2,1)} %get-tuple-element.268), calls=%async_computation.1 | async-start | bytes 2621440 | tf_op jit(solution)/shard_map/all_to_all | solution.py:2115
  97.5 145.6 %all-gather.9.cloned.1.call-start = ((), (), s32[]{:S(2)}) async-start(), calls=%async_computation.21 | async-start | bytes 11796480 | tf_op jit(solution)/shard_map/all_gather | solution.py:1913
  129.9 40.9 %all-to-all-start.2 = ((bf16[4,256,768]{2,1,0:T(8,128)(2,1)}), bf16[4,256,768]{2,1,0:T(8,128)(2,1)}, u32[]{:S(2)}, u32[]{:S(2)}) async-start(bf16[4,256,768]{2,1,0:T(8,128)(2,1)} %get-tuple-element.270), calls=%async_computation.2 | async-start | bytes 3145728 | tf_op jit(solution)/shard_map/all_to_all | solution.py:1900
  134.3 191.7 %all-gather.11.cloned.1.call-start = ((), (), s32[]{:S(2)}) async-start(), calls=%async_computation.22 | async-start | bytes 14155776 | tf_op jit(solution)/shard_map/all_gather | solution.py:1908
  154.8 27.4 %collective-permute-start.13 = (bf16[256,640]{1,0:T(8,128)(2,1)}, bf16[256,640]{1,0:T(8,128)(2,1)}, u32[]{:S(2)}, u32[]{:S(2)}) collective-permute-start(bf16[256,640]{1,0:T(8,128)(2,1)} %get-tuple-element.537), channel_id=1, source_target_pairs={{0,1},{1,0},{2,3},{3,2},{4,5},{5,4},{6,7},{7,6},{8,9},{9,8},{10,11... | collective-permute-start | bytes 983048 | tf_op jit(solution)/shard_map/ppermute | solution.py:1874
  238.5 87.5 %all-to-all-start.3 = ((bf16[4,256,768]{2,1,0:T(8,128)(2,1)}), bf16[4,256,768]{2,1,0:T(8,128)(2,1)}, u32[]{:S(2)}, u32[]{:S(2)}) async-start(bf16[4,256,768]{2,1,0:T(8,128)(2,1)} %get-tuple-element.290), calls=%async_computation.3 | async-start | bytes 3145728 | tf_op jit(solution)/shard_map/all_to_all | solution.py:1900
  242.8 181.0 %all-gather.13.cloned.1.call-start = ((), (), s32[]{:S(2)}) async-start(), calls=%async_computation.23 | async-start | bytes 14155776 | tf_op jit(solution)/shard_map/all_gather | solution.py:1908
  251.7 44.3 %collective-permute-start.23 = (bf16[64,2048]{1,0:T(8,128)(2,1)S(1)}, bf16[64,2048]{1,0:T(8,128)(2,1)S(1)}, u32[]{:S(2)}, u32[]{:S(2)}) collective-permute-start(bf16[64,2048]{1,0:T(8,128)(2,1)S(1)} %get-tuple-element.288), channel_id=1, source_target_pairs={{0,8},{4,12},{8,0},{12,4},{1,9},{5,13},{9,1},{13,5},{2,10},{6,14},... | collective-permute-start | bytes 786440 | tf_op jit(solution)/shard_map/ppermute | solution.py:1874
  253.8 42.3 %collective-permute-start.24 = (bf16[64,2048]{1,0:T(8,128)(2,1)S(1)}, bf16[64,2048]{1,0:T(8,128)(2,1)S(1)}, u32[]{:S(2)}, u32[]{:S(2)}) collective-permute-start(bf16[64,2048]{1,0:T(8,128)(2,1)S(1)} %get-tuple-element.289), channel_id=1, source_target_pairs={{0,12},{4,8},{8,4},{12,0},{1,13},{5,9},{9,5},{13,1},{2,14},{6,10},... | collective-permute-start | bytes 786440 | tf_op jit(solution)/shard_map/ppermute | solution.py:1874
  296.7 29.2 %collective-permute-start.26 = (bf16[64,2048]{1,0:T(8,128)(2,1)S(1)}, bf16[64,2048]{1,0:T(8,128)(2,1)S(1)}, u32[]{:S(2)}, u32[]{:S(2)}) collective-permute-start(bf16[64,2048]{1,0:T(8,128)(2,1)S(1)} %sum_pieces.8.refs_3_), channel_id=1, source_target_pairs={{0,8},{4,12},{8,0},{12,4},{1,9},{5,13},{9,1},{13,5},{2,10},{6,14},... | collective-permute-start | bytes 786440 | tf_op jit(solution)/shard_map/ppermute | solution.py:1852
  342.8 64.1 %all-to-all-start.4 = ((bf16[4,640,256]{2,1,0:T(8,128)(2,1)}), bf16[4,640,256]{2,1,0:T(8,128)(2,1)S(1)}, u32[]{:S(2)}, u32[]{:S(2)}) async-start(bf16[4,640,256]{2,1,0:T(8,128)(2,1)} %get-tuple-element.300), calls=%async_computation.4 | async-start | bytes 2621440 | tf_op jit(solution)/shard_map/all_to_all | solution.py:1904
  346.3 160.4 %all-gather.15.cloned.1.call-start = ((), (), s32[]{:S(2)}) async-start(), calls=%async_computation.24 | async-start | bytes 11796480 | tf_op jit(solution)/shard_map/all_gather | solution.py:1913
  347.7 46.2 %collective-permute-start.29 = (bf16[64,2048]{1,0:T(8,128)(2,1)S(1)}, bf16[64,2048]{1,0:T(8,128)(2,1)S(1)}, u32[]{:S(2)}, u32[]{:S(2)}) collective-permute-start(bf16[64,2048]{1,0:T(8,128)(2,1)S(1)} %get-tuple-element.298), channel_id=1, source_target_pairs={{0,8},{4,12},{8,0},{12,4},{1,9},{5,13},{9,1},{13,5},{2,10},{6,14},... | collective-permute-start | bytes 786440 | tf_op jit(solution)/shard_map/ppermute | solution.py:1874
  349.8 44.1 %collective-permute-start.30 = (bf16[64,2048]{1,0:T(8,128)(2,1)S(1)}, bf16[64,2048]{1,0:T(8,128)(2,1)S(1)}, u32[]{:S(2)}, u32[]{:S(2)}) collective-permute-start(bf16[64,2048]{1,0:T(8,128)(2,1)S(1)} %get-tuple-element.299), channel_id=1, source_target_pairs={{0,12},{4,8},{8,4},{12,0},{1,13},{5,9},{9,5},{13,1},{2,14},{6,10},... | collective-permute-start | bytes 786440 | tf_op jit(solution)/shard_map/ppermute | solution.py:1874
  394.2 29.6 %collective-permute-start.32 = (bf16[64,2048]{1,0:T(8,128)(2,1)S(1)}, bf16[64,2048]{1,0:T(8,128)(2,1)S(1)}, u32[]{:S(2)}, u32[]{:S(2)}) collective-permute-start(bf16[64,2048]{1,0:T(8,128)(2,1)S(1)} %sum_pieces.9.refs_3_), channel_id=1, source_target_pairs={{0,8},{4,12},{8,0},{12,4},{1,9},{5,13},{9,1},{13,5},{2,10},{6,14},... | collective-permute-start | bytes 786440 | tf_op jit(solution)/shard_map/ppermute | solution.py:1852
  443.7 53.9 %all-to-all-start.5 = ((bf16[4,256,768]{2,1,0:T(8,128)(2,1)}), bf16[4,256,768]{2,1,0:T(8,128)(2,1)}, u32[]{:S(2)}, u32[]{:S(2)}) async-start(bf16[4,256,768]{2,1,0:T(8,128)(2,1)} %get-tuple-element.317), calls=%async_computation.5 | async-start | bytes 3145728 | tf_op jit(solution)/shard_map/all_to_all | solution.py:1900
  448.1 132.5 %all-gather.17.cloned.1.call-start = ((), (), s32[]{:S(2)}) async-start(), calls=%async_computation.25 | async-start | bytes 14155776 | tf_op jit(solution)/shard_map/all_gather | solution.py:1908
  497.7 233.3 %reduce-scatter.7.cloned.1.call-start = ((), (), s32[]{:S(2)}) async-start(), calls=%async_computation.26 | async-start | bytes 14155776 | tf_op jit(solution)/shard_map/reduce_scatter | solution.py:1918
  620.1 195.5 %reduce-scatter.9.cloned.1.call-start = ((), (), s32[]{:S(2)}) async-start(), calls=%async_computation.27 | async-start | bytes 11796480 | tf_op jit(solution)/shard_map/reduce_scatter | solution.py:1924
  690.1 38.8 %collective-permute-start.55 = (bf16[64,2048]{1,0:T(8,128)(2,1)S(1)}, bf16[64,2048]{1,0:T(8,128)(2,1)S(1)}, u32[]{:S(2)}, u32[]{:S(2)}) collective-permute-start(bf16[64,2048]{1,0:T(8,128)(2,1)S(1)} %copy-done.164), channel_id=1, source_target_pairs={{0,4},{4,0},{8,12},{12,8},{1,5},{5,1},{9,13},{13,9},{2,6},{6,2},{1... | collective-permute-start | bytes 786440 | tf_op jit(solution)/shard_map/ppermute | solution.py:1874
  691.0 38.6 %collective-permute-start.56 = (bf16[64,2048]{1,0:T(8,128)(2,1)S(1)}, bf16[64,2048]{1,0:T(8,128)(2,1)S(1)}, u32[]{:S(2)}, u32[]{:S(2)}) collective-permute-start(bf16[64,2048]{1,0:T(8,128)(2,1)S(1)} %copy-done.162), channel_id=1, source_target_pairs={{0,8},{4,12},{8,0},{12,4},{1,9},{5,13},{9,1},{13,5},{2,10},{6,14},... | collective-permute-start | bytes 786440 | tf_op jit(solution)/shard_map/ppermute | solution.py:1874
  693.0 37.3 %collective-permute-start.57 = (bf16[64,2048]{1,0:T(8,128)(2,1)S(1)}, bf16[64,2048]{1,0:T(8,128)(2,1)S(1)}, u32[]{:S(2)}, u32[]{:S(2)}) collective-permute-start(bf16[64,2048]{1,0:T(8,128)(2,1)S(1)} %copy-done.160), channel_id=1, source_target_pairs={{0,12},{4,8},{8,4},{12,0},{1,13},{5,9},{9,5},{13,1},{2,14},{6,10},... | collective-permute-start | bytes 786440 | tf_op jit(solution)/shard_map/ppermute | solution.py:1874
  731.1 40.4 %all-to-all-start.6 = ((bf16[4,256,768]{2,1,0:T(8,128)(2,1)}), bf16[4,256,768]{2,1,0:T(8,128)(2,1)S(1)}, u32[]{:S(2)}, u32[]{:S(2)}) async-start(bf16[4,256,768]{2,1,0:T(8,128)(2,1)} %bitcast.318), calls=%async_computation.7 | async-start | bytes 3145728 | tf_op jit(solution)/shard_map/all_to_all | solution.py:1931
  735.0 185.4 %reduce-scatter.11.cloned.1.call-start = ((), (), s32[]{:S(2)}) async-start(), calls=%async_computation.28 | async-start | bytes 14155776 | tf_op jit(solution)/shard_map/reduce_scatter | solution.py:1918
  824.0 81.1 %all-to-all-start.7 = ((bf16[4,640,256]{2,1,0:T(8,128)(2,1)}), bf16[4,640,256]{2,1,0:T(8,128)(2,1)}, u32[]{:S(2)}, u32[]{:S(2)}) async-start(bf16[4,640,256]{2,1,0:T(8,128)(2,1)} %copy-done.9), calls=%async_computation.9 | async-start | bytes 2621440 | tf_op jit(solution)/shard_map/all_to_all | solution.py:1935
  828.3 203.4 %reduce-scatter.13.cloned.1.call-start = ((), (), s32[]{:S(2)}) async-start(), calls=%async_computation.29 | async-start | bytes 14155776 | tf_op jit(solution)/shard_map/reduce_scatter | solution.py:1918
  845.0 29.4 %collective-permute-start.72 = (bf16[64,2048]{1,0:T(8,128)(2,1)S(1)}, bf16[64,2048]{1,0:T(8,128)(2,1)S(1)}, u32[]{:S(2)}, u32[]{:S(2)}) collective-permute-start(bf16[64,2048]{1,0:T(8,128)(2,1)S(1)} %get-tuple-element.414), channel_id=1, source_target_pairs={{0,8},{4,12},{8,0},{12,4},{1,9},{5,13},{9,1},{13,5},{2,10},{6,14},... | collective-permute-start | bytes 786440 | tf_op jit(solution)/shard_map/ppermute | solution.py:1874
  847.1 27.3 %collective-permute-start.73 = (bf16[64,2048]{1,0:T(8,128)(2,1)S(1)}, bf16[64,2048]{1,0:T(8,128)(2,1)S(1)}, u32[]{:S(2)}, u32[]{:S(2)}) collective-permute-start(bf16[64,2048]{1,0:T(8,128)(2,1)S(1)} %get-tuple-element.415), channel_id=1, source_target_pairs={{0,12},{4,8},{8,4},{12,0},{1,13},{5,9},{9,5},{13,1},{2,14},{6,10},... | collective-permute-start | bytes 786440 | tf_op jit(solution)/shard_map/ppermute | solution.py:1874
  874.9 29.5 %collective-permute-start.75 = (bf16[64,2048]{1,0:T(8,128)(2,1)S(1)}, bf16[64,2048]{1,0:T(8,128)(2,1)S(1)}, u32[]{:S(2)}, u32[]{:S(2)}) collective-permute-start(bf16[64,2048]{1,0:T(8,128)(2,1)S(1)} %sum_pieces.14.refs_2_), channel_id=1, source_target_pairs={{0,8},{4,12},{8,0},{12,4},{1,9},{5,13},{9,1},{13,5},{2,10},{6,14},... | collective-permute-start | bytes 786440 | tf_op jit(solution)/shard_map/ppermute | solution.py:1852
  936.7 47.7 %all-to-all-start.8 = ((bf16[4,256,768]{2,1,0:T(8,128)(2,1)}), bf16[4,256,768]{2,1,0:T(8,128)(2,1)S(1)}, u32[]{:S(2)}, u32[]{:S(2)}) async-start(bf16[4,256,768]{2,1,0:T(8,128)(2,1)} %bitcast.319), calls=%async_computation.11 | async-start | bytes 3145728 | tf_op jit(solution)/shard_map/all_to_all | solution.py:1931
  940.3 210.2 %reduce-scatter.15.cloned.1.call-start = ((), (), s32[]{:S(2)}) async-start(), calls=%async_computation.30 | async-start | bytes 11796480 | tf_op jit(solution)/shard_map/reduce_scatter | solution.py:1924
  1037.9 30.7 %collective-permute-start.87 = (bf16[64,2048]{1,0:T(8,128)(2,1)S(1)}, bf16[64,2048]{1,0:T(8,128)(2,1)S(1)}, u32[]{:S(2)}, u32[]{:S(2)}) collective-permute-start(bf16[64,2048]{1,0:T(8,128)(2,1)S(1)} %sum_pieces.15.refs_2_), channel_id=1, source_target_pairs={{0,8},{4,12},{8,0},{12,4},{1,9},{5,13},{9,1},{13,5},{2,10},{6,14},... | collective-permute-start | bytes 786440 | tf_op jit(solution)/shard_map/ppermute | solution.py:1852
  1074.6 52.9 %all-to-all-start.9 = ((bf16[4,256,768]{2,1,0:T(8,128)(2,1)}), bf16[4,256,768]{2,1,0:T(8,128)(2,1)}, u32[]{:S(2)}, u32[]{:S(2)}) async-start(bf16[4,256,768]{2,1,0:T(8,128)(2,1)} %bitcast.317), calls=%async_computation.14 | async-start | bytes 3145728 | tf_op jit(solution)/shard_map/all_to_all | solution.py:1931
  1078.9 168.2 %reduce-scatter.17.cloned.1.call-start = ((), (), s32[]{:S(2)}) async-start(), calls=%async_computation.31 | async-start | bytes 14155776 | tf_op jit(solution)/shard_map/reduce_scatter | solution.py:1918
  1086.3 37.0 %collective-permute-start.91 = (bf16[2,64,2048]{2,1,0:T(8,128)(2,1)S(1)}, bf16[2,64,2048]{2,1,0:T(8,128)(2,1)S(1)}, u32[]{:S(2)}, u32[]{:S(2)}) collective-permute-start(bf16[2,64,2048]{2,1,0:T(8,128)(2,1)S(1)} %pad_maximum_fusion.1.refs_0_), channel_id=1, source_target_pairs={{0,2},{1,3},{2,0},{3,1},{4,6},{5,7},{6,4},{7,5},{8,10},{9,11},{10,... | collective-permute-start | bytes 1572872 | tf_op jit(solution)/shard_map/ppermute | solution.py:1852
  1088.6 37.4 %collective-permute-start.90 = (bf16[2,64,2048]{2,1,0:T(8,128)(2,1)S(1)}, bf16[2,64,2048]{2,1,0:T(8,128)(2,1)S(1)}, u32[]{:S(2)}, u32[]{:S(2)}) collective-permute-start(bf16[2,64,2048]{2,1,0:T(8,128)(2,1)S(1)} %pad_maximum_fusion.1.refs_0_), channel_id=1, source_target_pairs={{0,1},{1,0},{2,3},{3,2},{4,5},{5,4},{6,7},{7,6},{8,9},{9,8},{10,11... | collective-permute-start | bytes 1572872 | tf_op jit(solution)/shard_map/ppermute | solution.py:1852
  1174.5 35.6 %all-to-all-start.10 = ((bf16[4,640,256]{2,1,0:T(8,128)(2,1)}), bf16[4,640,256]{2,1,0:T(8,128)(2,1)}, u32[]{:S(2)}, u32[]{:S(2)}) async-start(bf16[4,640,256]{2,1,0:T(8,128)(2,1)} %copy-done.10), calls=%async_computation.16 | async-start | bytes 2621440 | tf_op jit(solution)/shard_map/all_to_all | solution.py:1935
  1185.3 28.7 %collective-permute-start.96 = (f32[4360]{0:T(1024)S(1)}, f32[4360]{0:T(1024)S(1)}, u32[]{:S(2)}, u32[]{:S(2)}) collective-permute-start(f32[4360]{0:T(1024)S(1)} %slice.426), channel_id=1, source_target_pairs={{0,1},{1,0},{2,3},{3,2},{4,5},{5,4},{6,7},{7,6},{8,9},{9,8},{10,11... | collective-permute-start | bytes 52328 | tf_op jit(solution)/shard_map/ppermute | solution.py:30
  1189.0 47.8 %collective-permute-start.94 = (bf16[4,256,768]{2,1,0:T(8,128)(2,1)}, bf16[4,256,768]{2,1,0:T(8,128)(2,1)}, u32[]{:S(2)}, u32[]{:S(2)}) collective-permute-start(bf16[4,256,768]{2,1,0:T(8,128)(2,1)} %broadcast_select_fusion.1), channel_id=1, source_target_pairs={{0,16},{16,0},{1,17},{17,1},{2,18},{18,2},{3,19},{19,3},{4,20},{20... | collective-permute-start | bytes 4718600 | tf_op jit(solution)/shard_map/ppermute | solution.py:30
  1212.6 29.5 %collective-permute-start.93 = (bf16[4,640,256]{2,1,0:T(8,128)(2,1)}, bf16[4,640,256]{2,1,0:T(8,128)(2,1)}, u32[]{:S(2)}, u32[]{:S(2)}) collective-permute-start(bf16[4,640,256]{2,1,0:T(8,128)(2,1)} %broadcast_select_fusion.6), channel_id=1, source_target_pairs={{0,16},{16,0},{1,17},{17,1},{2,18},{18,2},{3,19},{19,3},{4,20},{20... | collective-permute-start | bytes 3932168 | tf_op jit(solution)/shard_map/ppermute | solution.py:30
  1247.1 40.4 %all-to-all-start.13 = ((bf16[4,256,768]{2,1,0:T(8,128)(2,1)}), bf16[4,256,768]{2,1,0:T(8,128)(2,1)S(1)}, u32[]{:S(2)}, u32[]{:S(2)}) async-start(bf16[4,256,768]{2,1,0:T(8,128)(2,1)} %bitcast.316), calls=%async_computation.19 | async-start | bytes 3145728 | tf_op jit(solution)/shard_map/all_to_all | solution.py:1931
  1258.0 32.7 %collective-permute-start.70 = (bf16[2,64,2048]{2,1,0:T(8,128)(2,1)}, bf16[2,64,2048]{2,1,0:T(8,128)(2,1)}, u32[]{:S(2)}, u32[]{:S(2)}) collective-permute-start(bf16[2,64,2048]{2,1,0:T(8,128)(2,1)} %pad_maximum_fusion.refs_0_), channel_id=1, source_target_pairs={{0,3},{1,2},{2,1},{3,0},{4,7},{5,6},{6,5},{7,4},{8,11},{9,10},{10,... | collective-permute-start | bytes 1572872 | tf_op jit(solution)/shard_map/ppermute | solution.py:1852
  1260.3 30.3 %collective-permute-start.69 = (bf16[2,64,2048]{2,1,0:T(8,128)(2,1)}, bf16[2,64,2048]{2,1,0:T(8,128)(2,1)}, u32[]{:S(2)}, u32[]{:S(2)}) collective-permute-start(bf16[2,64,2048]{2,1,0:T(8,128)(2,1)} %pad_maximum_fusion.refs_0_), channel_id=1, source_target_pairs={{0,2},{1,3},{2,0},{3,1},{4,6},{5,7},{6,4},{7,5},{8,10},{9,11},{10,... | collective-permute-start | bytes 1572872 | tf_op jit(solution)/shard_map/ppermute | solution.py:1852
  1260.6 30.1 %collective-permute-start.68 = (bf16[2,64,2048]{2,1,0:T(8,128)(2,1)}, bf16[2,64,2048]{2,1,0:T(8,128)(2,1)}, u32[]{:S(2)}, u32[]{:S(2)}) collective-permute-start(bf16[2,64,2048]{2,1,0:T(8,128)(2,1)} %pad_maximum_fusion.refs_0_), channel_id=1, source_target_pairs={{0,1},{1,0},{2,3},{3,2},{4,5},{5,4},{6,7},{7,6},{8,9},{9,8},{10,11... | collective-permute-start | bytes 1572872 | tf_op jit(solution)/shard_map/ppermute | solution.py:1852
  (298 other events, 3521.9 us)
Sparse Core Ops, SparseCore 0:
  68.6 72.5 all-gather.6
  143.6 79.4 all-gather.8
  225.0 72.1 all-gather.10
  326.1 72.1 all-gather.12
  424.0 82.7 all-gather.14
  508.5 72.1 all-gather.16
  620.2 96.5 reduce-scatter.6
  731.1 84.4 reduce-scatter.8
  819.1 92.3 reduce-scatter.10
  920.6 100.7 reduce-scatter.12
  1031.9 118.5 reduce-scatter.14
  1153.8 93.2 reduce-scatter.16

commit v4 on v3

--- a/solution.py
+++ b/solution.py
@@ -16,7 +16,7 @@
 HEAD = "head"
 LANES = 128
 RECUR_FLOPS = 40_000_000
-VMEM_LIMIT = 48 * 1024 * 1024
+VMEM_LIMIT = 62 * 1024 * 1024
 HALO = 8
 EXTRA = 128
 GROUP = 8
@@ -1969,7 +1969,7 @@
     grad_proj = grad_rows(normed, grad_pre)
     pieces = swap_pieces(pieces, SEQ)
     pieces, _ = lax.optimization_barrier((pieces, grad_proj))
-    sums, sum_both = sum_cols(grad_both, (sum_gu, dxh), pieces)
+    sums, sum_both = sum_cols(grad_both, (sum_gu, dxh), grad_pre, pieces)
     sums, running = lax.optimization_barrier((sums, running))
     sums = before_end(sums)
     grad_resid, dattn = norm_back(me, attn_gain, sums, resid, grad_mid)
@@ -2131,31 +2131,28 @@
             xh, gu0 = lax.optimization_barrier((xh, gu0))
             w_gu = spread_rows(gu0)
             weights[0] = (w_proj, w_mix, w_cols, w_gu)
-            masked = my_tokens(after(masked, gu0))
+            proj1 = move_rows(after(proj_parts[1], gu0))
+            cols1 = move_cols(after(cols_parts[1], proj1))
         mixed, states, inverse = recur_forward(place_at, xh, aux, *small[layer][:2], parts)
         mixed = swap_pieces(mixed, HEAD)
         if layer == 0:
-            mixed, masked = lax.optimization_barrier((mixed, masked))
-            proj1 = move_rows(after(proj_parts[1], mixed))
+            mixed, proj1, cols1 = lax.optimization_barrier((mixed, proj1, cols1))
         else:
-            mixed, gu1 = lax.optimization_barrier((mixed, gu1))
+            mixed, gu1, masked = lax.optimization_barrier((mixed, gu1, masked))
             w_gu = spread_rows(gu1)
             weights[1] = (w_proj, w_mix, w_cols, w_gu)
         gated, kept, pieces = output(me, place_at, mixed, gate_pre, small[layer][2], w_cols, shards)
         mixer = (xh, states, inverse, kept, gated)
         mix_parts = exchange(pieces)
-        if layer == 0:
-            mix_parts, proj1 = lax.optimization_barrier((mix_parts, proj1))
         base, ffn_in, gate_up, hidden, pieces, stat = feed(
             me, valid, mlp_gain, mix_parts, resid, w_gu, w_cols
         )
         stats.append(stat)
         saved.append((resid, normed, gate_pre, mixer, base, ffn_in, gate_up, hidden))
         if layer == 0:
-            cols1 = move_cols(after(cols_parts[1], pieces))
             token_parts = exchange(pieces)
-            token_parts, cols1 = lax.optimization_barrier((token_parts, cols1))
             gu1 = move_rows(after(gu_parts[1], token_parts))
+            masked = my_tokens(after(masked, token_parts))
             weights.append((spread_rows(proj1), mix_all[1], spread_cols(cols1), None))
     h1 = saved[1][0]
     stats0 = jnp.stack([stats[2][0, 0], stats[1][0, 0], stats[2][0, 1]]) / shards
@@ -2192,7 +2189,7 @@
         def at_out(pieces, running):
             return lax.optimization_barrier((pieces, running))
 
-        def sum_cols(grad_both, due, pieces):
+        def sum_cols(grad_both, due, grad_pre, pieces):
             sum_both = reduce_cols(after(grad_both, due))
             return lax.optimization_barrier((all_sums(pieces), sum_both))
 
@@ -2233,8 +2230,8 @@
         def at_out(pieces, running):
             return pieces, running
 
-        def sum_cols(grad_both, due, pieces):
-            sum_both = reduce_cols(after(grad_both, (due, pieces)))
+        def sum_cols(grad_both, due, grad_pre, pieces):
+            sum_both = reduce_cols(after(grad_both, (due, grad_pre)))
             return all_sums(pieces), sum_both
 
         def before_end(sums):
@@ -2242,7 +2239,8 @@
 
         def last_due(sum_both, sums, sum_gu, grad_resid):
             early["gu"] = collect_rows(after(sum_gu, grad_resid))
-            return sum_both, early["gu"], placed_tokens(grad_resid, grad_h1)
+            early["grads"] = placed_tokens(grad_resid, grad_h1)
+            return sum_both, early["gu"], early["grads"]
 
         return at_mid, sum_rows, start, at_end, at_out, sum_cols, before_end, last_due
 
@@ -2253,7 +2251,7 @@
     moved_both1 = early["both"]
     moved_gu0 = early["gu"]
     moved_both0 = collect_cols(after(sum_both0, moved_gu0))
-    input_grads = placed_tokens(grad_tokens, grad_h1)
+    input_grads = early["grads"]
     side = core[None].astype(jnp.int32)
     grad_down, grad_out = finish_cols(
         side, moved_both0, moved_both1, partner(pick(first, moved_both1, moved_both0)), hidden_width

time: 1320 us -> 1250 us (0.947)
  local copies, waits for them, and re-layouts: 152 us -> 62.5 us
  Pallas kernels: 285 us -> 360 us
  starting transfers between devices: 229 us -> 194 us
  waiting for transfers between devices: 589 us -> 571 us
    unnamed x445 -> x231, local copies, waits for them, and re-layouts: 115 us -> 22.2 us
    pallas_call x39, Pallas kernels: 183 us -> 252 us  [run(): pl.pallas_call(kernel, grid=grid, in_specs=in_specs, out_specs=out_specs,...]
    ppermute x48, waiting for transfers between devices: 223 us -> 157 us  [swap_pieces(): lax.ppermute(pieces[n], axis, [(i, i ^ n) for i in range(size)])]
    all_to_all x4, waiting for transfers between devices: 39.2 us -> 85.3 us  [move_rows(): return lax.all_to_all(part, SEQ, 0, 0).reshape(-1, part.shape[2])]
    ppermute x42, starting transfers between devices: 108 us -> 69.8 us  [by_partner(): lax.ppermute(value, axis, [(i, i ^ k) for i in range(size)])]
    reduce_scatter x2, waiting for transfers between devices: 23.4 us -> 0.01 us  [reduce_cols(): lax.psum_scatter(grad.reshape(-1, grad.shape[2]), (SECTION, HEAD), scatte...]
  transfers between devices with their start and end apart: 130 -> 130, of which waited for: 61 -> 59; matrix products, arithmetic and copies ran while one was open for 6% -> 6% of each run, Pallas kernels for 19% -> 26%
where the time goes in v4:
time: 1250 us; the launch traced here: 1230 us
  waiting for transfers between devices  571 us (46%)
  Pallas kernels  360 us (29%)
  starting transfers between devices  194 us (16%)
  local copies, waits for them, and re-layouts  62.5 us (5%)
  other arithmetic  29.3 us (2%)
  between operations  17.4 us (1%)
    pallas_call x39, Pallas kernels, run(): pl.pallas_call(kernel, grid=grid, in_specs=in_specs, out_specs=out_specs,...  252 us
    ppermute x42, waiting for transfers between devices, by_partner(): lax.ppermute(value, axis, [(i, i ^ k) for i in range(size)])  207 us
    ppermute x48, waiting for transfers between devices, swap_pieces(): lax.ppermute(pieces[n], axis, [(i, i ^ n) for i in range(size)])  157 us
    all_to_all x4, waiting for transfers between devices, move_rows(): return lax.all_to_all(part, SEQ, 0, 0).reshape(-1, part.shape[2])  85.3 us
    ppermute x42, starting transfers between devices, by_partner(): lax.ppermute(value, axis, [(i, i ^ k) for i in range(size)])  69.8 us
    pallas_call x2, Pallas kernels, recur_backward(): pl.pallas_call(functools.partial(backward_kernel, parts), out_shape=(jax....  65.6 us
    ppermute x48, starting transfers between devices, swap_pieces(): lax.ppermute(pieces[n], axis, [(i, i ^ n) for i in range(size)])  50.1 us
    all_to_all x4, waiting for transfers between devices, collect_rows(): return lax.all_to_all(part.reshape(shards, -1, part.shape[1]), SEQ, 0, 0)  42.8 us
  transfers between devices with their start and end apart: 130, of which 59 were waited for; matrix products, arithmetic and copies ran while one was open for 6% of the time, Pallas kernels for 26%

profile of v4, /device:TPU:1, one launch (start us, length us, event | category | flops | bytes accessed | tf_op | source)
XLA Modules:
  0.0 1234.3 jit_solution(6800058053261454273)
XLA Ops:
  41.7 24.6 %all-to-all-done = bf16[4,256,768]{2,1,0:T(8,128)(2,1)} async-done(((bf16[4,256,768]{2,1,0:T(8,128)(2,1)}), bf16[4,256,768]{2,1,0:T(8,128)(2,1)}, u32[]{:S(2)}, u32[]{:S(2)}) %all-to-all-start) | async-done | bytes 1572896 | tf_op jit(solution)/shard_map/all_to_all | solution.py:1900
  79.1 12.9 %collective-permute-done.3 = f32[1,10496]{1,0:T(1,128)S(1)} collective-permute-done((f32[1,10496]{1,0:T(1,128)S(1)}, f32[1,10496]{1,0:T(1,128)S(1)}, u32[]{:S(2)}, u32[]{:S(2)}) %collective-permute-start.3) | collective-permute-done | bytes 42016 | tf_op jit(solution)/shard_map/ppermute | solution.py:1852
  103.3 17.0 %collective-permute-done.5.refs_4_ = bf16[64,2048]{1,0:T(8,128)(2,1)S(1)} collective-permute-done((bf16[64,2048]{1,0:T(8,128)(2,1)S(1)}, bf16[64,2048]{1,0:T(8,128)(2,1)S(1)}, u32[]{:S(2)}, u32[]{:S(2)}) %collective-permute-start.5) | collective-permute-done | bytes 262176 | tf_op jit(solution)/shard_map/ppermute | solution.py:1852
  139.2 9.7 project_first.1
  153.9 17.6 %all-to-all-done.2 = bf16[4,256,768]{2,1,0:T(8,128)(2,1)S(1)} async-done(((bf16[4,256,768]{2,1,0:T(8,128)(2,1)}), bf16[4,256,768]{2,1,0:T(8,128)(2,1)S(1)}, u32[]{:S(2)}, u32[]{:S(2)}) %all-to-all-start.2) | async-done | bytes 1572896 | tf_op jit(solution)/shard_map/all_to_all | solution.py:1900
  186.8 34.3 %all-to-all-done.3 = bf16[4,256,768]{2,1,0:T(8,128)(2,1)S(1)} async-done(((bf16[4,256,768]{2,1,0:T(8,128)(2,1)}), bf16[4,256,768]{2,1,0:T(8,128)(2,1)S(1)}, u32[]{:S(2)}, u32[]{:S(2)}) %all-to-all-start.3) | async-done | bytes 1572896 | tf_op jit(solution)/shard_map/all_to_all | solution.py:1900
  226.0 21.0 %recur_forward.2 = (bf16[256,256]{1,0:T(8,128)(2,1)}, bf16[256,256]{1,0:T(8,128)(2,1)}, bf16[256,256]{1,0:T(8,128)(2,1)}, bf16[256,256]{1,0:T(8,128)(2,1)}, f32[16,128,256]{2,1,0:T(8,128)}, /*index=5*/f32[1024,64]{1,0:T(8,128)}) custom-call(s32[1]{0:T(128)} %bitcast.piece_ref.me_ref, bf16[256,640]{1,0:T(8,128)(2,1)} %get-tuple-element.263.refs_0_, ...), custom_call_target="tpu_custom_call" | custom-call | flops 40960000000 | bytes 8388608 | tf_op jit(solution)/shard_map/recur_forward/pallas_call | solution.py:980
  269.1 8.0 collective-permute-done.19.refs_1_
  295.0 20.8 %collective-permute-done.23.refs_5_ = bf16[64,2048]{1,0:T(8,128)(2,1)S(1)} collective-permute-done((bf16[64,2048]{1,0:T(8,128)(2,1)}, bf16[64,2048]{1,0:T(8,128)(2,1)S(1)}, u32[]{:S(2)}, u32[]{:S(2)}) %collective-permute-start.23) | collective-permute-done | bytes 262176 | tf_op jit(solution)/shard_map/ppermute | solution.py:1852
  316.5 15.8 %feed.2 = (f32[256,2048]{1,0:T(8,128)}, bf16[256,2048]{1,0:T(8,128)(2,1)}, f32[4,256,768]{2,1,0:T(8,128)}, bf16[256,1536]{1,0:T(8,128)(2,1)}, bf16[64,2048]{1,0:...) custom-call(s32[1]{0:T(128)} %bitcast.1.refs_0_.me_ref, ...), custom_call_target="tpu_custom_call" | custom-call | flops 4831838208 | bytes 27262976 | tf_op jit(solution)/shard_map/feed/pallas_call | solution.py:1070
  342.8 9.2 collective-permute-done.26.refs_2_
  362.1 20.2 %collective-permute-done.29.refs_5_ = bf16[64,2048]{1,0:T(8,128)(2,1)S(1)} collective-permute-done((bf16[64,2048]{1,0:T(8,128)(2,1)}, bf16[64,2048]{1,0:T(8,128)(2,1)S(1)}, u32[]{:S(2)}, u32[]{:S(2)}) %collective-permute-start.29) | collective-permute-done | bytes 262176 | tf_op jit(solution)/shard_map/ppermute | solution.py:1852
  383.2 10.9 project_next.1
  407.9 9.5 collective-permute-done.32.refs_2_
  422.4 21.0 %recur_forward.3 = (bf16[256,256]{1,0:T(8,128)(2,1)}, bf16[256,256]{1,0:T(8,128)(2,1)}, bf16[256,256]{1,0:T(8,128)(2,1)}, bf16[256,256]{1,0:T(8,128)(2,1)}, f32[16,128,256]{2,1,0:T(8,128)}, /*index=5*/f32[1024,64]{1,0:T(8,128)}) custom-call(s32[1]{0:T(128)} %bitcast.piece_ref.me_ref, bf16[256,640]{1,0:T(8,128)(2,1)} %get-tuple-element.518.refs_0_, ...), custom_call_target="tpu_custom_call" | custom-call | flops 40960000000 | bytes 8388608 | tf_op jit(solution)/shard_map/recur_forward/pallas_call | solution.py:980
  446.2 8.9 all-to-all-done.5
  465.3 8.0 collective-permute-done.40.refs_1_
  492.5 16.2 %collective-permute-done.44.refs_5_ = bf16[64,2048]{1,0:T(8,128)(2,1)S(1)} collective-permute-done((bf16[64,2048]{1,0:T(8,128)(2,1)}, bf16[64,2048]{1,0:T(8,128)(2,1)S(1)}, u32[]{:S(2)}, u32[]{:S(2)}) %collective-permute-start.44) | collective-permute-done | bytes 262176 | tf_op jit(solution)/shard_map/ppermute | solution.py:1852
  508.7 20.8 %all-gather.17.cloned.1.call-done = bf16[8192,768]{1,0:T(8,128)(2,1)} async-done(((bf16[1024,768]{1,0:T(8,128)(2,1)}), bf16[8192,768]{1,0:T(8,128)(2,1)}) %all-gather.17.cloned.1.call-update) | async-done | bytes 12582928 | tf_op jit(solution)/shard_map/all_gather | solution.py:1908
  529.6 14.9 %feed.3 = (f32[256,2048]{1,0:T(8,128)}, bf16[256,2048]{1,0:T(8,128)(2,1)}, f32[4,256,768]{2,1,0:T(8,128)}, bf16[256,1536]{1,0:T(8,128)(2,1)}, bf16[64,2048]{1,0:...) custom-call(s32[1]{0:T(128)} %bitcast.1.refs_0_.me_ref, ...), custom_call_target="tpu_custom_call" | custom-call | flops 4831838208 | bytes 27262976 | tf_op jit(solution)/shard_map/feed/pallas_call | solution.py:1070
  544.5 14.1 %feed_back.2 = (bf16[4,256,768]{2,1,0:T(8,128)(2,1)}, bf16[64,2048]{1,0:T(8,128)(2,1)}, bf16[64,2048]{1,0:T(8,128)(2,1)}, bf16[64,2048]{1,0:T(8,128)(2,1)}, bf16[64,2048]{1,0:T(8,128)(2,1)}) custom-call(s32[1]{0:T(128)} %bitcast.1.refs_0_.me_ref, bf16[256,2048]{1,0:T(8,128)(2,1)} %place.1.up_ref.refs_7_, f32[4,256,768]{2,1,0:T(8,128)} %get-tuple-element.313.gate_up_ref, ...), custom_call_target="tpu_custom_call" | custom-call | flops 4831838208 | bytes 25690112 | tf_op jit(solution)/shard_map/feed_back/pallas_call | solution.py:1070
  558.6 8.2 grad_rows.4
  571.3 9.1 collective-permute-done.46.refs_1_
  580.4 8.1 collective-permute-done.48.refs_3_
  598.4 19.8 %collective-permute-done.50.refs_4_ = bf16[64,2048]{1,0:T(8,128)(2,1)S(1)} collective-permute-done((bf16[64,2048]{1,0:T(8,128)(2,1)}, bf16[64,2048]{1,0:T(8,128)(2,1)S(1)}, u32[]{:S(2)}, u32[]{:S(2)}) %collective-permute-start.50) | collective-permute-done | bytes 262176 | tf_op jit(solution)/shard_map/ppermute | solution.py:1852
  619.1 8.9 mid_back.2
  632.4 10.5 grad_cols.2
  646.6 32.9 %recur_backward.2 = (bf16[256,640]{1,0:T(8,128)(2,1)}, bf16[256,640]{1,0:T(8,128)(2,1)}, bf16[256,640]{1,0:T(8,128)(2,1)}, bf16[256,640]{1,0:T(8,128)(2,1)}, f32[8,512]{1,0:T(8,128)}, /*index=5*/f32[8,128]{1,0:T(8,128)}) custom-call(s32[1]{0:T(128)} %bitcast.piece_ref.me_ref, bf16[256,640]{1,0:T(8,128)(2,1)} %get-tuple-element.518.refs_0_, ...), custom_call_target="tpu_custom_call" | custom-call | flops 40960000000 | bytes 8388608 | tf_op jit(solution)/shard_map/recur_backward/pallas_call | solution.py:1005
  698.6 11.6 project_back.2
  710.3 10.2 all-to-all-done.6.layer1_ref
  724.1 8.3 grad_rows.5
  749.1 21.0 %collective-permute-done.65.refs_4_ = bf16[64,2048]{1,0:T(8,128)(2,1)} collective-permute-done((bf16[64,2048]{1,0:T(8,128)(2,1)}, bf16[64,2048]{1,0:T(8,128)(2,1)}, u32[]{:S(2)}, u32[]{:S(2)}) %collective-permute-start.65) | collective-permute-done | bytes 262176 | tf_op jit(solution)/shard_map/ppermute | solution.py:1852
  782.9 15.5 %feed_back.3 = (bf16[4,256,768]{2,1,0:T(8,128)(2,1)}, bf16[64,2048]{1,0:T(8,128)(2,1)}, bf16[64,2048]{1,0:T(8,128)(2,1)}, bf16[64,2048]{1,0:T(8,128)(2,1)}, bf16[64,2048]{1,0:T(8,128)(2,1)}) custom-call(s32[1]{0:T(128)} %bitcast.1.refs_0_.me_ref, bf16[256,2048]{1,0:T(8,128)(2,1)} %get-tuple-element.394.up_ref.refs_7_, ...), custom_call_target="tpu_custom_call" | custom-call | flops 4831838208 | bytes 25690112 | tf_op jit(solution)/shard_map/feed_back/pallas_call | solution.py:1070
  802.1 8.1 grad_rows.6
  810.2 20.5 %collective-permute-done.72.refs_2_ = bf16[64,2048]{1,0:T(8,128)(2,1)} collective-permute-done((bf16[64,2048]{1,0:T(8,128)(2,1)}, bf16[64,2048]{1,0:T(8,128)(2,1)}, u32[]{:S(2)}, u32[]{:S(2)}) %collective-permute-start.72) | collective-permute-done | bytes 262176 | tf_op jit(solution)/shard_map/ppermute | solution.py:1874
  840.0 20.0 %collective-permute-done.75.refs_4_ = bf16[64,2048]{1,0:T(8,128)(2,1)} collective-permute-done((bf16[64,2048]{1,0:T(8,128)(2,1)}, bf16[64,2048]{1,0:T(8,128)(2,1)}, u32[]{:S(2)}, u32[]{:S(2)}) %collective-permute-start.75) | collective-permute-done | bytes 262176 | tf_op jit(solution)/shard_map/ppermute | solution.py:1852
  860.0 8.8 mid_back.3
  873.2 11.0 grad_cols.3
  889.1 32.7 %recur_backward.3 = (bf16[256,640]{1,0:T(8,128)(2,1)}, bf16[256,640]{1,0:T(8,128)(2,1)}, bf16[256,640]{1,0:T(8,128)(2,1)}, bf16[256,640]{1,0:T(8,128)(2,1)}, f32[8,512]{1,0:T(8,128)}, /*index=5*/f32[8,128]{1,0:T(8,128)}) custom-call(s32[1]{0:T(128)} %bitcast.piece_ref.me_ref, bf16[256,640]{1,0:T(8,128)(2,1)} %get-tuple-element.263.refs_0_, ...), custom_call_target="tpu_custom_call" | custom-call | flops 40960000000 | bytes 8388608 | tf_op jit(solution)/shard_map/recur_backward/pallas_call | solution.py:1005
  928.2 10.2 collective-permute-done.80.refs_1_
  946.3 11.6 project_back.3
  969.0 8.1 grad_rows.7
  977.7 8.3 collective-permute-done.85.refs_3_
  995.4 20.7 %collective-permute-done.87.refs_4_ = bf16[64,2048]{1,0:T(8,128)(2,1)} collective-permute-done((bf16[64,2048]{1,0:T(8,128)(2,1)}, bf16[64,2048]{1,0:T(8,128)(2,1)}, u32[]{:S(2)}, u32[]{:S(2)}) %collective-permute-start.87) | collective-permute-done | bytes 262176 | tf_op jit(solution)/shard_map/ppermute | solution.py:1852
  1032.3 19.3 %collective-permute-done.92.refs_3_ = bf16[2,64,2048]{2,1,0:T(8,128)(2,1)S(1)} collective-permute-done((bf16[2,64,2048]{2,1,0:T(8,128)(2,1)S(1)}, bf16[2,64,2048]{2,1,0:T(8,128)(2,1)S(1)}, u32[]{:S(2)}, u32[]{:S(2)}) %collective-permute-start.92) | collective-permute-done | bytes 524320 | tf_op jit(solution)/shard_map/ppermute | solution.py:1852
  1051.7 15.1 %collective-permute-done.91.refs_2_ = bf16[2,64,2048]{2,1,0:T(8,128)(2,1)S(1)} collective-permute-done((bf16[2,64,2048]{2,1,0:T(8,128)(2,1)S(1)}, bf16[2,64,2048]{2,1,0:T(8,128)(2,1)S(1)}, u32[]{:S(2)}, u32[]{:S(2)}) %collective-permute-start.91) | collective-permute-done | bytes 524320 | tf_op jit(solution)/shard_map/ppermute | solution.py:1852
  1107.8 23.9 %all-to-all-done.10.layer0_ref = bf16[4,640,256]{2,1,0:T(8,128)(2,1)S(1)} async-done(((bf16[4,640,256]{2,1,0:T(8,128)(2,1)}), bf16[4,640,256]{2,1,0:T(8,128)(2,1)S(1)}, u32[]{:S(2)}, u32[]{:S(2)}) %all-to-all-start.10) | async-done | bytes 1310752 | tf_op jit(solution)/shard_map/all_to_all | solution.py:1935
  1180.2 28.8 %all-to-all-done.13.layer0_ref = bf16[4,256,768]{2,1,0:T(8,128)(2,1)S(1)} async-done(((bf16[4,256,768]{2,1,0:T(8,128)(2,1)}), bf16[4,256,768]{2,1,0:T(8,128)(2,1)S(1)}, u32[]{:S(2)}, u32[]{:S(2)}) %all-to-all-start.13) | async-done | bytes 1572896 | tf_op jit(solution)/shard_map/all_to_all | solution.py:1931
  (653 shorter events, 470.3 us)
Async XLA Ops:
  24.3 42.0 %all-to-all-start = ((bf16[4,256,768]{2,1,0:T(8,128)(2,1)}), bf16[4,256,768]{2,1,0:T(8,128)(2,1)}, u32[]{:S(2)}, u32[]{:S(2)}) async-start(bf16[4,256,768]{2,1,0:T(8,128)(2,1)} %get-tuple-element.498), calls=%async_computation | async-start | bytes 3145728 | tf_op jit(solution)/shard_map/all_to_all | solution.py:1900
  29.7 109.5 %all-gather.7.cloned.1.call-start = ((), (), s32[]{:S(2)}) async-start(), calls=%async_computation.20 | async-start | bytes 14155776 | tf_op jit(solution)/shard_map/all_gather | solution.py:1908
  67.8 35.5 %collective-permute-start.7 = (bf16[64,2048]{1,0:T(8,128)(2,1)S(1)}, bf16[64,2048]{1,0:T(8,128)(2,1)S(1)}, u32[]{:S(2)}, u32[]{:S(2)}) collective-permute-start(bf16[64,2048]{1,0:T(8,128)(2,1)S(1)} %reshape.346.refs_3_), channel_id=1, source_target_pairs={{0,12},{4,8},{8,4},{12,0},{1,13},{5,9},{9,5},{13,1},{2,14},{6,10},... | collective-permute-start | bytes 786440 | tf_op jit(solution)/shard_map/ppermute | solution.py:1852
  68.7 34.7 %collective-permute-start.6 = (bf16[64,2048]{1,0:T(8,128)(2,1)S(1)}, bf16[64,2048]{1,0:T(8,128)(2,1)S(1)}, u32[]{:S(2)}, u32[]{:S(2)}) collective-permute-start(bf16[64,2048]{1,0:T(8,128)(2,1)S(1)} %reshape.346.refs_3_), channel_id=1, source_target_pairs={{0,8},{4,12},{8,0},{12,4},{1,9},{5,13},{9,1},{13,5},{2,10},{6,14},... | collective-permute-start | bytes 786440 | tf_op jit(solution)/shard_map/ppermute | solution.py:1852
  92.5 34.4 %all-to-all-start.1 = ((bf16[4,640,256]{2,1,0:T(8,128)(2,1)}), bf16[4,640,256]{2,1,0:T(8,128)(2,1)S(1)}, u32[]{:S(2)}, u32[]{:S(2)}) async-start(bf16[4,640,256]{2,1,0:T(8,128)(2,1)} %get-tuple-element.260), calls=%async_computation.1 | async-start | bytes 2621440 | tf_op jit(solution)/shard_map/all_to_all | solution.py:2115
  96.0 164.6 %all-gather.9.cloned.1.call-start = ((), (), s32[]{:S(2)}) async-start(), calls=%async_computation.21 | async-start | bytes 11796480 | tf_op jit(solution)/shard_map/all_gather | solution.py:1913
  131.4 40.1 %all-to-all-start.2 = ((bf16[4,256,768]{2,1,0:T(8,128)(2,1)}), bf16[4,256,768]{2,1,0:T(8,128)(2,1)S(1)}, u32[]{:S(2)}, u32[]{:S(2)}) async-start(bf16[4,256,768]{2,1,0:T(8,128)(2,1)} %get-tuple-element.262), calls=%async_computation.2 | async-start | bytes 3145728 | tf_op jit(solution)/shard_map/all_to_all | solution.py:1900
  135.1 180.7 %all-gather.11.cloned.1.call-start = ((), (), s32[]{:S(2)}) async-start(), calls=%async_computation.22 | async-start | bytes 14155776 | tf_op jit(solution)/shard_map/all_gather | solution.py:1908
  153.6 26.6 %collective-permute-start.13 = (bf16[256,640]{1,0:T(8,128)(2,1)S(1)}, bf16[256,640]{1,0:T(8,128)(2,1)}, u32[]{:S(2)}, u32[]{:S(2)}) collective-permute-start(bf16[256,640]{1,0:T(8,128)(2,1)S(1)} %get-tuple-element.521), channel_id=1, source_target_pairs={{0,1},{1,0},{2,3},{3,2},{4,5},{5,4},{6,7},{7,6},{8,9},{9,8},{10,11... | collective-permute-start | bytes 983048 | tf_op jit(solution)/shard_map/ppermute | solution.py:1874
  180.3 40.8 %all-to-all-start.3 = ((bf16[4,256,768]{2,1,0:T(8,128)(2,1)}), bf16[4,256,768]{2,1,0:T(8,128)(2,1)S(1)}, u32[]{:S(2)}, u32[]{:S(2)}) async-start(bf16[4,256,768]{2,1,0:T(8,128)(2,1)} %get-tuple-element.272), calls=%async_computation.3 | async-start | bytes 3145728 | tf_op jit(solution)/shard_map/all_to_all | solution.py:1900
  221.1 35.2 %all-to-all-start.4 = ((bf16[4,640,256]{2,1,0:T(8,128)(2,1)}), bf16[4,640,256]{2,1,0:T(8,128)(2,1)}, u32[]{:S(2)}, u32[]{:S(2)}) async-start(bf16[4,640,256]{2,1,0:T(8,128)(2,1)} %get-tuple-element.273), calls=%async_computation.4 | async-start | bytes 2621440 | tf_op jit(solution)/shard_map/all_to_all | solution.py:1904
  225.5 156.9 %all-gather.13.cloned.1.call-start = ((), (), s32[]{:S(2)}) async-start(), calls=%async_computation.23 | async-start | bytes 14155776 | tf_op jit(solution)/shard_map/all_gather | solution.py:1908
  260.0 196.8 %all-gather.15.cloned.1.call-start = ((), (), s32[]{:S(2)}) async-start(), calls=%async_computation.24 | async-start | bytes 11796480 | tf_op jit(solution)/shard_map/all_gather | solution.py:1913
  288.3 27.4 %collective-permute-start.23 = (bf16[64,2048]{1,0:T(8,128)(2,1)}, bf16[64,2048]{1,0:T(8,128)(2,1)S(1)}, u32[]{:S(2)}, u32[]{:S(2)}) collective-permute-start(bf16[64,2048]{1,0:T(8,128)(2,1)} %sum_pieces.8.refs_3_), channel_id=1, source_target_pairs={{0,8},{4,12},{8,0},{12,4},{1,9},{5,13},{9,1},{13,5},{2,10},{6,14},... | collective-permute-start | bytes 786440 | tf_op jit(solution)/shard_map/ppermute | solution.py:1852
  355.8 26.5 %collective-permute-start.29 = (bf16[64,2048]{1,0:T(8,128)(2,1)}, bf16[64,2048]{1,0:T(8,128)(2,1)S(1)}, u32[]{:S(2)}, u32[]{:S(2)}) collective-permute-start(bf16[64,2048]{1,0:T(8,128)(2,1)} %sum_pieces.9.refs_3_), channel_id=1, source_target_pairs={{0,8},{4,12},{8,0},{12,4},{1,9},{5,13},{9,1},{13,5},{2,10},{6,14},... | collective-permute-start | bytes 786440 | tf_op jit(solution)/shard_map/ppermute | solution.py:1852
  399.7 44.0 %collective-permute-start.39 = (bf16[64,2048]{1,0:T(8,128)(2,1)S(1)}, bf16[64,2048]{1,0:T(8,128)(2,1)}, u32[]{:S(2)}, u32[]{:S(2)}) collective-permute-start(bf16[64,2048]{1,0:T(8,128)(2,1)S(1)} %reshape.360.refs_1_), channel_id=1, source_target_pairs={{0,12},{4,8},{8,4},{12,0},{1,13},{5,9},{9,5},{13,1},{2,14},{6,10},... | collective-permute-start | bytes 786440 | tf_op jit(solution)/shard_map/ppermute | solution.py:1852
  400.9 45.3 %collective-permute-start.38 = (bf16[64,2048]{1,0:T(8,128)(2,1)S(1)}, bf16[64,2048]{1,0:T(8,128)(2,1)}, u32[]{:S(2)}, u32[]{:S(2)}) collective-permute-start(bf16[64,2048]{1,0:T(8,128)(2,1)S(1)} %reshape.360.refs_1_), channel_id=1, source_target_pairs={{0,8},{4,12},{8,0},{12,4},{1,9},{5,13},{9,1},{13,5},{2,10},{6,14},... | collective-permute-start | bytes 786440 | tf_op jit(solution)/shard_map/ppermute | solution.py:1852
  400.9 54.2 %all-to-all-start.5 = ((bf16[4,256,768]{2,1,0:T(8,128)(2,1)}), bf16[4,256,768]{2,1,0:T(8,128)(2,1)S(1)}, u32[]{:S(2)}, u32[]{:S(2)}) async-start(bf16[4,256,768]{2,1,0:T(8,128)(2,1)} %get-tuple-element.296), calls=%async_computation.5 | async-start | bytes 3145728 | tf_op jit(solution)/shard_map/all_to_all | solution.py:1900
  404.6 125.0 %all-gather.17.cloned.1.call-start = ((), (), s32[]{:S(2)}) async-start(), calls=%async_computation.25 | async-start | bytes 14155776 | tf_op jit(solution)/shard_map/all_gather | solution.py:1908
  407.9 38.3 %collective-permute-start.37 = (bf16[64,2048]{1,0:T(8,128)(2,1)S(1)}, bf16[64,2048]{1,0:T(8,128)(2,1)}, u32[]{:S(2)}, u32[]{:S(2)}) collective-permute-start(bf16[64,2048]{1,0:T(8,128)(2,1)S(1)} %reshape.360.refs_1_), channel_id=1, source_target_pairs={{0,4},{4,0},{8,12},{12,8},{1,5},{5,1},{9,13},{13,9},{2,6},{6,2},{1... | collective-permute-start | bytes 786440 | tf_op jit(solution)/shard_map/ppermute | solution.py:1852
  456.3 223.2 %reduce-scatter.7.cloned.1.call-start = ((), (), s32[]{:S(2)}) async-start(), calls=%async_computation.26 | async-start | bytes 14155776 | tf_op jit(solution)/shard_map/reduce_scatter | solution.py:1918
  566.8 203.3 %reduce-scatter.9.cloned.1.call-start = ((), (), s32[]{:S(2)}) async-start(), calls=%async_computation.27 | async-start | bytes 11796480 | tf_op jit(solution)/shard_map/reduce_scatter | solution.py:1924
  642.9 36.5 %collective-permute-start.55 = (bf16[64,2048]{1,0:T(8,128)(2,1)S(1)}, bf16[64,2048]{1,0:T(8,128)(2,1)S(1)}, u32[]{:S(2)}, u32[]{:S(2)}) collective-permute-start(bf16[64,2048]{1,0:T(8,128)(2,1)S(1)} %copy-done.102), channel_id=1, source_target_pairs={{0,4},{4,0},{8,12},{12,8},{1,5},{5,1},{9,13},{13,9},{2,6},{6,2},{1... | collective-permute-start | bytes 786440 | tf_op jit(solution)/shard_map/ppermute | solution.py:1874
  643.0 36.5 %collective-permute-start.56 = (bf16[64,2048]{1,0:T(8,128)(2,1)S(1)}, bf16[64,2048]{1,0:T(8,128)(2,1)S(1)}, u32[]{:S(2)}, u32[]{:S(2)}) collective-permute-start(bf16[64,2048]{1,0:T(8,128)(2,1)S(1)} %copy-done.101), channel_id=1, source_target_pairs={{0,8},{4,12},{8,0},{12,4},{1,9},{5,13},{9,1},{13,5},{2,10},{6,14},... | collective-permute-start | bytes 786440 | tf_op jit(solution)/shard_map/ppermute | solution.py:1874
  645.5 34.0 %collective-permute-start.57 = (bf16[64,2048]{1,0:T(8,128)(2,1)S(1)}, bf16[64,2048]{1,0:T(8,128)(2,1)S(1)}, u32[]{:S(2)}, u32[]{:S(2)}) collective-permute-start(bf16[64,2048]{1,0:T(8,128)(2,1)S(1)} %copy-done.100), channel_id=1, source_target_pairs={{0,12},{4,8},{8,4},{12,0},{1,13},{5,9},{9,5},{13,1},{2,14},{6,10},... | collective-permute-start | bytes 786440 | tf_op jit(solution)/shard_map/ppermute | solution.py:1874
  680.4 40.1 %all-to-all-start.6 = ((bf16[4,256,768]{2,1,0:T(8,128)(2,1)}), bf16[4,256,768]{2,1,0:T(8,128)(2,1)S(1)}, u32[]{:S(2)}, u32[]{:S(2)}) async-start(bf16[4,256,768]{2,1,0:T(8,128)(2,1)} %bitcast.311), calls=%async_computation.7 | async-start | bytes 3145728 | tf_op jit(solution)/shard_map/all_to_all | solution.py:1931
  684.1 184.7 %reduce-scatter.11.cloned.1.call-start = ((), (), s32[]{:S(2)}) async-start(), calls=%async_computation.28 | async-start | bytes 14155776 | tf_op jit(solution)/shard_map/reduce_scatter | solution.py:1918
  742.6 27.5 %collective-permute-start.65 = (bf16[64,2048]{1,0:T(8,128)(2,1)}, bf16[64,2048]{1,0:T(8,128)(2,1)}, u32[]{:S(2)}, u32[]{:S(2)}) collective-permute-start(bf16[64,2048]{1,0:T(8,128)(2,1)} %sum_pieces.12.refs_2_), channel_id=1, source_target_pairs={{0,8},{4,12},{8,0},{12,4},{1,9},{5,13},{9,1},{13,5},{2,10},{6,14},... | collective-permute-start | bytes 786440 | tf_op jit(solution)/shard_map/ppermute | solution.py:1852
  778.5 81.4 %all-to-all-start.7 = ((bf16[4,640,256]{2,1,0:T(8,128)(2,1)}), bf16[4,640,256]{2,1,0:T(8,128)(2,1)}, u32[]{:S(2)}, u32[]{:S(2)}) async-start(bf16[4,640,256]{2,1,0:T(8,128)(2,1)} %split_cols.2), calls=%async_computation.9 | async-start | bytes 2621440 | tf_op jit(solution)/shard_map/all_to_all | solution.py:1935
  782.9 182.4 %reduce-scatter.13.cloned.1.call-start = ((), (), s32[]{:S(2)}) async-start(), calls=%async_computation.29 | async-start | bytes 14155776 | tf_op jit(solution)/shard_map/reduce_scatter | solution.py:1918
  800.0 30.7 %collective-permute-start.72 = (bf16[64,2048]{1,0:T(8,128)(2,1)}, bf16[64,2048]{1,0:T(8,128)(2,1)}, u32[]{:S(2)}, u32[]{:S(2)}) collective-permute-start(bf16[64,2048]{1,0:T(8,128)(2,1)} %get-tuple-element.398), channel_id=1, source_target_pairs={{0,8},{4,12},{8,0},{12,4},{1,9},{5,13},{9,1},{13,5},{2,10},{6,14},... | collective-permute-start | bytes 786440 | tf_op jit(solution)/shard_map/ppermute | solution.py:1874
  802.1 28.6 %collective-permute-start.73 = (bf16[64,2048]{1,0:T(8,128)(2,1)}, bf16[64,2048]{1,0:T(8,128)(2,1)}, u32[]{:S(2)}, u32[]{:S(2)}) collective-permute-start(bf16[64,2048]{1,0:T(8,128)(2,1)} %get-tuple-element.399), channel_id=1, source_target_pairs={{0,12},{4,8},{8,4},{12,0},{1,13},{5,9},{9,5},{13,1},{2,14},{6,10},... | collective-permute-start | bytes 786440 | tf_op jit(solution)/shard_map/ppermute | solution.py:1874
  833.9 26.1 %collective-permute-start.75 = (bf16[64,2048]{1,0:T(8,128)(2,1)}, bf16[64,2048]{1,0:T(8,128)(2,1)}, u32[]{:S(2)}, u32[]{:S(2)}) collective-permute-start(bf16[64,2048]{1,0:T(8,128)(2,1)} %sum_pieces.14.refs_2_), channel_id=1, source_target_pairs={{0,8},{4,12},{8,0},{12,4},{1,9},{5,13},{9,1},{13,5},{2,10},{6,14},... | collective-permute-start | bytes 786440 | tf_op jit(solution)/shard_map/ppermute | solution.py:1852
  884.2 41.3 %all-to-all-start.8 = ((bf16[4,256,768]{2,1,0:T(8,128)(2,1)}), bf16[4,256,768]{2,1,0:T(8,128)(2,1)}, u32[]{:S(2)}, u32[]{:S(2)}) async-start(bf16[4,256,768]{2,1,0:T(8,128)(2,1)} %bitcast.312), calls=%async_computation.11 | async-start | bytes 3145728 | tf_op jit(solution)/shard_map/all_to_all | solution.py:1931
  889.0 183.0 %reduce-scatter.15.cloned.1.call-start = ((), (), s32[]{:S(2)}) async-start(), calls=%async_computation.30 | async-start | bytes 11796480 | tf_op jit(solution)/shard_map/reduce_scatter | solution.py:1924
  989.5 26.7 %collective-permute-start.87 = (bf16[64,2048]{1,0:T(8,128)(2,1)}, bf16[64,2048]{1,0:T(8,128)(2,1)}, u32[]{:S(2)}, u32[]{:S(2)}) collective-permute-start(bf16[64,2048]{1,0:T(8,128)(2,1)} %sum_pieces.15.refs_2_), channel_id=1, source_target_pairs={{0,8},{4,12},{8,0},{12,4},{1,9},{5,13},{9,1},{13,5},{2,10},{6,14},... | collective-permute-start | bytes 786440 | tf_op jit(solution)/shard_map/ppermute | solution.py:1852
  1021.1 50.9 %all-to-all-start.9 = ((bf16[4,256,768]{2,1,0:T(8,128)(2,1)}), bf16[4,256,768]{2,1,0:T(8,128)(2,1)}, u32[]{:S(2)}, u32[]{:S(2)}) async-start(bf16[4,256,768]{2,1,0:T(8,128)(2,1)} %bitcast.310), calls=%async_computation.14 | async-start | bytes 3145728 | tf_op jit(solution)/shard_map/all_to_all | solution.py:1931
  1025.6 143.3 %reduce-scatter.17.cloned.1.call-start = ((), (), s32[]{:S(2)}) async-start(), calls=%async_computation.31 | async-start | bytes 14155776 | tf_op jit(solution)/shard_map/reduce_scatter | solution.py:1918
  1030.9 35.9 %collective-permute-start.91 = (bf16[2,64,2048]{2,1,0:T(8,128)(2,1)S(1)}, bf16[2,64,2048]{2,1,0:T(8,128)(2,1)S(1)}, u32[]{:S(2)}, u32[]{:S(2)}) collective-permute-start(bf16[2,64,2048]{2,1,0:T(8,128)(2,1)S(1)} %pad_maximum_fusion.1.refs_0_), channel_id=1, source_target_pairs={{0,2},{1,3},{2,0},{3,1},{4,6},{5,7},{6,4},{7,5},{8,10},{9,11},{10,... | collective-permute-start | bytes 1572872 | tf_op jit(solution)/shard_map/ppermute | solution.py:1852
  1031.9 37.0 %collective-permute-start.90 = (bf16[2,64,2048]{2,1,0:T(8,128)(2,1)S(1)}, bf16[2,64,2048]{2,1,0:T(8,128)(2,1)}, u32[]{:S(2)}, u32[]{:S(2)}) collective-permute-start(bf16[2,64,2048]{2,1,0:T(8,128)(2,1)S(1)} %pad_maximum_fusion.1.refs_0_), channel_id=1, source_target_pairs={{0,1},{1,0},{2,3},{3,2},{4,5},{5,4},{6,7},{7,6},{8,9},{9,8},{10,11... | collective-permute-start | bytes 1572872 | tf_op jit(solution)/shard_map/ppermute | solution.py:1852
  1096.1 35.6 %all-to-all-start.10 = ((bf16[4,640,256]{2,1,0:T(8,128)(2,1)}), bf16[4,640,256]{2,1,0:T(8,128)(2,1)S(1)}, u32[]{:S(2)}, u32[]{:S(2)}) async-start(bf16[4,640,256]{2,1,0:T(8,128)(2,1)} %split_cols.3), calls=%async_computation.16 | async-start | bytes 2621440 | tf_op jit(solution)/shard_map/all_to_all | solution.py:1935
  1104.5 31.8 %collective-permute-start.96 = (f32[4360]{0:T(1024)S(1)}, f32[4360]{0:T(1024)S(1)}, u32[]{:S(2)}, u32[]{:S(2)}) collective-permute-start(f32[4360]{0:T(1024)S(1)} %slice.426), channel_id=1, source_target_pairs={{0,1},{1,0},{2,3},{3,2},{4,5},{5,4},{6,7},{7,6},{8,9},{9,8},{10,11... | collective-permute-start | bytes 52328 | tf_op jit(solution)/shard_map/ppermute | solution.py:30
  1107.8 49.4 %collective-permute-start.94 = (bf16[4,256,768]{2,1,0:T(8,128)(2,1)}, bf16[4,256,768]{2,1,0:T(8,128)(2,1)S(1)}, u32[]{:S(2)}, u32[]{:S(2)}) collective-permute-start(bf16[4,256,768]{2,1,0:T(8,128)(2,1)} %broadcast_select_fusion.1), channel_id=1, source_target_pairs={{0,16},{16,0},{1,17},{17,1},{2,18},{18,2},{3,19},{19,3},{4,20},{20... | collective-permute-start | bytes 4718600 | tf_op jit(solution)/shard_map/ppermute | solution.py:30
  1133.1 30.9 %collective-permute-start.93 = (bf16[4,640,256]{2,1,0:T(8,128)(2,1)}, bf16[4,640,256]{2,1,0:T(8,128)(2,1)}, u32[]{:S(2)}, u32[]{:S(2)}) collective-permute-start(bf16[4,640,256]{2,1,0:T(8,128)(2,1)} %broadcast_select_fusion.6), channel_id=1, source_target_pairs={{0,16},{16,0},{1,17},{17,1},{2,18},{18,2},{3,19},{19,3},{4,20},{20... | collective-permute-start | bytes 3932168 | tf_op jit(solution)/shard_map/ppermute | solution.py:30
  1168.9 40.1 %all-to-all-start.13 = ((bf16[4,256,768]{2,1,0:T(8,128)(2,1)}), bf16[4,256,768]{2,1,0:T(8,128)(2,1)S(1)}, u32[]{:S(2)}, u32[]{:S(2)}) async-start(bf16[4,256,768]{2,1,0:T(8,128)(2,1)} %bitcast.309), calls=%async_computation.19 | async-start | bytes 3145728 | tf_op jit(solution)/shard_map/all_to_all | solution.py:1931
  1177.5 36.4 %collective-permute-start.70 = (bf16[2,64,2048]{2,1,0:T(8,128)(2,1)S(1)}, bf16[2,64,2048]{2,1,0:T(8,128)(2,1)S(1)}, u32[]{:S(2)}, u32[]{:S(2)}) collective-permute-start(bf16[2,64,2048]{2,1,0:T(8,128)(2,1)S(1)} %pad_maximum_fusion.refs_0_), channel_id=1, source_target_pairs={{0,3},{1,2},{2,1},{3,0},{4,7},{5,6},{6,5},{7,4},{8,11},{9,10},{10,... | collective-permute-start | bytes 1572872 | tf_op jit(solution)/shard_map/ppermute | solution.py:1852
  1179.8 34.0 %collective-permute-start.69 = (bf16[2,64,2048]{2,1,0:T(8,128)(2,1)S(1)}, bf16[2,64,2048]{2,1,0:T(8,128)(2,1)S(1)}, u32[]{:S(2)}, u32[]{:S(2)}) collective-permute-start(bf16[2,64,2048]{2,1,0:T(8,128)(2,1)S(1)} %pad_maximum_fusion.refs_0_), channel_id=1, source_target_pairs={{0,2},{1,3},{2,0},{3,1},{4,6},{5,7},{6,4},{7,5},{8,10},{9,11},{10,... | collective-permute-start | bytes 1572872 | tf_op jit(solution)/shard_map/ppermute | solution.py:1852
  1180.0 33.9 %collective-permute-start.68 = (bf16[2,64,2048]{2,1,0:T(8,128)(2,1)S(1)}, bf16[2,64,2048]{2,1,0:T(8,128)(2,1)}, u32[]{:S(2)}, u32[]{:S(2)}) collective-permute-start(bf16[2,64,2048]{2,1,0:T(8,128)(2,1)S(1)} %pad_maximum_fusion.refs_0_), channel_id=1, source_target_pairs={{0,1},{1,0},{2,3},{3,2},{4,5},{5,4},{6,7},{7,6},{8,9},{9,8},{10,11... | collective-permute-start | bytes 1572872 | tf_op jit(solution)/shard_map/ppermute | solution.py:1852
  (191 other events, 2446.4 us)
Sparse Core Ops, SparseCore 0:
  66.4 72.7 all-gather.6
  141.7 77.2 all-gather.8
  221.5 72.1 all-gather.10
  296.0 72.1 all-gather.12
  370.5 73.3 all-gather.14
  456.4 73.0 all-gather.16
  566.9 94.7 reduce-scatter.6
  679.7 82.3 reduce-scatter.8
  770.2 90.1 reduce-scatter.10
  869.0 96.3 reduce-scatter.12
  968.8 102.4 reduce-scatter.14
  1074.7 93.5 reduce-scatter.16

commit v5 on v4

--- a/solution.py
+++ b/solution.py
@@ -1628,6 +1628,77 @@
     return result.reshape(2, slices * (first + second), half)
 
 
+def run_sided(kernel, grid, side, in_specs, out_specs, out_shape, name, flops, moved, args):
+    return pl.pallas_call(
+        kernel,
+        grid_spec=pltpu.PrefetchScalarGridSpec(
+            num_scalar_prefetch=1, grid=grid, in_specs=in_specs, out_specs=out_specs
+        ),
+        out_shape=out_shape,
+        compiler_params=pltpu.CompilerParams(vmem_limit_bytes=VMEM_LIMIT),
+        cost_estimate=pl.CostEstimate(flops=flops, bytes_accessed=moved, transcendentals=0),
+        name=name,
+    )(side, *args)
+
+
+def half_of(rows, width):
+    return pl.BlockSpec((rows, width // 2), lambda step, side: (0, side[0]))
+
+
+def pair_rows_kernel(side_ref, left_ref, left_other_ref, right_ref, right_other_ref, out_ref):
+    total = inner_t(left_ref[...], right_ref[0]) + inner_t(left_other_ref[...], right_other_ref[0])
+    out_ref[0] = total.astype(jnp.bfloat16)
+
+
+def pair_rows(side, left, right):
+    rows, width = left[0].shape
+    slices, _, columns = right[0].shape
+    piece = pl.BlockSpec((1, rows, columns), lambda step, side: (step, 0, 0))
+    return run_sided(
+        pair_rows_kernel,
+        (slices,),
+        side,
+        [half_of(rows, width)] * 2 + [piece] * 2,
+        pl.BlockSpec((1, width // 2, columns), lambda step, side: (step, 0, 0)),
+        like((slices, width // 2, columns), jnp.bfloat16),
+        "pair_rows",
+        2 * rows * width * columns * slices,
+        slices * width * columns + rows * width * 2 + right[0].size * 4,
+        list(left) + list(right),
+    )
+
+
+def pair_cols_kernel(side_ref, *refs):
+    hidden, up, gated, grad = refs[0:2], refs[2:4], refs[4:6], refs[6:8]
+    out_ref = refs[8]
+    rows = hidden[0].shape[1]
+    out_ref[0, :-rows] = sum(inner_t(x[...], y[...]) for x, y in zip(gated, grad)).astype(jnp.bfloat16)
+    out_ref[0, -rows:] = sum(inner_t(x[...], y[...]) for x, y in zip(hidden, up)).astype(jnp.bfloat16)
+
+
+def pair_cols(side, hidden, upstream, gated, grad_attn, slices):
+    rows, width = upstream[0].shape
+    half = width // 2
+    first, second = hidden[0].shape[1] // slices, gated[0].shape[1] // slices
+
+    def piece(columns):
+        return [pl.BlockSpec((rows, columns), lambda step, side: (0, step))] * 2
+
+    result = run_sided(
+        pair_cols_kernel,
+        (slices,),
+        side,
+        piece(first) + [half_of(rows, width)] * 2 + piece(second) + [half_of(rows, width)] * 2,
+        pl.BlockSpec((1, first + second, half), lambda step, side: (step, 0, 0)),
+        like((slices, first + second, half), jnp.bfloat16),
+        "pair_cols",
+        4 * rows * (first + second) * slices * half,
+        slices * (first + second) * half * 2 + rows * width * 8,
+        list(hidden) + list(upstream) + list(gated) + list(grad_attn),
+    )
+    return result.reshape(slices * (first + second), half)
+
+
 def place_kernel(pieces, *refs):
     me_ref, out_ref = refs[0], refs[-1]
     for where, part in each_piece(me_ref, refs[1:-1]):
@@ -1676,10 +1747,10 @@
     )
 
 
-def finish_rows_kernel(widths, side_ref, layer0_ref, layer1_ref, received_ref, *out_refs):
+def finish_rows_kernel(widths, side_ref, layer0_ref, layer1_ref, received0_ref, received1_ref, *out_refs):
     side = side_ref[0]
     own = jnp.where(side == 0, layer0_ref[0], layer1_ref[0]).astype(jnp.float32)
-    other = received_ref[0].astype(jnp.float32)
+    other = jnp.where(side == 0, received0_ref[0], received1_ref[0]).astype(jnp.float32)
     rows = own.shape[0]
     start = 0
     for width, out_ref in zip(widths, out_refs):
@@ -1688,19 +1759,19 @@
         start += width
 
 
-def finish_rows(side, layer0, layer1, received, widths):
+def finish_rows(side, layer0, layer1, received0, received1, widths):
     shards, rows, columns = layer0.shape
     return run(
         functools.partial(finish_rows_kernel, widths),
         (shards,),
-        [in_smem()] + [slab((1, rows, columns), 0)] * 3,
+        [in_smem()] + [slab((1, rows, columns), 0)] * 4,
         tuple(slab((2 * rows, width), 1) for width in widths),
         tuple(like((2 * rows, shards * width), jnp.float32) for width in widths),
         [],
         "finish_rows",
         0,
         layer0.size * 14,
-        [side, layer0, layer1, received],
+        [side, layer0, layer1, received0, received1],
     )
 
 
@@ -1926,6 +1997,14 @@
     )
 
 
+def reduce_halves(grad):
+    return lax.psum_scatter(grad, HEAD, scatter_dimension=0, tiled=True)
+
+
+def with_other(value):
+    return value, partner(value)
+
+
 def collect_rows(part):
     shards = lax.axis_size(SEQ)
     return lax.all_to_all(part.reshape(shards, -1, part.shape[1]), SEQ, 0, 0)
@@ -1939,7 +2018,7 @@
     return lax.optimization_barrier((value, other))[0]
 
 
-def layer_backward_fast(me, piece, upstream, saved, gains, weights, small, aux, parts, plan):
+def layer_backward_fast(me, piece, upstream, saved, gains, weights, small, aux, parts, plan, pairs):
     at_mid, sum_rows, start, at_end, at_out, sum_cols, before_end, last_due = plan
     attn_gain, mlp_gain = gains
     w_proj, w_mix, w_cols, w_gu = weights
@@ -1956,7 +2035,12 @@
     grad_mid, grad_attn, dmlp, dmixed, dgate, dnorm = mid_back(
         me, mlp_gain, sums, mid, upstream, w_cols, mixed, gate_pre, norm_weight
     )
-    grad_both = grad_cols(hidden, upstream, gated, grad_attn, slices)
+    if pairs is None:
+        grad_both = grad_cols(hidden, upstream, gated, grad_attn, slices)
+    else:
+        grad_both = pair_cols(
+            pairs[0], pairs[2], with_other(upstream), pairs[1], with_other(grad_attn), slices
+        )
     grad_head = swap_pieces(for_partners(dmixed, piece), HEAD)
     grad_head, grad_both = lax.optimization_barrier((grad_head, grad_both))
     sum_gu = sum_rows(grad_gu, dmixed)
@@ -2104,6 +2188,7 @@
         mine = lax.dynamic_slice_in_dim(value, piece * sub, sub, 0)
         return by_partner(halved(mine), SEQ)
 
+    side = core[None].astype(jnp.int32)
     me = shard[None].astype(jnp.int32)
     place_at = piece[None].astype(jnp.int32)
     valid = valid[:, None]
@@ -2150,6 +2235,8 @@
         stats.append(stat)
         saved.append((resid, normed, gate_pre, mixer, base, ffn_in, gate_up, hidden))
         if layer == 0:
+            pairs = (side, with_other(gated), with_other(hidden))
+        if layer == 0:
             token_parts = exchange(pieces)
             gu1 = move_rows(after(gu_parts[1], token_parts))
             masked = my_tokens(after(masked, token_parts))
@@ -2202,7 +2289,7 @@
         return at_mid, sum_rows, start, at_end, at_out, sum_cols, before_end, last_due
 
     grad_h1, big1, small1, (last_sum, moved_gu1) = layer_backward_fast(
-        me, place_at, upstream, saved[1], gains[1], weights[1], small[1], aux, parts, plan_last()
+        me, place_at, upstream, saved[1], gains[1], weights[1], small[1], aux, parts, plan_last(), None
     )
     sum_proj1, sum_gu1, sum_both1 = big1
     last_sum = sum_pieces(last_sum)
@@ -2231,7 +2318,7 @@
             return pieces, running
 
         def sum_cols(grad_both, due, grad_pre, pieces):
-            sum_both = reduce_cols(after(grad_both, (due, grad_pre)))
+            sum_both = reduce_halves(after(grad_both, (due, grad_pre)))
             return all_sums(pieces), sum_both
 
         def before_end(sums):
@@ -2245,14 +2332,13 @@
         return at_mid, sum_rows, start, at_end, at_out, sum_cols, before_end, last_due
 
     grad_tokens, big0, small0, moved_proj1 = layer_backward_fast(
-        me, place_at, grad_h1, saved[0], gains[0], weights[0], small[0], aux, parts, plan_first()
+        me, place_at, grad_h1, saved[0], gains[0], weights[0], small[0], aux, parts, plan_first(), pairs
     )
     sum_proj0, sum_gu0, sum_both0 = big0
     moved_both1 = early["both"]
     moved_gu0 = early["gu"]
     moved_both0 = collect_cols(after(sum_both0, moved_gu0))
     input_grads = early["grads"]
-    side = core[None].astype(jnp.int32)
     grad_down, grad_out = finish_cols(
         side, moved_both0, moved_both1, partner(pick(first, moved_both1, moved_both0)), hidden_width
     )
@@ -2283,12 +2369,15 @@
     mix_grad = jnp.sum(lax.all_to_all(mix_grad, HEAD, 0, 0), axis=0)
     mix_grad = lax.all_to_all(jnp.transpose(mix_grad, (2, 0, 1, 3)), SEQ, 0, 0)
     mix_grad = jnp.transpose(mix_grad, (1, 2, 3, 0)).reshape(2, shard_rows, shards)
-    others = (input_grads, grad_down, grad_out, grad_gate, grad_up, mix_grad, norm_sum, gain_sums, per_head)
-    sum_proj0, others = lax.optimization_barrier((sum_proj0, others))
-    input_grads, grad_down, grad_out, grad_gate, grad_up, mix_grad, norm_sum, gain_sums, per_head = others
+    received_proj1 = partner(moved_proj1)
+    others = (input_grads, grad_down, grad_out, grad_gate, grad_up, mix_grad, norm_sum, gain_sums)
+    sum_proj0, others, per_head, received_proj1 = lax.optimization_barrier(
+        (sum_proj0, others, per_head, received_proj1)
+    )
+    input_grads, grad_down, grad_out, grad_gate, grad_up, mix_grad, norm_sum, gain_sums = others
     moved_proj0 = collect_rows(sum_proj0)
     grad_proj = finish_rows(
-        side, moved_proj0, moved_proj1, partner(pick(first, moved_proj1, moved_proj0)),
+        side, moved_proj0, moved_proj1, partner(moved_proj0), received_proj1,
         (HEAD_K, HEAD_K, HEAD_V, HEAD_V),
     )
     conv_grad = jnp.swapaxes(per_head[:, :taps_size].reshape(shards, CONVK, WIDTH), 0, 1)

time: 1250 us -> 1250 us (level)
  starting transfers between devices: 194 us -> 253 us
  waiting for transfers between devices: 571 us -> 515 us
    ppermute x42, waiting for transfers between devices: 207 us -> 164 us  [by_partner(): lax.ppermute(value, axis, [(i, i ^ k) for i in range(size)])]
    ppermute x48, waiting for transfers between devices: 157 us -> 134 us  [swap_pieces(): lax.ppermute(pieces[n], axis, [(i, i ^ n) for i in range(size)])]
    ppermute x48, starting transfers between devices: 50.1 us -> 71.3 us  [swap_pieces(): lax.ppermute(pieces[n], axis, [(i, i ^ n) for i in range(size)])]
    ppermute x42, starting transfers between devices: 69.8 us -> 85.7 us  [by_partner(): lax.ppermute(value, axis, [(i, i ^ k) for i in range(size)])]
    pallas_call x39 -> x38, Pallas kernels: 252 us -> 242 us  [run(): pl.pallas_call(kernel, grid=grid, in_specs=in_specs, out_specs=out_specs,...]
  transfers between devices with their start and end apart: 130 -> 135, of which waited for: 59 -> 71; matrix products, arithmetic and copies ran while one was open for 6% -> 5% of each run, Pallas kernels for 26% -> 26%
where the time goes in v5:
time: 1250 us; the launch traced here: 1240 us
  waiting for transfers between devices  515 us (41%)
  Pallas kernels  359 us (29%)
  starting transfers between devices  253 us (20%)
  local copies, waits for them, and re-layouts  65.2 us (5%)
  other arithmetic  27.7 us (2%)
  between operations  17.5 us (1%)
    pallas_call x38, Pallas kernels, run(): pl.pallas_call(kernel, grid=grid, in_specs=in_specs, out_specs=out_specs,...  242 us
    ppermute x42, waiting for transfers between devices, by_partner(): lax.ppermute(value, axis, [(i, i ^ k) for i in range(size)])  164 us
    ppermute x48, waiting for transfers between devices, swap_pieces(): lax.ppermute(pieces[n], axis, [(i, i ^ n) for i in range(size)])  134 us
    all_to_all x4, waiting for transfers between devices, move_rows(): return lax.all_to_all(part, SEQ, 0, 0).reshape(-1, part.shape[2])  90.8 us
    ppermute x42, starting transfers between devices, by_partner(): lax.ppermute(value, axis, [(i, i ^ k) for i in range(size)])  85.7 us
    ppermute x48, starting transfers between devices, swap_pieces(): lax.ppermute(pieces[n], axis, [(i, i ^ n) for i in range(size)])  71.3 us
    pallas_call x2, Pallas kernels, recur_backward(): pl.pallas_call(functools.partial(backward_kernel, parts), out_shape=(jax....  66 us
    all_to_all x4, waiting for transfers between devices, collect_rows(): return lax.all_to_all(part.reshape(shards, -1, part.shape[1]), SEQ, 0, 0)  45.4 us
  transfers between devices with their start and end apart: 135, of which 71 were waited for; matrix products, arithmetic and copies ran while one was open for 5% of the time, Pallas kernels for 26%

profile of v5, /device:TPU:1, one launch (start us, length us, event | category | flops | bytes accessed | tf_op | source)
XLA Modules:
  0.0 1236.3 jit_solution(6019139274320111278)
XLA Ops:
  41.6 24.6 %all-to-all-done = bf16[4,256,768]{2,1,0:T(8,128)(2,1)} async-done(((bf16[4,256,768]{2,1,0:T(8,128)(2,1)}), bf16[4,256,768]{2,1,0:T(8,128)(2,1)}, u32[]{:S(2)}, u32[]{:S(2)}) %all-to-all-start) | async-done | bytes 1572896 | tf_op jit(solution)/shard_map/all_to_all | solution.py:1971
  97.3 20.0 %collective-permute-done.7.refs_6_ = bf16[64,2048]{1,0:T(8,128)(2,1)S(1)} collective-permute-done((bf16[64,2048]{1,0:T(8,128)(2,1)S(1)}, bf16[64,2048]{1,0:T(8,128)(2,1)S(1)}, u32[]{:S(2)}, u32[]{:S(2)}) %collective-permute-start.7) | collective-permute-done | bytes 262176 | tf_op jit(solution)/shard_map/ppermute | solution.py:1923
  117.3 7.7 all-to-all-done.1.part_ref
  139.2 9.7 project_first.1
  153.8 19.8 %all-to-all-done.2 = bf16[4,256,768]{2,1,0:T(8,128)(2,1)S(1)} async-done(((bf16[4,256,768]{2,1,0:T(8,128)(2,1)}), bf16[4,256,768]{2,1,0:T(8,128)(2,1)S(1)}, u32[]{:S(2)}, u32[]{:S(2)}) %all-to-all-start.2) | async-done | bytes 1572896 | tf_op jit(solution)/shard_map/all_to_all | solution.py:1971
  187.1 34.3 %all-to-all-done.3 = bf16[4,256,768]{2,1,0:T(8,128)(2,1)S(1)} async-done(((bf16[4,256,768]{2,1,0:T(8,128)(2,1)}), bf16[4,256,768]{2,1,0:T(8,128)(2,1)S(1)}, u32[]{:S(2)}, u32[]{:S(2)}) %all-to-all-start.3) | async-done | bytes 1572896 | tf_op jit(solution)/shard_map/all_to_all | solution.py:1971
  226.0 21.1 %recur_forward.2 = (bf16[256,256]{1,0:T(8,128)(2,1)}, bf16[256,256]{1,0:T(8,128)(2,1)}, bf16[256,256]{1,0:T(8,128)(2,1)}, bf16[256,256]{1,0:T(8,128)(2,1)}, f32[16,128,256]{2,1,0:T(8,128)}, /*index=5*/f32[1024,64]{1,0:T(8,128)}) custom-call(s32[1]{0:T(128)} %bitcast.piece_ref.me_ref, bf16[256,640]{1,0:T(8,128)(2,1)} %get-tuple-element.264.refs_0_, ...), custom_call_target="tpu_custom_call" | custom-call | flops 40960000000 | bytes 8388608 | tf_op jit(solution)/shard_map/recur_forward/pallas_call | solution.py:980
  269.5 7.8 collective-permute-done.19.refs_1_
  277.3 8.0 collective-permute-done.20.refs_2_
  310.9 14.9 %feed.2 = (f32[256,2048]{1,0:T(8,128)}, bf16[256,2048]{1,0:T(8,128)(2,1)}, f32[4,256,768]{2,1,0:T(8,128)}, bf16[256,1536]{1,0:T(8,128)(2,1)}, bf16[64,2048]{1,0:...) custom-call(s32[1]{0:T(128)} %bitcast.1.refs_0_.me_ref, ...), custom_call_target="tpu_custom_call" | custom-call | flops 4831838208 | bytes 27262976 | tf_op jit(solution)/shard_map/feed/pallas_call | solution.py:1070
  325.8 8.8 collective-permute-start.25
  353.9 7.7 collective-permute-start.28
  367.2 13.4 %collective-permute-done.29.refs_5_ = bf16[64,2048]{1,0:T(8,128)(2,1)S(1)} collective-permute-done((bf16[64,2048]{1,0:T(8,128)(2,1)}, bf16[64,2048]{1,0:T(8,128)(2,1)S(1)}, u32[]{:S(2)}, u32[]{:S(2)}) %collective-permute-start.29) | collective-permute-done | bytes 262176 | tf_op jit(solution)/shard_map/ppermute | solution.py:1923
  381.4 10.9 project_next.1
  415.1 21.0 %recur_forward.3 = (bf16[256,256]{1,0:T(8,128)(2,1)}, bf16[256,256]{1,0:T(8,128)(2,1)}, bf16[256,256]{1,0:T(8,128)(2,1)}, bf16[256,256]{1,0:T(8,128)(2,1)}, f32[16,128,256]{2,1,0:T(8,128)}, /*index=5*/f32[1024,64]{1,0:T(8,128)}) custom-call(s32[1]{0:T(128)} %bitcast.piece_ref.me_ref, bf16[256,640]{1,0:T(8,128)(2,1)} %get-tuple-element.520.refs_0_, ...), custom_call_target="tpu_custom_call" | custom-call | flops 40960000000 | bytes 8388608 | tf_op jit(solution)/shard_map/recur_forward/pallas_call | solution.py:980
  445.2 12.1 all-to-all-done.5
  476.0 12.6 %collective-permute-done.41.refs_2_ = bf16[64,2048]{1,0:T(8,128)(2,1)S(1)} collective-permute-done((bf16[64,2048]{1,0:T(8,128)(2,1)}, bf16[64,2048]{1,0:T(8,128)(2,1)S(1)}, u32[]{:S(2)}, u32[]{:S(2)}) %collective-permute-start.41) | collective-permute-done | bytes 262176 | tf_op jit(solution)/shard_map/ppermute | solution.py:1945
  503.1 13.0 %collective-permute-done.44.refs_5_ = bf16[64,2048]{1,0:T(8,128)(2,1)S(1)} collective-permute-done((bf16[64,2048]{1,0:T(8,128)(2,1)}, bf16[64,2048]{1,0:T(8,128)(2,1)S(1)}, u32[]{:S(2)}, u32[]{:S(2)}) %collective-permute-start.44) | collective-permute-done | bytes 262176 | tf_op jit(solution)/shard_map/ppermute | solution.py:1923
  516.1 20.0 %all-gather.17.cloned.1.call-done = bf16[8192,768]{1,0:T(8,128)(2,1)} async-done(((bf16[1024,768]{1,0:T(8,128)(2,1)}), bf16[8192,768]{1,0:T(8,128)(2,1)}) %all-gather.17.cloned.1.call-update) | async-done | bytes 12582928 | tf_op jit(solution)/shard_map/all_gather | solution.py:1979
  536.1 14.9 %feed.3 = (f32[256,2048]{1,0:T(8,128)}, bf16[256,2048]{1,0:T(8,128)(2,1)}, f32[4,256,768]{2,1,0:T(8,128)}, bf16[256,1536]{1,0:T(8,128)(2,1)}, bf16[64,2048]{1,0:...) custom-call(s32[1]{0:T(128)} %bitcast.1.refs_0_.me_ref, ...), custom_call_target="tpu_custom_call" | custom-call | flops 4831838208 | bytes 27262976 | tf_op jit(solution)/shard_map/feed/pallas_call | solution.py:1070
  551.1 14.1 %feed_back.2 = (bf16[4,256,768]{2,1,0:T(8,128)(2,1)}, bf16[64,2048]{1,0:T(8,128)(2,1)}, bf16[64,2048]{1,0:T(8,128)(2,1)}, bf16[64,2048]{1,0:T(8,128)(2,1)}, bf16[64,2048]{1,0:T(8,128)(2,1)}) custom-call(s32[1]{0:T(128)} %bitcast.1.refs_0_.me_ref, bf16[256,2048]{1,0:T(8,128)(2,1)} %place.1.up_ref.refs_7_, f32[4,256,768]{2,1,0:T(8,128)} %get-tuple-element.314.gate_up_ref, ...), custom_call_target="tpu_custom_call" | custom-call | flops 4831838208 | bytes 25690112 | tf_op jit(solution)/shard_map/feed_back/pallas_call | solution.py:1070
  565.2 8.1 grad_rows.4
  577.7 9.1 collective-permute-done.46.refs_1_
  586.9 8.1 collective-permute-done.48.refs_3_
  613.6 8.4 collective-permute-done.51.refs_5_
  622.7 8.7 mid_back.2
  635.8 10.4 grad_cols.1
  654.7 33.1 %recur_backward.2 = (bf16[256,640]{1,0:T(8,128)(2,1)}, bf16[256,640]{1,0:T(8,128)(2,1)}, bf16[256,640]{1,0:T(8,128)(2,1)}, bf16[256,640]{1,0:T(8,128)(2,1)}, f32[8,512]{1,0:T(8,128)}, /*index=5*/f32[8,128]{1,0:T(8,128)}) custom-call(s32[1]{0:T(128)} %bitcast.piece_ref.me_ref, bf16[256,640]{1,0:T(8,128)(2,1)} %get-tuple-element.520.refs_0_, ...), custom_call_target="tpu_custom_call" | custom-call | flops 40960000000 | bytes 8388608 | tf_op jit(solution)/shard_map/recur_backward/pallas_call | solution.py:1005
  705.8 12.4 %project_back.2 = (bf16[4,256,768]{2,1,0:T(8,128)(2,1)}, f32[4,8,2048]{2,1,0:T(8,128)}, bf16[64,2048]{1,0:T(8,128)(2,1)}, bf16[64,2048]{1,0:T(8,128)(2,1)}, bf16...) custom-call(s32[1]{0:T(128)} %bitcast.1.refs_0_.me_ref, s32[1]{0:T(128)} %bitcast.piece_ref.me_ref, ...), custom_call_target="tpu_custom_call" | custom-call | flops 3221225472 | bytes 18874368 | tf_op jit(solution)/shard_map/project_back/pallas_call | solution.py:1070
  718.2 10.6 all-to-all-done.6.layer1_ref
  732.4 8.1 grad_rows.5
  780.8 9.4 all-to-all-start.7
  790.2 16.3 %feed_back.3 = (bf16[4,256,768]{2,1,0:T(8,128)(2,1)}, bf16[64,2048]{1,0:T(8,128)(2,1)}, bf16[64,2048]{1,0:T(8,128)(2,1)}, bf16[64,2048]{1,0:T(8,128)(2,1)}, bf16[64,2048]{1,0:T(8,128)(2,1)}) custom-call(s32[1]{0:T(128)} %bitcast.1.refs_0_.me_ref, bf16[256,2048]{1,0:T(8,128)(2,1)} %get-tuple-element.395.up_ref.refs_7_.refs_2_, ...), custom_call_target="tpu_custom_call" | custom-call | flops 4831838208 | bytes 25690112 | tf_op jit(solution)/shard_map/feed_back/pallas_call | solution.py:1070
  811.5 8.1 grad_rows.6
  819.7 18.3 %collective-permute-done.72.refs_2_ = bf16[64,2048]{1,0:T(8,128)(2,1)} collective-permute-done((bf16[64,2048]{1,0:T(8,128)(2,1)}, bf16[64,2048]{1,0:T(8,128)(2,1)}, u32[]{:S(2)}, u32[]{:S(2)}) %collective-permute-start.72) | collective-permute-done | bytes 262176 | tf_op jit(solution)/shard_map/ppermute | solution.py:1945
  862.0 8.9 mid_back.3
  889.3 8.3 pair_cols.1
  904.9 32.9 %recur_backward.3 = (bf16[256,640]{1,0:T(8,128)(2,1)}, bf16[256,640]{1,0:T(8,128)(2,1)}, bf16[256,640]{1,0:T(8,128)(2,1)}, bf16[256,640]{1,0:T(8,128)(2,1)}, f32[8,512]{1,0:T(8,128)}, /*index=5*/f32[8,128]{1,0:T(8,128)}) custom-call(s32[1]{0:T(128)} %bitcast.piece_ref.me_ref, bf16[256,640]{1,0:T(8,128)(2,1)} %get-tuple-element.264.refs_0_, ...), custom_call_target="tpu_custom_call" | custom-call | flops 40960000000 | bytes 8388608 | tf_op jit(solution)/shard_map/recur_backward/pallas_call | solution.py:1005
  949.5 9.3 collective-permute-done.86.refs_3_
  958.8 11.7 project_back.3
  981.2 8.1 grad_rows.7
  990.3 8.0 collective-permute-done.89.refs_3_
  1016.2 8.4 collective-permute-done.92.refs_5_
  1029.7 8.2 all-to-all-start.9
  1047.0 10.6 collective-permute-done.94.refs_1_
  1059.4 9.7 collective-permute-done.96.refs_3_
  1110.5 23.9 %all-to-all-done.10.layer0_ref = bf16[4,640,256]{2,1,0:T(8,128)(2,1)S(1)} async-done(((bf16[4,640,256]{2,1,0:T(8,128)(2,1)}), bf16[4,640,256]{2,1,0:T(8,128)(2,1)S(1)}, u32[]{:S(2)}, u32[]{:S(2)}) %all-to-all-start.10) | async-done | bytes 1310752 | tf_op jit(solution)/shard_map/all_to_all | solution.py:2014
  1186.4 27.4 %all-to-all-done.13.layer0_ref = bf16[4,256,768]{2,1,0:T(8,128)(2,1)S(1)} async-done(((bf16[4,256,768]{2,1,0:T(8,128)(2,1)}), bf16[4,256,768]{2,1,0:T(8,128)(2,1)S(1)}, u32[]{:S(2)}, u32[]{:S(2)}) %all-to-all-start.13) | async-done | bytes 1572896 | tf_op jit(solution)/shard_map/all_to_all | solution.py:2010
  (668 shorter events, 558.1 us)
Async XLA Ops:
  24.2 42.0 %all-to-all-start = ((bf16[4,256,768]{2,1,0:T(8,128)(2,1)}), bf16[4,256,768]{2,1,0:T(8,128)(2,1)}, u32[]{:S(2)}, u32[]{:S(2)}) async-start(bf16[4,256,768]{2,1,0:T(8,128)(2,1)} %get-tuple-element.500), calls=%async_computation | async-start | bytes 3145728 | tf_op jit(solution)/shard_map/all_to_all | solution.py:1971
  29.6 109.5 %all-gather.7.cloned.1.call-start = ((), (), s32[]{:S(2)}) async-start(), calls=%async_computation.20 | async-start | bytes 14155776 | tf_op jit(solution)/shard_map/all_gather | solution.py:1979
  67.8 29.5 %collective-permute-start.5 = (bf16[64,2048]{1,0:T(8,128)(2,1)S(1)}, bf16[64,2048]{1,0:T(8,128)(2,1)S(1)}, u32[]{:S(2)}, u32[]{:S(2)}) collective-permute-start(bf16[64,2048]{1,0:T(8,128)(2,1)S(1)} %reshape.343.refs_3_), channel_id=1, source_target_pairs={{0,4},{4,0},{8,12},{12,8},{1,5},{5,1},{9,13},{13,9},{2,6},{6,2},{1... | collective-permute-start | bytes 786440 | tf_op jit(solution)/shard_map/ppermute | solution.py:1923
  67.9 29.4 %collective-permute-start.6 = (bf16[64,2048]{1,0:T(8,128)(2,1)S(1)}, bf16[64,2048]{1,0:T(8,128)(2,1)S(1)}, u32[]{:S(2)}, u32[]{:S(2)}) collective-permute-start(bf16[64,2048]{1,0:T(8,128)(2,1)S(1)} %reshape.343.refs_3_), channel_id=1, source_target_pairs={{0,8},{4,12},{8,0},{12,4},{1,9},{5,13},{9,1},{13,5},{2,10},{6,14},... | collective-permute-start | bytes 786440 | tf_op jit(solution)/shard_map/ppermute | solution.py:1923
  85.0 40.0 %all-to-all-start.1 = ((bf16[4,640,256]{2,1,0:T(8,128)(2,1)}), bf16[4,640,256]{2,1,0:T(8,128)(2,1)S(1)}, u32[]{:S(2)}, u32[]{:S(2)}) async-start(bf16[4,640,256]{2,1,0:T(8,128)(2,1)} %get-tuple-element.261), calls=%async_computation.1 | async-start | bytes 2621440 | tf_op jit(solution)/shard_map/all_to_all | solution.py:2200
  88.6 172.3 %all-gather.9.cloned.1.call-start = ((), (), s32[]{:S(2)}) async-start(), calls=%async_computation.21 | async-start | bytes 11796480 | tf_op jit(solution)/shard_map/all_gather | solution.py:1984
  92.9 24.4 %collective-permute-start.7 = (bf16[64,2048]{1,0:T(8,128)(2,1)S(1)}, bf16[64,2048]{1,0:T(8,128)(2,1)S(1)}, u32[]{:S(2)}, u32[]{:S(2)}) collective-permute-start(bf16[64,2048]{1,0:T(8,128)(2,1)S(1)} %reshape.343.refs_3_), channel_id=1, source_target_pairs={{0,12},{4,8},{8,4},{12,0},{1,13},{5,9},{9,5},{13,1},{2,14},{6,10},... | collective-permute-start | bytes 786440 | tf_op jit(solution)/shard_map/ppermute | solution.py:1923
  129.6 44.0 %all-to-all-start.2 = ((bf16[4,256,768]{2,1,0:T(8,128)(2,1)}), bf16[4,256,768]{2,1,0:T(8,128)(2,1)S(1)}, u32[]{:S(2)}, u32[]{:S(2)}) async-start(bf16[4,256,768]{2,1,0:T(8,128)(2,1)} %get-tuple-element.263), calls=%async_computation.2 | async-start | bytes 3145728 | tf_op jit(solution)/shard_map/all_to_all | solution.py:1971
  137.1 173.1 %all-gather.11.cloned.1.call-start = ((), (), s32[]{:S(2)}) async-start(), calls=%async_computation.22 | async-start | bytes 14155776 | tf_op jit(solution)/shard_map/all_gather | solution.py:1979
  151.2 22.4 %collective-permute-start.13 = (bf16[256,640]{1,0:T(8,128)(2,1)S(1)}, bf16[256,640]{1,0:T(8,128)(2,1)S(1)}, u32[]{:S(2)}, u32[]{:S(2)}) collective-permute-start(bf16[256,640]{1,0:T(8,128)(2,1)S(1)} %get-tuple-element.523), channel_id=1, source_target_pairs={{0,1},{1,0},{2,3},{3,2},{4,5},{5,4},{6,7},{7,6},{8,9},{9,8},{10,11... | collective-permute-start | bytes 983048 | tf_op jit(solution)/shard_map/ppermute | solution.py:1945
  152.4 21.2 %collective-permute-start.14 = (bf16[256,640]{1,0:T(8,128)(2,1)S(1)}, bf16[256,640]{1,0:T(8,128)(2,1)}, u32[]{:S(2)}, u32[]{:S(2)}) collective-permute-start(bf16[256,640]{1,0:T(8,128)(2,1)S(1)} %get-tuple-element.522), channel_id=1, source_target_pairs={{0,2},{1,3},{2,0},{3,1},{4,6},{5,7},{6,4},{7,5},{8,10},{9,11},{10,... | collective-permute-start | bytes 983048 | tf_op jit(solution)/shard_map/ppermute | solution.py:1945
  153.1 27.5 %collective-permute-start.15 = (bf16[256,640]{1,0:T(8,128)(2,1)S(1)}, bf16[256,640]{1,0:T(8,128)(2,1)}, u32[]{:S(2)}, u32[]{:S(2)}) collective-permute-start(bf16[256,640]{1,0:T(8,128)(2,1)S(1)} %get-tuple-element.521), channel_id=1, source_target_pairs={{0,3},{1,2},{2,1},{3,0},{4,7},{5,6},{6,5},{7,4},{8,11},{9,10},{10,... | collective-permute-start | bytes 983048 | tf_op jit(solution)/shard_map/ppermute | solution.py:1945
  180.7 40.7 %all-to-all-start.3 = ((bf16[4,256,768]{2,1,0:T(8,128)(2,1)}), bf16[4,256,768]{2,1,0:T(8,128)(2,1)S(1)}, u32[]{:S(2)}, u32[]{:S(2)}) async-start(bf16[4,256,768]{2,1,0:T(8,128)(2,1)} %get-tuple-element.273), calls=%async_computation.3 | async-start | bytes 3145728 | tf_op jit(solution)/shard_map/all_to_all | solution.py:1971
  221.4 35.2 %all-to-all-start.4 = ((bf16[4,640,256]{2,1,0:T(8,128)(2,1)}), bf16[4,640,256]{2,1,0:T(8,128)(2,1)}, u32[]{:S(2)}, u32[]{:S(2)}) async-start(bf16[4,640,256]{2,1,0:T(8,128)(2,1)} %get-tuple-element.274), calls=%async_computation.4 | async-start | bytes 2621440 | tf_op jit(solution)/shard_map/all_to_all | solution.py:1975
  225.8 154.8 %all-gather.13.cloned.1.call-start = ((), (), s32[]{:S(2)}) async-start(), calls=%async_computation.23 | async-start | bytes 14155776 | tf_op jit(solution)/shard_map/all_gather | solution.py:1979
  260.3 198.6 %all-gather.15.cloned.1.call-start = ((), (), s32[]{:S(2)}) async-start(), calls=%async_computation.24 | async-start | bytes 11796480 | tf_op jit(solution)/shard_map/all_gather | solution.py:1984
  399.0 40.8 %collective-permute-start.37 = (bf16[64,2048]{1,0:T(8,128)(2,1)S(1)}, bf16[64,2048]{1,0:T(8,128)(2,1)}, u32[]{:S(2)}, u32[]{:S(2)}) collective-permute-start(bf16[64,2048]{1,0:T(8,128)(2,1)S(1)} %reshape.357.refs_1_), channel_id=1, source_target_pairs={{0,4},{4,0},{8,12},{12,8},{1,5},{5,1},{9,13},{13,9},{2,6},{6,2},{1... | collective-permute-start | bytes 786440 | tf_op jit(solution)/shard_map/ppermute | solution.py:1923
  405.0 34.9 %collective-permute-start.38 = (bf16[64,2048]{1,0:T(8,128)(2,1)S(1)}, bf16[64,2048]{1,0:T(8,128)(2,1)}, u32[]{:S(2)}, u32[]{:S(2)}) collective-permute-start(bf16[64,2048]{1,0:T(8,128)(2,1)S(1)} %reshape.357.refs_1_), channel_id=1, source_target_pairs={{0,8},{4,12},{8,0},{12,4},{1,9},{5,13},{9,1},{13,5},{2,10},{6,14},... | collective-permute-start | bytes 786440 | tf_op jit(solution)/shard_map/ppermute | solution.py:1923
  405.0 52.3 %all-to-all-start.5 = ((bf16[4,256,768]{2,1,0:T(8,128)(2,1)}), bf16[4,256,768]{2,1,0:T(8,128)(2,1)S(1)}, u32[]{:S(2)}, u32[]{:S(2)}) async-start(bf16[4,256,768]{2,1,0:T(8,128)(2,1)} %get-tuple-element.297), calls=%async_computation.5 | async-start | bytes 3145728 | tf_op jit(solution)/shard_map/all_to_all | solution.py:1971
  408.6 127.5 %all-gather.17.cloned.1.call-start = ((), (), s32[]{:S(2)}) async-start(), calls=%async_computation.25 | async-start | bytes 14155776 | tf_op jit(solution)/shard_map/all_gather | solution.py:1979
  409.1 36.1 %collective-permute-start.39 = (bf16[64,2048]{1,0:T(8,128)(2,1)S(1)}, bf16[64,2048]{1,0:T(8,128)(2,1)}, u32[]{:S(2)}, u32[]{:S(2)}) collective-permute-start(bf16[64,2048]{1,0:T(8,128)(2,1)S(1)} %reshape.357.refs_1_), channel_id=1, source_target_pairs={{0,12},{4,8},{8,4},{12,0},{1,13},{5,9},{9,5},{13,1},{2,14},{6,10},... | collective-permute-start | bytes 786440 | tf_op jit(solution)/shard_map/ppermute | solution.py:1923
  436.1 21.2 %collective-permute-start.34 = (bf16[256,256]{1,0:T(8,128)(2,1)}, bf16[256,256]{1,0:T(8,128)(2,1)S(1)}, u32[]{:S(2)}, u32[]{:S(2)}) collective-permute-start(bf16[256,256]{1,0:T(8,128)(2,1)} %get-tuple-element.294), channel_id=1, source_target_pairs={{0,1},{1,0},{2,3},{3,2},{4,5},{5,4},{6,7},{7,6},{8,9},{9,8},{10,11... | collective-permute-start | bytes 393224 | tf_op jit(solution)/shard_map/ppermute | solution.py:1945
  436.2 21.1 %collective-permute-start.35 = (bf16[256,256]{1,0:T(8,128)(2,1)}, bf16[256,256]{1,0:T(8,128)(2,1)S(1)}, u32[]{:S(2)}, u32[]{:S(2)}) collective-permute-start(bf16[256,256]{1,0:T(8,128)(2,1)} %get-tuple-element.295), channel_id=1, source_target_pairs={{0,2},{1,3},{2,0},{3,1},{4,6},{5,7},{6,4},{7,5},{8,10},{9,11},{10,... | collective-permute-start | bytes 393224 | tf_op jit(solution)/shard_map/ppermute | solution.py:1945
  458.6 229.2 %reduce-scatter.7.cloned.1.call-start = ((), (), s32[]{:S(2)}) async-start(), calls=%async_computation.26 | async-start | bytes 14155776 | tf_op jit(solution)/shard_map/reduce_scatter | solution.py:1989
  573.3 199.1 %reduce-scatter.9.cloned.1.call-start = ((), (), s32[]{:S(2)}) async-start(), calls=%async_computation.27 | async-start | bytes 11796480 | tf_op jit(solution)/shard_map/reduce_scatter | solution.py:1995
  646.3 41.5 %collective-permute-start.55 = (bf16[64,2048]{1,0:T(8,128)(2,1)S(1)}, bf16[64,2048]{1,0:T(8,128)(2,1)S(1)}, u32[]{:S(2)}, u32[]{:S(2)}) collective-permute-start(bf16[64,2048]{1,0:T(8,128)(2,1)S(1)} %copy-done.105), channel_id=1, source_target_pairs={{0,4},{4,0},{8,12},{12,8},{1,5},{5,1},{9,13},{13,9},{2,6},{6,2},{1... | collective-permute-start | bytes 786440 | tf_op jit(solution)/shard_map/ppermute | solution.py:1945
  652.5 35.3 %collective-permute-start.56 = (bf16[64,2048]{1,0:T(8,128)(2,1)S(1)}, bf16[64,2048]{1,0:T(8,128)(2,1)S(1)}, u32[]{:S(2)}, u32[]{:S(2)}) collective-permute-start(bf16[64,2048]{1,0:T(8,128)(2,1)S(1)} %copy-done.104), channel_id=1, source_target_pairs={{0,8},{4,12},{8,0},{12,4},{1,9},{5,13},{9,1},{13,5},{2,10},{6,14},... | collective-permute-start | bytes 786440 | tf_op jit(solution)/shard_map/ppermute | solution.py:1945
  653.5 34.3 %collective-permute-start.57 = (bf16[64,2048]{1,0:T(8,128)(2,1)S(1)}, bf16[64,2048]{1,0:T(8,128)(2,1)S(1)}, u32[]{:S(2)}, u32[]{:S(2)}) collective-permute-start(bf16[64,2048]{1,0:T(8,128)(2,1)S(1)} %copy-done.103), channel_id=1, source_target_pairs={{0,12},{4,8},{8,4},{12,0},{1,13},{5,9},{9,5},{13,1},{2,14},{6,10},... | collective-permute-start | bytes 786440 | tf_op jit(solution)/shard_map/ppermute | solution.py:1945
  688.7 40.1 %all-to-all-start.6 = ((bf16[4,256,768]{2,1,0:T(8,128)(2,1)}), bf16[4,256,768]{2,1,0:T(8,128)(2,1)S(1)}, u32[]{:S(2)}, u32[]{:S(2)}) async-start(bf16[4,256,768]{2,1,0:T(8,128)(2,1)} %bitcast.311), calls=%async_computation.7 | async-start | bytes 3145728 | tf_op jit(solution)/shard_map/all_to_all | solution.py:2010
  692.4 179.9 %reduce-scatter.11.cloned.1.call-start = ((), (), s32[]{:S(2)}) async-start(), calls=%async_computation.28 | async-start | bytes 14155776 | tf_op jit(solution)/shard_map/reduce_scatter | solution.py:1989
  780.8 81.2 %all-to-all-start.7 = ((bf16[4,640,256]{2,1,0:T(8,128)(2,1)}), bf16[4,640,256]{2,1,0:T(8,128)(2,1)}, u32[]{:S(2)}, u32[]{:S(2)}) async-start(bf16[4,640,256]{2,1,0:T(8,128)(2,1)} %split_cols.2), calls=%async_computation.9 | async-start | bytes 2621440 | tf_op jit(solution)/shard_map/all_to_all | solution.py:2014
  790.2 187.4 %reduce-scatter.13.cloned.1.call-start = ((), (), s32[]{:S(2)}) async-start(), calls=%async_computation.29 | async-start | bytes 14155776 | tf_op jit(solution)/shard_map/reduce_scatter | solution.py:1989
  809.4 28.6 %collective-permute-start.72 = (bf16[64,2048]{1,0:T(8,128)(2,1)}, bf16[64,2048]{1,0:T(8,128)(2,1)}, u32[]{:S(2)}, u32[]{:S(2)}) collective-permute-start(bf16[64,2048]{1,0:T(8,128)(2,1)} %get-tuple-element.399), channel_id=1, source_target_pairs={{0,8},{4,12},{8,0},{12,4},{1,9},{5,13},{9,1},{13,5},{2,10},{6,14},... | collective-permute-start | bytes 786440 | tf_op jit(solution)/shard_map/ppermute | solution.py:1945
  810.1 27.9 %collective-permute-start.73 = (bf16[64,2048]{1,0:T(8,128)(2,1)}, bf16[64,2048]{1,0:T(8,128)(2,1)}, u32[]{:S(2)}, u32[]{:S(2)}) collective-permute-start(bf16[64,2048]{1,0:T(8,128)(2,1)} %get-tuple-element.400), channel_id=1, source_target_pairs={{0,12},{4,8},{8,4},{12,0},{1,13},{5,9},{9,5},{13,1},{2,14},{6,10},... | collective-permute-start | bytes 786440 | tf_op jit(solution)/shard_map/ppermute | solution.py:1945
  897.6 43.9 %all-to-all-start.8 = ((bf16[4,256,768]{2,1,0:T(8,128)(2,1)}), bf16[4,256,768]{2,1,0:T(8,128)(2,1)}, u32[]{:S(2)}, u32[]{:S(2)}) async-start(bf16[4,256,768]{2,1,0:T(8,128)(2,1)} %bitcast.310), calls=%async_computation.11 | async-start | bytes 3145728 | tf_op jit(solution)/shard_map/all_to_all | solution.py:2010
  904.9 171.0 %reduce-scatter.15.cloned.1.call-start = ((), (), s32[]{:S(2)}) async-start(), calls=%async_computation.30 | async-start | bytes 6553600 | tf_op jit(solution)/shard_map/reduce_scatter | solution.py:2001
  1029.7 46.2 %all-to-all-start.9 = ((bf16[4,256,768]{2,1,0:T(8,128)(2,1)}), bf16[4,256,768]{2,1,0:T(8,128)(2,1)}, u32[]{:S(2)}, u32[]{:S(2)}) async-start(bf16[4,256,768]{2,1,0:T(8,128)(2,1)} %bitcast.309), calls=%async_computation.14 | async-start | bytes 3145728 | tf_op jit(solution)/shard_map/all_to_all | solution.py:2010
  1037.9 135.8 %reduce-scatter.17.cloned.1.call-start = ((), (), s32[]{:S(2)}) async-start(), calls=%async_computation.31 | async-start | bytes 14155776 | tf_op jit(solution)/shard_map/reduce_scatter | solution.py:1989
  1046.2 22.8 %collective-permute-start.96 = (bf16[2,64,2048]{2,1,0:T(8,128)(2,1)S(1)}, bf16[2,64,2048]{2,1,0:T(8,128)(2,1)}, u32[]{:S(2)}, u32[]{:S(2)}) collective-permute-start(bf16[2,64,2048]{2,1,0:T(8,128)(2,1)S(1)} %pad_maximum_fusion.1.refs_0_), channel_id=1, source_target_pairs={{0,3},{1,2},{2,1},{3,0},{4,7},{5,6},{6,5},{7,4},{8,11},{9,10},{10,... | collective-permute-start | bytes 1572872 | tf_op jit(solution)/shard_map/ppermute | solution.py:1923
  1099.9 34.5 %all-to-all-start.10 = ((bf16[4,640,256]{2,1,0:T(8,128)(2,1)}), bf16[4,640,256]{2,1,0:T(8,128)(2,1)S(1)}, u32[]{:S(2)}, u32[]{:S(2)}) async-start(bf16[4,640,256]{2,1,0:T(8,128)(2,1)} %split_cols.3), calls=%async_computation.16 | async-start | bytes 2621440 | tf_op jit(solution)/shard_map/all_to_all | solution.py:2014
  1105.5 68.1 %collective-permute-start.107 = (bf16[4,256,768]{2,1,0:T(8,128)(2,1)}, bf16[4,256,768]{2,1,0:T(8,128)(2,1)}, u32[]{:S(2)}, u32[]{:S(2)}) collective-permute-start(bf16[4,256,768]{2,1,0:T(8,128)(2,1)} %all-to-all-done.8.layer1_ref), channel_id=1, source_target_pairs={{0,16},{16,0},{1,17},{17,1},{2,18},{18,2},{3,19},{19,3},{4,20},{20... | collective-permute-start | bytes 4718600 | tf_op jit(solution)/shard_map/ppermute | solution.py:30
  1106.6 32.3 %collective-permute-start.100 = (f32[4360]{0:T(1024)S(1)}, f32[4360]{0:T(1024)S(1)}, u32[]{:S(2)}, u32[]{:S(2)}) collective-permute-start(f32[4360]{0:T(1024)S(1)} %slice.426), channel_id=1, source_target_pairs={{0,1},{1,0},{2,3},{3,2},{4,5},{5,4},{6,7},{7,6},{8,9},{9,8},{10,11... | collective-permute-start | bytes 52328 | tf_op jit(solution)/shard_map/ppermute | solution.py:30
  1110.5 51.5 %collective-permute-start.98 = (bf16[4,256,768]{2,1,0:T(8,128)(2,1)}, bf16[4,256,768]{2,1,0:T(8,128)(2,1)S(1)}, u32[]{:S(2)}, u32[]{:S(2)}) collective-permute-start(bf16[4,256,768]{2,1,0:T(8,128)(2,1)} %broadcast_select_fusion), channel_id=1, source_target_pairs={{0,16},{16,0},{1,17},{17,1},{2,18},{18,2},{3,19},{19,3},{4,20},{20... | collective-permute-start | bytes 4718600 | tf_op jit(solution)/shard_map/ppermute | solution.py:30
  1135.9 33.0 %collective-permute-start.97 = (bf16[4,640,256]{2,1,0:T(8,128)(2,1)}, bf16[4,640,256]{2,1,0:T(8,128)(2,1)}, u32[]{:S(2)}, u32[]{:S(2)}) collective-permute-start(bf16[4,640,256]{2,1,0:T(8,128)(2,1)} %broadcast_select_fusion.5), channel_id=1, source_target_pairs={{0,16},{16,0},{1,17},{17,1},{2,18},{18,2},{3,19},{19,3},{4,20},{20... | collective-permute-start | bytes 3932168 | tf_op jit(solution)/shard_map/ppermute | solution.py:30
  1173.7 40.1 %all-to-all-start.13 = ((bf16[4,256,768]{2,1,0:T(8,128)(2,1)}), bf16[4,256,768]{2,1,0:T(8,128)(2,1)S(1)}, u32[]{:S(2)}, u32[]{:S(2)}) async-start(bf16[4,256,768]{2,1,0:T(8,128)(2,1)} %bitcast.308), calls=%async_computation.19 | async-start | bytes 3145728 | tf_op jit(solution)/shard_map/all_to_all | solution.py:2010
  1183.7 31.6 %collective-permute-start.68 = (bf16[2,64,2048]{2,1,0:T(8,128)(2,1)S(1)}, bf16[2,64,2048]{2,1,0:T(8,128)(2,1)S(1)}, u32[]{:S(2)}, u32[]{:S(2)}) collective-permute-start(bf16[2,64,2048]{2,1,0:T(8,128)(2,1)S(1)} %pad_maximum_fusion.refs_0_), channel_id=1, source_target_pairs={{0,1},{1,0},{2,3},{3,2},{4,5},{5,4},{6,7},{7,6},{8,9},{9,8},{10,11... | collective-permute-start | bytes 1572872 | tf_op jit(solution)/shard_map/ppermute | solution.py:1923
  1184.6 30.7 %collective-permute-start.69 = (bf16[2,64,2048]{2,1,0:T(8,128)(2,1)S(1)}, bf16[2,64,2048]{2,1,0:T(8,128)(2,1)}, u32[]{:S(2)}, u32[]{:S(2)}) collective-permute-start(bf16[2,64,2048]{2,1,0:T(8,128)(2,1)S(1)} %pad_maximum_fusion.refs_0_), channel_id=1, source_target_pairs={{0,2},{1,3},{2,0},{3,1},{4,6},{5,7},{6,4},{7,5},{8,10},{9,11},{10,... | collective-permute-start | bytes 1572872 | tf_op jit(solution)/shard_map/ppermute | solution.py:1923
  1185.7 30.4 %collective-permute-start.70 = (bf16[2,64,2048]{2,1,0:T(8,128)(2,1)S(1)}, bf16[2,64,2048]{2,1,0:T(8,128)(2,1)}, u32[]{:S(2)}, u32[]{:S(2)}) collective-permute-start(bf16[2,64,2048]{2,1,0:T(8,128)(2,1)S(1)} %pad_maximum_fusion.refs_0_), channel_id=1, source_target_pairs={{0,3},{1,2},{2,1},{3,0},{4,7},{5,6},{6,5},{7,4},{8,11},{9,10},{10,... | collective-permute-start | bytes 1572872 | tf_op jit(solution)/shard_map/ppermute | solution.py:1923
  (199 other events, 2396.9 us)
Sparse Core Ops, SparseCore 0:
  66.3 72.7 all-gather.6
  141.6 77.2 all-gather.8
  221.4 72.1 all-gather.10
  295.9 72.1 all-gather.12
  370.4 74.2 all-gather.14
  458.7 77.3 all-gather.16
  573.4 93.7 reduce-scatter.6
  688.0 84.3 reduce-scatter.8
  775.9 96.3 reduce-scatter.10
  875.6 101.8 reduce-scatter.12
  980.6 61.3 reduce-scatter.14
  1076.1 92.1 reduce-scatter.16
